TPU v7x, 32 devices: a whole 2x2x4 slice. The times are simulated.
32 devices in a mesh: dp: 8 (over z, x), head: 4 (over y, core).
Axes of the slice: x: 2, y: 2, z: 4, core: 2. Of those that a mesh axis runs over, the one named last changes fastest.
Arguments:
- frames: bfloat16 [16384, 1024], P(('dp', 'head')), may hold values from -6 to 6
- ffn_inner: bfloat16 [2, 1024, 4096], P(None, ('dp', 'head')), may hold values from -0.1875 to 0.1875
- ffn_outer: bfloat16 [2, 4096, 1024], P(None, ('dp', 'head')), may hold values from -0.09375 to 0.09375
- attn_qkv: bfloat16 [1024, 3072], P(('dp', 'head')), may hold values from -0.1875 to 0.1875
- attn_proj: bfloat16 [1024, 1024], P(('dp', 'head')), may hold values from -0.75 to 0.75
- conv_expand: bfloat16 [1024, 2048], P(('dp', 'head')), may hold values from -0.1875 to 0.1875
- conv_depth: bfloat16 [32, 1024], P(None, ('dp', 'head')), may hold values from -1 to 1
- conv_proj: bfloat16 [1024, 1024], P(('dp', 'head')), may hold values from -0.1875 to 0.1875
- norm_gains: bfloat16 [6, 1024], P(None, ('dp', 'head')), may hold values from 0.099609375 to 1.8984375
- head_proj: bfloat16 [1024, 8192], P('dp', 'head'), may hold values from -0.1875 to 0.1875
- lengths: int32 [32], P(('dp', 'head')), may hold values from 256 to 512, as said below
- mask_starts: int32 [32, 20], P(('dp', 'head')), may hold values from 0 to 512, as said below
- target_codes: int32 [16384], P(('dp', 'head')), may hold values from 0 to 8191
- out_grad: bfloat16 [16384, 1024], P(('dp', 'head')), may hold values from -6 to 6
Outputs:
- activations: bfloat16 [16384, 1024], P(('dp', 'head'))
- loss: float32 [], replicated
- input_grad: float32 [16384, 1024], P(('dp', 'head'))
- ffn_inner_grad: float32 [2, 1024, 4096], P(None, ('dp', 'head'))
- ffn_outer_grad: float32 [2, 4096, 1024], P(None, ('dp', 'head'))
- attn_qkv_grad: float32 [1024, 3072], P(('dp', 'head'))
- attn_proj_grad: float32 [1024, 1024], P(('dp', 'head'))
- conv_expand_grad: float32 [1024, 2048], P(('dp', 'head'))
- conv_depth_grad: float32 [32, 1024], P(None, ('dp', 'head'))
- conv_proj_grad: float32 [1024, 1024], P(('dp', 'head'))
- norm_gains_grad: float32 [6, 1024], P(None, ('dp', 'head'))
- head_proj_grad: float32 [1024, 8192], P('dp', 'head')
Inputs may be any that keep to these rules, and one draw needn't show every extreme that they name: `lengths`: each utterance has at least half of its 512 frames valid; in every draw some device has all of its utterances fully valid. `mask_starts`: span place i of an utterance starts between i * (25) and (i + 1) * 25 - 10, or holds 512 when unused, so spans never intersect. At most 200 frames of one device are masked, and in every draw some device has exactly 200.
All inputs are finite; a program needn't handle non-finite values.
Results may differ from a plain program's by a relative error of at most 0.017.
Values may be sent and summed in bfloat16 or wider, within the bound.
No kernel may reach another device: no remote copies, remote signals or barrier semaphores. Data moves between devices by JAX's collectives and lax.ppermute only.
A program may use at most 448 MiB of HBM per device.

v0:
```python
import jax
import jax.numpy as jnp
from jax import lax
from jax.sharding import PartitionSpec as P

D = 1024
H = 8
HD = 128
VOCAB = 8192
SEQ = 512
SPAN = 10
NSPAN = 20
UTT_DEV = 1


eps = 1e-05


def layer_norm(values, gain_row):
    center = values - jnp.mean(values, axis=-1, keepdims=True)
    variance = jnp.mean(center * center, axis=-1, keepdims=True)
    return center * lax.rsqrt(variance + eps) * gain_row


def rotate(values, cosine, sine_table):
    half_width = values.shape[-1] // 2
    lead_part = values[..., :half_width]
    tail_part = values[..., half_width:]
    return jnp.concatenate(
        [lead_part * cosine - tail_part * sine_table, tail_part * cosine + lead_part * sine_table],
        axis=-1,
    )


def rotate_back(grads, cosine, sine_table):
    half_width = grads.shape[-1] // 2
    lead_part = grads[..., :half_width]
    tail_part = grads[..., half_width:]
    return jnp.concatenate(
        [lead_part * cosine + tail_part * sine_table, tail_part * cosine - lead_part * sine_table],
        axis=-1,
    )


def depthwise(values, tap_weights):
    kernel = tap_weights.shape[0]
    length = values.shape[1]
    padded = jnp.pad(values, ((0, 0), (kernel // 2, kernel - 1 - kernel // 2), (0, 0)))
    result = padded[:, 0:length] * tap_weights[0]
    for tap_at in range(1, kernel):
        result = result + padded[:, tap_at : tap_at + length] * tap_weights[tap_at]
    return result


def lowered(values):
    return values.astype(jnp.bfloat16)


def matmul(operand, weight):
    return jnp.dot(operand, weight, preferred_element_type=jnp.float32)


def matmul_tn(operand, weight):
    return lax.dot_general(
        operand, weight, (((0,), (0,)), ((), ())), preferred_element_type=jnp.float32
    )


def matmul_nt(operand, weight):
    return lax.dot_general(
        operand, weight, (((1,), (1,)), ((), ())), preferred_element_type=jnp.float32
    )


def norm_back(values, gain_row, grads):
    unused, pullback = jax.vjp(layer_norm, values, gain_row)
    return pullback(grads)


def silu_back(values, grads):
    return jax.vjp(jax.nn.silu, values)[1](grads)[0]


def feed_back(grad_in, normed_lo, pre_act, act_lo, inner_weight, outer_weight):
    grad_out_lo = lowered(0.5 * grad_in)
    outer_grad = matmul_tn(act_lo, grad_out_lo)
    grad_pre = lowered(silu_back(pre_act, matmul_nt(grad_out_lo, outer_weight)))
    inner_grad = matmul_tn(normed_lo, grad_pre)
    return (matmul_nt(grad_pre, inner_weight), inner_grad, outer_grad)


def shards(
    frames,
    ffn_inner,
    ffn_outer,
    attn_qkv,
    attn_proj,
    conv_expand,
    conv_depth,
    conv_proj,
    norm_gains,
    head_proj,
    lengths,
    mask_starts,
    target_codes,
    out_grad,
):
    (
        inner_weight,
        outer_weight,
        mix_weight,
        proj_weight,
        expand_weight,
        depth_weight,
        conv_weight,
        gain_rows,
    ) = (
        lax.all_gather(ffn_inner, ("dp", "head"), axis=1, tiled=True),
        lax.all_gather(ffn_outer, ("dp", "head"), axis=1, tiled=True),
        lax.all_gather(attn_qkv, ("dp", "head"), axis=0, tiled=True),
        lax.all_gather(attn_proj, ("dp", "head"), axis=0, tiled=True),
        lax.all_gather(conv_expand, ("dp", "head"), axis=0, tiled=True),
        lax.all_gather(conv_depth, ("dp", "head"), axis=1, tiled=True),
        lax.all_gather(conv_proj, ("dp", "head"), axis=0, tiled=True),
        lax.all_gather(norm_gains, ("dp", "head"), axis=1, tiled=True),
    )
    gain_f = gain_rows.astype(jnp.float32)
    depth_f = depth_weight.astype(jnp.float32)
    row_total = UTT_DEV * SEQ
    positions = jnp.arange(SEQ, dtype=jnp.int32)
    valid_mat = positions[None, :] < lengths[:, None]
    span_hits = (positions[None, None, :] >= mask_starts[:, :, None]) & (
        positions[None, None, :] < mask_starts[:, :, None] + SPAN
    )
    masked = (jnp.any(span_hits, axis=1) & valid_mat).reshape(row_total)
    valid_rows = valid_mat.reshape(row_total).astype(jnp.float32)
    frequency = 10000.0 ** (-(jnp.arange(HD // 2, dtype=jnp.float32) * 2.0) / HD)
    angles = positions.astype(jnp.float32)[:, None] * frequency[None, :]
    cosine = jnp.cos(angles)[:, None, :]
    sine_table = jnp.sin(angles)[:, None, :]
    score_scale = HD ** (-0.5)
    inputs = frames.astype(jnp.float32)
    norm_first = lowered(layer_norm(inputs, gain_f[0]))
    pre_first = matmul(norm_first, inner_weight[0])
    act_first = lowered(jax.nn.silu(pre_first))
    after_first = inputs + 0.5 * matmul(act_first, outer_weight[0])
    norm_attn = lowered(layer_norm(after_first, gain_f[1]))
    mixed = matmul(norm_attn, mix_weight).reshape(UTT_DEV, SEQ, 3, H, HD)
    queries = lowered(rotate(mixed[:, :, 0], cosine, sine_table))
    key_rows = lowered(rotate(mixed[:, :, 1], cosine, sine_table))
    value_rows = lowered(mixed[:, :, 2])

    def scores_of(query_one, key_one, key_ok):
        scores = (
            jnp.einsum("qhd,khd->hqk", query_one, key_one, preferred_element_type=jnp.float32)
            * score_scale
        )
        return jnp.where(key_ok[None, None, :], scores, -1e30)

    def attend_one(batch_items):
        query_one, key_one, value_one, key_ok = batch_items
        scores = scores_of(query_one, key_one, key_ok)
        row_top = jnp.max(scores, axis=-1, keepdims=True)
        weights = jnp.exp(scores - row_top)
        totals = jnp.sum(weights, axis=-1, keepdims=True)
        attn_probs = weights / totals
        attended = jnp.einsum(
            "hqk,khd->qhd", lowered(attn_probs), value_one, preferred_element_type=jnp.float32
        )
        return (attended, row_top[..., 0] + jnp.log(totals[..., 0]))

    attended, log_totals = lax.map(attend_one, (queries, key_rows, value_rows, valid_mat))
    attended_lo = lowered(attended.reshape(row_total, D))
    after_attention = after_first + matmul(attended_lo, proj_weight)
    norm_conv = lowered(layer_norm(after_attention, gain_f[2]))
    expanded = matmul(norm_conv, expand_weight)

    def gate_rows(expanded_rows):
        return expanded_rows[:, :D] * jax.nn.sigmoid(expanded_rows[:, D:]) * valid_rows[:, None]

    def conv_rows(gated_rows, tap_weights):
        return depthwise(gated_rows.reshape(UTT_DEV, SEQ, D), tap_weights).reshape(row_total, D)

    gated_rows = gate_rows(expanded)
    conv_out = conv_rows(gated_rows, depth_f)
    weighted = conv_out * valid_rows[:, None]
    col_sum, col_squares, frame_count = lax.psum(
        (jnp.sum(weighted, axis=0), jnp.sum(weighted * conv_out, axis=0), jnp.sum(valid_rows)),
        ("dp", "head"),
    )
    channel_mean = col_sum / frame_count
    variance = col_squares / frame_count - channel_mean * channel_mean
    inverse = lax.rsqrt(variance + eps)
    normalized = (conv_out - channel_mean) * inverse
    normed_bn = normalized * gain_f[3]
    swish_lo = lowered(jax.nn.silu(normed_bn))
    after_conv = after_attention + matmul(swish_lo, conv_weight)
    norm_second = lowered(layer_norm(after_conv, gain_f[4]))
    pre_second = matmul(norm_second, inner_weight[1])
    act_second = lowered(jax.nn.silu(pre_second))
    after_second = after_conv + 0.5 * matmul(act_second, outer_weight[1])
    output_lo = lowered(layer_norm(after_second, gain_f[5]))
    slots = UTT_DEV * NSPAN * SPAN
    cumulative = jnp.cumsum(masked.astype(jnp.int32))
    slot_ids = jnp.arange(slots, dtype=jnp.int32)
    chosen = jnp.minimum(jnp.searchsorted(cumulative, slot_ids + 1, side="left"), row_total - 1)
    slot_live = (slot_ids < cumulative[-1]).astype(jnp.float32)
    picked_rows = jnp.take(output_lo, chosen, axis=0)
    picked_codes = jnp.where(slot_live > 0, jnp.take(target_codes, chosen), -1)
    head_part = lax.all_gather(head_proj, "dp", axis=0, tiled=True)
    head_whole = lax.all_gather(head_part, "head", axis=1, tiled=True)
    logits = matmul(picked_rows, head_whole)
    row_top = jnp.max(logits, axis=1)
    log_norm = row_top + jnp.log(jnp.sum(jnp.exp(logits - row_top[:, None]), axis=1))
    onehot = jnp.arange(VOCAB, dtype=jnp.int32)[None, :] == picked_codes[:, None]
    target_logit = jnp.sum(jnp.where(onehot, logits, 0.0), axis=1)
    ce_local = jnp.sum((log_norm - target_logit) * slot_live)
    grad_logits = lowered(
        (jnp.exp(logits - log_norm[:, None]) - onehot.astype(jnp.float32)) * slot_live[:, None]
    )
    row_grads = matmul_nt(grad_logits, head_whole)
    head_grad_part = lax.psum_scatter(
        matmul_tn(picked_rows, grad_logits).astype(jnp.bfloat16),
        "head",
        scatter_dimension=1,
        tiled=True,
    )
    head_grad = lax.psum_scatter(head_grad_part, "dp", scatter_dimension=0, tiled=True).astype(
        jnp.float32
    )
    ce_sum = lax.psum(ce_local, ("dp", "head"))
    maskable = lax.axis_size("dp") * lax.axis_size("head") * UTT_DEV * NSPAN * SPAN
    loss = ce_sum / jnp.float32(maskable)
    grad_output = out_grad.astype(jnp.float32) + jnp.zeros((row_total, D), jnp.float32).at[
        chosen
    ].add(row_grads * slot_live[:, None])
    grad_second, gain_grad_final = norm_back(after_second, gain_f[5], grad_output)
    below_second, inner_second, outer_second = feed_back(
        grad_second, norm_second, pre_second, act_second, inner_weight[1], outer_weight[1]
    )
    norm_part, gain_grad_second = norm_back(after_conv, gain_f[4], below_second)
    grad_conv_res = grad_second + norm_part
    conv_res_lo = lowered(grad_conv_res)
    conv_proj_grad = matmul_tn(swish_lo, conv_res_lo)
    grad_bn = silu_back(normed_bn, matmul_nt(conv_res_lo, conv_weight))
    gain_grad_bn = jnp.sum(grad_bn * normalized, axis=0)
    grad_normalized = grad_bn * gain_f[3]
    sum_plain, sum_scaled = lax.psum(
        (jnp.sum(grad_normalized, axis=0), jnp.sum(grad_normalized * normalized, axis=0)),
        ("dp", "head"),
    )
    grad_variance = -0.5 * inverse * inverse * sum_scaled
    grad_mean = -inverse * sum_plain - 2.0 * channel_mean * grad_variance
    grad_conv_out = (
        grad_normalized * inverse
        + (grad_mean + 2.0 * grad_variance * conv_out) * valid_rows[:, None] / frame_count
    )
    grad_gated, depth_grad = jax.vjp(conv_rows, gated_rows, depth_f)[1](grad_conv_out)
    grad_expanded = lowered(jax.vjp(gate_rows, expanded)[1](grad_gated)[0])
    expand_grad = matmul_tn(norm_conv, grad_expanded)
    norm_part, gain_grad_conv = norm_back(
        after_attention, gain_f[2], matmul_nt(grad_expanded, expand_weight)
    )
    grad_attn_res = grad_conv_res + norm_part
    attn_res_lo = lowered(grad_attn_res)
    proj_grad = matmul_tn(attended_lo, attn_res_lo)
    grad_attended = lowered(matmul_nt(attn_res_lo, proj_weight)).reshape(UTT_DEV, SEQ, H, HD)

    def attend_back(batch_items):
        query_one, key_one, value_one, key_ok, log_total, grad_one = batch_items
        attn_probs = jnp.exp(scores_of(query_one, key_one, key_ok) - log_total[:, :, None])
        grad_value = jnp.einsum(
            "hqk,qhd->khd", lowered(attn_probs), grad_one, preferred_element_type=jnp.float32
        )
        grad_probs = jnp.einsum(
            "qhd,khd->hqk", grad_one, value_one, preferred_element_type=jnp.float32
        )
        grad_scores = lowered(
            attn_probs * (grad_probs - jnp.sum(attn_probs * grad_probs, axis=-1, keepdims=True))
        )
        grad_query = (
            jnp.einsum("hqk,khd->qhd", grad_scores, key_one, preferred_element_type=jnp.float32)
            * score_scale
        )
        grad_key = (
            jnp.einsum("hqk,qhd->khd", grad_scores, query_one, preferred_element_type=jnp.float32)
            * score_scale
        )
        return (grad_query, grad_key, grad_value)

    grad_query, grad_key, grad_value = lax.map(
        attend_back, (queries, key_rows, value_rows, valid_mat, log_totals, grad_attended)
    )
    grad_mixed = jnp.stack(
        [
            rotate_back(grad_query, cosine, sine_table),
            rotate_back(grad_key, cosine, sine_table),
            grad_value,
        ],
        axis=2,
    )
    grad_mixed = lowered(grad_mixed.reshape(row_total, 3 * D))
    mix_grad = matmul_tn(norm_attn, grad_mixed)
    norm_part, gain_grad_attn = norm_back(after_first, gain_f[1], matmul_nt(grad_mixed, mix_weight))
    grad_first_res = grad_attn_res + norm_part
    below_first, inner_first, outer_first = feed_back(
        grad_first_res, norm_first, pre_first, act_first, inner_weight[0], outer_weight[0]
    )
    norm_part, gain_grad_first = norm_back(inputs, gain_f[0], below_first)
    input_grad = grad_first_res + norm_part
    gain_grad = jnp.stack(
        [
            gain_grad_first,
            gain_grad_attn,
            gain_grad_conv,
            gain_grad_bn,
            gain_grad_second,
            gain_grad_final,
        ],
        axis=0,
    )
    inner_grad = jnp.stack([inner_first, inner_second], axis=0)
    outer_grad = jnp.stack([outer_first, outer_second], axis=0)
    scattered = (
        lax.psum_scatter(inner_grad, ("dp", "head"), scatter_dimension=1, tiled=True),
        lax.psum_scatter(outer_grad, ("dp", "head"), scatter_dimension=1, tiled=True),
        lax.psum_scatter(mix_grad, ("dp", "head"), scatter_dimension=0, tiled=True),
        lax.psum_scatter(proj_grad, ("dp", "head"), scatter_dimension=0, tiled=True),
        lax.psum_scatter(expand_grad, ("dp", "head"), scatter_dimension=0, tiled=True),
        lax.psum_scatter(depth_grad, ("dp", "head"), scatter_dimension=1, tiled=True),
        lax.psum_scatter(conv_proj_grad, ("dp", "head"), scatter_dimension=0, tiled=True),
        lax.psum_scatter(gain_grad, ("dp", "head"), scatter_dimension=1, tiled=True),
    )
    return (
        output_lo,
        loss,
        input_grad,
        scattered[0],
        scattered[1],
        scattered[2],
        scattered[3],
        scattered[4],
        scattered[5],
        scattered[6],
        scattered[7],
        head_grad,
    )


def solution(mesh):
    placed = (
        P(("dp", "head"), None),
        P(None, ("dp", "head"), None),
        P(None, ("dp", "head"), None),
        P(("dp", "head"), None),
        P(("dp", "head"), None),
        P(("dp", "head"), None),
        P(None, ("dp", "head")),
        P(("dp", "head"), None),
        P(None, ("dp", "head")),
        P("dp", "head"),
        P(("dp", "head")),
        P(("dp", "head"), None),
        P(("dp", "head")),
        P(("dp", "head"), None),
    )
    return jax.shard_map(
        shards,
        mesh=mesh,
        in_specs=placed,
        out_specs=(
            P(("dp", "head"), None),
            P(),
            P(("dp", "head"), None),
            P(None, ("dp", "head"), None),
            P(None, ("dp", "head"), None),
            P(("dp", "head"), None),
            P(("dp", "head"), None),
            P(("dp", "head"), None),
            P(None, ("dp", "head")),
            P(("dp", "head"), None),
            P(None, ("dp", "head")),
            P("dp", "head"),
        ),
        check_vma=False,
    )
```

profile of v0, /device:TPU:0, one launch (start us, length us, event | category | flops | bytes accessed | tf_op | source)
XLA Modules:
  0.0 2609.1 jit_solution(4069249002942337815)
XLA Ops:
  14.6 71.6 %all-gather.22.cloned.1.call-done = bf16[1024,2048]{1,0:T(8,128)(2,1)} async-done(((bf16[128,2048]{1,0:T(8,128)(2,1)}), bf16[1024,2048]{1,0:T(8,128)(2,1)}) %all-gather.22.cloned.1.call-update) | async-done | bytes 4194320 | tf_op jit(solution)/shard_map/all_gather | solution.py:210
  86.4 20.2 while.35
  107.2 39.6 %all-gather = bf16[32,32,6]{1,2,0:T(8,128)(2,1)S(1)} all-gather(bf16[1,32,6]{1,2,0:T(8,128)(2,1)S(1)} %bitcast.475), channel_id=1, replica_groups=mesh['dp'=8,'head'=4] {'dp','head'}, dimensions={0}, use_global_device_ids=true | all-gather | bytes 12672 | tf_op jit(solution)/shard_map/all_gather | solution.py:125
  147.0 38.8 %all_gather.36 = bf16[32,1024]{0,1:T(8,128)(2,1)S(1)} all-gather(bf16[32,32]{0,1:T(8,128)(2,1)S(1)} %copy.117), channel_id=1, replica_groups=mesh['dp'=8,'head'=4] {'dp','head'}, dimensions={1}, use_global_device_ids=true | all-gather | bytes 67584 | tf_op jit(solution)/shard_map/all_gather | solution.py:123
  214.7 106.0 %all-gather.12.cloned.1.call-done = bf16[2,4096,1024]{2,1,0:T(8,128)(2,1)} async-done(((bf16[2,128,1024]{2,1,0:T(8,128)(2,1)}), bf16[2,4096,1024]{2,1,0:T(8,128)(2,1)}) %all-gather.12.cloned.1.call-update) | async-done | bytes 16777232 | tf_op jit(solution)/shard_map/all_gather | solution.py:119
  332.8 58.4 %all-gather.14.cloned.1.call-done = bf16[1024,3072]{1,0:T(8,128)(2,1)} async-done(((bf16[32,3072]{1,0:T(8,128)(2,1)}), bf16[1024,3072]{1,0:T(8,128)(2,1)}) %all-gather.14.cloned.1.call-update) | async-done | bytes 6291472 | tf_op jit(solution)/shard_map/all_gather | solution.py:120
  416.7 32.1 %all-gather.16.cloned.1.call-done = bf16[1024,1024]{1,0:T(8,128)(2,1)} async-done(((bf16[32,1024]{1,0:T(8,128)(2,1)}), bf16[1024,1024]{1,0:T(8,128)(2,1)}) %all-gather.16.cloned.1.call-update) | async-done | bytes 2097168 | tf_op jit(solution)/shard_map/all_gather | solution.py:121
  454.3 58.1 %all-gather.18.cloned.1.call-done = bf16[1024,2048]{1,0:T(8,128)(2,1)} async-done(((bf16[32,2048]{1,0:T(8,128)(2,1)}), bf16[1024,2048]{1,0:T(8,128)(2,1)}) %all-gather.18.cloned.1.call-update) | async-done | bytes 4194320 | tf_op jit(solution)/shard_map/all_gather | solution.py:122
  530.8 39.6 %all-reduce.68 = (f32[1024]{0:T(1024)S(1)}, f32[]{:T(128)}, f32[1024]{0:T(1024)S(1)}) all-reduce(f32[1024]{0:T(1024)S(1)} %get-tuple-element.193, f32[]{:T(128)} %convert_reduce_fusion.1, f32[1024]{0:T(1024)S(1)} %get-tuple-element.192), channel_id=1, replica_groups=mesh['dp'=8,'head'=4] {'dp','head'}, use_global_device_ids=true, to_apply=%region_13.14 | all-reduce | flops 2049 | bytes 16392 | tf_op jit(solution)/shard_map/psum | solution.py:187
  599.3 77.6 %all-gather.24.cloned.1.call-done = bf16[1024,8192]{1,0:T(8,128)(2,1)} async-done(((bf16[1024,2048]{1,0:T(8,128)(2,1)}), bf16[1024,8192]{1,0:T(8,128)(2,1)}) %all-gather.24.cloned.1.call-update) | async-done | bytes 16777232 | tf_op jit(solution)/shard_map/all_gather | solution.py:211
  702.1 15.7 convolution_multiply_fusion
  752.1 40.0 %all-reduce.67 = (f32[]{:T(128)}, f32[1024]{0:T(1024)S(1)}, f32[1024]{0:T(1024)S(1)}) all-reduce(f32[]{:T(128)} %get-tuple-element.252, f32[1024]{0:T(1024)S(1)} %get-tuple-element.149, f32[1024]{0:T(1024)S(1)} %get-tuple-element.191), channel_id=1, replica_groups=mesh['dp'=8,'head'=4] {'dp','head'}, use_global_device_ids=true, to_apply=%region_27.28 | all-reduce | flops 2049 | bytes 16392 | tf_op jit(solution)/shard_map/psum | solution.py:231
  820.6 21.8 pad_add_fusion
  990.1 19.1 pad_maximum_fusion
  1029.5 19.1 pad_maximum_fusion.1
  1053.9 21.0 reduce-scatter.33.cloned.1.call-done
  1076.3 131.4 %reduce-scatter.31.cloned.1.call-done = f32[32,32]{1,0:T(8,128)} async-done(((f32[1024,32]{1,0:T(8,128)}), f32[32,32]{1,0:T(8,128)}) %reduce-scatter.31.cloned.1.call-update) | async-done | bytes 4112
  1209.1 86.5 %reduce-scatter.29.cloned.1.call-done = bf16[128,2048]{1,0:T(8,128)(2,1)} async-done(((bf16[1024,2048]{1,0:T(8,128)(2,1)}), bf16[128,2048]{1,0:T(8,128)(2,1)}) %reduce-scatter.29.cloned.1.call-update) | async-done | bytes 524304 | tf_op jit(solution)/shard_map/reduce_scatter | solution.py:228
  1297.7 141.6 %reduce-scatter.21.cloned.1.call-done = f32[32,1024]{1,0:T(8,128)} async-done(((f32[1024,1024]{1,0:T(8,128)}), f32[32,1024]{1,0:T(8,128)}) %reduce-scatter.21.cloned.1.call-update) | async-done | bytes 131088 | tf_op jit(solution)/shard_map/reduce_scatter | solution.py:328
  1439.3 139.6 %reduce-scatter.25.cloned.1.call-done = f32[32,1024]{1,0:T(8,128)} async-done(((f32[1024,1024]{1,0:T(8,128)}), f32[32,1024]{1,0:T(8,128)}) %reduce-scatter.25.cloned.1.call-update) | async-done | bytes 131088 | tf_op jit(solution)/shard_map/reduce_scatter | solution.py:331
  1578.9 157.7 %reduce-scatter.19.cloned.1.call-done = f32[32,3072]{1,0:T(8,128)} async-done(((f32[1024,3072]{1,0:T(8,128)}), f32[32,3072]{1,0:T(8,128)}) %reduce-scatter.19.cloned.1.call-update) | async-done | bytes 393232 | tf_op jit(solution)/shard_map/reduce_scatter | solution.py:327
  1736.7 150.6 %reduce-scatter.23.cloned.1.call-done = f32[32,2048]{1,0:T(8,128)} async-done(((f32[1024,2048]{1,0:T(8,128)}), f32[32,2048]{1,0:T(8,128)}) %reduce-scatter.23.cloned.1.call-update) | async-done | bytes 262160 | tf_op jit(solution)/shard_map/reduce_scatter | solution.py:329
  1887.3 352.8 %reduce-scatter.15.cloned.1.call-done = f32[2,32,4096]{2,1,0:T(8,128)} async-done(((f32[2,1024,4096]{2,1,0:T(8,128)}), f32[2,32,4096]{2,1,0:T(8,128)}) %reduce-scatter.15.cloned.1.call-update) | async-done | bytes 1048592 | tf_op jit(solution)/shard_map/reduce_scatter | solution.py:325
  2240.1 360.6 %reduce-scatter.17.cloned.1.call-done = f32[2,128,1024]{2,1,0:T(8,128)} async-done(((f32[2,4096,1024]{2,1,0:T(8,128)}), f32[2,128,1024]{2,1,0:T(8,128)}) %reduce-scatter.17.cloned.1.call-update) | async-done | bytes 1048592 | tf_op jit(solution)/shard_map/reduce_scatter | solution.py:326
  (417 shorter events, 410.4 us)
Async XLA Ops:
  7.2 79.1 %all-gather.22.cloned.1.call-start = ((), (), s32[]{:S(2)}) async-start(), calls=%async_computation.16 | async-start | bytes 4718592 | tf_op jit(solution)/shard_map/all_gather | solution.py:210
  7.9 196.2 %all-gather.10.cloned.1.call-start = ((), (), s32[]{:S(2)}) async-start(), calls=%async_computation.10 | async-start | bytes 17301504 | tf_op jit(solution)/shard_map/all_gather | solution.py:118
  8.7 312.0 %all-gather.12.cloned.1.call-start = ((), (), s32[]{:S(2)}) async-start(), calls=%async_computation.11 | async-start | bytes 17301504 | tf_op jit(solution)/shard_map/all_gather | solution.py:119
  9.4 381.8 %all-gather.14.cloned.1.call-start = ((), (), s32[]{:S(2)}) async-start(), calls=%async_computation.12 | async-start | bytes 6488064 | tf_op jit(solution)/shard_map/all_gather | solution.py:120
  10.0 438.8 %all-gather.16.cloned.1.call-start = ((), (), s32[]{:S(2)}) async-start(), calls=%async_computation.13 | async-start | bytes 2162688 | tf_op jit(solution)/shard_map/all_gather | solution.py:121
  10.6 501.9 %all-gather.18.cloned.1.call-start = ((), (), s32[]{:S(2)}) async-start(), calls=%async_computation.14 | async-start | bytes 4325376 | tf_op jit(solution)/shard_map/all_gather | solution.py:122
  11.2 559.9 %all-gather.20.cloned.1.call-start = ((), (), s32[]{:S(2)}) async-start(), calls=%async_computation.15 | async-start | bytes 2162688 | tf_op jit(solution)/shard_map/all_gather | solution.py:124
  11.9 665.0 %all-gather.24.cloned.1.call-start = ((), (), s32[]{:S(2)}) async-start(), calls=%async_computation.17 | async-start | bytes 20971520 | tf_op jit(solution)/shard_map/all_gather | solution.py:211
  86.3 855.2 %reduce-scatter.27.cloned.1.call-start = ((), (), s32[]{:S(2)}) async-start(), calls=%async_computation.24 | async-start | bytes 20971520 | tf_op jit(solution)/shard_map/reduce_scatter | solution.py:222
  194.1 197.1 %copy-start.76 = (f32[1,1024]{1,0:T(1,128)}, f32[1,1024]{1,0:T(1,128)S(1)}, u32[]{:S(2)}) copy-start(f32[1,1024]{1,0:T(1,128)S(1)} %get-tuple-element.309) | copy-start | bytes 12292
  194.1 318.3 %copy-start.74 = (f32[1,1024]{1,0:T(1,128)}, f32[1,1024]{1,0:T(1,128)S(1)}, u32[]{:S(2)}) copy-start(f32[1,1024]{1,0:T(1,128)S(1)} %get-tuple-element.308) | copy-start | bytes 12292
  194.2 551.4 %copy-start.72 = (f32[1,1024]{1,0:T(1,128)}, f32[1,1024]{1,0:T(1,128)S(1)}, u32[]{:S(2)}) copy-start(f32[1,1024]{1,0:T(1,128)S(1)} %get-tuple-element.306) | copy-start | bytes 12292
  195.1 211.4 %copy-start.46 = (f32[512,64]{1,0:T(8,128)}, f32[512,64]{1,0:T(8,128)S(1)}, u32[]{:S(2)}) copy-start(f32[512,64]{1,0:T(8,128)S(1)} %get-tuple-element.315) | copy-start | bytes 393220
  195.2 211.4 %copy-start.48 = (f32[512,64]{1,0:T(8,128)}, f32[512,64]{1,0:T(8,128)S(1)}, u32[]{:S(2)}) copy-start(f32[512,64]{1,0:T(8,128)S(1)} %get-tuple-element.316) | copy-start | bytes 393220
  700.6 374.3 %reduce-scatter.33.cloned.1.call-start = ((), (), s32[]{:S(2)}) async-start(), calls=%async_computation.27 | async-start | bytes 540672
  940.1 267.6 %reduce-scatter.31.cloned.1.call-start = ((), (), s32[]{:S(2)}) async-start(), calls=%async_computation.26 | async-start | bytes 540672
  941.4 354.2 %reduce-scatter.29.cloned.1.call-start = ((), (), s32[]{:S(2)}) async-start(), calls=%async_computation.25 | async-start | bytes 4718592 | tf_op jit(solution)/shard_map/reduce_scatter | solution.py:228
  942.0 497.3 %reduce-scatter.21.cloned.1.call-start = ((), (), s32[]{:S(2)}) async-start(), calls=%async_computation.21 | async-start | bytes 4325376 | tf_op jit(solution)/shard_map/reduce_scatter | solution.py:328
  947.6 631.4 %reduce-scatter.25.cloned.1.call-start = ((), (), s32[]{:S(2)}) async-start(), calls=%async_computation.23 | async-start | bytes 4325376 | tf_op jit(solution)/shard_map/reduce_scatter | solution.py:331
  954.1 782.6 %reduce-scatter.19.cloned.1.call-start = ((), (), s32[]{:S(2)}) async-start(), calls=%async_computation.20 | async-start | bytes 12976128 | tf_op jit(solution)/shard_map/reduce_scatter | solution.py:327
  964.4 922.9 %reduce-scatter.23.cloned.1.call-start = ((), (), s32[]{:S(2)}) async-start(), calls=%async_computation.22 | async-start | bytes 8650752 | tf_op jit(solution)/shard_map/reduce_scatter | solution.py:329
  974.1 1266.0 %reduce-scatter.15.cloned.1.call-start = ((), (), s32[]{:S(2)}) async-start(), calls=%async_computation.18 | async-start | bytes 34603008 | tf_op jit(solution)/shard_map/reduce_scatter | solution.py:325
  1009.2 1591.5 %reduce-scatter.17.cloned.1.call-start = ((), (), s32[]{:S(2)}) async-start(), calls=%async_computation.19 | async-start | bytes 34603008 | tf_op jit(solution)/shard_map/reduce_scatter | solution.py:326
  1050.3 1550.5 %copy-start.1 = (s32[512]{0:T(512)S(1)}, s32[512]{0:T(512)}, u32[]{:S(2)}) copy-start(s32[512]{0:T(512)} %param.28) | copy-start | bytes 6148
  (94 other events, 1666.6 us)
Sparse Core Ops, SparseCore 0:
  10.2 76.0 all-gather.21
  89.2 114.8 all-gather.9
  207.1 113.4 all-gather.11
  323.4 67.7 all-gather.13
  393.9 54.8 all-gather.15
  451.6 60.8 all-gather.17
  515.3 55.1 all-gather.19
  572.0 104.7 all-gather.23
  700.8 127.5 reduce-scatter.26
  940.2 134.6 reduce-scatter.32
  1077.8 129.9 reduce-scatter.30
  1211.6 83.9 reduce-scatter.28
  1298.5 140.8 reduce-scatter.20
  1442.0 136.8 reduce-scatter.24
  1585.4 151.2 reduce-scatter.18
  1739.5 147.7 reduce-scatter.22
  1890.1 349.9 reduce-scatter.14
  2242.9 357.7 reduce-scatter.16
where the time goes:
time: 2620 us; the launch traced here: 2610 us
  waiting for transfers between devices  1950 us (74%)
  matrix products  230 us (9%)
  other arithmetic  167 us (6%)
  blocking collectives  158 us (6%)
  local copies, waits for them, and re-layouts  79.1 us (3%)
    reduce_scatter x1, waiting for transfers between devices, shards(): lax.psum_scatter(outer_grad, ('dp', 'head'), scatter_dimension=1, tiled=T...  361 us
    reduce_scatter x1, waiting for transfers between devices, shards(): lax.psum_scatter(inner_grad, ('dp', 'head'), scatter_dimension=1, tiled=T...  353 us
    reduce_scatter x1, waiting for transfers between devices, shards(): lax.psum_scatter(mix_grad, ('dp', 'head'), scatter_dimension=0, tiled=True)  158 us
    unnamed x20, waiting for transfers between devices  157 us
    reduce_scatter x1, waiting for transfers between devices, shards(): lax.psum_scatter(expand_grad, ('dp', 'head'), scatter_dimension=0, tiled=...  151 us
    reduce_scatter x1, waiting for transfers between devices, shards(): lax.psum_scatter(proj_grad, ('dp', 'head'), scatter_dimension=0, tiled=True)  142 us
    reduce_scatter x1, waiting for transfers between devices, shards(): lax.psum_scatter(conv_proj_grad, ('dp', 'head'), scatter_dimension=0, til...  140 us
    all_gather x1, waiting for transfers between devices, shards(): lax.all_gather(ffn_outer, ('dp', 'head'), axis=1, tiled=True)  106 us
  transfers between devices with their start and end apart: 18, of which 16 were waited for; matrix products, arithmetic and copies ran while one was open for 16% of the time, Pallas kernels for 0%

commit v1 on v0

v1 whole, which is shorter than its diff:
```python
import functools

import jax
import jax.numpy as jnp
from jax import lax
from jax.sharding import PartitionSpec as P

D = 1024
H = 8
HD = 128
VOCAB = 8192
SEQ = 512
SPAN = 10
NSPAN = 20
UTT_DEV = 1


eps = 1e-05


def layer_norm(values, gain_row):
    center = values - jnp.mean(values, axis=-1, keepdims=True)
    variance = jnp.mean(center * center, axis=-1, keepdims=True)
    return center * lax.rsqrt(variance + eps) * gain_row


def rotate(values, cosine, sine_table):
    half_width = values.shape[-1] // 2
    lead_part = values[..., :half_width]
    tail_part = values[..., half_width:]
    return jnp.concatenate(
        [lead_part * cosine - tail_part * sine_table, tail_part * cosine + lead_part * sine_table],
        axis=-1,
    )


def rotate_back(grads, cosine, sine_table):
    half_width = grads.shape[-1] // 2
    lead_part = grads[..., :half_width]
    tail_part = grads[..., half_width:]
    return jnp.concatenate(
        [lead_part * cosine + tail_part * sine_table, tail_part * cosine - lead_part * sine_table],
        axis=-1,
    )


def depthwise(values, tap_weights):
    kernel = tap_weights.shape[0]
    length = values.shape[1]
    padded = jnp.pad(values, ((0, 0), (kernel // 2, kernel - 1 - kernel // 2), (0, 0)))
    result = padded[:, 0:length] * tap_weights[0]
    for tap_at in range(1, kernel):
        result = result + padded[:, tap_at : tap_at + length] * tap_weights[tap_at]
    return result


def lowered(values):
    return values.astype(jnp.bfloat16)


def matmul(operand, weight):
    return jnp.dot(operand, weight, preferred_element_type=jnp.float32)


def matmul_tn(operand, weight):
    return lax.dot_general(
        operand, weight, (((0,), (0,)), ((), ())), preferred_element_type=jnp.float32
    )


def matmul_nt(operand, weight):
    return lax.dot_general(
        operand, weight, (((1,), (1,)), ((), ())), preferred_element_type=jnp.float32
    )


def norm_back(values, gain_row, grads):
    unused, pullback = jax.vjp(layer_norm, values, gain_row)
    return pullback(grads)


def silu_back(values, grads):
    return jax.vjp(jax.nn.silu, values)[1](grads)[0]


AXES = ("dp", "head")


class Cube:
    def __init__(self, sizes):
        self.sizes = sizes
        self.bits = []
        for axis in AXES:
            bit = sizes[axis] // 2
            while bit:
                self.bits.append((axis, bit))
                bit //= 2

    def orders(self):
        whole = list(range(len(self.bits)))
        dp_count = sum(axis == "dp" for axis, bit in self.bits)
        if self.sizes == {"dp": 8, "head": 4}:
            return [0, 1, 2, 3, 4], [0, 1, 3, 2, 4], [2, 0, 1]
        return whole, whole, whole[:dp_count]

    def mine(self, at):
        axis, bit = self.bits[at]
        return (lax.axis_index(axis) // bit) % 2

    def swap(self, values, at):
        axis, bit = self.bits[at]
        return lax.ppermute(values, axis, [(i, i ^ bit) for i in range(self.sizes[axis])])

    def gather(self, shard, order):
        held = []
        values = shard
        for at in order:
            place = sum(other < at for other in held)
            got = self.swap(values, at)
            mine = self.mine(at)
            first = jnp.where(mine == 0, values, got)
            second = jnp.where(mine == 0, got, values)
            values = jnp.stack([first, second], axis=place)
            held.append(at)
        return values

    def scatter(self, values, order, final=jnp.float32):
        held = sorted(order)
        for step, at in enumerate(order[::-1]):
            place = held.index(at)
            mine = self.mine(at)
            send = lax.dynamic_index_in_dim(values, 1 - mine, place, keepdims=False)
            keep = lax.dynamic_index_in_dim(values, mine, place, keepdims=False)
            got = self.swap(send, at)
            total = keep.astype(jnp.float32) + got.astype(jnp.float32)
            values = total.astype(final if step == len(order) - 1 else values.dtype)
            held.remove(at)
        return values

    def total(self, values, only=None):
        for at in range(len(self.bits)):
            if only is None or self.bits[at][0] == only:
                values = values + self.swap(values, at)
        return values


def rows_of(values, count):
    return values.reshape(count, values.shape[-1])


def shards(
    sizes,
    frames,
    ffn_inner,
    ffn_outer,
    attn_qkv,
    attn_proj,
    conv_expand,
    conv_depth,
    conv_proj,
    norm_gains,
    head_proj,
    lengths,
    mask_starts,
    target_codes,
    out_grad,
):
    cube = Cube(sizes)
    order_a, order_b, order_dp = cube.orders()
    devices = sizes["dp"] * sizes["head"]
    ff = ffn_inner.shape[2]

    def gathered(shard):
        half = shard.shape[1] // 2
        return (
            rows_of(cube.gather(shard[:, :half], order_a), shard.shape[0] * devices),
            rows_of(cube.gather(shard[:, half:], order_b), shard.shape[0] * devices),
        )

    def scattered(left, right):
        bits = (2,) * len(cube.bits)
        rows = left.shape[0] // devices
        return jnp.concatenate(
            [
                cube.scatter(left.reshape(bits + (rows, -1)), order_a),
                cube.scatter(right.reshape(bits + (rows, -1)), order_b),
            ],
            axis=1,
        )

    vectors = jnp.concatenate([norm_gains, conv_depth], axis=0)
    vectors = cube.gather(vectors, order_a)
    vectors = jnp.moveaxis(vectors.reshape((devices,) + vectors.shape[-2:]), 0, 1).reshape(-1, D)
    vectors = vectors.astype(jnp.float32)
    gain_f, depth_f = vectors[:6], vectors[6:]
    inner_a0, inner_b0 = gathered(ffn_inner[0])
    outer_a0, outer_b0 = gathered(ffn_outer[0])
    mix_a, mix_b = gathered(attn_qkv)
    mid = jnp.concatenate([attn_proj, conv_expand, conv_proj], axis=1)
    mid_a, mid_b = gathered(mid)
    inner_a1, inner_b1 = gathered(ffn_inner[1])
    head_cols = cube.gather(head_proj, order_dp).reshape(D, -1)
    outer_a1, outer_b1 = gathered(ffn_outer[1])
    proj_weight, lead_weight = mid_a[:, :D], mid_a[:, D:]
    gate_weight, conv_weight = mid_b[:, :D], mid_b[:, D:]

    row_total = UTT_DEV * SEQ
    positions = jnp.arange(SEQ, dtype=jnp.int32)
    valid_mat = positions[None, :] < lengths[:, None]
    valid_rows = valid_mat.reshape(row_total).astype(jnp.float32)
    frequency = 10000.0 ** (-(jnp.arange(HD // 2, dtype=jnp.float32) * 2.0) / HD)
    angles = positions.astype(jnp.float32)[:, None] * frequency[None, :]
    cosine = jnp.cos(angles)[:, None, :]
    sine_table = jnp.sin(angles)[:, None, :]
    score_scale = HD ** (-0.5)

    slots = UTT_DEV * NSPAN * SPAN
    slot_at = (mask_starts[:, :, None] + jnp.arange(SPAN, dtype=jnp.int32)).reshape(UTT_DEV, -1)
    slot_ok = slot_at < lengths[:, None]
    chosen = (slot_at + SEQ * jnp.arange(UTT_DEV, dtype=jnp.int32)[:, None]).reshape(slots)
    slot_live = slot_ok.reshape(slots)
    pick = (
        (chosen[:, None] == jnp.arange(row_total, dtype=jnp.int32)[None, :]) & slot_live[:, None]
    )
    picked_codes = jnp.sum(jnp.where(pick, target_codes[None, :], 0), axis=1)
    picked_codes = jnp.where(slot_live, picked_codes, -1)
    pick_lo = pick.astype(jnp.bfloat16)
    head_order = [at for at in range(len(cube.bits)) if cube.bits[at][0] == "head"]
    group = sizes["head"]
    vocab_cols = head_proj.shape[1]
    group_codes = cube.gather(picked_codes, head_order).reshape(group * slots)
    group_live = (group_codes >= 0).astype(jnp.float32)
    local_codes = group_codes - lax.axis_index("head") * vocab_cols

    inputs = frames.astype(jnp.float32)
    norm_first = lowered(layer_norm(inputs, gain_f[0]))
    pre_first = [matmul(norm_first, inner_a0), matmul(norm_first, inner_b0)]
    act_first = jnp.concatenate([lowered(jax.nn.silu(part)) for part in pre_first], axis=1)
    after_first = inputs + 0.5 * jnp.concatenate(
        [matmul(act_first, outer_a0), matmul(act_first, outer_b0)], axis=1
    )
    norm_attn = lowered(layer_norm(after_first, gain_f[1]))
    mixed = jnp.concatenate([matmul(norm_attn, mix_a), matmul(norm_attn, mix_b)], axis=1)
    mixed = mixed.reshape(UTT_DEV, SEQ, 3, H, HD)
    queries = lowered(rotate(mixed[:, :, 0], cosine, sine_table))
    key_rows = lowered(rotate(mixed[:, :, 1], cosine, sine_table))
    value_rows = lowered(mixed[:, :, 2])

    def scores_of(query_one, key_one, key_ok):
        scores = (
            jnp.einsum("qhd,khd->hqk", query_one, key_one, preferred_element_type=jnp.float32)
            * score_scale
        )
        return jnp.where(key_ok[None, None, :], scores, -1e30)

    def attend_one(query_one, key_one, value_one, key_ok):
        scores = scores_of(query_one, key_one, key_ok)
        row_top = jnp.max(scores, axis=-1, keepdims=True)
        weights = jnp.exp(scores - row_top)
        totals = jnp.sum(weights, axis=-1, keepdims=True)
        attn_probs = weights / totals
        attended = jnp.einsum(
            "hqk,khd->qhd", lowered(attn_probs), value_one, preferred_element_type=jnp.float32
        )
        return (attended, row_top[..., 0] + jnp.log(totals[..., 0]))

    attended, log_totals = attend_one(queries[0], key_rows[0], value_rows[0], valid_mat[0])
    attended_lo = lowered(attended.reshape(row_total, D))
    after_attention = after_first + matmul(attended_lo, proj_weight)
    norm_conv = lowered(layer_norm(after_attention, gain_f[2]))
    lead = matmul(norm_conv, lead_weight)
    gate = matmul(norm_conv, gate_weight)

    def gate_rows(lead_rows, gate_in):
        return lead_rows * jax.nn.sigmoid(gate_in) * valid_rows[:, None]

    def conv_rows(gated_rows, tap_weights):
        return depthwise(gated_rows.reshape(UTT_DEV, SEQ, D), tap_weights).reshape(row_total, D)

    gated_rows = gate_rows(lead, gate)
    conv_out = conv_rows(gated_rows, depth_f)
    weighted = conv_out * valid_rows[:, None]
    sums = cube.total(
        jnp.stack(
            [
                jnp.sum(weighted, axis=0),
                jnp.sum(weighted * conv_out, axis=0),
                jnp.broadcast_to(jnp.sum(valid_rows), (D,)),
            ]
        )
    )
    frame_count = sums[2, 0]
    channel_mean = sums[0] / frame_count
    variance = sums[1] / frame_count - channel_mean * channel_mean
    inverse = lax.rsqrt(variance + eps)
    normalized = (conv_out - channel_mean) * inverse
    normed_bn = normalized * gain_f[3]
    swish_lo = lowered(jax.nn.silu(normed_bn))
    after_conv = after_attention + matmul(swish_lo, conv_weight)
    norm_second = lowered(layer_norm(after_conv, gain_f[4]))
    pre_second = [matmul(norm_second, inner_a1), matmul(norm_second, inner_b1)]
    act_second = jnp.concatenate([lowered(jax.nn.silu(part)) for part in pre_second], axis=1)
    after_second = after_conv + 0.5 * jnp.concatenate(
        [matmul(act_second, outer_a1), matmul(act_second, outer_b1)], axis=1
    )
    output_lo = lowered(layer_norm(after_second, gain_f[5]))

    picked_rows = lowered(matmul(pick_lo, output_lo))
    group_rows = cube.gather(picked_rows, head_order).reshape(group * slots, D)
    logits = matmul(group_rows, head_cols)
    row_top = jnp.max(logits, axis=1)
    row_sum = jnp.sum(jnp.exp(logits - row_top[:, None]), axis=1)
    onehot = jnp.arange(vocab_cols, dtype=jnp.int32)[None, :] == local_codes[:, None]
    target_logit = jnp.sum(jnp.where(onehot, logits, 0.0), axis=1)
    stats = cube.gather(jnp.stack([row_top, row_sum, target_logit]), head_order)
    stats = stats.reshape(group, 3, group * slots)
    whole_top = jnp.max(stats[:, 0], axis=0)
    whole_sum = jnp.sum(stats[:, 1] * jnp.exp(stats[:, 0] - whole_top), axis=0)
    log_norm = whole_top + jnp.log(whole_sum)
    ce_group = jnp.sum((log_norm - jnp.sum(stats[:, 2], axis=0)) * group_live)
    grad_logits = lowered(
        (jnp.exp(logits - log_norm[:, None]) - onehot.astype(jnp.float32)) * group_live[:, None]
    )
    head_bits = (2,) * len(order_dp)
    head_grad = cube.scatter(
        lowered(matmul_tn(group_rows, grad_logits)).reshape(
            head_bits + (head_proj.shape[0], vocab_cols)
        ),
        order_dp,
    )
    row_grads = lowered(matmul_nt(grad_logits, head_cols))
    row_grads = cube.scatter(
        row_grads.reshape((2,) * len(head_order) + (slots, D)), head_order, jnp.bfloat16
    )
    grad_output = out_grad.astype(jnp.float32) + matmul_tn(pick_lo, row_grads)

    def feed_back_parts(grad_in, normed_lo, pre_act, act_lo, inner_parts, outer_parts):
        grad_out_lo = lowered(0.5 * grad_in)
        half = D // 2
        outer_grads = [
            lowered(matmul_tn(act_lo, grad_out_lo[:, :half])),
            lowered(matmul_tn(act_lo, grad_out_lo[:, half:])),
        ]
        outer_grad = scattered(*outer_grads)
        grad_act = matmul_nt(grad_out_lo, jnp.concatenate(outer_parts, axis=1))
        grad_pre = [
            lowered(silu_back(pre_act[0], grad_act[:, : ff // 2])),
            lowered(silu_back(pre_act[1], grad_act[:, ff // 2 :])),
        ]
        inner_grad = scattered(
            lowered(matmul_tn(normed_lo, grad_pre[0])), lowered(matmul_tn(normed_lo, grad_pre[1]))
        )
        below = matmul_nt(grad_pre[0], inner_parts[0]) + matmul_nt(grad_pre[1], inner_parts[1])
        return (below, inner_grad, outer_grad)

    grad_second, gain_grad_final = norm_back(after_second, gain_f[5], grad_output)
    below_second, inner_second, outer_second = feed_back_parts(
        grad_second,
        norm_second,
        pre_second,
        act_second,
        (inner_a1, inner_b1),
        (outer_a1, outer_b1),
    )
    norm_part, gain_grad_second = norm_back(after_conv, gain_f[4], below_second)
    grad_conv_res = grad_second + norm_part
    conv_res_lo = lowered(grad_conv_res)
    grad_bn = silu_back(normed_bn, matmul_nt(conv_res_lo, conv_weight))
    gain_grad_bn = jnp.sum(grad_bn * normalized, axis=0)
    grad_normalized = grad_bn * gain_f[3]
    back_sums = cube.total(
        jnp.stack(
            [
                jnp.sum(grad_normalized, axis=0),
                jnp.sum(grad_normalized * normalized, axis=0),
                jnp.broadcast_to(ce_group / group, (D,)),
            ]
        )
    )
    conv_proj_grad = lowered(matmul_tn(swish_lo, conv_res_lo))
    sum_plain, sum_scaled = back_sums[0], back_sums[1]
    loss = back_sums[2, 0] / jnp.float32(devices * UTT_DEV * NSPAN * SPAN)
    grad_variance = -0.5 * inverse * inverse * sum_scaled
    grad_mean = -inverse * sum_plain - 2.0 * channel_mean * grad_variance
    grad_conv_out = (
        grad_normalized * inverse
        + (grad_mean + 2.0 * grad_variance * conv_out) * valid_rows[:, None] / frame_count
    )
    grad_gated, depth_grad = jax.vjp(conv_rows, gated_rows, depth_f)[1](grad_conv_out)
    grad_lead, grad_gate = jax.vjp(gate_rows, lead, gate)[1](grad_gated)
    grad_lead, grad_gate = lowered(grad_lead), lowered(grad_gate)
    norm_part, gain_grad_conv = norm_back(
        after_attention,
        gain_f[2],
        matmul_nt(grad_lead, lead_weight) + matmul_nt(grad_gate, gate_weight),
    )
    grad_attn_res = grad_conv_res + norm_part
    attn_res_lo = lowered(grad_attn_res)
    mid_grad = scattered(
        lowered(
            jnp.concatenate(
                [matmul_tn(attended_lo, attn_res_lo), matmul_tn(norm_conv, grad_lead)], axis=1
            )
        ),
        lowered(
            jnp.concatenate([matmul_tn(norm_conv, grad_gate), matmul_tn(swish_lo, conv_res_lo)], axis=1)
        ),
    )
    grad_attended = lowered(matmul_nt(attn_res_lo, proj_weight)).reshape(UTT_DEV, SEQ, H, HD)

    def attend_back(query_one, key_one, value_one, key_ok, log_total, grad_one):
        attn_probs = jnp.exp(scores_of(query_one, key_one, key_ok) - log_total[:, :, None])
        grad_value = jnp.einsum(
            "hqk,qhd->khd", lowered(attn_probs), grad_one, preferred_element_type=jnp.float32
        )
        grad_probs = jnp.einsum(
            "qhd,khd->hqk", grad_one, value_one, preferred_element_type=jnp.float32
        )
        grad_scores = lowered(
            attn_probs * (grad_probs - jnp.sum(attn_probs * grad_probs, axis=-1, keepdims=True))
        )
        grad_query = (
            jnp.einsum("hqk,khd->qhd", grad_scores, key_one, preferred_element_type=jnp.float32)
            * score_scale
        )
        grad_key = (
            jnp.einsum("hqk,qhd->khd", grad_scores, query_one, preferred_element_type=jnp.float32)
            * score_scale
        )
        return (grad_query, grad_key, grad_value)

    grad_query, grad_key, grad_value = attend_back(
        queries[0], key_rows[0], value_rows[0], valid_mat[0], log_totals, grad_attended[0]
    )
    grad_mixed = jnp.concatenate(
        [
            lowered(rotate_back(grad_query, cosine[:, :, :], sine_table)).reshape(row_total, D),
            lowered(rotate_back(grad_key, cosine, sine_table)).reshape(row_total, D),
            lowered(grad_value).reshape(row_total, D),
        ],
        axis=1,
    )
    mix_half = 3 * D // 2
    mix_grad = scattered(
        lowered(matmul_tn(norm_attn, grad_mixed[:, :mix_half])),
        lowered(matmul_tn(norm_attn, grad_mixed[:, mix_half:])),
    )
    norm_part, gain_grad_attn = norm_back(
        after_first,
        gain_f[1],
        matmul_nt(grad_mixed[:, :mix_half], mix_a) + matmul_nt(grad_mixed[:, mix_half:], mix_b),
    )
    grad_first_res = grad_attn_res + norm_part
    below_first, inner_first, outer_first = feed_back_parts(
        grad_first_res, norm_first, pre_first, act_first, (inner_a0, inner_b0), (outer_a0, outer_b0)
    )
    norm_part, gain_grad_first = norm_back(inputs, gain_f[0], below_first)
    input_grad = grad_first_res + norm_part
    vector_grad = jnp.concatenate(
        [
            jnp.stack(
                [
                    gain_grad_first,
                    gain_grad_attn,
                    gain_grad_conv,
                    gain_grad_bn,
                    gain_grad_second,
                    gain_grad_final,
                ],
                axis=0,
            ),
            depth_grad,
        ],
        axis=0,
    )
    vector_grad = jnp.moveaxis(vector_grad.reshape(vector_grad.shape[0], devices, -1), 1, 0)
    vector_grad = cube.scatter(
        vector_grad.reshape((2,) * len(cube.bits) + vector_grad.shape[1:]), order_a
    )
    return (
        output_lo,
        loss,
        input_grad,
        jnp.stack([inner_first, inner_second], axis=0),
        jnp.stack([outer_first, outer_second], axis=0),
        mix_grad,
        mid_grad[:, :D],
        mid_grad[:, D : 3 * D],
        vector_grad[6:],
        mid_grad[:, 3 * D :],
        vector_grad[:6],
        head_grad,
    )


def solution(mesh):
    placed = (
        P(("dp", "head"), None),
        P(None, ("dp", "head"), None),
        P(None, ("dp", "head"), None),
        P(("dp", "head"), None),
        P(("dp", "head"), None),
        P(("dp", "head"), None),
        P(None, ("dp", "head")),
        P(("dp", "head"), None),
        P(None, ("dp", "head")),
        P("dp", "head"),
        P(("dp", "head")),
        P(("dp", "head"), None),
        P(("dp", "head")),
        P(("dp", "head"), None),
    )
    sizes = {axis: mesh.shape[axis] for axis in AXES}
    return jax.shard_map(
        functools.partial(shards, sizes),
        mesh=mesh,
        in_specs=placed,
        out_specs=(
            P(("dp", "head"), None),
            P(),
            P(("dp", "head"), None),
            P(None, ("dp", "head"), None),
            P(None, ("dp", "head"), None),
            P(("dp", "head"), None),
            P(("dp", "head"), None),
            P(("dp", "head"), None),
            P(None, ("dp", "head")),
            P(("dp", "head"), None),
            P(None, ("dp", "head")),
            P("dp", "head"),
        ),
        check_vma=False,
    )
```

time: 2620 us -> 1430 us (0.55)
  waiting for transfers between devices: 1950 us -> 658 us
  blocking collectives: 158 us -> 0 us
  local copies, waits for them, and re-layouts: 79.1 us -> 219 us
  starting transfers between devices: 0.71 us -> 130 us
  other arithmetic: 167 us -> 237 us
  matrix products: 230 us -> 164 us
    reduce_scatter x8 -> x0, waiting for transfers between devices: 1390 us -> none  [the longest x1 361 us: shards(): lax.psum_scatter(outer_grad, ('dp', 'head'), scatter_dimension=1, tiled=T...]
    ppermute x0 -> x154, waiting for transfers between devices: none -> 658 us  [swap(): lax.ppermute(values, axis, [(i, i ^ bit) for i in range(self.sizes[axis])])]
    all_gather x8 -> x0, waiting for transfers between devices: 408 us -> none  [the longest x1 106 us: shards(): lax.all_gather(ffn_outer, ('dp', 'head'), axis=1, tiled=True)]
    unnamed x20 -> x0, waiting for transfers between devices: 157 us -> none
    ppermute x0 -> x154, starting transfers between devices: none -> 130 us  [swap(): lax.ppermute(values, axis, [(i, i ^ bit) for i in range(self.sizes[axis])])]
    psum x2 -> x0, blocking collectives: 79.5 us -> none  [the longest x1 40 us: shards(): ce_sum = lax.psum(ce_local, ('dp', 'head'))]
    all_gather x2 -> x0, blocking collectives: 78.4 us -> none  [the longest x1 39.6 us: shards(): lax.all_gather(norm_gains, ('dp', 'head'), axis=1, tiled=True)]
    dynamic_slice x0 -> x23, local copies, waits for them, and re-layouts: none -> 43.3 us  [the longest x12 24.7 us: scatter(): keep = lax.dynamic_index_in_dim(values, mine, place, keepdims=False)]
  transfers between devices with their start and end apart: 18 -> 154, of which waited for: 16 -> 73; matrix products, arithmetic and copies ran while one was open for 16% -> 39% of each run, Pallas kernels for 0% -> 0%
where the time goes in v1:
time: 1430 us; the launch traced here: 1420 us
  waiting for transfers between devices  658 us (46%)
  other arithmetic  237 us (17%)
  local copies, waits for them, and re-layouts  219 us (15%)
  matrix products  164 us (11%)
  starting transfers between devices  130 us (9%)
    ppermute x154, waiting for transfers between devices, swap(): lax.ppermute(values, axis, [(i, i ^ bit) for i in range(self.sizes[axis])])  658 us
    ppermute x154, starting transfers between devices, swap(): lax.ppermute(values, axis, [(i, i ^ bit) for i in range(self.sizes[axis])])  130 us
    another operation x144, other arithmetic, gather(): values = jnp.stack([first, second], axis=place)  71.1 us
    unnamed x668, local copies, waits for them, and re-layouts  58.6 us
    dot_general x16, matrix products, matmul_tn(): lax.dot_general(operand, weight, (((0,), (0,)), ((), ())), preferred_elem...  57.2 us
    dot_general x16, matrix products, matmul(): return jnp.dot(operand, weight, preferred_element_type=jnp.float32)  45.5 us
    dot_general x13, matrix products, matmul_nt(): lax.dot_general(operand, weight, (((1,), (1,)), ((), ())), preferred_elem...  42.7 us
    mul x31, local copies, waits for them, and re-layouts, depthwise(): result = result + padded[:, tap_at:tap_at + length] * tap_weights[tap_at]  34.3 us
  transfers between devices with their start and end apart: 154, of which 73 were waited for; matrix products, arithmetic and copies ran while one was open for 39% of the time, Pallas kernels for 0%

profile of v1, /device:TPU:0, one launch (start us, length us, event | category | flops | bytes accessed | tf_op | source)
XLA Modules:
  0.0 1418.3 jit_solution(16363462621693889420)
XLA Ops:
  120.6 11.0 collective-permute-done.55
  160.1 10.4 collective-permute-done.51
  219.0 26.8 %collective-permute-done.52 = bf16[2,2,32,2048]{3,2,0,1:T(8,128)(2,1)S(1)} collective-permute-done((bf16[2,2,32,2048]{3,2,0,1:T(8,128)(2,1)S(1)}, bf16[2,2,32,2048]{3,2,0,1:T(8,128)(2,1)S(1)}, u32[]{:S(2)}, u32[]{:S(2)}) %collective-permute-start.52) | collective-permute-done | bytes 524320 | tf_op jit(solution)/shard_map/ppermute | solution.py:112
  256.9 36.3 %collective-permute-done.57 = bf16[2,2,32,2048]{3,2,1,0:T(8,128)(2,1)S(1)} collective-permute-done((bf16[2,2,32,2048]{3,2,1,0:T(8,128)(2,1)S(1)}, bf16[2,2,32,2048]{3,2,1,0:T(8,128)(2,1)S(1)}, u32[]{:S(2)}, u32[]{:S(2)}) %collective-permute-start.57) | collective-permute-done | bytes 524320 | tf_op jit(solution)/shard_map/ppermute | solution.py:112
  301.9 11.7 collective-permute-done.28
  320.1 61.0 %collective-permute-done.8 = bf16[2,2,2,32,2048]{4,3,0,1,2:T(8,128)(2,1)S(1)} collective-permute-done((bf16[2,2,2,32,2048]{4,3,0,1,2:T(8,128)(2,1)S(1)}, bf16[2,2,2,32,2048]{4,3,0,1,2:T(8,128)(2,1)S(1)}, u32[]{:S(2)}, u32[]{:S(2)}) %collective-permute-start.8) | collective-permute-done | bytes 1048608 | tf_op jit(solution)/shard_map/ppermute | solution.py:112
  381.8 19.9 %collective-permute-done.38 = bf16[2,2,2,32,2048]{4,3,0,1,2:T(8,128)(2,1)S(1)} collective-permute-done((bf16[2,2,2,32,2048]{4,3,0,1,2:T(8,128)(2,1)S(1)}, bf16[2,2,2,32,2048]{4,3,0,1,2:T(8,128)(2,1)S(1)}, u32[]{:S(2)}, u32[]{:S(2)}) %collective-permute-start.38) | collective-permute-done | bytes 1048608 | tf_op jit(solution)/shard_map/ppermute | solution.py:112
  418.4 33.8 %collective-permute-done.68 = bf16[2,2,2,128,512]{4,3,2,1,0:T(8,128)(2,1)} collective-permute-done((bf16[2,2,2,128,512]{4,3,2,1,0:T(8,128)(2,1)}, bf16[2,2,2,128,512]{4,3,2,1,0:T(8,128)(2,1)}, u32[]{:S(2)}, u32[]{:S(2)}) %collective-permute-start.68) | collective-permute-done | bytes 1048608 | tf_op jit(solution)/shard_map/ppermute | solution.py:112
  453.7 16.6 %collective-permute-done.13 = bf16[2,2,2,32,2048]{4,3,0,1,2:T(8,128)(2,1)} collective-permute-done((bf16[2,2,2,32,2048]{4,3,0,1,2:T(8,128)(2,1)}, bf16[2,2,2,32,2048]{4,3,0,1,2:T(8,128)(2,1)}, u32[]{:S(2)}, u32[]{:S(2)}) %collective-permute-start.13) | collective-permute-done | bytes 1048608 | tf_op jit(solution)/shard_map/ppermute | solution.py:112
  581.4 10.1 multiply_reduce_fusion.1
  788.6 9.7 multiply_bitcast_fusion.32
  798.5 12.3 multiply_bitcast_fusion.33
  810.8 21.9 %pad_add_fusion = f32[1,543,1024]{2,1,0:T(8,128)} fusion(f32[1,512,1024]{2,1,0:T(8,128)} %get-tuple-element.248, f32[1,512,1024]{2,1,0:T(8,128)} %get-tuple-element.249, f32[1,512,1024]{2,1,0:T(8,128)} %get-tuple-element.250, f32[1,512,1024]{2,1,0:T(8,128)} %get-tuple-element.251, f32[1,512,1024]{2,1,0:T(8,128)} %get-tuple-element.252, ...), kind=kLoop, calls=%fused_computation.126 | loop fusion | flops 13900800 | bytes 56750080 | tf_op jit(solution)/shard_map/transpose(jvp())/add_any | solution.py:53
  1012.8 45.9 %collective-permute-done.152 = bf16[2,128,2048]{2,1,0:T(8,128)(2,1)S(1)} collective-permute-done((bf16[2,128,2048]{2,1,0:T(8,128)(2,1)S(1)}, bf16[2,128,2048]{2,1,0:T(8,128)(2,1)S(1)}, u32[]{:S(2)}, u32[]{:S(2)}) %collective-permute-start.152) | collective-permute-done | bytes 1048608 | tf_op jit(solution)/shard_map/ppermute | solution.py:112
  1105.9 8.5 collective-permute-done.153
  1116.9 50.4 %collective-permute-done.128 = bf16[2,2,32,1536]{3,2,0,1:T(8,128)(2,1)S(1)} collective-permute-done((bf16[2,2,32,1536]{3,2,0,1:T(8,128)(2,1)S(1)}, bf16[2,2,32,1536]{3,2,0,1:T(8,128)(2,1)S(1)}, u32[]{:S(2)}, u32[]{:S(2)}) %collective-permute-start.128) | collective-permute-done | bytes 393248 | tf_op jit(solution)/shard_map/ppermute | solution.py:112
  1168.4 9.7 collective-permute-done.133
  1210.2 19.2 %collective-permute-done.137 = bf16[2,2,2,32,2048]{4,3,2,1,0:T(8,128)(2,1)S(1)} collective-permute-done((bf16[2,2,2,32,2048]{4,3,2,1,0:T(8,128)(2,1)S(1)}, bf16[2,2,2,32,2048]{4,3,2,1,0:T(8,128)(2,1)S(1)}, u32[]{:S(2)}, u32[]{:S(2)}) %collective-permute-start.137) | collective-permute-done | bytes 1048608 | tf_op jit(solution)/shard_map/ppermute | solution.py:112
  1232.4 19.5 %collective-permute-done.87 = bf16[2,2,2,32,2048]{4,3,0,1,2:T(8,128)(2,1)S(1)} collective-permute-done((bf16[2,2,2,32,2048]{4,3,0,1,2:T(8,128)(2,1)S(1)}, bf16[2,2,2,32,2048]{4,3,0,1,2:T(8,128)(2,1)S(1)}, u32[]{:S(2)}, u32[]{:S(2)}) %collective-permute-start.87) | collective-permute-done | bytes 1048608 | tf_op jit(solution)/shard_map/ppermute | solution.py:112
  1255.2 19.2 %collective-permute-done.107 = bf16[2,2,2,128,512]{4,3,0,1,2:T(8,128)(2,1)S(1)} collective-permute-done((bf16[2,2,2,128,512]{4,3,0,1,2:T(8,128)(2,1)S(1)}, bf16[2,2,2,128,512]{4,3,0,1,2:T(8,128)(2,1)S(1)}, u32[]{:S(2)}, u32[]{:S(2)}) %collective-permute-start.107) | collective-permute-done | bytes 1048608 | tf_op jit(solution)/shard_map/ppermute | solution.py:112
  1277.2 9.4 collective-permute-done.98
  1299.4 9.6 collective-permute-done.138
  1380.9 12.3 collective-permute-done.125
  1396.4 12.3 collective-permute-done.90
  (1503 shorter events, 910.5 us)
Async XLA Ops:
  13.2 88.1 %collective-permute-start.25 = (bf16[32,1536]{1,0:T(8,128)(2,1)}, bf16[32,1536]{1,0:T(8,128)(2,1)}, u32[]{:S(2)}, u32[]{:S(2)}) collective-permute-start(bf16[32,1536]{1,0:T(8,128)(2,1)} %slice.538), channel_id=1, source_target_pairs={{0,16},{4,20},{8,24},{12,28},{16,0},{20,4},{24,8},{28,12},{1,17},{... | collective-permute-start | bytes 294920 | tf_op jit(solution)/shard_map/ppermute | solution.py:112
  14.5 87.8 %collective-permute-start.40 = (bf16[32,2048]{1,0:T(8,128)(2,1)S(1)}, bf16[32,2048]{1,0:T(8,128)(2,1)}, u32[]{:S(2)}, u32[]{:S(2)}) collective-permute-start(bf16[32,2048]{1,0:T(8,128)(2,1)S(1)} %get-tuple-element.392), channel_id=1, source_target_pairs={{0,16},{4,20},{8,24},{12,28},{16,0},{20,4},{24,8},{28,12},{1,17},{... | collective-permute-start | bytes 393224 | tf_op jit(solution)/shard_map/ppermute | solution.py:112
  17.2 89.0 %collective-permute-start.35 = (bf16[32,2048]{1,0:T(8,128)(2,1)S(1)}, bf16[32,2048]{1,0:T(8,128)(2,1)S(1)}, u32[]{:S(2)}, u32[]{:S(2)}) collective-permute-start(bf16[32,2048]{1,0:T(8,128)(2,1)S(1)} %get-tuple-element.393), channel_id=1, source_target_pairs={{0,16},{4,20},{8,24},{12,28},{16,0},{20,4},{24,8},{28,12},{1,17},{... | collective-permute-start | bytes 393224 | tf_op jit(solution)/shard_map/ppermute | solution.py:112
  42.5 66.3 %collective-permute-start.5 = (bf16[32,2048]{1,0:T(8,128)(2,1)}, bf16[32,2048]{1,0:T(8,128)(2,1)}, u32[]{:S(2)}, u32[]{:S(2)}) collective-permute-start(bf16[32,2048]{1,0:T(8,128)(2,1)} %slice.655), channel_id=1, source_target_pairs={{0,16},{4,20},{8,24},{12,28},{16,0},{20,4},{24,8},{28,12},{1,17},{... | collective-permute-start | bytes 393224 | tf_op jit(solution)/shard_map/ppermute | solution.py:112
  106.2 100.0 %collective-permute-start.72 = (bf16[128,2048]{1,0:T(8,128)(2,1)S(1)}, bf16[128,2048]{1,0:T(8,128)(2,1)S(1)}, u32[]{:S(2)}, u32[]{:S(2)}) collective-permute-start(bf16[128,2048]{1,0:T(8,128)(2,1)S(1)} %copy-done.147), channel_id=1, source_target_pairs={{0,4},{4,0},{8,12},{12,8},{16,20},{20,16},{24,28},{28,24},{1,5},{5... | collective-permute-start | bytes 1572872 | tf_op jit(solution)/shard_map/ppermute | solution.py:112
  297.6 118.5 %collective-permute-start.18 = (bf16[2,2,2,128,512]{4,3,0,1,2:T(8,128)(2,1)S(1)}, bf16[2,2,2,128,512]{4,3,0,1,2:T(8,128)(2,1)S(1)}, u32[]{:S(2)}, u32[]{:S(2)}) collective-permute-start(bf16[2,2,2,128,512]{4,3,0,1,2:T(8,128)(2,1)S(1)} %pad_maximum_fusion.33), channel_id=1, source_target_pairs={{0,2},{1,3},{2,0},{3,1},{4,6},{5,7},{6,4},{7,5},{8,10},{9,11},{10,... | collective-permute-start | bytes 3145736 | tf_op jit(solution)/shard_map/ppermute | solution.py:112
  299.2 114.7 %collective-permute-start.63 = (bf16[2,2,2,128,512]{4,3,0,1,2:T(8,128)(2,1)S(1)}, bf16[2,2,2,128,512]{4,3,0,1,2:T(8,128)(2,1)S(1)}, u32[]{:S(2)}, u32[]{:S(2)}) collective-permute-start(bf16[2,2,2,128,512]{4,3,0,1,2:T(8,128)(2,1)S(1)} %pad_maximum_fusion.41), channel_id=1, source_target_pairs={{0,2},{1,3},{2,0},{3,1},{4,6},{5,7},{6,4},{7,5},{8,10},{9,11},{10,... | collective-permute-start | bytes 3145736 | tf_op jit(solution)/shard_map/ppermute | solution.py:112
  313.6 67.4 %collective-permute-start.8 = (bf16[2,2,2,32,2048]{4,3,0,1,2:T(8,128)(2,1)S(1)}, bf16[2,2,2,32,2048]{4,3,0,1,2:T(8,128)(2,1)S(1)}, u32[]{:S(2)}, u32[]{:S(2)}) collective-permute-start(bf16[2,2,2,32,2048]{4,3,0,1,2:T(8,128)(2,1)S(1)} %pad_maximum_fusion.31), channel_id=1, source_target_pairs={{0,2},{1,3},{2,0},{3,1},{4,6},{5,7},{6,4},{7,5},{8,10},{9,11},{10,... | collective-permute-start | bytes 3145736 | tf_op jit(solution)/shard_map/ppermute | solution.py:112
  315.6 86.1 %collective-permute-start.38 = (bf16[2,2,2,32,2048]{4,3,0,1,2:T(8,128)(2,1)S(1)}, bf16[2,2,2,32,2048]{4,3,0,1,2:T(8,128)(2,1)S(1)}, u32[]{:S(2)}, u32[]{:S(2)}) collective-permute-start(bf16[2,2,2,32,2048]{4,3,0,1,2:T(8,128)(2,1)S(1)} %pad_maximum_fusion.37), channel_id=1, source_target_pairs={{0,2},{1,3},{2,0},{3,1},{4,6},{5,7},{6,4},{7,5},{8,10},{9,11},{10,... | collective-permute-start | bytes 3145736 | tf_op jit(solution)/shard_map/ppermute | solution.py:112
  318.3 94.6 %collective-permute-start.53 = (bf16[2,2,2,32,2048]{4,3,0,1,2:T(8,128)(2,1)S(1)}, bf16[2,2,2,32,2048]{4,3,0,1,2:T(8,128)(2,1)S(1)}, u32[]{:S(2)}, u32[]{:S(2)}) collective-permute-start(bf16[2,2,2,32,2048]{4,3,0,1,2:T(8,128)(2,1)S(1)} %pad_maximum_fusion.39), channel_id=1, source_target_pairs={{0,2},{1,3},{2,0},{3,1},{4,6},{5,7},{6,4},{7,5},{8,10},{9,11},{10,... | collective-permute-start | bytes 3145736 | tf_op jit(solution)/shard_map/ppermute | solution.py:112
  401.7 71.7 %collective-permute-start.23 = (bf16[2,2,2,128,512]{4,3,2,1,0:T(8,128)(2,1)}, bf16[2,2,2,128,512]{4,3,2,1,0:T(8,128)(2,1)}, u32[]{:S(2)}, u32[]{:S(2)}) collective-permute-start(bf16[2,2,2,128,512]{4,3,2,1,0:T(8,128)(2,1)} %pad_maximum_fusion.34), channel_id=1, source_target_pairs={{0,4},{4,0},{8,12},{12,8},{16,20},{20,16},{24,28},{28,24},{1,5},{5... | collective-permute-start | bytes 3145736 | tf_op jit(solution)/shard_map/ppermute | solution.py:112
  413.9 67.5 %collective-permute-start.58 = (bf16[2,2,2,32,2048]{4,3,2,1,0:T(8,128)(2,1)}, bf16[2,2,2,32,2048]{4,3,2,1,0:T(8,128)(2,1)S(1)}, u32[]{:S(2)}, u32[]{:S(2)}) collective-permute-start(bf16[2,2,2,32,2048]{4,3,2,1,0:T(8,128)(2,1)} %pad_maximum_fusion.40), channel_id=1, source_target_pairs={{0,4},{4,0},{8,12},{12,8},{16,20},{20,16},{24,28},{28,24},{1,5},{5... | collective-permute-start | bytes 3145736 | tf_op jit(solution)/shard_map/ppermute | solution.py:112
  416.1 70.4 %collective-permute-start.29 = (bf16[2,2,2,2,32,1536]{5,4,3,2,1,0:T(8,128)(2,1)S(1)}, bf16[2,2,2,2,32,1536]{5,4,3,2,1,0:T(8,128)(2,1)S(1)}, u32[]{:S(2)}, u32[]{:S(2)}) collective-permute-start(bf16[2,2,2,2,32,1536]{5,4,3,2,1,0:T(8,128)(2,1)S(1)} %copy.610), channel_id=1, source_target_pairs={{0,1},{1,0},{2,3},{3,2},{4,5},{5,4},{6,7},{7,6},{8,9},{9,8},{10,11... | collective-permute-start | bytes 4718600 | tf_op jit(solution)/shard_map/ppermute | solution.py:112
  452.2 199.6 %collective-permute-start.74 = (bf16[2,2,128,2048]{3,2,1,0:T(8,128)(2,1)}, bf16[2,2,128,2048]{3,2,1,0:T(8,128)(2,1)}, u32[]{:S(2)}, u32[]{:S(2)}) collective-permute-start(bf16[2,2,128,2048]{3,2,1,0:T(8,128)(2,1)} %pad_maximum_fusion.25), channel_id=1, source_target_pairs={{0,8},{4,12},{8,0},{12,4},{16,24},{20,28},{24,16},{28,20},{1,9},{5... | collective-permute-start | bytes 6291464 | tf_op jit(solution)/shard_map/ppermute | solution.py:112
  505.3 100.6 %collective-permute-start.69 = (bf16[2,2,2,2,128,512]{5,4,3,2,1,0:T(8,128)(2,1)}, bf16[2,2,2,2,128,512]{5,4,3,2,1,0:T(8,128)(2,1)}, u32[]{:S(2)}, u32[]{:S(2)}) collective-permute-start(bf16[2,2,2,2,128,512]{5,4,3,2,1,0:T(8,128)(2,1)} %pad_maximum_fusion.24), channel_id=1, source_target_pairs={{0,1},{1,0},{2,3},{3,2},{4,5},{5,4},{6,7},{7,6},{8,9},{9,8},{10,11... | collective-permute-start | bytes 6291464 | tf_op jit(solution)/shard_map/ppermute | solution.py:112
  516.1 86.6 %collective-permute-start.59 = (bf16[2,2,2,2,32,2048]{5,4,3,2,1,0:T(8,128)(2,1)}, bf16[2,2,2,2,32,2048]{5,4,3,2,1,0:T(8,128)(2,1)}, u32[]{:S(2)}, u32[]{:S(2)}) collective-permute-start(bf16[2,2,2,2,32,2048]{5,4,3,2,1,0:T(8,128)(2,1)} %pad_maximum_fusion.22), channel_id=1, source_target_pairs={{0,1},{1,0},{2,3},{3,2},{4,5},{5,4},{6,7},{7,6},{8,9},{9,8},{10,11... | collective-permute-start | bytes 6291464 | tf_op jit(solution)/shard_map/ppermute | solution.py:112
  703.1 300.1 %collective-permute-start.151 = (bf16[2,2,128,2048]{3,2,1,0:T(8,128)(2,1)}, bf16[2,2,128,2048]{3,2,1,0:T(8,128)(2,1)}, u32[]{:S(2)}, u32[]{:S(2)}) collective-permute-start(bf16[2,2,128,2048]{3,2,1,0:T(8,128)(2,1)} %dynamic-slice_bitcast_fusion), channel_id=1, source_target_pairs={{0,8},{4,12},{8,0},{12,4},{16,24},{20,28},{24,16},{28,20},{1,9},{5... | collective-permute-start | bytes 6291464 | tf_op jit(solution)/shard_map/ppermute | solution.py:112
  759.9 302.9 %collective-permute-start.96 = (bf16[2,2,2,2,32,2048]{5,4,0,1,2,3:T(8,128)(2,1)}, bf16[2,2,2,2,32,2048]{5,4,0,1,2,3:T(8,128)(2,1)}, u32[]{:S(2)}, u32[]{:S(2)}) collective-permute-start(bf16[2,2,2,2,32,2048]{5,4,0,1,2,3:T(8,128)(2,1)} %bitcast.1173), channel_id=1, source_target_pairs={{0,1},{1,0},{2,3},{3,2},{4,5},{5,4},{6,7},{7,6},{8,9},{9,8},{10,11... | collective-permute-start | bytes 6291464 | tf_op jit(solution)/shard_map/ppermute | solution.py:112
  759.9 306.3 %collective-permute-start.101 = (bf16[2,2,2,2,32,2048]{5,4,0,1,3,2:T(8,128)(2,1)}, bf16[2,2,2,2,32,2048]{5,4,0,1,3,2:T(8,128)(2,1)}, u32[]{:S(2)}, u32[]{:S(2)}) collective-permute-start(bf16[2,2,2,2,32,2048]{5,4,0,1,3,2:T(8,128)(2,1)} %bitcast.1172), channel_id=1, source_target_pairs={{0,1},{1,0},{2,3},{3,2},{4,5},{5,4},{6,7},{7,6},{8,9},{9,8},{10,11... | collective-permute-start | bytes 6291464 | tf_op jit(solution)/shard_map/ppermute | solution.py:112
  1087.3 121.1 %collective-permute-start.97 = (bf16[2,2,2,32,2048]{4,3,0,1,2:T(8,128)(2,1)S(1)}, bf16[2,2,2,32,2048]{4,3,0,1,2:T(8,128)(2,1)S(1)}, u32[]{:S(2)}, u32[]{:S(2)}) collective-permute-start(bf16[2,2,2,32,2048]{4,3,0,1,2:T(8,128)(2,1)S(1)} %dynamic-slice_bitcast_fusion.9), channel_id=1, source_target_pairs={{0,2},{1,3},{2,0},{3,1},{4,6},{5,7},{6,4},{7,5},{8,10},{9,11},{10,... | collective-permute-start | bytes 3145736 | tf_op jit(solution)/shard_map/ppermute | solution.py:112
  1089.7 119.7 %collective-permute-start.102 = (bf16[2,2,2,32,2048]{4,3,0,1,2:T(8,128)(2,1)S(1)}, bf16[2,2,2,32,2048]{4,3,0,1,2:T(8,128)(2,1)S(1)}, u32[]{:S(2)}, u32[]{:S(2)}) collective-permute-start(bf16[2,2,2,32,2048]{4,3,0,1,2:T(8,128)(2,1)S(1)} %copy-done.134), channel_id=1, source_target_pairs={{0,4},{4,0},{8,12},{12,8},{16,20},{20,16},{24,28},{28,24},{1,5},{5... | collective-permute-start | bytes 3145736 | tf_op jit(solution)/shard_map/ppermute | solution.py:112
  1098.9 105.4 %collective-permute-start.122 = (bf16[2,2,2,128,512]{4,3,0,1,2:T(8,128)(2,1)S(1)}, bf16[2,2,2,128,512]{4,3,0,1,2:T(8,128)(2,1)S(1)}, u32[]{:S(2)}, u32[]{:S(2)}) collective-permute-start(bf16[2,2,2,128,512]{4,3,0,1,2:T(8,128)(2,1)S(1)} %copy-done.137), channel_id=1, source_target_pairs={{0,4},{4,0},{8,12},{12,8},{16,20},{20,16},{24,28},{28,24},{1,5},{5... | collective-permute-start | bytes 3145736 | tf_op jit(solution)/shard_map/ppermute | solution.py:112
  1103.3 102.9 %collective-permute-start.117 = (bf16[2,2,2,128,512]{4,3,0,1,2:T(8,128)(2,1)S(1)}, bf16[2,2,2,128,512]{4,3,0,1,2:T(8,128)(2,1)S(1)}, u32[]{:S(2)}, u32[]{:S(2)}) collective-permute-start(bf16[2,2,2,128,512]{4,3,0,1,2:T(8,128)(2,1)S(1)} %copy-done.136), channel_id=1, source_target_pairs={{0,2},{1,3},{2,0},{3,1},{4,6},{5,7},{6,4},{7,5},{8,10},{9,11},{10,... | collective-permute-start | bytes 3145736 | tf_op jit(solution)/shard_map/ppermute | solution.py:112
  1209.4 65.0 %collective-permute-start.107 = (bf16[2,2,2,128,512]{4,3,0,1,2:T(8,128)(2,1)S(1)}, bf16[2,2,2,128,512]{4,3,0,1,2:T(8,128)(2,1)S(1)}, u32[]{:S(2)}, u32[]{:S(2)}) collective-permute-start(bf16[2,2,2,128,512]{4,3,0,1,2:T(8,128)(2,1)S(1)} %dynamic-slice_bitcast_fusion.7), channel_id=1, source_target_pairs={{0,2},{1,3},{2,0},{3,1},{4,6},{5,7},{6,4},{7,5},{8,10},{9,11},{10,... | collective-permute-start | bytes 3145736 | tf_op jit(solution)/shard_map/ppermute | solution.py:112
  (459 other events, 5965.7 us)

commit v2 on v1

--- a/solution.py
+++ b/solution.py
@@ -3,6 +3,8 @@
 import jax
 import jax.numpy as jnp
 from jax import lax
+from jax.experimental import pallas as pl
+from jax.experimental.pallas import tpu as pltpu
 from jax.sharding import PartitionSpec as P
 
 D = 1024
@@ -84,11 +86,79 @@
 
 
 AXES = ("dp", "head")
+ANY = pl.BlockSpec(memory_space=pl.ANY)
+VMEM = pl.BlockSpec(memory_space=pltpu.VMEM)
+Z1, Z0, X, Y, C = range(5)
+
+
+def place_copies(refs, out, sem, wheres):
+    copies = []
+    for at, (ref, where) in enumerate(zip(refs, wheres)):
+        copies.append(pltpu.make_async_copy(ref, out.at[where], sem.at[at]))
+        copies[-1].start()
+    for copy in copies:
+        copy.wait()
+
+
+def weave_z_kernel(own, far, near, both, out, sem):
+    z = lax.axis_index("dp") // 2
+    high, low = z // 2, z % 2
+    wheres = []
+    for flip_high, flip_low in ((0, 0), (1, 0), (0, 1), (1, 1)):
+        wheres.append((high + flip_high) % 2 * 2 + (low + flip_low) % 2)
+    place_copies((own, far, near, both), out, sem, wheres)
+
+
+def weave_z(parts):
+    return pl.pallas_call(
+        weave_z_kernel,
+        out_shape=jax.ShapeDtypeStruct((4,) + parts[0].shape, parts[0].dtype),
+        in_specs=[ANY] * 4,
+        out_specs=VMEM,
+        scratch_shapes=[pltpu.SemaphoreType.DMA((4,))],
+        compiler_params=pltpu.CompilerParams(vmem_limit_bytes=16 << 20),
+    )(*parts)
+
+
+def weave_kernel(*refs):
+    bufs, out, sem = refs[:-2], refs[-2], refs[-1]
+    x, y, c = lax.axis_index("dp") % 2, lax.axis_index("head") // 2, lax.axis_index("head") % 2
+    half = bufs[0].shape[-1]
+    wheres = []
+    for side in range(2):
+        for flip_c in range(2):
+            for flip_first, flip_second in ((0, 0), (1, 0), (0, 1), (1, 1)):
+                flip_x, flip_y = ((flip_first, flip_second), (flip_second, flip_first))[side]
+                wheres.append(
+                    (
+                        slice(None),
+                        (x + flip_x) % 2,
+                        (y + flip_y) % 2,
+                        (c + flip_c) % 2,
+                        slice(None),
+                        pl.ds(side * half, half),
+                    )
+                )
+    place_copies(bufs, out, sem, wheres)
+
+
+def weave(bufs):
+    _, rows, half = bufs[0].shape
+    whole = pl.pallas_call(
+        weave_kernel,
+        out_shape=jax.ShapeDtypeStruct((4, 2, 2, 2, rows, 2 * half), bufs[0].dtype),
+        in_specs=[ANY] * 16,
+        out_specs=VMEM,
+        scratch_shapes=[pltpu.SemaphoreType.DMA((16,))],
+        compiler_params=pltpu.CompilerParams(vmem_limit_bytes=16 << 20),
+    )(*bufs)
+    return whole.reshape(32 * rows, 2 * half)
 
 
 class Cube:
     def __init__(self, sizes):
         self.sizes = sizes
+        self.tuned = sizes == {"dp": 8, "head": 4}
         self.bits = []
         for axis in AXES:
             bit = sizes[axis] // 2
@@ -96,13 +166,6 @@
                 self.bits.append((axis, bit))
                 bit //= 2
 
-    def orders(self):
-        whole = list(range(len(self.bits)))
-        dp_count = sum(axis == "dp" for axis, bit in self.bits)
-        if self.sizes == {"dp": 8, "head": 4}:
-            return [0, 1, 2, 3, 4], [0, 1, 3, 2, 4], [2, 0, 1]
-        return whole, whole, whole[:dp_count]
-
     def mine(self, at):
         axis, bit = self.bits[at]
         return (lax.axis_index(axis) // bit) % 2
@@ -116,32 +179,222 @@
         values = shard
         for at in order:
             place = sum(other < at for other in held)
-            got = self.swap(values, at)
-            mine = self.mine(at)
-            first = jnp.where(mine == 0, values, got)
-            second = jnp.where(mine == 0, got, values)
-            values = jnp.stack([first, second], axis=place)
+            values = self.join(values, self.swap(values, at), at, place)
             held.append(at)
         return values
 
-    def scatter(self, values, order, final=jnp.float32):
-        held = sorted(order)
-        for step, at in enumerate(order[::-1]):
-            place = held.index(at)
-            mine = self.mine(at)
-            send = lax.dynamic_index_in_dim(values, 1 - mine, place, keepdims=False)
-            keep = lax.dynamic_index_in_dim(values, mine, place, keepdims=False)
-            got = self.swap(send, at)
-            total = keep.astype(jnp.float32) + got.astype(jnp.float32)
-            values = total.astype(final if step == len(order) - 1 else values.dtype)
-            held.remove(at)
+    def join(self, values, got, at, place):
+        mine = self.mine(at)
+        first = jnp.where(mine == 0, values, got)
+        second = jnp.where(mine == 0, got, values)
+        return jnp.stack([first, second], axis=place)
+
+    def total(self, values):
+        for at in range(len(self.bits)):
+            values = values + self.swap(values, at)
         return values
 
-    def total(self, values, only=None):
-        for at in range(len(self.bits)):
-            if only is None or self.bits[at][0] == only:
-                values = values + self.swap(values, at)
-        return values
+
+def weave_head_kernel(*refs):
+    bufs, out, sem = refs[:-2], refs[-2], refs[-1]
+    place = lax.axis_index("dp")
+    width = bufs[0].shape[-1]
+    wheres = []
+    for at in range(len(bufs)):
+        flip_x, flip_far, flip_near = at % 2, at // 2 % 2, at // 4 % 2
+        high = (place // 4 + flip_far) % 2
+        low = (place // 2 + flip_near) % 2
+        wheres.append(
+            (
+                high * 4 + low * 2 + (place + flip_x) % 2,
+                slice(None),
+                pl.ds(at // 8 * width, width),
+            )
+        )
+    place_copies(bufs, out, sem, wheres)
+
+
+def weave_head(bufs):
+    rows, width = bufs[0].shape
+    columns = len(bufs) // 8 * width
+    whole = pl.pallas_call(
+        weave_head_kernel,
+        out_shape=jax.ShapeDtypeStruct((8, rows, columns), bufs[0].dtype),
+        in_specs=[ANY] * len(bufs),
+        out_specs=VMEM,
+        scratch_shapes=[pltpu.SemaphoreType.DMA((len(bufs),))],
+        compiler_params=pltpu.CompilerParams(vmem_limit_bytes=16 << 20),
+    )(*bufs)
+    return whole.reshape(8 * rows, columns)
+
+
+class HeadGathering:
+    def __init__(self, cube, shard):
+        self.cube = cube
+        self.state = [shard]
+
+    def step(self, phase):
+        if not self.cube.tuned:
+            if phase == "x":
+                self.state = [lax.all_gather(self.state[0], "dp", axis=0, tiled=True)]
+            return
+        at = {"x": X, "far": Z1, "near": Z0}[phase]
+        self.state = self.state + [self.cube.swap(part, at) for part in self.state]
+
+
+class Gathering:
+    def __init__(self, cube, shard):
+        self.cube = cube
+        half = shard.shape[1] // 2
+        self.state = [shard[:, :half], shard[:, half:]] if cube.tuned else [shard]
+
+    def step(self, phase):
+        cube, state = self.cube, self.state
+        if not cube.tuned:
+            if phase == "z":
+                self.state = [lax.all_gather(state[0], AXES, axis=0, tiled=True)]
+            return
+        if phase == "z":
+            parts = []
+            for own in state:
+                far, near = cube.swap(own, Z1), cube.swap(own, Z0)
+                parts += [own, far, near, cube.swap(far, Z0)]
+            self.state = parts
+        if phase == "m":
+            left, right = weave_z(state[:4]), weave_z(state[4:])
+            self.state = [left, cube.swap(left, X), right, cube.swap(right, Y)]
+        if phase == "n":
+            a, b, c, d = state
+            self.state = [
+                a, b, cube.swap(a, Y), cube.swap(b, Y), c, d, cube.swap(c, X), cube.swap(d, X)
+            ]
+        if phase == "c":
+            other = [cube.swap(part, C) for part in state]
+            self.state = [weave(state[:4] + other[:4] + state[4:] + other[4:])]
+
+    @property
+    def whole(self):
+        return self.state[0]
+
+
+def pick_of(values, index, place):
+    return lax.dynamic_index_in_dim(values, index, place, keepdims=False)
+
+
+class Summing:
+    def __init__(self, cube, values, order):
+        self.cube, self.order = cube, list(order)
+        self.held = sorted(order)
+        self.keep, self.got, self.last = values, None, None
+
+    @property
+    def state(self):
+        return [part for part in (self.keep, self.got) if part is not None]
+
+    @state.setter
+    def state(self, parts):
+        self.keep = parts[0]
+        if len(parts) > 1:
+            self.got = parts[1]
+
+    def part(self, at, want_mine):
+        keep, got = self.keep, self.got
+        if self.last is not None:
+            keep = pick_of(keep, self.cube.mine(self.last[0]), self.last[1])
+        if at is not None:
+            mine, place = self.cube.mine(at), self.held.index(at)
+            index = mine if want_mine else 1 - mine
+            keep = pick_of(keep, index, place)
+            got = None if got is None else pick_of(got, index, place)
+        if got is None:
+            return keep
+        return keep.astype(jnp.float32) + got.astype(jnp.float32)
+
+    def step(self):
+        at = self.order.pop(0)
+        kind = self.keep.dtype
+        place = self.held.index(at)
+        send = self.part(at, False).astype(kind)
+        if self.got is None:
+            self.last = (at, place)
+        else:
+            self.keep = self.part(at, True).astype(kind)
+            self.last = None
+        self.got = self.cube.swap(send, at)
+        self.held.remove(at)
+
+    def result(self):
+        return self.part(None, True)
+
+
+class Scattering:
+    def __init__(self, cube, left, right, rows):
+        self.cube = cube
+        if not cube.tuned:
+            self.parts = []
+            self.whole = jnp.concatenate([left, right], axis=1)
+            return
+        bits = (2,) * len(cube.bits)
+        self.parts = [
+            Summing(cube, left.reshape(bits + (rows, -1)), (C, Y, X, Z0, Z1)),
+            Summing(cube, right.reshape(bits + (rows, -1)), (C, X, Y, Z0, Z1)),
+        ]
+
+    @property
+    def state(self):
+        if not self.cube.tuned:
+            return [self.whole]
+        return [self.parts[0].state, self.parts[1].state]
+
+    @state.setter
+    def state(self, values):
+        if not self.cube.tuned:
+            self.whole = values[0]
+        else:
+            self.parts[0].state, self.parts[1].state = values
+
+    def step(self, count=1):
+        if self.cube.tuned:
+            for _ in range(count):
+                for part in self.parts:
+                    part.step()
+
+    def result(self):
+        if not self.cube.tuned:
+            return lax.psum_scatter(self.whole, AXES, scatter_dimension=0, tiled=True).astype(
+                jnp.float32
+            )
+        return jnp.concatenate([part.result() for part in self.parts], axis=1)
+
+
+class HeadScattering:
+    def __init__(self, cube, values, rows):
+        self.cube = cube
+        if not cube.tuned:
+            self.whole = values
+            return
+        half = values.shape[1] // 2
+        self.parts = [
+            Summing(cube, values[:, :half].reshape(2, 2, 2, rows, half), (X, Z0, Z1)),
+            Summing(cube, values[:, half:].reshape(2, 2, 2, rows, half), (Z0, Z1, X)),
+        ]
+
+    state = Scattering.state
+    step = Scattering.step
+
+    def result(self):
+        if not self.cube.tuned:
+            return lax.psum_scatter(self.whole, "dp", scatter_dimension=0, tiled=True).astype(
+                jnp.float32
+            )
+        return jnp.concatenate([part.result() for part in self.parts], axis=1)
+
+
+def fence(flows, *values):
+    states, values = lax.optimization_barrier(([flow.state for flow in flows], values))
+    for flow, state in zip(flows, states):
+        flow.state = state
+    return values[0] if len(values) == 1 else values
 
 
 def rows_of(values, count):
@@ -166,43 +419,27 @@
     out_grad,
 ):
     cube = Cube(sizes)
-    order_a, order_b, order_dp = cube.orders()
     devices = sizes["dp"] * sizes["head"]
     ff = ffn_inner.shape[2]
-
-    def gathered(shard):
-        half = shard.shape[1] // 2
-        return (
-            rows_of(cube.gather(shard[:, :half], order_a), shard.shape[0] * devices),
-            rows_of(cube.gather(shard[:, half:], order_b), shard.shape[0] * devices),
-        )
-
-    def scattered(left, right):
-        bits = (2,) * len(cube.bits)
-        rows = left.shape[0] // devices
-        return jnp.concatenate(
-            [
-                cube.scatter(left.reshape(bits + (rows, -1)), order_a),
-                cube.scatter(right.reshape(bits + (rows, -1)), order_b),
-            ],
-            axis=1,
-        )
-
-    vectors = jnp.concatenate([norm_gains, conv_depth], axis=0)
-    vectors = cube.gather(vectors, order_a)
-    vectors = jnp.moveaxis(vectors.reshape((devices,) + vectors.shape[-2:]), 0, 1).reshape(-1, D)
-    vectors = vectors.astype(jnp.float32)
-    gain_f, depth_f = vectors[:6], vectors[6:]
-    inner_a0, inner_b0 = gathered(ffn_inner[0])
-    outer_a0, outer_b0 = gathered(ffn_outer[0])
-    mix_a, mix_b = gathered(attn_qkv)
+    all_bits = list(range(len(cube.bits)))
+
     mid = jnp.concatenate([attn_proj, conv_expand, conv_proj], axis=1)
-    mid_a, mid_b = gathered(mid)
-    inner_a1, inner_b1 = gathered(ffn_inner[1])
-    head_cols = cube.gather(head_proj, order_dp).reshape(D, -1)
-    outer_a1, outer_b1 = gathered(ffn_outer[1])
-    proj_weight, lead_weight = mid_a[:, :D], mid_a[:, D:]
-    gate_weight, conv_weight = mid_b[:, :D], mid_b[:, D:]
+    pieces = [
+        Gathering(cube, shard)
+        for shard in (
+            ffn_inner[0],
+            ffn_outer[0],
+            attn_qkv,
+            mid,
+            ffn_inner[1],
+            ffn_outer[1],
+        )
+    ]
+    head_half = head_proj.shape[1] // 2
+    heads = [
+        HeadGathering(cube, head_proj[:, :head_half]),
+        HeadGathering(cube, head_proj[:, head_half:]),
+    ]
 
     row_total = UTT_DEV * SEQ
     positions = jnp.arange(SEQ, dtype=jnp.int32)
@@ -228,19 +465,55 @@
     head_order = [at for at in range(len(cube.bits)) if cube.bits[at][0] == "head"]
     group = sizes["head"]
     vocab_cols = head_proj.shape[1]
+
+    vectors = cube.gather(jnp.concatenate([norm_gains, conv_depth], axis=0), all_bits)
+    vectors = jnp.moveaxis(vectors.reshape((devices,) + vectors.shape[-2:]), 0, 1).reshape(-1, D)
     group_codes = cube.gather(picked_codes, head_order).reshape(group * slots)
+    pieces[0].step("z")
+    heads[0].step("x")
+    heads[1].step("x")
+    vectors, group_codes = fence([pieces[0], *heads], vectors, group_codes)
+    gain_f, depth_f = vectors[:6].astype(jnp.float32), vectors[6:].astype(jnp.float32)
     group_live = (group_codes >= 0).astype(jnp.float32)
     local_codes = group_codes - lax.axis_index("head") * vocab_cols
 
+
+    pieces[0].step("m")
+    pieces[1].step("z")
     inputs = frames.astype(jnp.float32)
     norm_first = lowered(layer_norm(inputs, gain_f[0]))
-    pre_first = [matmul(norm_first, inner_a0), matmul(norm_first, inner_b0)]
-    act_first = jnp.concatenate([lowered(jax.nn.silu(part)) for part in pre_first], axis=1)
-    after_first = inputs + 0.5 * jnp.concatenate(
-        [matmul(act_first, outer_a0), matmul(act_first, outer_b0)], axis=1
-    )
+    norm_first = fence(pieces[:2], norm_first)
+
+    pieces[0].step("n")
+    pieces[1].step("m")
+    pieces[2].step("z")
+    norm_first = fence(pieces[:3], norm_first)
+
+    pieces[0].step("c")
+    pieces[1].step("n")
+    pieces[2].step("m")
+    pieces[3].step("z")
+    inner_0 = pieces[0].whole
+    pre_first = matmul(norm_first, inner_0)
+    act_first = lowered(jax.nn.silu(pre_first))
+    pre_first, act_first = fence(pieces[:4], pre_first, act_first)
+
+    pieces[1].step("c")
+    pieces[2].step("n")
+    pieces[3].step("m")
+    pieces[4].step("z")
+    outer_0 = pieces[1].whole
+    after_first = inputs + 0.5 * matmul(act_first, outer_0)
     norm_attn = lowered(layer_norm(after_first, gain_f[1]))
-    mixed = jnp.concatenate([matmul(norm_attn, mix_a), matmul(norm_attn, mix_b)], axis=1)
+    after_first, norm_attn = fence(pieces[1:5], after_first, norm_attn)
+
+    pieces[2].step("c")
+    pieces[3].step("n")
+    pieces[4].step("m")
+    pieces[5].step("z")
+    heads[0].step("far")
+    mix_weight = pieces[2].whole
+    mixed = matmul(norm_attn, mix_weight)
     mixed = mixed.reshape(UTT_DEV, SEQ, 3, H, HD)
     queries = lowered(rotate(mixed[:, :, 0], cosine, sine_table))
     key_rows = lowered(rotate(mixed[:, :, 1], cosine, sine_table))
@@ -266,18 +539,29 @@
 
     attended, log_totals = attend_one(queries[0], key_rows[0], value_rows[0], valid_mat[0])
     attended_lo = lowered(attended.reshape(row_total, D))
+    attended_lo, queries, key_rows, value_rows, log_totals = fence(
+        [*pieces[2:6], heads[0]], attended_lo, queries, key_rows, value_rows, log_totals
+    )
+
+    pieces[3].step("c")
+    pieces[4].step("n")
+    pieces[5].step("m")
+    heads[0].step("near")
+    heads[1].step("far")
+    mid_weight = pieces[3].whole
+    proj_weight, conv_weight = mid_weight[:, :D], mid_weight[:, 3 * D :]
+    expand_weight = mid_weight[:, D : 3 * D]
     after_attention = after_first + matmul(attended_lo, proj_weight)
     norm_conv = lowered(layer_norm(after_attention, gain_f[2]))
-    lead = matmul(norm_conv, lead_weight)
-    gate = matmul(norm_conv, gate_weight)
-
-    def gate_rows(lead_rows, gate_in):
-        return lead_rows * jax.nn.sigmoid(gate_in) * valid_rows[:, None]
+    expanded = matmul(norm_conv, expand_weight)
+
+    def gate_rows(expanded_rows):
+        return expanded_rows[:, :D] * jax.nn.sigmoid(expanded_rows[:, D:]) * valid_rows[:, None]
 
     def conv_rows(gated_rows, tap_weights):
         return depthwise(gated_rows.reshape(UTT_DEV, SEQ, D), tap_weights).reshape(row_total, D)
 
-    gated_rows = gate_rows(lead, gate)
+    gated_rows = gate_rows(expanded)
     conv_out = conv_rows(gated_rows, depth_f)
     weighted = conv_out * valid_rows[:, None]
     sums = cube.total(
@@ -289,6 +573,14 @@
             ]
         )
     )
+    sums, conv_out, after_attention, expanded, norm_conv = fence(
+        [*pieces[3:6], *heads], sums, conv_out, after_attention, expanded, norm_conv
+    )
+
+    pieces[4].step("c")
+    pieces[5].step("n")
+    heads[1].step("near")
+    inner_1 = pieces[4].whole
     frame_count = sums[2, 0]
     channel_mean = sums[0] / frame_count
     variance = sums[1] / frame_count - channel_mean * channel_mean
@@ -298,11 +590,19 @@
     swish_lo = lowered(jax.nn.silu(normed_bn))
     after_conv = after_attention + matmul(swish_lo, conv_weight)
     norm_second = lowered(layer_norm(after_conv, gain_f[4]))
-    pre_second = [matmul(norm_second, inner_a1), matmul(norm_second, inner_b1)]
-    act_second = jnp.concatenate([lowered(jax.nn.silu(part)) for part in pre_second], axis=1)
-    after_second = after_conv + 0.5 * jnp.concatenate(
-        [matmul(act_second, outer_a1), matmul(act_second, outer_b1)], axis=1
-    )
+    pre_second = matmul(norm_second, inner_1)
+    act_second = lowered(jax.nn.silu(pre_second))
+    after_conv, norm_second, pre_second, act_second, swish_lo = fence(
+        [*pieces[4:6], *heads], after_conv, norm_second, pre_second, act_second, swish_lo
+    )
+
+    pieces[5].step("c")
+    outer_1 = pieces[5].whole
+    if cube.tuned:
+        head_cols = weave_head(heads[0].state + heads[1].state)
+    else:
+        head_cols = jnp.concatenate(heads[0].state + heads[1].state, axis=1)
+    after_second = after_conv + 0.5 * matmul(act_second, outer_1)
     output_lo = lowered(layer_norm(after_second, gain_f[5]))
 
     picked_rows = lowered(matmul(pick_lo, output_lo))
@@ -321,47 +621,43 @@
     grad_logits = lowered(
         (jnp.exp(logits - log_norm[:, None]) - onehot.astype(jnp.float32)) * group_live[:, None]
     )
-    head_bits = (2,) * len(order_dp)
-    head_grad = cube.scatter(
-        lowered(matmul_tn(group_rows, grad_logits)).reshape(
-            head_bits + (head_proj.shape[0], vocab_cols)
-        ),
-        order_dp,
-    )
+    head_grad = lowered(matmul_tn(group_rows, grad_logits))
+    head_flow = HeadScattering(cube, head_grad, head_proj.shape[0])
     row_grads = lowered(matmul_nt(grad_logits, head_cols))
-    row_grads = cube.scatter(
-        row_grads.reshape((2,) * len(head_order) + (slots, D)), head_order, jnp.bfloat16
-    )
+    row_sum = Summing(cube, row_grads.reshape((2,) * len(head_order) + (slots, D)), head_order[::-1])
+    head_flow.step()
+    for _ in head_order:
+        row_sum.step()
+    row_grads = lowered(row_sum.result())
     grad_output = out_grad.astype(jnp.float32) + matmul_tn(pick_lo, row_grads)
 
-    def feed_back_parts(grad_in, normed_lo, pre_act, act_lo, inner_parts, outer_parts):
+    def outer_back(grad_in, act_lo):
         grad_out_lo = lowered(0.5 * grad_in)
         half = D // 2
-        outer_grads = [
-            lowered(matmul_tn(act_lo, grad_out_lo[:, :half])),
-            lowered(matmul_tn(act_lo, grad_out_lo[:, half:])),
-        ]
-        outer_grad = scattered(*outer_grads)
-        grad_act = matmul_nt(grad_out_lo, jnp.concatenate(outer_parts, axis=1))
-        grad_pre = [
-            lowered(silu_back(pre_act[0], grad_act[:, : ff // 2])),
-            lowered(silu_back(pre_act[1], grad_act[:, ff // 2 :])),
-        ]
-        inner_grad = scattered(
-            lowered(matmul_tn(normed_lo, grad_pre[0])), lowered(matmul_tn(normed_lo, grad_pre[1]))
-        )
-        below = matmul_nt(grad_pre[0], inner_parts[0]) + matmul_nt(grad_pre[1], inner_parts[1])
-        return (below, inner_grad, outer_grad)
+        left = lowered(matmul_tn(act_lo, grad_out_lo[:, :half]))
+        right = lowered(matmul_tn(act_lo, grad_out_lo[:, half:]))
+        return grad_out_lo, Scattering(cube, left, right, ffn_outer.shape[1])
+
+    def inner_back(grad_out_lo, normed_lo, pre_act, inner_weight, outer_weight):
+        grad_pre = lowered(silu_back(pre_act, matmul_nt(grad_out_lo, outer_weight)))
+        half = ff // 2
+        left = lowered(matmul_tn(normed_lo, grad_pre[:, :half]))
+        right = lowered(matmul_tn(normed_lo, grad_pre[:, half:]))
+        below = matmul_nt(grad_pre, inner_weight)
+        return below, Scattering(cube, left, right, ffn_inner.shape[1])
 
     grad_second, gain_grad_final = norm_back(after_second, gain_f[5], grad_output)
-    below_second, inner_second, outer_second = feed_back_parts(
-        grad_second,
-        norm_second,
-        pre_second,
-        act_second,
-        (inner_a1, inner_b1),
-        (outer_a1, outer_b1),
-    )
+    grad_out_lo, outer_flow_1 = outer_back(grad_second, act_second)
+    grad_second, grad_out_lo = fence([head_flow, outer_flow_1], grad_second, grad_out_lo)
+
+    head_flow.step()
+    outer_flow_1.step(2)
+    below_second, inner_flow_1 = inner_back(grad_out_lo, norm_second, pre_second, inner_1, outer_1)
+    below_second = fence([head_flow, outer_flow_1, inner_flow_1], below_second)
+
+    head_flow.step()
+    outer_flow_1.step()
+    inner_flow_1.step(2)
     norm_part, gain_grad_second = norm_back(after_conv, gain_f[4], below_second)
     grad_conv_res = grad_second + norm_part
     conv_res_lo = lowered(grad_conv_res)
@@ -378,6 +674,16 @@
         )
     )
     conv_proj_grad = lowered(matmul_tn(swish_lo, conv_res_lo))
+    back_sums, grad_normalized, grad_conv_res, conv_proj_grad = fence(
+        [head_flow, outer_flow_1, inner_flow_1],
+        back_sums,
+        grad_normalized,
+        grad_conv_res,
+        conv_proj_grad,
+    )
+
+    outer_flow_1.step(2)
+    inner_flow_1.step()
     sum_plain, sum_scaled = back_sums[0], back_sums[1]
     loss = back_sums[2, 0] / jnp.float32(devices * UTT_DEV * NSPAN * SPAN)
     grad_variance = -0.5 * inverse * inverse * sum_scaled
@@ -387,25 +693,26 @@
         + (grad_mean + 2.0 * grad_variance * conv_out) * valid_rows[:, None] / frame_count
     )
     grad_gated, depth_grad = jax.vjp(conv_rows, gated_rows, depth_f)[1](grad_conv_out)
-    grad_lead, grad_gate = jax.vjp(gate_rows, lead, gate)[1](grad_gated)
-    grad_lead, grad_gate = lowered(grad_lead), lowered(grad_gate)
+    grad_expanded = lowered(jax.vjp(gate_rows, expanded)[1](grad_gated)[0])
+    expand_grad = lowered(matmul_tn(norm_conv, grad_expanded))
     norm_part, gain_grad_conv = norm_back(
-        after_attention,
-        gain_f[2],
-        matmul_nt(grad_lead, lead_weight) + matmul_nt(grad_gate, gate_weight),
+        after_attention, gain_f[2], matmul_nt(grad_expanded, expand_weight)
     )
     grad_attn_res = grad_conv_res + norm_part
     attn_res_lo = lowered(grad_attn_res)
-    mid_grad = scattered(
-        lowered(
-            jnp.concatenate(
-                [matmul_tn(attended_lo, attn_res_lo), matmul_tn(norm_conv, grad_lead)], axis=1
-            )
-        ),
-        lowered(
-            jnp.concatenate([matmul_tn(norm_conv, grad_gate), matmul_tn(swish_lo, conv_res_lo)], axis=1)
-        ),
-    )
+    proj_grad = lowered(matmul_tn(attended_lo, attn_res_lo))
+    mid_flow = Scattering(
+        cube,
+        jnp.concatenate([proj_grad, expand_grad[:, :D]], axis=1),
+        jnp.concatenate([expand_grad[:, D:], conv_proj_grad], axis=1),
+        attn_proj.shape[0],
+    )
+    grad_attn_res, attn_res_lo = fence(
+        [outer_flow_1, inner_flow_1, mid_flow], grad_attn_res, attn_res_lo
+    )
+
+    inner_flow_1.step(2)
+    mid_flow.step(2)
     grad_attended = lowered(matmul_nt(attn_res_lo, proj_weight)).reshape(UTT_DEV, SEQ, H, HD)
 
     def attend_back(query_one, key_one, value_one, key_ok, log_total, grad_one):
@@ -440,20 +747,27 @@
         ],
         axis=1,
     )
+    grad_mixed = fence([inner_flow_1, mid_flow], grad_mixed)
+
+    mid_flow.step()
     mix_half = 3 * D // 2
-    mix_grad = scattered(
+    mix_flow = Scattering(
+        cube,
         lowered(matmul_tn(norm_attn, grad_mixed[:, :mix_half])),
         lowered(matmul_tn(norm_attn, grad_mixed[:, mix_half:])),
-    )
-    norm_part, gain_grad_attn = norm_back(
-        after_first,
-        gain_f[1],
-        matmul_nt(grad_mixed[:, :mix_half], mix_a) + matmul_nt(grad_mixed[:, mix_half:], mix_b),
-    )
+        attn_qkv.shape[0],
+    )
+    norm_part, gain_grad_attn = norm_back(after_first, gain_f[1], matmul_nt(grad_mixed, mix_weight))
     grad_first_res = grad_attn_res + norm_part
-    below_first, inner_first, outer_first = feed_back_parts(
-        grad_first_res, norm_first, pre_first, act_first, (inner_a0, inner_b0), (outer_a0, outer_b0)
-    )
+    grad_out_lo, outer_flow_0 = outer_back(grad_first_res, act_first)
+    grad_first_res, grad_out_lo = fence(
+        [mid_flow, mix_flow, outer_flow_0], grad_first_res, grad_out_lo
+    )
+
+    mid_flow.step(2)
+    mix_flow.step(2)
+    outer_flow_0.step(2)
+    below_first, inner_flow_0 = inner_back(grad_out_lo, norm_first, pre_first, inner_0, outer_0)
     norm_part, gain_grad_first = norm_back(inputs, gain_f[0], below_first)
     input_grad = grad_first_res + norm_part
     vector_grad = jnp.concatenate(
@@ -474,22 +788,39 @@
         axis=0,
     )
     vector_grad = jnp.moveaxis(vector_grad.reshape(vector_grad.shape[0], devices, -1), 1, 0)
-    vector_grad = cube.scatter(
-        vector_grad.reshape((2,) * len(cube.bits) + vector_grad.shape[1:]), order_a
-    )
+    vector_flow = Summing(
+        cube, vector_grad.reshape((2,) * len(cube.bits) + vector_grad.shape[1:]), all_bits[::-1]
+    )
+    input_grad = fence([mid_flow, mix_flow, outer_flow_0, inner_flow_0, vector_flow], input_grad)
+
+    mix_flow.step()
+    outer_flow_0.step()
+    inner_flow_0.step(2)
+    for _ in all_bits:
+        vector_flow.step()
+    fence([mix_flow, outer_flow_0, inner_flow_0, vector_flow], loss)
+
+    mix_flow.step(2)
+    outer_flow_0.step(2)
+    inner_flow_0.step()
+    fence([mix_flow, outer_flow_0, inner_flow_0], loss)
+
+    inner_flow_0.step(2)
+    mid_grad = mid_flow.result()
+    vector_grad = vector_flow.result()
     return (
         output_lo,
         loss,
         input_grad,
-        jnp.stack([inner_first, inner_second], axis=0),
-        jnp.stack([outer_first, outer_second], axis=0),
-        mix_grad,
+        jnp.stack([inner_flow_0.result(), inner_flow_1.result()], axis=0),
+        jnp.stack([outer_flow_0.result(), outer_flow_1.result()], axis=0),
+        mix_flow.result(),
         mid_grad[:, :D],
         mid_grad[:, D : 3 * D],
         vector_grad[6:],
         mid_grad[:, 3 * D :],
         vector_grad[:6],
-        head_grad,
+        head_flow.result(),
     )
 
 

time: 1430 us -> 1170 us (0.82)
  waiting for transfers between devices: 658 us -> 414 us
  local copies, waits for them, and re-layouts: 219 us -> 90.8 us
  starting transfers between devices: 130 us -> 208 us
  Pallas kernels: 0 us -> 18.3 us
  other arithmetic: 237 us -> 253 us
    ppermute x154 -> x228, waiting for transfers between devices: 658 us -> 414 us  [swap(): lax.ppermute(values, axis, [(i, i ^ bit) for i in range(self.sizes[axis])])]
    ppermute x154 -> x228, starting transfers between devices: 130 us -> 208 us  [swap(): lax.ppermute(values, axis, [(i, i ^ bit) for i in range(self.sizes[axis])])]
    another operation x151 -> x29, other arithmetic: 74.1 us -> 9.63 us  [the longest x21 5.18 us: join(): return jnp.stack([first, second], axis=place)]
    convert_element_type x52 -> x56, other arithmetic: 30.8 us -> 75.3 us  [the longest x41 61.5 us: step(): send = self.part(at, False).astype(kind)]
    dynamic_slice x23 -> x0, local copies, waits for them, and re-layouts: 43.3 us -> none  [the longest x12 24.7 us: scatter(): keep = lax.dynamic_index_in_dim(values, mine, place, keepdims=False)]
    mul x38 -> x0, local copies, waits for them, and re-layouts: 42.7 us -> none  [the longest x31 34.3 us: depthwise(): result = result + padded[:, tap_at:tap_at + length] * tap_weights[tap_at]]
    reduce_sum x1, other arithmetic: 10.1 us -> 32.7 us  [shards(): jnp.sum(weighted, axis=0)]
    pallas_call x0 -> x19, Pallas kernels: none -> 18.3 us  [the longest x12 9.35 us: weave_z(): pl.pallas_call(weave_z_kernel, out_shape=jax.ShapeDtypeStruct((4,) + part...]
  transfers between devices with their start and end apart: 154 -> 228, of which waited for: 73 -> 100; matrix products, arithmetic and copies ran while one was open for 39% -> 28% of each run, Pallas kernels for 0% -> 1%
where the time goes in v2:
time: 1170 us; the launch traced here: 1160 us
  waiting for transfers between devices  414 us (35%)
  other arithmetic  253 us (22%)
  starting transfers between devices  208 us (18%)
  matrix products  162 us (14%)
  local copies, waits for them, and re-layouts  90.8 us (8%)
  Pallas kernels  18.3 us (2%)
    ppermute x228, waiting for transfers between devices, swap(): lax.ppermute(values, axis, [(i, i ^ bit) for i in range(self.sizes[axis])])  414 us
    ppermute x228, starting transfers between devices, swap(): lax.ppermute(values, axis, [(i, i ^ bit) for i in range(self.sizes[axis])])  208 us
    convert_element_type x41, other arithmetic, step(): send = self.part(at, False).astype(kind)  61.5 us
    dot_general x15, matrix products, matmul_tn(): lax.dot_general(operand, weight, (((0,), (0,)), ((), ())), preferred_elem...  54 us
    dot_general x9, matrix products, matmul_nt(): lax.dot_general(operand, weight, (((1,), (1,)), ((), ())), preferred_elem...  47.2 us
    unnamed x682, local copies, waits for them, and re-layouts  42 us
    dot_general x10, matrix products, matmul(): return jnp.dot(operand, weight, preferred_element_type=jnp.float32)  40.8 us
    reduce_sum x1, other arithmetic, shards(): jnp.sum(weighted, axis=0)  32.7 us
  transfers between devices with their start and end apart: 228, of which 100 were waited for; matrix products, arithmetic and copies ran while one was open for 28% of the time, Pallas kernels for 1%

profile of v2, /device:TPU:0, one launch (start us, length us, event | category | flops | bytes accessed | tf_op | source)
XLA Modules:
  0.0 1155.5 jit_solution(13467510769181873971)
XLA Ops:
  86.4 10.0 collective-permute-done.24.refs_3_
  97.0 11.2 collective-permute-done.26.refs_11_
  127.4 8.6 collective-permute-done.52.far
  162.5 13.6 %collective-permute-done.48.refs_9_ = bf16[4,32,1536]{2,1,0:T(8,128)(2,1)S(1)} collective-permute-done((bf16[4,32,1536]{2,1,0:T(8,128)(2,1)S(1)}, bf16[4,32,1536]{2,1,0:T(8,128)(2,1)S(1)}, u32[]{:S(2)}, u32[]{:S(2)}) %collective-permute-start.48) | collective-permute-done | bytes 393248 | tf_op jit(solution)/shard_map/ppermute | solution.py:175
  179.7 9.8 collective-permute-done.69.far
  219.6 8.4 collective-permute-done.66.refs_11_
  228.0 8.6 collective-permute-done.67.refs_1_
  251.2 8.7 copy.224
  304.6 11.2 collective-permute-done.86.refs_11_
  315.9 8.9 collective-permute-done.87.refs_1_
  342.0 32.7 %multiply_reduce_fusion.1 = (f32[1024]{0:T(1024)S(1)}, f32[1024]{0:T(1024)S(1)}, f32[512,1024]{1,0:T(8,128)}) fusion(f32[512]{0:T(512)S(1)} %fusion.301, f32[1024]{0:T(1024)S(1)} %bitcast.1110, f32[1024]{0:T(1024)S(1)} %bitcast.1066, f32[1024]{0:T(1024)S(1)} %bitcast.1068, f32[1024]{0:T(1024)S(1)} %bitcast.1070, f32[1024]{0:T(1024)S(1)} %bitcast.1072, ...), kind=kLoop, calls=%fused_computation.64 | loop fusion | flops 37746688 | bytes 8529920 | tf_op jit(solution)/shard_map/reduce_sum | solution.py:570
  433.9 11.2 collective-permute-done.108.refs_11_
  445.2 10.2 collective-permute-done.109.refs_1_
  481.7 8.3 multiply_convert_fusion.1
  517.0 10.1 collective-permute-done.146
  643.5 10.2 collective-permute-done.157
  692.6 11.0 collective-permute-done.171
  725.6 13.0 %multiply_bitcast_fusion.33 = (f32[1,512,1024]{2,1,0:T(8,128)}, f32[1,512,1024]{2,1,0:T(8,128)}, f32[1,512,1024]{2,1,0:T(8,128)}, f32[1,512,1024]{2,1,0:T(8,128)...) fusion(f32[512,1024]{1,0:T(8,128)S(1)} %get-tuple-element.661, ...), kind=kLoop, calls=%fused_computation.275 | loop fusion | flops 9437184 | bytes 39919616 | tf_op jit(solution)/shard_map/transpose(jvp())/mul | solution.py:55
  738.8 10.0 multiply_bitcast_fusion.32
  772.1 21.6 %pad_add_fusion = f32[1,543,1024]{2,1,0:T(8,128)} fusion(f32[1,512,1024]{2,1,0:T(8,128)} %get-tuple-element.750, f32[1,512,1024]{2,1,0:T(8,128)} %get-tuple-element.751, f32[1,512,1024]{2,1,0:T(8,128)} %get-tuple-element.752, f32[1,512,1024]{2,1,0:T(8,128)} %get-tuple-element.753, f32[1,512,1024]{2,1,0:T(8,128)} %get-tuple-element.754, ...), kind=kLoop, calls=%fused_computation.68 | loop fusion | flops 13900800 | bytes 56750080 | tf_op jit(solution)/shard_map/transpose(jvp())/add_any | solution.py:55
  793.7 8.2 fusion.33
  934.7 10.3 fusion.329
  1004.8 19.9 %collective-permute-done.196 = bf16[2,2,2,32,1536]{4,3,1,0,2:T(8,128)(2,1)} collective-permute-done((bf16[2,2,2,32,1536]{4,3,1,0,2:T(8,128)(2,1)}, bf16[2,2,2,32,1536]{4,3,1,0,2:T(8,128)(2,1)}, u32[]{:S(2)}, u32[]{:S(2)}) %collective-permute-start.196) | collective-permute-done | bytes 786464 | tf_op jit(solution)/shard_map/ppermute | solution.py:175
  1065.2 29.2 %collective-permute-done.202 = bf16[2,2,32,1536]{3,2,1,0:T(8,128)(2,1)S(1)} collective-permute-done((bf16[2,2,32,1536]{3,2,1,0:T(8,128)(2,1)S(1)}, bf16[2,2,32,1536]{3,2,1,0:T(8,128)(2,1)S(1)}, u32[]{:S(2)}, u32[]{:S(2)}) %collective-permute-start.202) | collective-permute-done | bytes 393248 | tf_op jit(solution)/shard_map/ppermute | solution.py:175
  (1463 shorter events, 841.7 us)
Async XLA Ops:
  2.6 36.8 %collective-permute-start = (bf16[32,2048]{1,0:T(8,128)(2,1)S(1)}, bf16[32,2048]{1,0:T(8,128)(2,1)S(1)}, u32[]{:S(2)}, u32[]{:S(2)}) collective-permute-start(bf16[32,2048]{1,0:T(8,128)(2,1)S(1)} %get-tuple-element.299.own), channel_id=1, source_target_pairs={{0,16},{4,20},{8,24},{12,28},{16,0},{20,4},{24,8},{28,12},{1,17},{... | collective-permute-start | bytes 393224 | tf_op jit(solution)/shard_map/ppermute | solution.py:175
  6.7 33.1 %collective-permute-start.1 = (bf16[32,2048]{1,0:T(8,128)(2,1)S(1)}, bf16[32,2048]{1,0:T(8,128)(2,1)S(1)}, u32[]{:S(2)}, u32[]{:S(2)}) collective-permute-start(bf16[32,2048]{1,0:T(8,128)(2,1)S(1)} %get-tuple-element.299.own), channel_id=1, source_target_pairs={{0,8},{4,12},{8,0},{12,4},{16,24},{20,28},{24,16},{28,20},{1,9},{5... | collective-permute-start | bytes 393224 | tf_op jit(solution)/shard_map/ppermute | solution.py:175
  8.6 36.1 %collective-permute-start.4 = (bf16[32,2048]{1,0:T(8,128)(2,1)S(1)}, bf16[32,2048]{1,0:T(8,128)(2,1)S(1)}, u32[]{:S(2)}, u32[]{:S(2)}) collective-permute-start(bf16[32,2048]{1,0:T(8,128)(2,1)S(1)} %get-tuple-element.303.own), channel_id=1, source_target_pairs={{0,8},{4,12},{8,0},{12,4},{16,24},{20,28},{24,16},{28,20},{1,9},{5... | collective-permute-start | bytes 393224 | tf_op jit(solution)/shard_map/ppermute | solution.py:175
  244.6 34.0 %collective-permute-start.92 = (bf16[128,512]{1,0:T(8,128)(2,1)S(1)}, bf16[128,512]{1,0:T(8,128)(2,1)}, u32[]{:S(2)}, u32[]{:S(2)}) collective-permute-start(bf16[128,512]{1,0:T(8,128)(2,1)S(1)} %get-tuple-element.402.own), channel_id=1, source_target_pairs={{0,16},{4,20},{8,24},{12,28},{16,0},{20,4},{24,8},{28,12},{1,17},{... | collective-permute-start | bytes 393224 | tf_op jit(solution)/shard_map/ppermute | solution.py:175
  245.8 33.4 %collective-permute-start.93 = (bf16[128,512]{1,0:T(8,128)(2,1)S(1)}, bf16[128,512]{1,0:T(8,128)(2,1)}, u32[]{:S(2)}, u32[]{:S(2)}) collective-permute-start(bf16[128,512]{1,0:T(8,128)(2,1)S(1)} %get-tuple-element.402.own), channel_id=1, source_target_pairs={{0,8},{4,12},{8,0},{12,4},{16,24},{20,28},{24,16},{28,20},{1,9},{5... | collective-permute-start | bytes 393224 | tf_op jit(solution)/shard_map/ppermute | solution.py:175
  247.4 43.5 %collective-permute-start.95 = (bf16[128,1024]{1,0:T(8,128)(2,1)S(1)}, bf16[128,1024]{1,0:T(8,128)(2,1)}, u32[]{:S(2)}, u32[]{:S(2)}) collective-permute-start(bf16[128,1024]{1,0:T(8,128)(2,1)S(1)} %get-tuple-element.451.refs_0_), channel_id=1, source_target_pairs={{0,16},{4,20},{8,24},{12,28},{16,0},{20,4},{24,8},{28,12},{1,17},{... | collective-permute-start | bytes 786440 | tf_op jit(solution)/shard_map/ppermute | solution.py:175
  381.5 44.3 %collective-permute-start.105 = (bf16[4,32,2048]{2,1,0:T(8,128)(2,1)S(1)}, bf16[4,32,2048]{2,1,0:T(8,128)(2,1)S(1)}, u32[]{:S(2)}, u32[]{:S(2)}) collective-permute-start(bf16[4,32,2048]{2,1,0:T(8,128)(2,1)S(1)} %shard_map.243.refs_0_), channel_id=1, source_target_pairs={{0,2},{1,3},{2,0},{3,1},{4,6},{5,7},{6,4},{7,5},{8,10},{9,11},{10,... | collective-permute-start | bytes 1572872 | tf_op jit(solution)/shard_map/ppermute | solution.py:175
  602.9 40.6 %collective-permute-start.154 = (bf16[2,128,1024]{2,1,0:T(8,128)(2,1)}, bf16[2,128,1024]{2,1,0:T(8,128)(2,1)}, u32[]{:S(2)}, u32[]{:S(2)}) collective-permute-start(bf16[2,128,1024]{2,1,0:T(8,128)(2,1)} %get-tuple-element.719), channel_id=1, source_target_pairs={{0,8},{4,12},{8,0},{12,4},{16,24},{20,28},{24,16},{28,20},{1,9},{5... | collective-permute-start | bytes 1572872 | tf_op jit(solution)/shard_map/ppermute | solution.py:175
  604.9 38.6 %collective-permute-start.155 = (bf16[2,128,1024]{2,1,0:T(8,128)(2,1)}, bf16[2,128,1024]{2,1,0:T(8,128)(2,1)}, u32[]{:S(2)}, u32[]{:S(2)}) collective-permute-start(bf16[2,128,1024]{2,1,0:T(8,128)(2,1)} %get-tuple-element.717), channel_id=1, source_target_pairs={{0,16},{4,20},{8,24},{12,28},{16,0},{20,4},{24,8},{28,12},{1,17},{... | collective-permute-start | bytes 1572872 | tf_op jit(solution)/shard_map/ppermute | solution.py:175
  680.6 42.1 %collective-permute-start.165 = (bf16[2,2,2,32,2048]{4,3,1,0,2:T(8,128)(2,1)}, bf16[2,2,2,32,2048]{4,3,1,0,2:T(8,128)(2,1)}, u32[]{:S(2)}, u32[]{:S(2)}) collective-permute-start(bf16[2,2,2,32,2048]{4,3,1,0,2:T(8,128)(2,1)} %get-tuple-element.701), channel_id=1, source_target_pairs={{0,2},{1,3},{2,0},{3,1},{4,6},{5,7},{6,4},{7,5},{8,10},{9,11},{10,... | collective-permute-start | bytes 3145736 | tf_op jit(solution)/shard_map/ppermute | solution.py:175
  683.5 39.2 %collective-permute-start.167 = (bf16[2,2,2,32,2048]{4,3,1,0,2:T(8,128)(2,1)}, bf16[2,2,2,32,2048]{4,3,1,0,2:T(8,128)(2,1)}, u32[]{:S(2)}, u32[]{:S(2)}) collective-permute-start(bf16[2,2,2,32,2048]{4,3,1,0,2:T(8,128)(2,1)} %get-tuple-element.699), channel_id=1, source_target_pairs={{0,4},{4,0},{8,12},{12,8},{16,20},{20,16},{24,28},{28,24},{1,5},{5... | collective-permute-start | bytes 3145736 | tf_op jit(solution)/shard_map/ppermute | solution.py:175
  760.3 63.4 %collective-permute-start.173 = (bf16[2,128,512]{2,1,0:T(8,128)(2,1)}, bf16[2,128,512]{2,1,0:T(8,128)(2,1)}, u32[]{:S(2)}, u32[]{:S(2)}) collective-permute-start(bf16[2,128,512]{2,1,0:T(8,128)(2,1)} %get-tuple-element.808), channel_id=1, source_target_pairs={{0,8},{4,12},{8,0},{12,4},{16,24},{20,28},{24,16},{28,20},{1,9},{5... | collective-permute-start | bytes 786440 | tf_op jit(solution)/shard_map/ppermute | solution.py:175
  763.0 64.8 %collective-permute-start.175 = (bf16[2,128,512]{2,1,0:T(8,128)(2,1)}, bf16[2,128,512]{2,1,0:T(8,128)(2,1)}, u32[]{:S(2)}, u32[]{:S(2)}) collective-permute-start(bf16[2,128,512]{2,1,0:T(8,128)(2,1)} %get-tuple-element.806), channel_id=1, source_target_pairs={{0,8},{4,12},{8,0},{12,4},{16,24},{20,28},{24,16},{28,20},{1,9},{5... | collective-permute-start | bytes 786440 | tf_op jit(solution)/shard_map/ppermute | solution.py:175
  766.8 70.1 %collective-permute-start.177 = (bf16[2,2,32,2048]{3,2,1,0:T(8,128)(2,1)}, bf16[2,2,32,2048]{3,2,1,0:T(8,128)(2,1)}, u32[]{:S(2)}, u32[]{:S(2)}) collective-permute-start(bf16[2,2,32,2048]{3,2,1,0:T(8,128)(2,1)} %get-tuple-element.777), channel_id=1, source_target_pairs={{0,4},{4,0},{8,12},{12,8},{16,20},{20,16},{24,28},{28,24},{1,5},{5... | collective-permute-start | bytes 1572872 | tf_op jit(solution)/shard_map/ppermute | solution.py:175
  770.9 66.0 %collective-permute-start.178 = (bf16[2,2,32,2048]{3,2,1,0:T(8,128)(2,1)}, bf16[2,2,32,2048]{3,2,1,0:T(8,128)(2,1)}, u32[]{:S(2)}, u32[]{:S(2)}) collective-permute-start(bf16[2,2,32,2048]{3,2,1,0:T(8,128)(2,1)} %get-tuple-element.775), channel_id=1, source_target_pairs={{0,2},{1,3},{2,0},{3,1},{4,6},{5,7},{6,4},{7,5},{8,10},{9,11},{10,... | collective-permute-start | bytes 1572872 | tf_op jit(solution)/shard_map/ppermute | solution.py:175
  838.8 38.6 %collective-permute-start.179 = (bf16[2,32,2048]{2,1,0:T(8,128)(2,1)}, bf16[2,32,2048]{2,1,0:T(8,128)(2,1)}, u32[]{:S(2)}, u32[]{:S(2)}) collective-permute-start(bf16[2,32,2048]{2,1,0:T(8,128)(2,1)} %get-tuple-element.804), channel_id=1, source_target_pairs={{0,8},{4,12},{8,0},{12,4},{16,24},{20,28},{24,16},{28,20},{1,9},{5... | collective-permute-start | bytes 786440 | tf_op jit(solution)/shard_map/ppermute | solution.py:175
  840.7 40.2 %collective-permute-start.181 = (bf16[2,32,2048]{2,1,0:T(8,128)(2,1)}, bf16[2,32,2048]{2,1,0:T(8,128)(2,1)}, u32[]{:S(2)}, u32[]{:S(2)}) collective-permute-start(bf16[2,32,2048]{2,1,0:T(8,128)(2,1)} %get-tuple-element.802), channel_id=1, source_target_pairs={{0,8},{4,12},{8,0},{12,4},{16,24},{20,28},{24,16},{28,20},{1,9},{5... | collective-permute-start | bytes 786440 | tf_op jit(solution)/shard_map/ppermute | solution.py:175
  979.3 45.4 %collective-permute-start.198 = (bf16[2,2,2,128,512]{4,3,1,0,2:T(8,128)(2,1)}, bf16[2,2,2,128,512]{4,3,1,0,2:T(8,128)(2,1)}, u32[]{:S(2)}, u32[]{:S(2)}) collective-permute-start(bf16[2,2,2,128,512]{4,3,1,0,2:T(8,128)(2,1)} %get-tuple-element.693), channel_id=1, source_target_pairs={{0,2},{1,3},{2,0},{3,1},{4,6},{5,7},{6,4},{7,5},{8,10},{9,11},{10,... | collective-permute-start | bytes 3145736 | tf_op jit(solution)/shard_map/ppermute | solution.py:175
  982.9 41.8 %collective-permute-start.200 = (bf16[2,2,2,128,512]{4,3,1,0,2:T(8,128)(2,1)}, bf16[2,2,2,128,512]{4,3,1,0,2:T(8,128)(2,1)}, u32[]{:S(2)}, u32[]{:S(2)}) collective-permute-start(bf16[2,2,2,128,512]{4,3,1,0,2:T(8,128)(2,1)} %get-tuple-element.691), channel_id=1, source_target_pairs={{0,4},{4,0},{8,12},{12,8},{16,20},{20,16},{24,28},{28,24},{1,5},{5... | collective-permute-start | bytes 3145736 | tf_op jit(solution)/shard_map/ppermute | solution.py:175
  985.4 39.3 %collective-permute-start.196 = (bf16[2,2,2,32,1536]{4,3,1,0,2:T(8,128)(2,1)}, bf16[2,2,2,32,1536]{4,3,1,0,2:T(8,128)(2,1)}, u32[]{:S(2)}, u32[]{:S(2)}) collective-permute-start(bf16[2,2,2,32,1536]{4,3,1,0,2:T(8,128)(2,1)} %get-tuple-element.709), channel_id=1, source_target_pairs={{0,4},{4,0},{8,12},{12,8},{16,20},{20,16},{24,28},{28,24},{1,5},{5... | collective-permute-start | bytes 2359304 | tf_op jit(solution)/shard_map/ppermute | solution.py:175
  1042.5 51.9 %collective-permute-start.203 = (bf16[2,2,128,512]{3,2,1,0:T(8,128)(2,1)S(1)}, bf16[2,2,128,512]{3,2,1,0:T(8,128)(2,1)S(1)}, u32[]{:S(2)}, u32[]{:S(2)}) collective-permute-start(bf16[2,2,128,512]{3,2,1,0:T(8,128)(2,1)S(1)} %get-tuple-element.737), channel_id=1, source_target_pairs={{0,4},{4,0},{8,12},{12,8},{16,20},{20,16},{24,28},{28,24},{1,5},{5... | collective-permute-start | bytes 1572872 | tf_op jit(solution)/shard_map/ppermute | solution.py:175
  1052.1 42.4 %collective-permute-start.206 = (bf16[2,2,2,32,2048]{4,3,1,0,2:T(8,128)(2,1)S(1)}, bf16[2,2,2,32,2048]{4,3,1,0,2:T(8,128)(2,1)S(1)}, u32[]{:S(2)}, u32[]{:S(2)}) collective-permute-start(bf16[2,2,2,32,2048]{4,3,1,0,2:T(8,128)(2,1)S(1)} %get-tuple-element.689), channel_id=1, source_target_pairs={{0,2},{1,3},{2,0},{3,1},{4,6},{5,7},{6,4},{7,5},{8,10},{9,11},{10,... | collective-permute-start | bytes 3145736 | tf_op jit(solution)/shard_map/ppermute | solution.py:175
  1054.8 39.7 %collective-permute-start.208 = (bf16[2,2,2,32,2048]{4,3,1,0,2:T(8,128)(2,1)S(1)}, bf16[2,2,2,32,2048]{4,3,1,0,2:T(8,128)(2,1)S(1)}, u32[]{:S(2)}, u32[]{:S(2)}) collective-permute-start(bf16[2,2,2,32,2048]{4,3,1,0,2:T(8,128)(2,1)S(1)} %get-tuple-element.687), channel_id=1, source_target_pairs={{0,4},{4,0},{8,12},{12,8},{16,20},{20,16},{24,28},{28,24},{1,5},{5... | collective-permute-start | bytes 3145736 | tf_op jit(solution)/shard_map/ppermute | solution.py:175
  1060.9 33.6 %collective-permute-start.204 = (bf16[2,2,128,512]{3,2,1,0:T(8,128)(2,1)S(1)}, bf16[2,2,128,512]{3,2,1,0:T(8,128)(2,1)S(1)}, u32[]{:S(2)}, u32[]{:S(2)}) collective-permute-start(bf16[2,2,128,512]{3,2,1,0:T(8,128)(2,1)S(1)} %get-tuple-element.735), channel_id=1, source_target_pairs={{0,2},{1,3},{2,0},{3,1},{4,6},{5,7},{6,4},{7,5},{8,10},{9,11},{10,... | collective-permute-start | bytes 1572872 | tf_op jit(solution)/shard_map/ppermute | solution.py:175
  (543 other events, 6966.2 us)

commit v3 on v2

--- a/solution.py
+++ b/solution.py
@@ -1,4 +1,5 @@
 import functools
+import math
 
 import jax
 import jax.numpy as jnp
@@ -46,16 +47,6 @@
     )
 
 
-def depthwise(values, tap_weights):
-    kernel = tap_weights.shape[0]
-    length = values.shape[1]
-    padded = jnp.pad(values, ((0, 0), (kernel // 2, kernel - 1 - kernel // 2), (0, 0)))
-    result = padded[:, 0:length] * tap_weights[0]
-    for tap_at in range(1, kernel):
-        result = result + padded[:, tap_at : tap_at + length] * tap_weights[tap_at]
-    return result
-
-
 def lowered(values):
     return values.astype(jnp.bfloat16)
 
@@ -91,68 +82,35 @@
 Z1, Z0, X, Y, C = range(5)
 
 
-def place_copies(refs, out, sem, wheres):
-    copies = []
-    for at, (ref, where) in enumerate(zip(refs, wheres)):
-        copies.append(pltpu.make_async_copy(ref, out.at[where], sem.at[at]))
-        copies[-1].start()
-    for copy in copies:
-        copy.wait()
-
-
-def weave_z_kernel(own, far, near, both, out, sem):
-    z = lax.axis_index("dp") // 2
-    high, low = z // 2, z % 2
-    wheres = []
-    for flip_high, flip_low in ((0, 0), (1, 0), (0, 1), (1, 1)):
-        wheres.append((high + flip_high) % 2 * 2 + (low + flip_low) % 2)
-    place_copies((own, far, near, both), out, sem, wheres)
-
-
-def weave_z(parts):
-    return pl.pallas_call(
-        weave_z_kernel,
-        out_shape=jax.ShapeDtypeStruct((4,) + parts[0].shape, parts[0].dtype),
-        in_specs=[ANY] * 4,
-        out_specs=VMEM,
-        scratch_shapes=[pltpu.SemaphoreType.DMA((4,))],
+def local_copies(plan, inputs, outputs):
+    count = len(inputs)
+
+    def kernel(*refs):
+        sources, targets, sem = refs[:count], refs[count:-1], refs[-1]
+        dp, head = lax.axis_index("dp"), lax.axis_index("head")
+        where = (dp // 4, dp // 2 % 2, dp % 2, head // 2, head % 2)
+        copies = []
+        for at, (source, target) in enumerate(plan(where, sources, targets)):
+            copies.append(pltpu.make_async_copy(source, target, sem.at[at]))
+            copies[-1].start()
+        for copy in copies:
+            copy.wait()
+
+    size = sum(math.prod(shape) for shape in outputs) * inputs[0].dtype.itemsize
+    results = pl.pallas_call(
+        kernel,
+        out_shape=[jax.ShapeDtypeStruct(shape, inputs[0].dtype) for shape in outputs],
+        in_specs=[ANY] * count,
+        out_specs=[VMEM] * len(outputs),
+        scratch_shapes=[pltpu.SemaphoreType.DMA((16,))],
+        cost_estimate=pl.CostEstimate(flops=0, bytes_accessed=2 * size, transcendentals=0),
         compiler_params=pltpu.CompilerParams(vmem_limit_bytes=16 << 20),
-    )(*parts)
-
-
-def weave_kernel(*refs):
-    bufs, out, sem = refs[:-2], refs[-2], refs[-1]
-    x, y, c = lax.axis_index("dp") % 2, lax.axis_index("head") // 2, lax.axis_index("head") % 2
-    half = bufs[0].shape[-1]
-    wheres = []
-    for side in range(2):
-        for flip_c in range(2):
-            for flip_first, flip_second in ((0, 0), (1, 0), (0, 1), (1, 1)):
-                flip_x, flip_y = ((flip_first, flip_second), (flip_second, flip_first))[side]
-                wheres.append(
-                    (
-                        slice(None),
-                        (x + flip_x) % 2,
-                        (y + flip_y) % 2,
-                        (c + flip_c) % 2,
-                        slice(None),
-                        pl.ds(side * half, half),
-                    )
-                )
-    place_copies(bufs, out, sem, wheres)
-
-
-def weave(bufs):
-    _, rows, half = bufs[0].shape
-    whole = pl.pallas_call(
-        weave_kernel,
-        out_shape=jax.ShapeDtypeStruct((4, 2, 2, 2, rows, 2 * half), bufs[0].dtype),
-        in_specs=[ANY] * 16,
-        out_specs=VMEM,
-        scratch_shapes=[pltpu.SemaphoreType.DMA((16,))],
-        compiler_params=pltpu.CompilerParams(vmem_limit_bytes=16 << 20),
-    )(*bufs)
-    return whole.reshape(32 * rows, 2 * half)
+    )(*inputs)
+    return list(results)
+
+
+def flip(bit, by):
+    return (bit + by) % 2
 
 
 class Cube:
@@ -195,39 +153,6 @@
         return values
 
 
-def weave_head_kernel(*refs):
-    bufs, out, sem = refs[:-2], refs[-2], refs[-1]
-    place = lax.axis_index("dp")
-    width = bufs[0].shape[-1]
-    wheres = []
-    for at in range(len(bufs)):
-        flip_x, flip_far, flip_near = at % 2, at // 2 % 2, at // 4 % 2
-        high = (place // 4 + flip_far) % 2
-        low = (place // 2 + flip_near) % 2
-        wheres.append(
-            (
-                high * 4 + low * 2 + (place + flip_x) % 2,
-                slice(None),
-                pl.ds(at // 8 * width, width),
-            )
-        )
-    place_copies(bufs, out, sem, wheres)
-
-
-def weave_head(bufs):
-    rows, width = bufs[0].shape
-    columns = len(bufs) // 8 * width
-    whole = pl.pallas_call(
-        weave_head_kernel,
-        out_shape=jax.ShapeDtypeStruct((8, rows, columns), bufs[0].dtype),
-        in_specs=[ANY] * len(bufs),
-        out_specs=VMEM,
-        scratch_shapes=[pltpu.SemaphoreType.DMA((len(bufs),))],
-        compiler_params=pltpu.CompilerParams(vmem_limit_bytes=16 << 20),
-    )(*bufs)
-    return whole.reshape(8 * rows, columns)
-
-
 class HeadGathering:
     def __init__(self, cube, shard):
         self.cube = cube
@@ -238,39 +163,111 @@
             if phase == "x":
                 self.state = [lax.all_gather(self.state[0], "dp", axis=0, tiled=True)]
             return
-        at = {"x": X, "far": Z1, "near": Z0}[phase]
-        self.state = self.state + [self.cube.swap(part, at) for part in self.state]
+        if phase == "x":
+            (own,) = self.state
+            self.state = [own, self.cube.swap(own, X)]
+        if phase == "far":
+            own, got = self.state
+
+            def plan(where, sources, targets):
+                for by in range(2):
+                    yield sources[by], targets[0].at[flip(where[X], by)]
+
+            (pair,) = local_copies(plan, self.state, [(2,) + own.shape])
+            self.state = [pair, self.cube.swap(pair, Z1)]
+        if phase == "near":
+            pair, got = self.state
+
+            def plan(where, sources, targets):
+                for by in range(2):
+                    yield sources[by], targets[0].at[flip(where[Z1], by)]
+
+            (four,) = local_copies(plan, self.state, [(2,) + pair.shape])
+            self.state = [four, self.cube.swap(four, Z0)]
+
+
+def joined_heads(cube, heads):
+    if not cube.tuned:
+        return jnp.concatenate([part.state[0] for part in heads], axis=1)
+    parts = [part for flow in heads for part in flow.state]
+    _, _, rows, half = parts[0].shape
+
+    def plan(where, sources, targets):
+        for at in range(4):
+            columns = pl.ds(at // 2 * half, half)
+            yield sources[at], targets[0].at[:, flip(where[Z0], at % 2), :, :, columns]
+
+    (whole,) = local_copies(plan, parts, [(2, 2, 2, rows, 2 * half)])
+    return whole.reshape(8 * rows, 2 * half)
 
 
 class Gathering:
     def __init__(self, cube, shard):
         self.cube = cube
-        half = shard.shape[1] // 2
-        self.state = [shard[:, :half], shard[:, half:]] if cube.tuned else [shard]
+        self.rows, self.columns = shard.shape
+        self.state = [shard]
 
     def step(self, phase):
-        cube, state = self.cube, self.state
+        cube, state, rows = self.cube, self.state, self.rows
+        half = self.columns // 2
         if not cube.tuned:
             if phase == "z":
                 self.state = [lax.all_gather(state[0], AXES, axis=0, tiled=True)]
             return
         if phase == "z":
-            parts = []
-            for own in state:
-                far, near = cube.swap(own, Z1), cube.swap(own, Z0)
-                parts += [own, far, near, cube.swap(far, Z0)]
-            self.state = parts
+            (own,) = state
+
+            def plan(where, sources, targets):
+                for by in range(2):
+                    yield sources[by], targets[0].at[flip(where[Z1], by)]
+
+            (pair,) = local_copies(plan, [own, cube.swap(own, Z1)], [(2,) + own.shape])
+            self.state = [pair, cube.swap(pair, Z0)]
         if phase == "m":
-            left, right = weave_z(state[:4]), weave_z(state[4:])
+
+            def plan(where, sources, targets):
+                for by in range(2):
+                    for side in range(2):
+                        columns = pl.ds(side * half, half)
+                        yield (
+                            sources[by].at[:, :, columns],
+                            targets[side].at[:, flip(where[Z0], by)],
+                        )
+
+            left, right = local_copies(plan, state, [(2, 2, rows, half)] * 2)
             self.state = [left, cube.swap(left, X), right, cube.swap(right, Y)]
         if phase == "n":
-            a, b, c, d = state
-            self.state = [
-                a, b, cube.swap(a, Y), cube.swap(b, Y), c, d, cube.swap(c, X), cube.swap(d, X)
-            ]
+
+            def plan(where, sources, targets):
+                for by in range(2):
+                    yield sources[by], targets[0].at[:, :, flip(where[X], by)]
+                    yield sources[2 + by], targets[1].at[:, :, flip(where[Y], by)]
+
+            left, right = local_copies(plan, state, [(2, 2, 2, rows, half)] * 2)
+            self.state = [left, cube.swap(left, Y), right, cube.swap(right, X)]
         if phase == "c":
-            other = [cube.swap(part, C) for part in state]
-            self.state = [weave(state[:4] + other[:4] + state[4:] + other[4:])]
+
+            def plan(where, sources, targets):
+                for by in range(2):
+                    yield (
+                        sources[by],
+                        targets[0].at[:, :, :, flip(where[Y], by), :, pl.ds(0, half)],
+                    )
+                    yield (
+                        sources[2 + by],
+                        targets[0].at[:, :, flip(where[X], by), :, :, pl.ds(half, half)],
+                    )
+
+            (most,) = local_copies(plan, state, [(2, 2, 2, 2, rows, self.columns)])
+
+            def plan_whole(where, sources, targets):
+                for by in range(2):
+                    yield sources[by], targets[0].at[:, :, :, :, flip(where[C], by)]
+
+            (whole,) = local_copies(
+                plan_whole, [most, cube.swap(most, C)], [(2, 2, 2, 2, 2, rows, self.columns)]
+            )
+            self.state = [whole.reshape(32 * rows, self.columns)]
 
     @property
     def whole(self):
@@ -328,43 +325,56 @@
 
 
 class Scattering:
-    def __init__(self, cube, left, right, rows):
+    def __init__(self, cube, values, rows):
         self.cube = cube
-        if not cube.tuned:
-            self.parts = []
-            self.whole = jnp.concatenate([left, right], axis=1)
-            return
-        bits = (2,) * len(cube.bits)
-        self.parts = [
-            Summing(cube, left.reshape(bits + (rows, -1)), (C, Y, X, Z0, Z1)),
-            Summing(cube, right.reshape(bits + (rows, -1)), (C, X, Y, Z0, Z1)),
-        ]
-
-    @property
-    def state(self):
-        if not self.cube.tuned:
-            return [self.whole]
-        return [self.parts[0].state, self.parts[1].state]
-
-    @state.setter
-    def state(self, values):
-        if not self.cube.tuned:
-            self.whole = values[0]
-        else:
-            self.parts[0].state, self.parts[1].state = values
+        self.phase = 0
+        self.state = [values.reshape((2,) * len(cube.bits) + (rows, -1)) if cube.tuned else values]
+
+    def both(self, keep, got, at, place, columns=slice(None)):
+        halves = []
+        for index in (1 - self.cube.mine(at), self.cube.mine(at)):
+            first = pick_of(keep[..., columns], index, place).astype(jnp.float32)
+            second = pick_of(got[..., columns], index, place).astype(jnp.float32)
+            halves.append((first + second).astype(keep.dtype))
+        return halves
 
     def step(self, count=1):
-        if self.cube.tuned:
-            for _ in range(count):
-                for part in self.parts:
-                    part.step()
+        cube = self.cube
+        for _ in range(count if cube.tuned else 0):
+            if self.phase == 0:
+                (values,) = self.state
+                send = pick_of(values, 1 - cube.mine(C), 4)
+                self.state = [values, cube.swap(send, C)]
+            if self.phase == 1:
+                values, got = self.state
+                keep = pick_of(values, cube.mine(C), 4)
+                half = keep.shape[-1] // 2
+                send_a, keep_a = self.both(keep, got, Y, 3, slice(0, half))
+                send_b, keep_b = self.both(keep, got, X, 2, slice(half, None))
+                self.state = [keep_a, cube.swap(send_a, Y), keep_b, cube.swap(send_b, X)]
+            if self.phase == 2:
+                keep_a, got_a, keep_b, got_b = self.state
+                send_a, keep_a = self.both(keep_a, got_a, X, 2)
+                send_b, keep_b = self.both(keep_b, got_b, Y, 2)
+                self.state = [keep_a, cube.swap(send_a, X), keep_b, cube.swap(send_b, Y)]
+            if self.phase == 3:
+                keep_a, got_a, keep_b, got_b = self.state
+                keep = jnp.concatenate([keep_a, keep_b], axis=-1)
+                got = jnp.concatenate([got_a, got_b], axis=-1)
+                send, keep = self.both(keep, got, Z0, 1)
+                self.state = [keep, cube.swap(send, Z0)]
+            if self.phase == 4:
+                send, keep = self.both(*self.state, Z1, 0)
+                self.state = [keep, cube.swap(send, Z1)]
+            self.phase += 1
 
     def result(self):
         if not self.cube.tuned:
-            return lax.psum_scatter(self.whole, AXES, scatter_dimension=0, tiled=True).astype(
+            return lax.psum_scatter(self.state[0], AXES, scatter_dimension=0, tiled=True).astype(
                 jnp.float32
             )
-        return jnp.concatenate([part.result() for part in self.parts], axis=1)
+        keep, got = self.state
+        return keep.astype(jnp.float32) + got.astype(jnp.float32)
 
 
 class HeadScattering:
@@ -379,8 +389,22 @@
             Summing(cube, values[:, half:].reshape(2, 2, 2, rows, half), (Z0, Z1, X)),
         ]
 
-    state = Scattering.state
-    step = Scattering.step
+    @property
+    def state(self):
+        return [part.state for part in self.parts] if self.cube.tuned else [self.whole]
+
+    @state.setter
+    def state(self, values):
+        if not self.cube.tuned:
+            self.whole = values[0]
+            return
+        for part, state in zip(self.parts, values):
+            part.state = state
+
+    def step(self):
+        if self.cube.tuned:
+            for part in self.parts:
+                part.step()
 
     def result(self):
         if not self.cube.tuned:
@@ -388,6 +412,157 @@
                 jnp.float32
             )
         return jnp.concatenate([part.result() for part in self.parts], axis=1)
+
+
+def shifted(pad_ref, shift_ref, rows):
+    for r in range(8):
+        shift_ref[r] = pad_ref[r : r + rows, :]
+
+
+def conv_forward_kernel(lead_ref, gate_ref, valid_ref, taps_ref, conv_ref, sums_ref, pad, shift):
+    length, width = lead_ref.shape
+    edge = jnp.zeros((16, width), jnp.float32)
+    valid = valid_ref[...]
+    pad[0:16, :] = edge
+    pad[16 : 16 + length, :] = lead_ref[...] * jax.nn.sigmoid(gate_ref[...]) * valid
+    pad[16 + length : 40 + length, :] = jnp.zeros((24, width), jnp.float32)
+    shifted(pad, shift, length + 32)
+    chunk = 64
+    taps = [taps_ref[j : j + 1, :] for j in range(32)]
+
+    def step(at, totals):
+        start = pl.multiple_of(at * chunk, chunk)
+        total = jnp.zeros((chunk, width), jnp.float32)
+        for j in range(32):
+            total += shift[j % 8, pl.ds(start + j // 8 * 8, chunk), :] * taps[j]
+        conv_ref[pl.ds(start, chunk), :] = total
+        weighted = total * valid_ref[pl.ds(start, chunk), :]
+        plain, squares = totals
+        return (
+            plain + jnp.sum(weighted, axis=0, keepdims=True),
+            squares + jnp.sum(weighted * total, axis=0, keepdims=True),
+        )
+
+    zero = jnp.zeros((1, width), jnp.float32)
+    plain, squares = lax.fori_loop(0, length // chunk, step, (zero, zero))
+    sums_ref[0:1, :] = plain
+    sums_ref[1:2, :] = squares
+    sums_ref[2:8, :] = jnp.zeros((6, width), jnp.float32)
+
+
+def conv_forward(expanded, valid, taps):
+    rows = expanded.shape[0]
+    width = 128
+    count = D // width
+    return pl.pallas_call(
+        conv_forward_kernel,
+        grid=(count,),
+        in_specs=[
+            pl.BlockSpec((rows, width), lambda i: (0, i)),
+            pl.BlockSpec((rows, width), lambda i: (0, i + count)),
+            pl.BlockSpec((rows, 1), lambda i: (0, 0)),
+            pl.BlockSpec((32, width), lambda i: (0, i)),
+        ],
+        out_specs=[
+            pl.BlockSpec((rows, width), lambda i: (0, i)),
+            pl.BlockSpec((8, width), lambda i: (0, i)),
+        ],
+        out_shape=[
+            jax.ShapeDtypeStruct((rows, D), jnp.float32),
+            jax.ShapeDtypeStruct((8, D), jnp.float32),
+        ],
+        scratch_shapes=[
+            pltpu.VMEM((rows + 40, width), jnp.float32),
+            pltpu.VMEM((8, rows + 32, width), jnp.float32),
+        ],
+        cost_estimate=pl.CostEstimate(
+            flops=80 * rows * D, bytes_accessed=16 * rows * D, transcendentals=rows * D
+        ),
+        compiler_params=pltpu.CompilerParams(vmem_limit_bytes=16 << 20),
+    )(expanded, expanded, valid, taps)
+
+
+def conv_backward_kernel(
+    lead_ref,
+    gate_ref,
+    valid_ref,
+    taps_ref,
+    conv_ref,
+    grad_ref,
+    vectors_ref,
+    out_lead_ref,
+    out_gate_ref,
+    taps_grad_ref,
+    pad,
+    shift,
+    tap_sums,
+):
+    length, width = lead_ref.shape
+    inverse, plain, scaled = vectors_ref[0:1, :], vectors_ref[1:2, :], vectors_ref[2:3, :]
+    pad[0:16, :] = jnp.zeros((16, width), jnp.float32)
+    pad[16 : 16 + length, :] = (
+        grad_ref[...] * inverse + (plain + scaled * conv_ref[...]) * valid_ref[...]
+    )
+    pad[16 + length : 40 + length, :] = jnp.zeros((24, width), jnp.float32)
+    shifted(pad, shift, length + 32)
+    tap_sums[...] = jnp.zeros(tap_sums.shape, jnp.float32)
+    chunk = 64
+    taps = [taps_ref[j : j + 1, :] for j in range(32)]
+
+    def step(at, carry):
+        start = pl.multiple_of(at * chunk, chunk)
+        here = pl.ds(start, chunk)
+        lead, valid = lead_ref[here, :], valid_ref[here, :]
+        gate = jax.nn.sigmoid(gate_ref[here, :])
+        gated = lead * gate * valid
+        total = jnp.zeros((chunk, width), jnp.float32)
+        for j in range(32):
+            off = 32 - j
+            part = shift[off % 8, pl.ds(start + off // 8 * 8, chunk), :]
+            total += part * taps[j]
+            tap_sums[j] += jnp.sum((part * gated).reshape(chunk // 8, 8, width), axis=0)
+        grad = total * valid
+        out_lead_ref[here, :] = (grad * gate).astype(jnp.bfloat16)
+        out_gate_ref[here, :] = (grad * lead * gate * (1.0 - gate)).astype(jnp.bfloat16)
+        return carry
+
+    lax.fori_loop(0, length // chunk, step, 0)
+    taps_grad_ref[...] = jnp.sum(tap_sums[...], axis=1)
+
+
+def conv_backward(expanded, valid, taps, conv_out, grads, vectors):
+    rows = expanded.shape[0]
+    width = 128
+    count = D // width
+    block = pl.BlockSpec((rows, width), lambda i: (0, i))
+    return pl.pallas_call(
+        conv_backward_kernel,
+        grid=(count,),
+        in_specs=[
+            block,
+            pl.BlockSpec((rows, width), lambda i: (0, i + count)),
+            pl.BlockSpec((rows, 1), lambda i: (0, 0)),
+            pl.BlockSpec((32, width), lambda i: (0, i)),
+            block,
+            block,
+            pl.BlockSpec((8, width), lambda i: (0, i)),
+        ],
+        out_specs=[block, block, pl.BlockSpec((32, width), lambda i: (0, i))],
+        out_shape=[
+            jax.ShapeDtypeStruct((rows, D), jnp.bfloat16),
+            jax.ShapeDtypeStruct((rows, D), jnp.bfloat16),
+            jax.ShapeDtypeStruct((32, D), jnp.float32),
+        ],
+        scratch_shapes=[
+            pltpu.VMEM((rows + 40, width), jnp.float32),
+            pltpu.VMEM((8, rows + 32, width), jnp.float32),
+            pltpu.VMEM((32, 8, width), jnp.float32),
+        ],
+        cost_estimate=pl.CostEstimate(
+            flops=160 * rows * D, bytes_accessed=20 * rows * D, transcendentals=rows * D
+        ),
+        compiler_params=pltpu.CompilerParams(vmem_limit_bytes=16 << 20),
+    )(expanded, expanded, valid, taps, conv_out, grads, vectors)
 
 
 def fence(flows, *values):
@@ -466,28 +641,27 @@
     group = sizes["head"]
     vocab_cols = head_proj.shape[1]
 
+    loss_scale = jnp.float32(devices * UTT_DEV * NSPAN * SPAN)
     vectors = cube.gather(jnp.concatenate([norm_gains, conv_depth], axis=0), all_bits)
     vectors = jnp.moveaxis(vectors.reshape((devices,) + vectors.shape[-2:]), 0, 1).reshape(-1, D)
     group_codes = cube.gather(picked_codes, head_order).reshape(group * slots)
     pieces[0].step("z")
     heads[0].step("x")
     heads[1].step("x")
-    vectors, group_codes = fence([pieces[0], *heads], vectors, group_codes)
-    gain_f, depth_f = vectors[:6].astype(jnp.float32), vectors[6:].astype(jnp.float32)
-    group_live = (group_codes >= 0).astype(jnp.float32)
-    local_codes = group_codes - lax.axis_index("head") * vocab_cols
-
-
+    fence([pieces[0], *heads], loss_scale)
     pieces[0].step("m")
     pieces[1].step("z")
     inputs = frames.astype(jnp.float32)
-    norm_first = lowered(layer_norm(inputs, gain_f[0]))
-    norm_first = fence(pieces[:2], norm_first)
+    fence(pieces[:2], loss_scale)
 
     pieces[0].step("n")
     pieces[1].step("m")
     pieces[2].step("z")
-    norm_first = fence(pieces[:3], norm_first)
+    vectors, group_codes = fence(pieces[:3], vectors, group_codes)
+    gain_f, depth_f = vectors[:6].astype(jnp.float32), vectors[6:].astype(jnp.float32)
+    norm_first = lowered(layer_norm(inputs, gain_f[0]))
+    group_live = (group_codes >= 0).astype(jnp.float32)
+    local_codes = group_codes - lax.axis_index("head") * vocab_cols
 
     pieces[0].step("c")
     pieces[1].step("n")
@@ -555,24 +729,9 @@
     norm_conv = lowered(layer_norm(after_attention, gain_f[2]))
     expanded = matmul(norm_conv, expand_weight)
 
-    def gate_rows(expanded_rows):
-        return expanded_rows[:, :D] * jax.nn.sigmoid(expanded_rows[:, D:]) * valid_rows[:, None]
-
-    def conv_rows(gated_rows, tap_weights):
-        return depthwise(gated_rows.reshape(UTT_DEV, SEQ, D), tap_weights).reshape(row_total, D)
-
-    gated_rows = gate_rows(expanded)
-    conv_out = conv_rows(gated_rows, depth_f)
-    weighted = conv_out * valid_rows[:, None]
-    sums = cube.total(
-        jnp.stack(
-            [
-                jnp.sum(weighted, axis=0),
-                jnp.sum(weighted * conv_out, axis=0),
-                jnp.broadcast_to(jnp.sum(valid_rows), (D,)),
-            ]
-        )
-    )
+    conv_out, conv_sums = conv_forward(expanded, valid_rows[:, None], depth_f)
+    valid_total = jnp.broadcast_to(jnp.sum(valid_rows), (1, D))
+    sums = cube.total(jnp.concatenate([conv_sums[:2], valid_total], axis=0))
     sums, conv_out, after_attention, expanded, norm_conv = fence(
         [*pieces[3:6], *heads], sums, conv_out, after_attention, expanded, norm_conv
     )
@@ -598,10 +757,7 @@
 
     pieces[5].step("c")
     outer_1 = pieces[5].whole
-    if cube.tuned:
-        head_cols = weave_head(heads[0].state + heads[1].state)
-    else:
-        head_cols = jnp.concatenate(heads[0].state + heads[1].state, axis=1)
+    head_cols = joined_heads(cube, heads)
     after_second = after_conv + 0.5 * matmul(act_second, outer_1)
     output_lo = lowered(layer_norm(after_second, gain_f[5]))
 
@@ -633,18 +789,14 @@
 
     def outer_back(grad_in, act_lo):
         grad_out_lo = lowered(0.5 * grad_in)
-        half = D // 2
-        left = lowered(matmul_tn(act_lo, grad_out_lo[:, :half]))
-        right = lowered(matmul_tn(act_lo, grad_out_lo[:, half:]))
-        return grad_out_lo, Scattering(cube, left, right, ffn_outer.shape[1])
+        weight_grad = lowered(matmul_tn(act_lo, grad_out_lo))
+        return grad_out_lo, Scattering(cube, weight_grad, ffn_outer.shape[1])
 
     def inner_back(grad_out_lo, normed_lo, pre_act, inner_weight, outer_weight):
         grad_pre = lowered(silu_back(pre_act, matmul_nt(grad_out_lo, outer_weight)))
-        half = ff // 2
-        left = lowered(matmul_tn(normed_lo, grad_pre[:, :half]))
-        right = lowered(matmul_tn(normed_lo, grad_pre[:, half:]))
+        weight_grad = lowered(matmul_tn(normed_lo, grad_pre))
         below = matmul_nt(grad_pre, inner_weight)
-        return below, Scattering(cube, left, right, ffn_inner.shape[1])
+        return below, Scattering(cube, weight_grad, ffn_inner.shape[1])
 
     grad_second, gain_grad_final = norm_back(after_second, gain_f[5], grad_output)
     grad_out_lo, outer_flow_1 = outer_back(grad_second, act_second)
@@ -685,26 +837,32 @@
     outer_flow_1.step(2)
     inner_flow_1.step()
     sum_plain, sum_scaled = back_sums[0], back_sums[1]
-    loss = back_sums[2, 0] / jnp.float32(devices * UTT_DEV * NSPAN * SPAN)
+    loss = back_sums[2, 0] / loss_scale
     grad_variance = -0.5 * inverse * inverse * sum_scaled
     grad_mean = -inverse * sum_plain - 2.0 * channel_mean * grad_variance
-    grad_conv_out = (
-        grad_normalized * inverse
-        + (grad_mean + 2.0 * grad_variance * conv_out) * valid_rows[:, None] / frame_count
-    )
-    grad_gated, depth_grad = jax.vjp(conv_rows, gated_rows, depth_f)[1](grad_conv_out)
-    grad_expanded = lowered(jax.vjp(gate_rows, expanded)[1](grad_gated)[0])
-    expand_grad = lowered(matmul_tn(norm_conv, grad_expanded))
+    back_vectors = jnp.stack(
+        [inverse, grad_mean / frame_count, 2.0 * grad_variance / frame_count]
+        + [jnp.zeros_like(inverse)] * 5
+    )
+    grad_lead, grad_gate, depth_grad = conv_backward(
+        expanded, valid_rows[:, None], depth_f, conv_out, grad_normalized, back_vectors
+    )
+    grad_expanded = jnp.concatenate([grad_lead, grad_gate], axis=1)
     norm_part, gain_grad_conv = norm_back(
         after_attention, gain_f[2], matmul_nt(grad_expanded, expand_weight)
     )
     grad_attn_res = grad_conv_res + norm_part
     attn_res_lo = lowered(grad_attn_res)
-    proj_grad = lowered(matmul_tn(attended_lo, attn_res_lo))
     mid_flow = Scattering(
         cube,
-        jnp.concatenate([proj_grad, expand_grad[:, :D]], axis=1),
-        jnp.concatenate([expand_grad[:, D:], conv_proj_grad], axis=1),
+        jnp.concatenate(
+            [
+                lowered(matmul_tn(attended_lo, attn_res_lo)),
+                lowered(matmul_tn(norm_conv, grad_expanded)),
+                conv_proj_grad,
+            ],
+            axis=1,
+        ),
         attn_proj.shape[0],
     )
     grad_attn_res, attn_res_lo = fence(
@@ -750,13 +908,7 @@
     grad_mixed = fence([inner_flow_1, mid_flow], grad_mixed)
 
     mid_flow.step()
-    mix_half = 3 * D // 2
-    mix_flow = Scattering(
-        cube,
-        lowered(matmul_tn(norm_attn, grad_mixed[:, :mix_half])),
-        lowered(matmul_tn(norm_attn, grad_mixed[:, mix_half:])),
-        attn_qkv.shape[0],
-    )
+    mix_flow = Scattering(cube, lowered(matmul_tn(norm_attn, grad_mixed)), attn_qkv.shape[0])
     norm_part, gain_grad_attn = norm_back(after_first, gain_f[1], matmul_nt(grad_mixed, mix_weight))
     grad_first_res = grad_attn_res + norm_part
     grad_out_lo, outer_flow_0 = outer_back(grad_first_res, act_first)

time: 1170 us -> 1030 us (0.88)
  other arithmetic: 253 us -> 117 us
  starting transfers between devices: 208 us -> 121 us
  local copies, waits for them, and re-layouts: 90.8 us -> 133 us
  Pallas kernels: 18.3 us -> 57.4 us
  waiting for transfers between devices: 414 us -> 433 us
    ppermute x228 -> x124, starting transfers between devices: 208 us -> 121 us  [swap(): lax.ppermute(values, axis, [(i, i ^ bit) for i in range(self.sizes[axis])])]
    convert_element_type x41 -> x5, other arithmetic: 61.5 us -> 7.05 us  [step(): send = self.part(at, False).astype(kind)]
    reduce_sum x5 -> x1, other arithmetic: 45.3 us -> 0.6 us  [shards(): valid_total = jnp.broadcast_to(jnp.sum(valid_rows), (1, D))]
    dynamic_slice x0 -> x20, local copies, waits for them, and re-layouts: none -> 43.7 us  [pick_of(): return lax.dynamic_index_in_dim(values, index, place, keepdims=False)]
    pallas_call x19 -> x37, Pallas kernels: 18.3 us -> 57.4 us  [the longest x35 31.7 us: local_copies(): pl.pallas_call(kernel, out_shape=[jax.ShapeDtypeStruct(shape, inputs[0].d...]
    mul x4 -> x0, other arithmetic: 31.8 us -> none  [the longest x2 23 us: depthwise(): result = result + padded[:, tap_at:tap_at + length] * tap_weights[tap_at]]
    convert_element_type x12 -> x42, other arithmetic: 13.7 us -> 36 us  [both(): halves.append((first + second).astype(keep.dtype))]
    add_any x2 -> x0, other arithmetic: 21.8 us -> none  [the longest x1 21.6 us: depthwise(): result = result + padded[:, tap_at:tap_at + length] * tap_weights[tap_at]]
  transfers between devices with their start and end apart: 228 -> 124, of which waited for: 100 -> 58; matrix products, arithmetic and copies ran while one was open for 28% -> 31% of each run, Pallas kernels for 1% -> 4%
where the time goes in v3:
time: 1030 us; the launch traced here: 1020 us
  waiting for transfers between devices  433 us (42%)
  matrix products  155 us (15%)
  local copies, waits for them, and re-layouts  133 us (13%)
  starting transfers between devices  121 us (12%)
  other arithmetic  117 us (11%)
  Pallas kernels  57.4 us (6%)
    ppermute x124, waiting for transfers between devices, swap(): lax.ppermute(values, axis, [(i, i ^ bit) for i in range(self.sizes[axis])])  433 us
    ppermute x124, starting transfers between devices, swap(): lax.ppermute(values, axis, [(i, i ^ bit) for i in range(self.sizes[axis])])  121 us
    dot_general x10, matrix products, matmul_tn(): lax.dot_general(operand, weight, (((0,), (0,)), ((), ())), preferred_elem...  47.5 us
    dot_general x9, matrix products, matmul_nt(): lax.dot_general(operand, weight, (((1,), (1,)), ((), ())), preferred_elem...  47.3 us
    dynamic_slice x20, local copies, waits for them, and re-layouts, pick_of(): return lax.dynamic_index_in_dim(values, index, place, keepdims=False)  43.7 us
    dot_general x10, matrix products, matmul(): return jnp.dot(operand, weight, preferred_element_type=jnp.float32)  40.6 us
    unnamed x409, local copies, waits for them, and re-layouts  36.6 us
    convert_element_type x42, other arithmetic, both(): halves.append((first + second).astype(keep.dtype))  36 us
  transfers between devices with their start and end apart: 124, of which 58 were waited for; matrix products, arithmetic and copies ran while one was open for 31% of the time, Pallas kernels for 4%

profile of v3, /device:TPU:0, one launch (start us, length us, event | category | flops | bytes accessed | tf_op | source)
XLA Modules:
  0.0 1024.0 jit_solution(13264649195727333311)
XLA Ops:
  13.6 15.8 %collective-permute-done.14 = bf16[38,32]{0,1:T(8,128)(2,1)S(1)} collective-permute-done((bf16[38,32]{0,1:T(8,128)(2,1)S(1)}, bf16[38,32]{0,1:T(8,128)(2,1)S(1)}, u32[]{:S(2)}, u32[]{:S(2)}) %collective-permute-start.14) | collective-permute-done | bytes 2464 | tf_op jit(solution)/shard_map/ppermute | solution.py:133
  40.9 8.7 collective-permute-done.1.refs_1_
  73.0 9.6 collective-permute-done.13.refs_1_
  82.6 16.2 %collective-permute-done.10.refs_1_ = bf16[2,2,128,512]{3,2,1,0:T(8,128)(2,1)} collective-permute-done((bf16[2,2,128,512]{3,2,1,0:T(8,128)(2,1)S(1)}, bf16[2,2,128,512]{3,2,1,0:T(8,128)(2,1)}, u32[]{:S(2)}, u32[]{:S(2)}) %collective-permute-start.10) | collective-permute-done | bytes 524320 | tf_op jit(solution)/shard_map/ppermute | solution.py:133
  104.1 12.3 %collective-permute-done.26.refs_1_ = bf16[32,4096]{1,0:T(8,128)(2,1)S(1)} collective-permute-done((bf16[32,4096]{1,0:T(8,128)(2,1)S(1)}, bf16[32,4096]{1,0:T(8,128)(2,1)S(1)}, u32[]{:S(2)}, u32[]{:S(2)}) %collective-permute-start.26) | collective-permute-done | bytes 262176 | tf_op jit(solution)/shard_map/ppermute | solution.py:133
  133.4 18.7 %collective-permute-done.24.refs_1_ = bf16[2,2,32,1536]{3,2,1,0:T(8,128)(2,1)S(1)} collective-permute-done((bf16[2,2,32,1536]{3,2,1,0:T(8,128)(2,1)S(1)}, bf16[2,2,32,1536]{3,2,1,0:T(8,128)(2,1)S(1)}, u32[]{:S(2)}, u32[]{:S(2)}) %collective-permute-start.24) | collective-permute-done | bytes 393248 | tf_op jit(solution)/shard_map/ppermute | solution.py:133
  156.3 12.5 %collective-permute-done.33.refs_1_ = bf16[32,4096]{1,0:T(8,128)(2,1)S(1)} collective-permute-done((bf16[32,4096]{1,0:T(8,128)(2,1)S(1)}, bf16[32,4096]{1,0:T(8,128)(2,1)S(1)}, u32[]{:S(2)}, u32[]{:S(2)}) %collective-permute-start.33) | collective-permute-done | bytes 262176 | tf_op jit(solution)/shard_map/ppermute | solution.py:133
  182.8 18.7 %collective-permute-done.31.refs_1_ = bf16[2,2,32,2048]{3,2,1,0:T(8,128)(2,1)S(1)} collective-permute-done((bf16[2,2,32,2048]{3,2,1,0:T(8,128)(2,1)S(1)}, bf16[2,2,32,2048]{3,2,1,0:T(8,128)(2,1)S(1)}, u32[]{:S(2)}, u32[]{:S(2)}) %collective-permute-start.31) | collective-permute-done | bytes 524320 | tf_op jit(solution)/shard_map/ppermute | solution.py:133
  205.0 12.2 %collective-permute-done.40.refs_1_ = bf16[128,1024]{1,0:T(8,128)(2,1)S(1)} collective-permute-done((bf16[128,1024]{1,0:T(8,128)(2,1)S(1)}, bf16[128,1024]{1,0:T(8,128)(2,1)S(1)}, u32[]{:S(2)}, u32[]{:S(2)}) %collective-permute-start.40) | collective-permute-done | bytes 262176 | tf_op jit(solution)/shard_map/ppermute | solution.py:133
  282.0 10.3 %shard_map.260 = (f32[512,1024]{1,0:T(8,128)S(1)}, f32[8,1024]{1,0:T(8,128)S(1)}) custom-call(f32[512,2048]{1,0:T(8,128)S(1)} %fusion.18.lead_ref.gate_ref, f32[512,2048]{1,0:T(8,128)S(1)} %fusion.18.lead_ref.gate_ref, f32[512,1]{1,0:T(8,128)S(1)} %fusion.177.valid_ref, f32[32,1024]{1,0:T(8,128)S(1)} %slice_convert_fusion.2.taps_ref), custom_call_target="tpu_custom_call" | custom-call | flops 41943040 | bytes 8388608 | tf_op jit(solution)/shard_map/pallas_call | solution.py:457
  294.6 9.3 collective-permute-done.50
  320.8 13.0 %collective-permute-done.46.refs_1_ = bf16[2,2,128,512]{3,2,1,0:T(8,128)(2,1)S(1)} collective-permute-done((bf16[2,2,128,512]{3,2,1,0:T(8,128)(2,1)S(1)}, bf16[2,2,128,512]{3,2,1,0:T(8,128)(2,1)S(1)}, u32[]{:S(2)}, u32[]{:S(2)}) %collective-permute-start.46) | collective-permute-done | bytes 524320 | tf_op jit(solution)/shard_map/ppermute | solution.py:133
  514.4 16.6 %collective-permute-done.71 = bf16[2,2,2,128,512]{4,3,1,0,2:T(8,128)(2,1)S(1)} collective-permute-done((bf16[2,2,2,128,512]{4,3,1,0,2:T(8,128)(2,1)S(1)}, bf16[2,2,2,128,512]{4,3,1,0,2:T(8,128)(2,1)S(1)}, u32[]{:S(2)}, u32[]{:S(2)}) %collective-permute-start.71) | collective-permute-done | bytes 1048608 | tf_op jit(solution)/shard_map/ppermute | solution.py:133
  576.5 21.2 %collective-permute-done.82 = f32[3,1024]{1,0:T(4,128)S(1)} collective-permute-done((f32[3,1024]{1,0:T(4,128)S(1)}, f32[3,1024]{1,0:T(4,128)S(1)}, u32[]{:S(2)}, u32[]{:S(2)}) %collective-permute-start.82) | collective-permute-done | bytes 12320 | tf_op jit(solution)/shard_map/ppermute | solution.py:133
  633.6 15.4 %shard_map.268 = (bf16[512,1024]{1,0:T(8,128)(2,1)S(1)}, bf16[512,1024]{1,0:T(8,128)(2,1)S(1)}, f32[32,1024]{1,0:T(8,128)S(1)}) custom-call(f32[512,2048]{1,0:T(8,128)S(1)} %copy-done.1, f32[512,2048]{1,0:T(8,128)S(1)} %copy-done.1, f32[512,1]{1,0:T(8,128)S(1)} %copy-done.13, f32[32,1024]{1,0:T(8,128)S(1)} %copy-done.16, f32[512,1024]{1,0:T(8,128)S(1)} %copy-done.4, ...), custom_call_target="tpu_custom_call" | custom-call | flops 83886080 | bytes 10485760 | tf_op jit(solution)/shard_map/pallas_call | solution.py:538
  733.9 11.0 %collective-permute-done.90 = bf16[32,4096]{1,0:T(8,128)(2,1)S(1)} collective-permute-done((bf16[32,4096]{1,0:T(8,128)(2,1)S(1)}, bf16[32,4096]{1,0:T(8,128)(2,1)S(1)}, u32[]{:S(2)}, u32[]{:S(2)}) %collective-permute-start.90) | collective-permute-done | bytes 262176 | tf_op jit(solution)/shard_map/ppermute | solution.py:133
  850.4 13.3 %collective-permute-done.97 = bf16[32,4096]{1,0:T(8,128)(2,1)S(1)} collective-permute-done((bf16[32,4096]{1,0:T(8,128)(2,1)S(1)}, bf16[32,4096]{1,0:T(8,128)(2,1)S(1)}, u32[]{:S(2)}, u32[]{:S(2)}) %collective-permute-start.97) | collective-permute-done | bytes 262176 | tf_op jit(solution)/shard_map/ppermute | solution.py:133
  863.8 23.8 %collective-permute-done.100 = bf16[2,2,2,32,1536]{4,3,1,0,2:T(8,128)(2,1)S(1)} collective-permute-done((bf16[2,2,2,32,1536]{4,3,1,0,2:T(8,128)(2,1)S(1)}, bf16[2,2,2,32,1536]{4,3,1,0,2:T(8,128)(2,1)S(1)}, u32[]{:S(2)}, u32[]{:S(2)}) %collective-permute-start.100) | collective-permute-done | bytes 786464 | tf_op jit(solution)/shard_map/ppermute | solution.py:133
  903.1 11.0 %collective-permute-done.112 = f32[2,2,2,38,32]{4,3,0,1,2:T(8,128)S(1)} collective-permute-done((f32[2,2,2,38,32]{4,3,0,1,2:T(8,128)S(1)}, f32[2,2,2,38,32]{4,3,0,1,2:T(8,128)S(1)}, u32[]{:S(2)}, u32[]{:S(2)}) %collective-permute-start.112) | collective-permute-done | bytes 38944 | tf_op jit(solution)/shard_map/ppermute | solution.py:133
  940.3 20.0 %collective-permute-done.109 = bf16[2,2,2,32,2048]{4,3,1,0,2:T(8,128)(2,1)S(1)} collective-permute-done((bf16[2,2,2,32,2048]{4,3,1,0,2:T(8,128)(2,1)S(1)}, bf16[2,2,2,32,2048]{4,3,1,0,2:T(8,128)(2,1)S(1)}, u32[]{:S(2)}, u32[]{:S(2)}) %collective-permute-start.109) | collective-permute-done | bytes 1048608 | tf_op jit(solution)/shard_map/ppermute | solution.py:133
  966.3 12.6 %collective-permute-done.118 = bf16[2,128,1024]{2,1,0:T(8,128)(2,1)S(1)} collective-permute-done((bf16[2,128,1024]{2,1,0:T(8,128)(2,1)S(1)}, bf16[2,128,1024]{2,1,0:T(8,128)(2,1)S(1)}, u32[]{:S(2)}, u32[]{:S(2)}) %collective-permute-start.118) | collective-permute-done | bytes 524320 | tf_op jit(solution)/shard_map/ppermute | solution.py:133
  987.1 10.6 %collective-permute-done.117 = bf16[32,3072]{1,0:T(8,128)(2,1)S(1)} collective-permute-done((bf16[32,3072]{1,0:T(8,128)(2,1)S(1)}, bf16[32,3072]{1,0:T(8,128)(2,1)S(1)}, u32[]{:S(2)}, u32[]{:S(2)}) %collective-permute-start.117) | collective-permute-done | bytes 196640 | tf_op jit(solution)/shard_map/ppermute | solution.py:133
  999.1 10.7 %collective-permute-done.122 = bf16[2,32,4096]{2,1,0:T(8,128)(2,1)S(1)} collective-permute-done((bf16[2,32,4096]{2,1,0:T(8,128)(2,1)S(1)}, bf16[2,32,4096]{2,1,0:T(8,128)(2,1)S(1)}, u32[]{:S(2)}, u32[]{:S(2)}) %collective-permute-start.122) | collective-permute-done | bytes 524320 | tf_op jit(solution)/shard_map/ppermute | solution.py:133
  1011.7 9.6 collective-permute-done.123
  (992 shorter events, 682.9 us)
Async XLA Ops:
  217.5 35.9 %collective-permute-start.41 = (bf16[2,128,1024]{2,1,0:T(8,128)(2,1)S(1)}, bf16[2,128,1024]{2,1,0:T(8,128)(2,1)S(1)}, u32[]{:S(2)}, u32[]{:S(2)}) collective-permute-start(bf16[2,128,1024]{2,1,0:T(8,128)(2,1)S(1)} %shard_map.252.refs_0_), channel_id=1, source_target_pairs={{0,8},{4,12},{8,0},{12,4},{16,24},{20,28},{24,16},{28,20},{1,9},{5... | collective-permute-start | bytes 1572872 | tf_op jit(solution)/shard_map/ppermute | solution.py:133
  217.8 39.0 %collective-permute-start.42 = (bf16[2,128,1024]{2,1,0:T(8,128)(2,1)S(1)}, bf16[2,128,1024]{2,1,0:T(8,128)(2,1)}, u32[]{:S(2)}, u32[]{:S(2)}) collective-permute-start(bf16[2,128,1024]{2,1,0:T(8,128)(2,1)S(1)} %shard_map.253.refs_0_), channel_id=1, source_target_pairs={{0,16},{4,20},{8,24},{12,28},{16,0},{20,4},{24,8},{28,12},{1,17},{... | collective-permute-start | bytes 1572872 | tf_op jit(solution)/shard_map/ppermute | solution.py:133
  221.7 43.8 %collective-permute-start.36 = (bf16[2,2,2,32,2048]{4,3,2,1,0:T(8,128)(2,1)S(1)}, bf16[2,2,2,32,2048]{4,3,2,1,0:T(8,128)(2,1)}, u32[]{:S(2)}, u32[]{:S(2)}) collective-permute-start(bf16[2,2,2,32,2048]{4,3,2,1,0:T(8,128)(2,1)S(1)} %get-tuple-element.289.refs_0_), channel_id=1, source_target_pairs={{0,2},{1,3},{2,0},{3,1},{4,6},{5,7},{6,4},{7,5},{8,10},{9,11},{10,... | collective-permute-start | bytes 3145736 | tf_op jit(solution)/shard_map/ppermute | solution.py:133
  222.3 43.2 %collective-permute-start.37 = (bf16[2,2,2,32,2048]{4,3,2,1,0:T(8,128)(2,1)}, bf16[2,2,2,32,2048]{4,3,2,1,0:T(8,128)(2,1)}, u32[]{:S(2)}, u32[]{:S(2)}) collective-permute-start(bf16[2,2,2,32,2048]{4,3,2,1,0:T(8,128)(2,1)} %get-tuple-element.291.refs_2_), channel_id=1, source_target_pairs={{0,4},{4,0},{8,12},{12,8},{16,20},{20,16},{24,28},{28,24},{1,5},{5... | collective-permute-start | bytes 3145736 | tf_op jit(solution)/shard_map/ppermute | solution.py:133
  268.6 50.8 %collective-permute-start.49 = (bf16[2,128,1024]{2,1,0:T(8,128)(2,1)S(1)}, bf16[2,128,1024]{2,1,0:T(8,128)(2,1)S(1)}, u32[]{:S(2)}, u32[]{:S(2)}) collective-permute-start(bf16[2,128,1024]{2,1,0:T(8,128)(2,1)S(1)} %shard_map.259.refs_0_), channel_id=1, source_target_pairs={{0,16},{4,20},{8,24},{12,28},{16,0},{20,4},{24,8},{28,12},{1,17},{... | collective-permute-start | bytes 1572872 | tf_op jit(solution)/shard_map/ppermute | solution.py:133
  270.6 63.7 %collective-permute-start.44 = (bf16[2,2,2,32,2048]{4,3,2,1,0:T(8,128)(2,1)S(1)}, bf16[2,2,2,32,2048]{4,3,2,1,0:T(8,128)(2,1)S(1)}, u32[]{:S(2)}, u32[]{:S(2)}) collective-permute-start(bf16[2,2,2,32,2048]{4,3,2,1,0:T(8,128)(2,1)S(1)} %get-tuple-element.311.refs_0_), channel_id=1, source_target_pairs={{0,2},{1,3},{2,0},{3,1},{4,6},{5,7},{6,4},{7,5},{8,10},{9,11},{10,... | collective-permute-start | bytes 3145736 | tf_op jit(solution)/shard_map/ppermute | solution.py:133
  272.3 62.0 %collective-permute-start.45 = (bf16[2,2,2,32,2048]{4,3,2,1,0:T(8,128)(2,1)S(1)}, bf16[2,2,2,32,2048]{4,3,2,1,0:T(8,128)(2,1)S(1)}, u32[]{:S(2)}, u32[]{:S(2)}) collective-permute-start(bf16[2,2,2,32,2048]{4,3,2,1,0:T(8,128)(2,1)S(1)} %get-tuple-element.313.refs_2_), channel_id=1, source_target_pairs={{0,4},{4,0},{8,12},{12,8},{16,20},{20,16},{24,28},{28,24},{1,5},{5... | collective-permute-start | bytes 3145736 | tf_op jit(solution)/shard_map/ppermute | solution.py:133
  275.0 59.3 %collective-permute-start.48 = (bf16[2,2,128,1024]{3,2,1,0:T(8,128)(2,1)S(1)}, bf16[2,2,128,1024]{3,2,1,0:T(8,128)(2,1)S(1)}, u32[]{:S(2)}, u32[]{:S(2)}) collective-permute-start(bf16[2,2,128,1024]{3,2,1,0:T(8,128)(2,1)S(1)} %shard_map.258.refs_0_), channel_id=1, source_target_pairs={{0,8},{4,12},{8,0},{12,4},{16,24},{20,28},{24,16},{28,20},{1,9},{5... | collective-permute-start | bytes 3145736 | tf_op jit(solution)/shard_map/ppermute | solution.py:133
  466.9 47.5 %collective-permute-start.68 = (bf16[2,128,1024]{2,1,0:T(8,128)(2,1)}, bf16[2,128,1024]{2,1,0:T(8,128)(2,1)}, u32[]{:S(2)}, u32[]{:S(2)}) collective-permute-start(bf16[2,128,1024]{2,1,0:T(8,128)(2,1)} %get-tuple-element.537), channel_id=1, source_target_pairs={{0,8},{4,12},{8,0},{12,4},{16,24},{20,28},{24,16},{28,20},{1,9},{5... | collective-permute-start | bytes 1572872 | tf_op jit(solution)/shard_map/ppermute | solution.py:133
  468.9 45.5 %collective-permute-start.69 = (bf16[2,128,1024]{2,1,0:T(8,128)(2,1)}, bf16[2,128,1024]{2,1,0:T(8,128)(2,1)}, u32[]{:S(2)}, u32[]{:S(2)}) collective-permute-start(bf16[2,128,1024]{2,1,0:T(8,128)(2,1)} %get-tuple-element.535), channel_id=1, source_target_pairs={{0,16},{4,20},{8,24},{12,28},{16,0},{20,4},{24,8},{28,12},{1,17},{... | collective-permute-start | bytes 1572872 | tf_op jit(solution)/shard_map/ppermute | solution.py:133
  543.1 60.7 %collective-permute-start.73 = (bf16[128,1024]{1,0:T(8,128)(2,1)S(1)}, bf16[128,1024]{1,0:T(8,128)(2,1)S(1)}, u32[]{:S(2)}, u32[]{:S(2)}) collective-permute-start(bf16[128,1024]{1,0:T(8,128)(2,1)S(1)} %get-tuple-element.597), channel_id=1, source_target_pairs={{0,16},{4,20},{8,24},{12,28},{16,0},{20,4},{24,8},{28,12},{1,17},{... | collective-permute-start | bytes 786440 | tf_op jit(solution)/shard_map/ppermute | solution.py:133
  567.4 50.8 %collective-permute-start.78 = (bf16[2,2,2,32,2048]{4,3,1,0,2:T(8,128)(2,1)}, bf16[2,2,2,32,2048]{4,3,1,0,2:T(8,128)(2,1)}, u32[]{:S(2)}, u32[]{:S(2)}) collective-permute-start(bf16[2,2,2,32,2048]{4,3,1,0,2:T(8,128)(2,1)} %fusion.77), channel_id=1, source_target_pairs={{0,2},{1,3},{2,0},{3,1},{4,6},{5,7},{6,4},{7,5},{8,10},{9,11},{10,... | collective-permute-start | bytes 3145736 | tf_op jit(solution)/shard_map/ppermute | solution.py:133
  571.0 47.2 %collective-permute-start.79 = (bf16[2,2,2,32,2048]{4,3,1,0,2:T(8,128)(2,1)}, bf16[2,2,2,32,2048]{4,3,1,0,2:T(8,128)(2,1)}, u32[]{:S(2)}, u32[]{:S(2)}) collective-permute-start(bf16[2,2,2,32,2048]{4,3,1,0,2:T(8,128)(2,1)} %get-tuple-element.515), channel_id=1, source_target_pairs={{0,4},{4,0},{8,12},{12,8},{16,20},{20,16},{24,28},{28,24},{1,5},{5... | collective-permute-start | bytes 3145736 | tf_op jit(solution)/shard_map/ppermute | solution.py:133
  620.9 49.3 %collective-permute-start.85 = (bf16[2,128,1024]{2,1,0:T(8,128)(2,1)}, bf16[2,128,1024]{2,1,0:T(8,128)(2,1)}, u32[]{:S(2)}, u32[]{:S(2)}) collective-permute-start(bf16[2,128,1024]{2,1,0:T(8,128)(2,1)} %get-tuple-element.574), channel_id=1, source_target_pairs={{0,8},{4,12},{8,0},{12,4},{16,24},{20,28},{24,16},{28,20},{1,9},{5... | collective-permute-start | bytes 1572872 | tf_op jit(solution)/shard_map/ppermute | solution.py:133
  623.8 54.5 %collective-permute-start.87 = (bf16[2,2,32,2048]{3,2,1,0:T(8,128)(2,1)}, bf16[2,2,32,2048]{3,2,1,0:T(8,128)(2,1)}, u32[]{:S(2)}, u32[]{:S(2)}) collective-permute-start(bf16[2,2,32,2048]{3,2,1,0:T(8,128)(2,1)} %get-tuple-element.571), channel_id=1, source_target_pairs={{0,4},{4,0},{8,12},{12,8},{16,20},{20,16},{24,28},{28,24},{1,5},{5... | collective-permute-start | bytes 1572872 | tf_op jit(solution)/shard_map/ppermute | solution.py:133
  627.6 50.6 %collective-permute-start.88 = (bf16[2,2,32,2048]{3,2,1,0:T(8,128)(2,1)}, bf16[2,2,32,2048]{3,2,1,0:T(8,128)(2,1)}, u32[]{:S(2)}, u32[]{:S(2)}) collective-permute-start(bf16[2,2,32,2048]{3,2,1,0:T(8,128)(2,1)} %get-tuple-element.569), channel_id=1, source_target_pairs={{0,2},{1,3},{2,0},{3,1},{4,6},{5,7},{6,4},{7,5},{8,10},{9,11},{10,... | collective-permute-start | bytes 1572872 | tf_op jit(solution)/shard_map/ppermute | solution.py:133
  690.0 38.9 %collective-permute-start.89 = (bf16[2,32,4096]{2,1,0:T(8,128)(2,1)}, bf16[2,32,4096]{2,1,0:T(8,128)(2,1)}, u32[]{:S(2)}, u32[]{:S(2)}) collective-permute-start(bf16[2,32,4096]{2,1,0:T(8,128)(2,1)} %get-tuple-element.568), channel_id=1, source_target_pairs={{0,8},{4,12},{8,0},{12,4},{16,24},{20,28},{24,16},{28,20},{1,9},{5... | collective-permute-start | bytes 1572872 | tf_op jit(solution)/shard_map/ppermute | solution.py:133
  782.5 65.3 %collective-permute-start.96 = (bf16[2,32,4096]{2,1,0:T(8,128)(2,1)}, bf16[2,32,4096]{2,1,0:T(8,128)(2,1)}, u32[]{:S(2)}, u32[]{:S(2)}) collective-permute-start(bf16[2,32,4096]{2,1,0:T(8,128)(2,1)} %get-tuple-element.562), channel_id=1, source_target_pairs={{0,8},{4,12},{8,0},{12,4},{16,24},{20,28},{24,16},{28,20},{1,9},{5... | collective-permute-start | bytes 1572872 | tf_op jit(solution)/shard_map/ppermute | solution.py:133
  787.1 49.9 %collective-permute-start.98 = (bf16[2,2,2,2,32,3072]{5,4,1,0,2,3:T(8,128)(2,1)}, bf16[2,2,2,2,32,3072]{5,4,1,0,2,3:T(8,128)(2,1)}, u32[]{:S(2)}, u32[]{:S(2)}) collective-permute-start(bf16[2,2,2,2,32,3072]{5,4,1,0,2,3:T(8,128)(2,1)} %bitcast.576), channel_id=1, source_target_pairs={{0,1},{1,0},{2,3},{3,2},{4,5},{5,4},{6,7},{7,6},{8,9},{9,8},{10,11... | collective-permute-start | bytes 9437192 | tf_op jit(solution)/shard_map/ppermute | solution.py:133
  796.5 43.6 %collective-permute-start.101 = (bf16[2,2,2,2,128,1024]{5,4,1,0,2,3:T(8,128)(2,1)}, bf16[2,2,2,2,128,1024]{5,4,1,0,2,3:T(8,128)(2,1)}, u32[]{:S(2)}, u32[]{:S(2)}) collective-permute-start(bf16[2,2,2,2,128,1024]{5,4,1,0,2,3:T(8,128)(2,1)} %bitcast.568), channel_id=1, source_target_pairs={{0,1},{1,0},{2,3},{3,2},{4,5},{5,4},{6,7},{7,6},{8,9},{9,8},{10,11... | collective-permute-start | bytes 12582920 | tf_op jit(solution)/shard_map/ppermute | solution.py:133
  843.0 44.7 %collective-permute-start.102 = (bf16[2,2,2,128,512]{4,3,1,0,2:T(8,128)(2,1)S(1)}, bf16[2,2,2,128,512]{4,3,1,0,2:T(8,128)(2,1)S(1)}, u32[]{:S(2)}, u32[]{:S(2)}) collective-permute-start(bf16[2,2,2,128,512]{4,3,1,0,2:T(8,128)(2,1)S(1)} %fusion.79), channel_id=1, source_target_pairs={{0,2},{1,3},{2,0},{3,1},{4,6},{5,7},{6,4},{7,5},{8,10},{9,11},{10,... | collective-permute-start | bytes 3145736 | tf_op jit(solution)/shard_map/ppermute | solution.py:133
  845.1 42.5 %collective-permute-start.103 = (bf16[2,2,2,128,512]{4,3,1,0,2:T(8,128)(2,1)S(1)}, bf16[2,2,2,128,512]{4,3,1,0,2:T(8,128)(2,1)S(1)}, u32[]{:S(2)}, u32[]{:S(2)}) collective-permute-start(bf16[2,2,2,128,512]{4,3,1,0,2:T(8,128)(2,1)S(1)} %get-tuple-element.503), channel_id=1, source_target_pairs={{0,4},{4,0},{8,12},{12,8},{16,20},{20,16},{24,28},{28,24},{1,5},{5... | collective-permute-start | bytes 3145736 | tf_op jit(solution)/shard_map/ppermute | solution.py:133
  846.7 40.9 %collective-permute-start.100 = (bf16[2,2,2,32,1536]{4,3,1,0,2:T(8,128)(2,1)S(1)}, bf16[2,2,2,32,1536]{4,3,1,0,2:T(8,128)(2,1)S(1)}, u32[]{:S(2)}, u32[]{:S(2)}) collective-permute-start(bf16[2,2,2,32,1536]{4,3,1,0,2:T(8,128)(2,1)S(1)} %get-tuple-element.529), channel_id=1, source_target_pairs={{0,4},{4,0},{8,12},{12,8},{16,20},{20,16},{24,28},{28,24},{1,5},{5... | collective-permute-start | bytes 2359304 | tf_op jit(solution)/shard_map/ppermute | solution.py:133
  896.8 35.4 %collective-permute-start.104 = (bf16[2,2,32,1536]{3,2,1,0:T(8,128)(2,1)S(1)}, bf16[2,2,32,1536]{3,2,1,0:T(8,128)(2,1)S(1)}, u32[]{:S(2)}, u32[]{:S(2)}) collective-permute-start(bf16[2,2,32,1536]{3,2,1,0:T(8,128)(2,1)S(1)} %get-tuple-element.585), channel_id=1, source_target_pairs={{0,4},{4,0},{8,12},{12,8},{16,20},{20,16},{24,28},{28,24},{1,5},{5... | collective-permute-start | bytes 1179656 | tf_op jit(solution)/shard_map/ppermute | solution.py:133
  (293 other events, 4259.7 us)

commit v4 on v3

--- a/solution.py
+++ b/solution.py
@@ -82,11 +82,11 @@
 Z1, Z0, X, Y, C = range(5)
 
 
-def local_copies(plan, inputs, outputs):
+def local_copies(plan, inputs, outputs, after=()):
     count = len(inputs)
 
     def kernel(*refs):
-        sources, targets, sem = refs[:count], refs[count:-1], refs[-1]
+        sources, targets, sem = refs[:count], refs[count + len(after) : -1], refs[-1]
         dp, head = lax.axis_index("dp"), lax.axis_index("head")
         where = (dp // 4, dp // 2 % 2, dp % 2, head // 2, head % 2)
         copies = []
@@ -100,12 +100,12 @@
     results = pl.pallas_call(
         kernel,
         out_shape=[jax.ShapeDtypeStruct(shape, inputs[0].dtype) for shape in outputs],
-        in_specs=[ANY] * count,
+        in_specs=[ANY] * (count + len(after)),
         out_specs=[VMEM] * len(outputs),
         scratch_shapes=[pltpu.SemaphoreType.DMA((16,))],
         cost_estimate=pl.CostEstimate(flops=0, bytes_accessed=2 * size, transcendentals=0),
-        compiler_params=pltpu.CompilerParams(vmem_limit_bytes=16 << 20),
-    )(*inputs)
+        compiler_params=pltpu.CompilerParams(vmem_limit_bytes=size + (1 << 20)),
+    )(*inputs, *after)
     return list(results)
 
 
@@ -153,6 +153,20 @@
         return values
 
 
+class VectorGathering:
+    def __init__(self, cube, shard, order):
+        self.cube, self.order, self.held = cube, list(order), []
+        self.state = [shard]
+
+    def step(self, count=1):
+        for _ in range(min(count, len(self.order))):
+            at = self.order.pop(0)
+            place = sum(other < at for other in self.held)
+            (values,) = self.state
+            self.state = [self.cube.join(values, self.cube.swap(values, at), at, place)]
+            self.held.append(at)
+
+
 class HeadGathering:
     def __init__(self, cube, shard):
         self.cube = cube
@@ -199,79 +213,6 @@
 
     (whole,) = local_copies(plan, parts, [(2, 2, 2, rows, 2 * half)])
     return whole.reshape(8 * rows, 2 * half)
-
-
-class Gathering:
-    def __init__(self, cube, shard):
-        self.cube = cube
-        self.rows, self.columns = shard.shape
-        self.state = [shard]
-
-    def step(self, phase):
-        cube, state, rows = self.cube, self.state, self.rows
-        half = self.columns // 2
-        if not cube.tuned:
-            if phase == "z":
-                self.state = [lax.all_gather(state[0], AXES, axis=0, tiled=True)]
-            return
-        if phase == "z":
-            (own,) = state
-
-            def plan(where, sources, targets):
-                for by in range(2):
-                    yield sources[by], targets[0].at[flip(where[Z1], by)]
-
-            (pair,) = local_copies(plan, [own, cube.swap(own, Z1)], [(2,) + own.shape])
-            self.state = [pair, cube.swap(pair, Z0)]
-        if phase == "m":
-
-            def plan(where, sources, targets):
-                for by in range(2):
-                    for side in range(2):
-                        columns = pl.ds(side * half, half)
-                        yield (
-                            sources[by].at[:, :, columns],
-                            targets[side].at[:, flip(where[Z0], by)],
-                        )
-
-            left, right = local_copies(plan, state, [(2, 2, rows, half)] * 2)
-            self.state = [left, cube.swap(left, X), right, cube.swap(right, Y)]
-        if phase == "n":
-
-            def plan(where, sources, targets):
-                for by in range(2):
-                    yield sources[by], targets[0].at[:, :, flip(where[X], by)]
-                    yield sources[2 + by], targets[1].at[:, :, flip(where[Y], by)]
-
-            left, right = local_copies(plan, state, [(2, 2, 2, rows, half)] * 2)
-            self.state = [left, cube.swap(left, Y), right, cube.swap(right, X)]
-        if phase == "c":
-
-            def plan(where, sources, targets):
-                for by in range(2):
-                    yield (
-                        sources[by],
-                        targets[0].at[:, :, :, flip(where[Y], by), :, pl.ds(0, half)],
-                    )
-                    yield (
-                        sources[2 + by],
-                        targets[0].at[:, :, flip(where[X], by), :, :, pl.ds(half, half)],
-                    )
-
-            (most,) = local_copies(plan, state, [(2, 2, 2, 2, rows, self.columns)])
-
-            def plan_whole(where, sources, targets):
-                for by in range(2):
-                    yield sources[by], targets[0].at[:, :, :, :, flip(where[C], by)]
-
-            (whole,) = local_copies(
-                plan_whole, [most, cube.swap(most, C)], [(2, 2, 2, 2, 2, rows, self.columns)]
-            )
-            self.state = [whole.reshape(32 * rows, self.columns)]
-
-    @property
-    def whole(self):
-        return self.state[0]
 
 
 def pick_of(values, index, place):
@@ -324,57 +265,310 @@
         return self.part(None, True)
 
 
-class Scattering:
-    def __init__(self, cube, values, rows):
+class Gather:
+    def __init__(self, cube, pieces):
         self.cube = cube
-        self.phase = 0
-        self.state = [values.reshape((2,) * len(cube.bits) + (rows, -1)) if cube.tuned else values]
-
-    def both(self, keep, got, at, place, columns=slice(None)):
-        halves = []
-        for index in (1 - self.cube.mine(at), self.cube.mine(at)):
-            first = pick_of(keep[..., columns], index, place).astype(jnp.float32)
-            second = pick_of(got[..., columns], index, place).astype(jnp.float32)
-            halves.append((first + second).astype(keep.dtype))
-        return halves
-
-    def step(self, count=1):
-        cube = self.cube
-        for _ in range(count if cube.tuned else 0):
-            if self.phase == 0:
-                (values,) = self.state
-                send = pick_of(values, 1 - cube.mine(C), 4)
-                self.state = [values, cube.swap(send, C)]
-            if self.phase == 1:
-                values, got = self.state
-                keep = pick_of(values, cube.mine(C), 4)
-                half = keep.shape[-1] // 2
-                send_a, keep_a = self.both(keep, got, Y, 3, slice(0, half))
-                send_b, keep_b = self.both(keep, got, X, 2, slice(half, None))
-                self.state = [keep_a, cube.swap(send_a, Y), keep_b, cube.swap(send_b, X)]
-            if self.phase == 2:
-                keep_a, got_a, keep_b, got_b = self.state
-                send_a, keep_a = self.both(keep_a, got_a, X, 2)
-                send_b, keep_b = self.both(keep_b, got_b, Y, 2)
-                self.state = [keep_a, cube.swap(send_a, X), keep_b, cube.swap(send_b, Y)]
-            if self.phase == 3:
-                keep_a, got_a, keep_b, got_b = self.state
-                keep = jnp.concatenate([keep_a, keep_b], axis=-1)
-                got = jnp.concatenate([got_a, got_b], axis=-1)
-                send, keep = self.both(keep, got, Z0, 1)
-                self.state = [keep, cube.swap(send, Z0)]
-            if self.phase == 4:
-                send, keep = self.both(*self.state, Z1, 0)
-                self.state = [keep, cube.swap(send, Z1)]
-            self.phase += 1
-
-    def result(self):
-        if not self.cube.tuned:
-            return lax.psum_scatter(self.state[0], AXES, scatter_dimension=0, tiled=True).astype(
-                jnp.float32
+        self.pieces = pieces
+        self.wholes = [None] * len(pieces)
+        if cube.tuned:
+            self.shards = [uniform_shard(kind, arrays) for kind, arrays in pieces]
+        self.state = {}
+
+    def stage(self, t):
+        cube, old, new = self.cube, self.state, {}
+        count = len(self.pieces)
+        live = lambda at: 0 <= at < count
+        if not cube.tuned:
+            if live(t - 1):
+                self.wholes[t - 1] = [
+                    lax.all_gather(array, AXES, axis=0, tiled=True)
+                    for array in self.pieces[t - 1][1]
+                ]
+            return
+        half = COLUMNS // 2
+        slots = 2 * live(t) + live(t + 1)
+        old_slots = 2 * live(t - 1) + live(t)
+        inputs, shapes, jobs = [], [], []
+
+        def give(name):
+            inputs.append(old[name])
+            return len(inputs) - 1
+
+        def make(shape):
+            shapes.append(shape)
+            return len(shapes) - 1
+
+        pair = None
+        if live(t + 2):
+            parts, pair = (give("z1s"), give("z1g")), make((2, ROWS, COLUMNS))
+            jobs.append(lambda w, s, o, parts=parts, pair=pair: [
+                (s[parts[by]], o[pair].at[flip(w[Z1], by)]) for by in range(2)
+            ])
+        if slots:
+            x_out, y_out = (make((2, 2, slots, ROWS, half)) for _ in range(2))
+        if live(t):
+            xs, xg, ys, yg = (give(name) for name in ("xs", "xg", "ys", "yg"))
+            jobs.append(lambda w, s, o: [
+                pair_of
+                for by in range(2)
+                for pair_of in (
+                    (s[(xs, xg)[by]].at[:, :, old_slots - 1], o[y_out].at[:, :, flip(w[X], by)]),
+                    (s[(ys, yg)[by]].at[:, :, old_slots - 1], o[x_out].at[:, :, flip(w[Y], by)]),
+                )
+            ])
+        if live(t + 1):
+            zs, zg = give("z0s"), give("z0g")
+            jobs.append(lambda w, s, o: [
+                (
+                    s[(zs, zg)[by]].at[:, :, pl.ds(side * half, half)],
+                    o[(x_out, y_out)[side]].at[:, flip(w[Z0], by), slots - 1],
+                )
+                for by in range(2)
+                for side in range(2)
+            ])
+        if jobs:
+            made = local_copies(
+                lambda w, s, o: [each for job in jobs for each in job(w, s, o)], inputs, shapes
             )
-        keep, got = self.state
-        return keep.astype(jnp.float32) + got.astype(jnp.float32)
+            if slots:
+                new["xs"], new["ys"] = made[x_out], made[y_out]
+                new["xg"], new["yg"] = cube.swap(made[x_out], X), cube.swap(made[y_out], Y)
+            if pair is not None:
+                new["z0s"], new["z0g"] = made[pair], cube.swap(made[pair], Z0)
+        if live(t + 3):
+            new["z1s"] = self.shards[t + 3]
+            new["z1g"] = cube.swap(self.shards[t + 3], Z1)
+        if live(t - 1):
+
+            def plan(w, s, o):
+                for by in range(2):
+                    yield (
+                        s[by].at[:, :, pl.ds(0, 2)],
+                        o[0].at[:, :, :, flip(w[Y], by), :, pl.ds(0, half)],
+                    )
+                    yield (
+                        s[2 + by].at[:, :, pl.ds(0, 2)],
+                        o[0].at[:, :, flip(w[X], by), :, :, pl.ds(half, half)],
+                    )
+
+            (most,) = local_copies(
+                plan,
+                [old[name] for name in ("ys", "yg", "xs", "xg")],
+                [(2, 2, 2, 2, ROWS, COLUMNS)],
+                [new[name] for name in ("xs", "z0s") if name in new][:1],
+            )
+            got = cube.swap(most, C)
+            kind, arrays = self.pieces[t - 1]
+
+            def plan_whole(w, s, o):
+                for by in range(2):
+                    for at, rows, columns in tiles_of(kind, arrays):
+                        yield (
+                            s[by].at[:, :, :, :, :, columns],
+                            o[at].at[:, :, :, :, flip(w[C], by), rows],
+                        )
+
+            made = local_copies(
+                plan_whole, [most, got], [(2, 2, 2, 2, 2) + array.shape for array in arrays]
+            )
+            self.wholes[t - 1] = [
+                whole.reshape(-1, array.shape[1]) for whole, array in zip(made, arrays)
+            ]
+        self.state = new
+
+
+ROWS, COLUMNS = 32, 4096
+
+
+def uniform_shard(kind, arrays):
+    if kind == "tall":
+        return jnp.concatenate([arrays[0][at : at + ROWS] for at in range(0, 4 * ROWS, ROWS)], axis=1)
+    spare = COLUMNS - sum(array.shape[1] for array in arrays)
+    extra = [arrays[0][:, :spare]] if spare else []
+    return jnp.concatenate(arrays + extra, axis=1) if len(arrays) > 1 else arrays[0]
+
+
+def tiles_of(kind, arrays):
+    if kind == "tall":
+        width = arrays[0].shape[1]
+        for at in range(4):
+            yield 0, pl.ds(at * ROWS, ROWS), pl.ds(at * width, width)
+    else:
+        start = 0
+        for at, array in enumerate(arrays):
+            yield at, pl.ds(0, ROWS), pl.ds(start, array.shape[1])
+            start += array.shape[1]
+
+
+def added(out, out_at, first, first_at, second, second_at):
+    total = first[first_at].astype(jnp.float32) + second[second_at].astype(jnp.float32)
+    out[out_at] = total.astype(out.dtype)
+
+
+class Scatter:
+    def __init__(self, cube):
+        self.cube = cube
+        self.state = {}
+        self.results = []
+
+    def stage(self, piece=None):
+        cube, old, new = self.cube, self.state, {}
+        if not cube.tuned:
+            if piece is not None:
+                self.results.append(
+                    [
+                        lax.psum_scatter(grad, AXES, scatter_dimension=0, tiled=True).astype(
+                            jnp.float32
+                        )
+                        for grad in piece[2]
+                    ]
+                )
+            return
+        half = COLUMNS // 2
+        inputs, shapes, jobs = [], [], []
+
+        def give(name):
+            inputs.append(old[name])
+            return len(inputs) - 1
+
+        def make(sent, *shape):
+            shapes.append((sent, shape))
+            return len(shapes) - 1
+
+        left, right = slice(0, half), slice(half, COLUMNS)
+        has_n, has_m = "ck" in old, "ak" in old
+        slots = 2 * has_n + has_m
+        if slots:
+            x_out, y_out = (make(1, 2, 2, slots, ROWS, half) for _ in range(2))
+        corners = [(a, b) for a in range(2) for b in range(2)]
+        if has_n:
+            ck, cg = give("ck"), give("cg")
+            a_out, b_out = (make(0, 2, 2, 2, ROWS, half) for _ in range(2))
+
+            def job_n(w, s, o, sent):
+                y, x = flip(w[Y], sent), flip(w[X], sent)
+                for a, b in corners:
+                    for k in range(2):
+                        from_a = (a, b, k, y, slice(None), left)
+                        from_b = (a, b, x, k, slice(None), right)
+                        out_a, out_b = o[y_out if sent else a_out], o[x_out if sent else b_out]
+                        added(out_a, (a, b, k), s[ck], from_a, s[cg], from_a)
+                        added(out_b, (a, b, k), s[ck], from_b, s[cg], from_b)
+
+            jobs.append(job_n)
+        if has_m:
+            ak, bk, xg, yg = (give(name) for name in ("ak", "bk", "xg", "yg"))
+            a4_out, b4_out = (make(0, 2, 2, ROWS, half) for _ in range(2))
+
+            def job_m(w, s, o, sent):
+                y, x = flip(w[Y], sent), flip(w[X], sent)
+                for a, b in corners:
+                    place = (a, b, slots - 1) if sent else (a, b)
+                    added(o[x_out if sent else a4_out], place, s[ak], (a, b, x), s[yg], (a, b, x))
+                    added(o[y_out if sent else b4_out], place, s[bk], (a, b, y), s[xg], (a, b, y))
+
+            jobs.append(job_m)
+        if "a4k" in old:
+            a4k, b4k = give("a4k"), give("b4k")
+            x4g, y4g = (xg, yg) if has_m else (give("xg"), give("yg"))
+            last = old["xg"].shape[2] - 1
+            z_out, zk_out = (make(sent, 2, ROWS, COLUMNS) for sent in (1, 0))
+
+            def job_z(w, s, o, sent):
+                z = flip(w[Z0], sent)
+                out = o[z_out if sent else zk_out]
+                for a in range(2):
+                    added(out, (a, slice(None), left), s[a4k], (a, z), s[x4g], (a, z, last))
+                    added(out, (a, slice(None), right), s[b4k], (a, z), s[y4g], (a, z, last))
+
+            jobs.append(job_z)
+        if "zk" in old:
+            zk, zg = give("zk"), give("zg")
+            f_out, fk_out = (make(sent, ROWS, COLUMNS) for sent in (1, 0))
+
+            def job_f(w, s, o, sent):
+                z = flip(w[Z1], sent)
+                added(o[f_out if sent else fk_out], slice(None), s[zk], z, s[zg], z)
+
+            jobs.append(job_f)
+        if "fk" in old:
+            kind, arrays = self.queue.pop(0)
+            total = old["fk"].astype(jnp.float32) + old["fg"].astype(jnp.float32)
+            self.results.append(split_shard(kind, arrays, total))
+        made = {}
+        for sent in (1, 0) if jobs else ():
+            chosen = [at for at, (side, shape) in enumerate(shapes) if side == sent]
+            after = [made[x_out if slots else z_out if "a4k" in old else f_out]] if made else []
+
+            def kernel(*refs):
+                dp, head = lax.axis_index("dp"), lax.axis_index("head")
+                where = (dp // 4, dp // 2 % 2, dp % 2, head // 2, head % 2)
+                outs = dict(zip(chosen, refs[len(inputs) + len(after) :]))
+                for job in jobs:
+                    job(where, refs[: len(inputs)], outs, sent)
+
+            size = sum(math.prod(shapes[at][1]) for at in chosen)
+            results = pl.pallas_call(
+                kernel,
+                out_shape=[jax.ShapeDtypeStruct(shapes[at][1], jnp.bfloat16) for at in chosen],
+                in_specs=[VMEM] * len(inputs) + [ANY] * len(after),
+                out_specs=[VMEM] * len(chosen),
+                cost_estimate=pl.CostEstimate(
+                    flops=size, bytes_accessed=6 * size, transcendentals=0
+                ),
+                compiler_params=pltpu.CompilerParams(
+                    vmem_limit_bytes=2 * size + 2 * sum(each.size for each in inputs) + (1 << 20)
+                ),
+            )(*inputs, *after)
+            made.update(zip(chosen, results))
+        if jobs:
+            if slots:
+                new["xg"], new["yg"] = cube.swap(made[x_out], X), cube.swap(made[y_out], Y)
+            if has_n:
+                new["ak"], new["bk"] = made[a_out], made[b_out]
+            if has_m:
+                new["a4k"], new["b4k"] = made[a4_out], made[b4_out]
+            if "a4k" in old:
+                new["zk"], new["zg"] = made[zk_out], cube.swap(made[z_out], Z0)
+            if "zk" in old:
+                new["fk"], new["fg"] = made[fk_out], cube.swap(made[f_out], Z1)
+        if piece is not None:
+            kind, arrays, grads = piece
+            self.queue = getattr(self, "queue", []) + [(kind, arrays)]
+            bits = [
+                grad.reshape((2, 2, 2, 2, 2) + array.shape) for grad, array in zip(grads, arrays)
+            ]
+
+            def plan(w, s, o):
+                for sent in range(2):
+                    for at, rows, columns in tiles_of(kind, arrays):
+                        yield (
+                            s[at].at[:, :, :, :, flip(w[C], sent), rows],
+                            o[sent].at[:, :, :, :, :, columns],
+                        )
+                    spare = COLUMNS - sum(array.size for array in arrays) // ROWS
+                    if spare:
+                        yield (
+                            s[0].at[:, :, :, :, flip(w[C], sent), :, pl.ds(0, spare)],
+                            o[sent].at[:, :, :, :, :, pl.ds(COLUMNS - spare, spare)],
+                        )
+
+            keep, send = local_copies(
+                plan, bits, [(2, 2, 2, 2, ROWS, COLUMNS)] * 2, [made[x_out]] if slots else []
+            )
+            new["ck"], new["cg"] = keep, cube.swap(send, C)
+        self.state = new
+
+
+def split_shard(kind, arrays, total):
+    if kind == "tall":
+        width = arrays[0].shape[1]
+        return [jnp.concatenate([total[:, at * width : (at + 1) * width] for at in range(4)], axis=0)]
+    parts, start = [], 0
+    for array in arrays:
+        parts.append(total[:, start : start + array.shape[1]])
+        start += array.shape[1]
+    return parts
 
 
 class HeadScattering:
@@ -478,7 +672,7 @@
         cost_estimate=pl.CostEstimate(
             flops=80 * rows * D, bytes_accessed=16 * rows * D, transcendentals=rows * D
         ),
-        compiler_params=pltpu.CompilerParams(vmem_limit_bytes=16 << 20),
+        compiler_params=pltpu.CompilerParams(vmem_limit_bytes=8 << 20),
     )(expanded, expanded, valid, taps)
 
 
@@ -561,7 +755,7 @@
         cost_estimate=pl.CostEstimate(
             flops=160 * rows * D, bytes_accessed=20 * rows * D, transcendentals=rows * D
         ),
-        compiler_params=pltpu.CompilerParams(vmem_limit_bytes=16 << 20),
+        compiler_params=pltpu.CompilerParams(vmem_limit_bytes=8 << 20),
     )(expanded, expanded, valid, taps, conv_out, grads, vectors)
 
 
@@ -598,18 +792,17 @@
     ff = ffn_inner.shape[2]
     all_bits = list(range(len(cube.bits)))
 
-    mid = jnp.concatenate([attn_proj, conv_expand, conv_proj], axis=1)
-    pieces = [
-        Gathering(cube, shard)
-        for shard in (
-            ffn_inner[0],
-            ffn_outer[0],
-            attn_qkv,
-            mid,
-            ffn_inner[1],
-            ffn_outer[1],
-        )
-    ]
+    rows_in = Gather(
+        cube,
+        [
+            ("wide", [ffn_inner[0]]),
+            ("tall", [ffn_outer[0]]),
+            ("wide", [attn_qkv, attn_proj]),
+            ("wide", [conv_expand, conv_proj]),
+            ("wide", [ffn_inner[1]]),
+            ("tall", [ffn_outer[1]]),
+        ],
+    )
     head_half = head_proj.shape[1] // 2
     heads = [
         HeadGathering(cube, head_proj[:, :head_half]),
@@ -642,51 +835,49 @@
     vocab_cols = head_proj.shape[1]
 
     loss_scale = jnp.float32(devices * UTT_DEV * NSPAN * SPAN)
-    vectors = cube.gather(jnp.concatenate([norm_gains, conv_depth], axis=0), all_bits)
-    vectors = jnp.moveaxis(vectors.reshape((devices,) + vectors.shape[-2:]), 0, 1).reshape(-1, D)
+    hops = [C, Z1, Z0, X, Y] if cube.tuned else all_bits
+    vector_in = VectorGathering(cube, jnp.concatenate([norm_gains, conv_depth], axis=0), hops)
+    vector_in.step(2)
     group_codes = cube.gather(picked_codes, head_order).reshape(group * slots)
-    pieces[0].step("z")
+    rows_in.stage(-3)
     heads[0].step("x")
     heads[1].step("x")
-    fence([pieces[0], *heads], loss_scale)
-    pieces[0].step("m")
-    pieces[1].step("z")
+    group_codes = fence([rows_in, vector_in, *heads], group_codes)
+
+    rows_in.stage(-2)
+    vector_in.step()
+    fence([rows_in, vector_in], loss_scale)
+
+    rows_in.stage(-1)
+    vector_in.step()
     inputs = frames.astype(jnp.float32)
-    fence(pieces[:2], loss_scale)
-
-    pieces[0].step("n")
-    pieces[1].step("m")
-    pieces[2].step("z")
-    vectors, group_codes = fence(pieces[:3], vectors, group_codes)
+    fence([rows_in, vector_in], loss_scale)
+
+    rows_in.stage(0)
+    vector_in.step(len(hops))
+    fence([rows_in, vector_in], loss_scale)
+    (vectors,) = vector_in.state
+    vectors = jnp.moveaxis(vectors.reshape((devices,) + vectors.shape[-2:]), 0, 1).reshape(-1, D)
     gain_f, depth_f = vectors[:6].astype(jnp.float32), vectors[6:].astype(jnp.float32)
     norm_first = lowered(layer_norm(inputs, gain_f[0]))
     group_live = (group_codes >= 0).astype(jnp.float32)
     local_codes = group_codes - lax.axis_index("head") * vocab_cols
 
-    pieces[0].step("c")
-    pieces[1].step("n")
-    pieces[2].step("m")
-    pieces[3].step("z")
-    inner_0 = pieces[0].whole
+    rows_in.stage(1)
+    (inner_0,) = rows_in.wholes[0]
     pre_first = matmul(norm_first, inner_0)
     act_first = lowered(jax.nn.silu(pre_first))
-    pre_first, act_first = fence(pieces[:4], pre_first, act_first)
-
-    pieces[1].step("c")
-    pieces[2].step("n")
-    pieces[3].step("m")
-    pieces[4].step("z")
-    outer_0 = pieces[1].whole
+    pre_first, act_first = fence([rows_in], pre_first, act_first)
+
+    rows_in.stage(2)
+    (outer_0,) = rows_in.wholes[1]
     after_first = inputs + 0.5 * matmul(act_first, outer_0)
     norm_attn = lowered(layer_norm(after_first, gain_f[1]))
-    after_first, norm_attn = fence(pieces[1:5], after_first, norm_attn)
-
-    pieces[2].step("c")
-    pieces[3].step("n")
-    pieces[4].step("m")
-    pieces[5].step("z")
+    after_first, norm_attn = fence([rows_in], after_first, norm_attn)
+
+    rows_in.stage(3)
     heads[0].step("far")
-    mix_weight = pieces[2].whole
+    mix_weight, proj_weight = rows_in.wholes[2]
     mixed = matmul(norm_attn, mix_weight)
     mixed = mixed.reshape(UTT_DEV, SEQ, 3, H, HD)
     queries = lowered(rotate(mixed[:, :, 0], cosine, sine_table))
@@ -713,33 +904,34 @@
 
     attended, log_totals = attend_one(queries[0], key_rows[0], value_rows[0], valid_mat[0])
     attended_lo = lowered(attended.reshape(row_total, D))
-    attended_lo, queries, key_rows, value_rows, log_totals = fence(
-        [*pieces[2:6], heads[0]], attended_lo, queries, key_rows, value_rows, log_totals
-    )
-
-    pieces[3].step("c")
-    pieces[4].step("n")
-    pieces[5].step("m")
+    after_attention = after_first + matmul(attended_lo, proj_weight)
+    norm_conv = lowered(layer_norm(after_attention, gain_f[2]))
+    after_attention, norm_conv, attended_lo, queries, key_rows, value_rows, log_totals = fence(
+        [rows_in, heads[0]],
+        after_attention,
+        norm_conv,
+        attended_lo,
+        queries,
+        key_rows,
+        value_rows,
+        log_totals,
+    )
+
+    rows_in.stage(4)
     heads[0].step("near")
     heads[1].step("far")
-    mid_weight = pieces[3].whole
-    proj_weight, conv_weight = mid_weight[:, :D], mid_weight[:, 3 * D :]
-    expand_weight = mid_weight[:, D : 3 * D]
-    after_attention = after_first + matmul(attended_lo, proj_weight)
-    norm_conv = lowered(layer_norm(after_attention, gain_f[2]))
+    expand_weight, conv_weight = rows_in.wholes[3]
     expanded = matmul(norm_conv, expand_weight)
-
     conv_out, conv_sums = conv_forward(expanded, valid_rows[:, None], depth_f)
     valid_total = jnp.broadcast_to(jnp.sum(valid_rows), (1, D))
     sums = cube.total(jnp.concatenate([conv_sums[:2], valid_total], axis=0))
     sums, conv_out, after_attention, expanded, norm_conv = fence(
-        [*pieces[3:6], *heads], sums, conv_out, after_attention, expanded, norm_conv
-    )
-
-    pieces[4].step("c")
-    pieces[5].step("n")
+        [rows_in, *heads], sums, conv_out, after_attention, expanded, norm_conv
+    )
+
+    rows_in.stage(5)
     heads[1].step("near")
-    inner_1 = pieces[4].whole
+    (inner_1,) = rows_in.wholes[4]
     frame_count = sums[2, 0]
     channel_mean = sums[0] / frame_count
     variance = sums[1] / frame_count - channel_mean * channel_mean
@@ -752,11 +944,11 @@
     pre_second = matmul(norm_second, inner_1)
     act_second = lowered(jax.nn.silu(pre_second))
     after_conv, norm_second, pre_second, act_second, swish_lo = fence(
-        [*pieces[4:6], *heads], after_conv, norm_second, pre_second, act_second, swish_lo
-    )
-
-    pieces[5].step("c")
-    outer_1 = pieces[5].whole
+        [rows_in, *heads], after_conv, norm_second, pre_second, act_second, swish_lo
+    )
+
+    rows_in.stage(6)
+    (outer_1,) = rows_in.wholes[5]
     head_cols = joined_heads(cube, heads)
     after_second = after_conv + 0.5 * matmul(act_second, outer_1)
     output_lo = lowered(layer_norm(after_second, gain_f[5]))
@@ -790,26 +982,26 @@
     def outer_back(grad_in, act_lo):
         grad_out_lo = lowered(0.5 * grad_in)
         weight_grad = lowered(matmul_tn(act_lo, grad_out_lo))
-        return grad_out_lo, Scattering(cube, weight_grad, ffn_outer.shape[1])
+        return grad_out_lo, ("tall", [ffn_outer[0]], [weight_grad])
 
     def inner_back(grad_out_lo, normed_lo, pre_act, inner_weight, outer_weight):
         grad_pre = lowered(silu_back(pre_act, matmul_nt(grad_out_lo, outer_weight)))
         weight_grad = lowered(matmul_tn(normed_lo, grad_pre))
         below = matmul_nt(grad_pre, inner_weight)
-        return below, Scattering(cube, weight_grad, ffn_inner.shape[1])
-
+        return below, ("wide", [ffn_inner[0]], [weight_grad])
+
+    rows_out = Scatter(cube)
     grad_second, gain_grad_final = norm_back(after_second, gain_f[5], grad_output)
-    grad_out_lo, outer_flow_1 = outer_back(grad_second, act_second)
-    grad_second, grad_out_lo = fence([head_flow, outer_flow_1], grad_second, grad_out_lo)
+    grad_out_lo, piece = outer_back(grad_second, act_second)
+    grad_second, grad_out_lo, piece[2][0] = fence(
+        [head_flow], grad_second, grad_out_lo, piece[2][0]
+    )
 
     head_flow.step()
-    outer_flow_1.step(2)
-    below_second, inner_flow_1 = inner_back(grad_out_lo, norm_second, pre_second, inner_1, outer_1)
-    below_second = fence([head_flow, outer_flow_1, inner_flow_1], below_second)
-
-    head_flow.step()
-    outer_flow_1.step()
-    inner_flow_1.step(2)
+    rows_out.stage(piece)
+    below_second, piece = inner_back(grad_out_lo, norm_second, pre_second, inner_1, outer_1)
+    below_second, piece[2][0] = fence([head_flow, rows_out], below_second, piece[2][0])
+
     norm_part, gain_grad_second = norm_back(after_conv, gain_f[4], below_second)
     grad_conv_res = grad_second + norm_part
     conv_res_lo = lowered(grad_conv_res)
@@ -827,15 +1019,15 @@
     )
     conv_proj_grad = lowered(matmul_tn(swish_lo, conv_res_lo))
     back_sums, grad_normalized, grad_conv_res, conv_proj_grad = fence(
-        [head_flow, outer_flow_1, inner_flow_1],
+        [],
         back_sums,
         grad_normalized,
         grad_conv_res,
         conv_proj_grad,
     )
 
-    outer_flow_1.step(2)
-    inner_flow_1.step()
+    head_flow.step()
+    rows_out.stage(piece)
     sum_plain, sum_scaled = back_sums[0], back_sums[1]
     loss = back_sums[2, 0] / loss_scale
     grad_variance = -0.5 * inverse * inverse * sum_scaled
@@ -848,29 +1040,16 @@
         expanded, valid_rows[:, None], depth_f, conv_out, grad_normalized, back_vectors
     )
     grad_expanded = jnp.concatenate([grad_lead, grad_gate], axis=1)
+    expand_grad = lowered(matmul_tn(norm_conv, grad_expanded))
+    grad_expanded, expand_grad = fence([rows_out, head_flow], grad_expanded, expand_grad)
+
+    rows_out.stage(("wide", [conv_expand, conv_proj], [expand_grad, conv_proj_grad]))
     norm_part, gain_grad_conv = norm_back(
         after_attention, gain_f[2], matmul_nt(grad_expanded, expand_weight)
     )
     grad_attn_res = grad_conv_res + norm_part
     attn_res_lo = lowered(grad_attn_res)
-    mid_flow = Scattering(
-        cube,
-        jnp.concatenate(
-            [
-                lowered(matmul_tn(attended_lo, attn_res_lo)),
-                lowered(matmul_tn(norm_conv, grad_expanded)),
-                conv_proj_grad,
-            ],
-            axis=1,
-        ),
-        attn_proj.shape[0],
-    )
-    grad_attn_res, attn_res_lo = fence(
-        [outer_flow_1, inner_flow_1, mid_flow], grad_attn_res, attn_res_lo
-    )
-
-    inner_flow_1.step(2)
-    mid_flow.step(2)
+    proj_grad = lowered(matmul_tn(attended_lo, attn_res_lo))
     grad_attended = lowered(matmul_nt(attn_res_lo, proj_weight)).reshape(UTT_DEV, SEQ, H, HD)
 
     def attend_back(query_one, key_one, value_one, key_ok, log_total, grad_one):
@@ -905,21 +1084,23 @@
         ],
         axis=1,
     )
-    grad_mixed = fence([inner_flow_1, mid_flow], grad_mixed)
-
-    mid_flow.step()
-    mix_flow = Scattering(cube, lowered(matmul_tn(norm_attn, grad_mixed)), attn_qkv.shape[0])
+    grad_mixed, proj_grad, grad_attn_res = fence([rows_out], grad_mixed, proj_grad, grad_attn_res)
+
+    rows_out.stage()
+    mix_grad = lowered(matmul_tn(norm_attn, grad_mixed))
     norm_part, gain_grad_attn = norm_back(after_first, gain_f[1], matmul_nt(grad_mixed, mix_weight))
     grad_first_res = grad_attn_res + norm_part
-    grad_out_lo, outer_flow_0 = outer_back(grad_first_res, act_first)
-    grad_first_res, grad_out_lo = fence(
-        [mid_flow, mix_flow, outer_flow_0], grad_first_res, grad_out_lo
-    )
-
-    mid_flow.step(2)
-    mix_flow.step(2)
-    outer_flow_0.step(2)
-    below_first, inner_flow_0 = inner_back(grad_out_lo, norm_first, pre_first, inner_0, outer_0)
+    grad_first_res, mix_grad = fence([rows_out], grad_first_res, mix_grad)
+
+    rows_out.stage(("wide", [attn_qkv, attn_proj], [mix_grad, proj_grad]))
+    grad_out_lo, piece = outer_back(grad_first_res, act_first)
+    grad_out_lo, piece[2][0] = fence([rows_out], grad_out_lo, piece[2][0])
+
+    rows_out.stage(piece)
+    below_first, piece = inner_back(grad_out_lo, norm_first, pre_first, inner_0, outer_0)
+    below_first, piece[2][0] = fence([rows_out], below_first, piece[2][0])
+
+    rows_out.stage(piece)
     norm_part, gain_grad_first = norm_back(inputs, gain_f[0], below_first)
     input_grad = grad_first_res + norm_part
     vector_grad = jnp.concatenate(
@@ -941,36 +1122,40 @@
     )
     vector_grad = jnp.moveaxis(vector_grad.reshape(vector_grad.shape[0], devices, -1), 1, 0)
     vector_flow = Summing(
-        cube, vector_grad.reshape((2,) * len(cube.bits) + vector_grad.shape[1:]), all_bits[::-1]
-    )
-    input_grad = fence([mid_flow, mix_flow, outer_flow_0, inner_flow_0, vector_flow], input_grad)
-
-    mix_flow.step()
-    outer_flow_0.step()
-    inner_flow_0.step(2)
-    for _ in all_bits:
+        cube, vector_grad.reshape((2,) * len(cube.bits) + vector_grad.shape[1:]), hops
+    )
+    vector_flow.step()
+    vector_flow.step()
+    input_grad = fence([rows_out, vector_flow], input_grad)
+
+    for _ in range(4):
+        rows_out.stage()
+        if vector_flow.order:
+            vector_flow.step()
+        fence([rows_out, vector_flow], loss)
+    for _ in vector_flow.order[:]:
         vector_flow.step()
-    fence([mix_flow, outer_flow_0, inner_flow_0, vector_flow], loss)
-
-    mix_flow.step(2)
-    outer_flow_0.step(2)
-    inner_flow_0.step()
-    fence([mix_flow, outer_flow_0, inner_flow_0], loss)
-
-    inner_flow_0.step(2)
-    mid_grad = mid_flow.result()
     vector_grad = vector_flow.result()
+    rows_out.stage()
+    (
+        (outer_grad_1,),
+        (inner_grad_1,),
+        (expand_grad, conv_proj_grad),
+        (mix_grad, proj_grad),
+        (outer_grad_0,),
+        (inner_grad_0,),
+    ) = rows_out.results
     return (
         output_lo,
         loss,
         input_grad,
-        jnp.stack([inner_flow_0.result(), inner_flow_1.result()], axis=0),
-        jnp.stack([outer_flow_0.result(), outer_flow_1.result()], axis=0),
-        mix_flow.result(),
-        mid_grad[:, :D],
-        mid_grad[:, D : 3 * D],
+        jnp.stack([inner_grad_0, inner_grad_1], axis=0),
+        jnp.stack([outer_grad_0, outer_grad_1], axis=0),
+        mix_grad,
+        proj_grad,
+        expand_grad,
         vector_grad[6:],
-        mid_grad[:, 3 * D :],
+        conv_proj_grad,
         vector_grad[:6],
         head_flow.result(),
     )

time: 1030 us -> 914 us (0.89)
  waiting for transfers between devices: 433 us -> 284 us
  Pallas kernels: 57.4 us -> 137 us
  local copies, waits for them, and re-layouts: 133 us -> 98.2 us
  other arithmetic: 117 us -> 95.8 us
  matrix products: 155 us -> 171 us
    ppermute x124 -> x106, waiting for transfers between devices: 433 us -> 284 us  [swap(): lax.ppermute(values, axis, [(i, i ^ bit) for i in range(self.sizes[axis])])]
    pallas_call x35 -> x31, Pallas kernels: 31.7 us -> 76.3 us  [local_copies(): pl.pallas_call(kernel, out_shape=[jax.ShapeDtypeStruct(shape, inputs[0].d...]
    dynamic_slice x20 -> x3, local copies, waits for them, and re-layouts: 43.7 us -> 0.76 us  [pick_of(): return lax.dynamic_index_in_dim(values, index, place, keepdims=False)]
    convert_element_type x42 -> x0, other arithmetic: 36 us -> none  [both(): halves.append((first + second).astype(keep.dtype))]
    pallas_call x0 -> x20, Pallas kernels: none -> 35.5 us  [stage(): pl.pallas_call(kernel, out_shape=[jax.ShapeDtypeStruct(shapes[at][1], jnp...]
    unnamed x409 -> x520, local copies, waits for them, and re-layouts: 36.6 us -> 57.5 us
    slice x14 -> x10, local copies, waits for them, and re-layouts: 19.7 us -> 3.74 us  [the longest x4 2.82 us: split_shard(): parts.append(total[:, start:start + array.shape[1]])]
    ppermute x124 -> x106, starting transfers between devices: 121 us -> 111 us  [swap(): lax.ppermute(values, axis, [(i, i ^ bit) for i in range(self.sizes[axis])])]
  transfers between devices with their start and end apart: 124 -> 106, of which waited for: 58 -> 51; matrix products, arithmetic and copies ran while one was open for 31% -> 31% of each run, Pallas kernels for 4% -> 7%
where the time goes in v4:
time: 914 us; the launch traced here: 905 us
  waiting for transfers between devices  284 us (31%)
  matrix products  171 us (19%)
  Pallas kernels  137 us (15%)
  starting transfers between devices  111 us (12%)
  local copies, waits for them, and re-layouts  98.2 us (11%)
  other arithmetic  95.8 us (10%)
    ppermute x106, waiting for transfers between devices, swap(): lax.ppermute(values, axis, [(i, i ^ bit) for i in range(self.sizes[axis])])  284 us
    ppermute x106, starting transfers between devices, swap(): lax.ppermute(values, axis, [(i, i ^ bit) for i in range(self.sizes[axis])])  111 us
    pallas_call x31, Pallas kernels, local_copies(): pl.pallas_call(kernel, out_shape=[jax.ShapeDtypeStruct(shape, inputs[0].d...  76.3 us
    unnamed x520, local copies, waits for them, and re-layouts  57.5 us
    dot_general x9, matrix products, matmul_nt(): lax.dot_general(operand, weight, (((1,), (1,)), ((), ())), preferred_elem...  55.4 us
    dot_general x10, matrix products, matmul_tn(): lax.dot_general(operand, weight, (((0,), (0,)), ((), ())), preferred_elem...  50.7 us
    dot_general x10, matrix products, matmul(): return jnp.dot(operand, weight, preferred_element_type=jnp.float32)  43.5 us
    pallas_call x20, Pallas kernels, stage(): pl.pallas_call(kernel, out_shape=[jax.ShapeDtypeStruct(shapes[at][1], jnp...  35.5 us
  transfers between devices with their start and end apart: 106, of which 51 were waited for; matrix products, arithmetic and copies ran while one was open for 31% of the time, Pallas kernels for 7%

profile of v4, /device:TPU:0, one launch (start us, length us, event | category | flops | bytes accessed | tf_op | source)
XLA Modules:
  0.0 905.0 jit_solution(16646920882612672606)
XLA Ops:
  26.2 17.7 %collective-permute-done.9 = bf16[2,2,38,32]{2,3,1,0:T(8,128)(2,1)S(1)} collective-permute-done((bf16[2,2,38,32]{2,3,1,0:T(8,128)(2,1)S(1)}, bf16[2,2,38,32]{2,3,1,0:T(8,128)(2,1)S(1)}, u32[]{:S(2)}, u32[]{:S(2)}) %collective-permute-start.9) | collective-permute-done | bytes 9760 | tf_op jit(solution)/shard_map/ppermute | solution.py:133
  72.1 31.3 %collective-permute-done.19 = bf16[2,2,2,2,38,32]{4,5,3,2,1,0:T(8,128)(2,1)S(1)} collective-permute-done((bf16[2,2,2,2,38,32]{4,5,3,2,1,0:T(8,128)(2,1)S(1)}, bf16[2,2,2,2,38,32]{4,5,3,2,1,0:T(8,128)(2,1)S(1)}, u32[]{:S(2)}, u32[]{:S(2)}) %collective-permute-start.19) | collective-permute-done | bytes 38944 | tf_op jit(solution)/shard_map/ppermute | solution.py:133
  119.2 8.7 multiply_convert_fusion.2
  129.0 17.1 %collective-permute-done.20.refs_3_ = bf16[2,2,3,32,2048]{4,3,2,1,0:T(8,128)(2,1)} collective-permute-done((bf16[2,2,3,32,2048]{4,3,2,1,0:T(8,128)(2,1)S(1)}, bf16[2,2,3,32,2048]{4,3,2,1,0:T(8,128)(2,1)}, u32[]{:S(2)}, u32[]{:S(2)}) %collective-permute-start.20) | collective-permute-done | bytes 1572896 | tf_op jit(solution)/shard_map/ppermute | solution.py:133
  177.4 16.9 %collective-permute-done.25.refs_3_ = bf16[2,2,3,32,2048]{4,3,2,1,0:T(8,128)(2,1)S(1)} collective-permute-done((bf16[2,2,3,32,2048]{4,3,2,1,0:T(8,128)(2,1)S(1)}, bf16[2,2,3,32,2048]{4,3,2,1,0:T(8,128)(2,1)S(1)}, u32[]{:S(2)}, u32[]{:S(2)}) %collective-permute-start.25) | collective-permute-done | bytes 1572896 | tf_op jit(solution)/shard_map/ppermute | solution.py:133
  214.9 8.6 copy.107
  270.2 10.3 %shard_map.250 = (f32[512,1024]{1,0:T(8,128)S(1)}, f32[8,1024]{1,0:T(8,128)S(1)}) custom-call(f32[512,2048]{1,0:T(8,128)S(1)} %fusion.114.lead_ref.gate_ref, f32[512,2048]{1,0:T(8,128)S(1)} %fusion.114.lead_ref.gate_ref, f32[512,1]{1,0:T(8,128)S(1)} %fusion.74.valid_ref, f32[32,1024]{1,0:T(8,128)S(1)} %copy.139.taps_ref), custom_call_target="tpu_custom_call" | custom-call | flops 41943040 | bytes 8388608 | tf_op jit(solution)/shard_map/pallas_call | solution.py:651
  283.7 9.1 %collective-permute-done.40 = f32[3,1024]{1,0:T(4,128)S(1)} collective-permute-done((f32[3,1024]{1,0:T(4,128)S(1)}, f32[3,1024]{1,0:T(4,128)S(1)}, u32[]{:S(2)}, u32[]{:S(2)}) %collective-permute-start.40) | collective-permute-done | bytes 12320 | tf_op jit(solution)/shard_map/ppermute | solution.py:133
  336.1 8.5 multiply_convert_fusion.1
  369.5 10.0 %collective-permute-done.50 = bf16[200,1024]{1,0:T(8,128)(2,1)S(1)} collective-permute-done((bf16[200,1024]{1,0:T(8,128)(2,1)S(1)}, bf16[200,1024]{1,0:T(8,128)(2,1)S(1)}, u32[]{:S(2)}, u32[]{:S(2)}) %collective-permute-start.50) | collective-permute-done | bytes 409632 | tf_op jit(solution)/shard_map/ppermute | solution.py:133
  472.0 7.2 fusion.2
  479.2 8.3 fusion.116
  487.5 7.8 convolution_convert_fusion.2
  524.3 16.8 %collective-permute-done.63 = f32[3,1024]{1,0:T(4,128)S(1)} collective-permute-done((f32[3,1024]{1,0:T(4,128)S(1)}, f32[3,1024]{1,0:T(4,128)S(1)}, u32[]{:S(2)}, u32[]{:S(2)}) %collective-permute-start.63) | collective-permute-done | bytes 12320 | tf_op jit(solution)/shard_map/ppermute | solution.py:133
  560.4 15.4 %shard_map.262 = (bf16[512,1024]{1,0:T(8,128)(2,1)S(1)}, bf16[512,1024]{1,0:T(8,128)(2,1)S(1)}, f32[32,1024]{1,0:T(8,128)S(1)}) custom-call(f32[512,2048]{1,0:T(8,128)S(1)} %copy-done.1, f32[512,2048]{1,0:T(8,128)S(1)} %copy-done.1, f32[512,1]{1,0:T(8,128)S(1)} %fusion.74.valid_ref, f32[32,1024]{1,0:T(8,128)S(1)} %copy.139.taps_ref, ...), custom_call_target="tpu_custom_call" | custom-call | flops 83886080 | bytes 10485760 | tf_op jit(solution)/shard_map/pallas_call | solution.py:732
  657.0 18.7 %collective-permute-done.74.refs_2_ = bf16[2,2,3,32,2048]{4,3,2,1,0:T(8,128)(2,1)S(1)} collective-permute-done((bf16[2,2,3,32,2048]{4,3,2,1,0:T(8,128)(2,1)S(1)}, bf16[2,2,3,32,2048]{4,3,2,1,0:T(8,128)(2,1)S(1)}, u32[]{:S(2)}, u32[]{:S(2)}) %collective-permute-start.74) | collective-permute-done | bytes 1572896 | tf_op jit(solution)/shard_map/ppermute | solution.py:133
  713.9 11.6 %fusion.117 = f32[512,4096]{1,0:T(8,128)} fusion(bf16[512,1024]{1,0:T(8,128)(2,1)} %copy-done.179, bf16[4096,1024]{1,0:T(8,128)(2,1)} %bitcast.329), kind=kOutput, calls=%fused_computation.358 | convolution fusion | flops 4294967296 | bytes 17825792 | tf_op jit(solution)/shard_map/dot_general | solution.py:65
  725.5 9.2 %fusion.5 = bf16[512,4096]{1,0:T(8,128)(2,1)} fusion(f32[512,4096]{1,0:T(8,128)} %get-tuple-element.545, f32[512,4096]{1,0:T(8,128)} %fusion.117), kind=kLoop, calls=%fused_computation.7 | loop fusion | flops 20971520 | bytes 20971520 | tf_op jit(solution)/shard_map/convert_element_type | solution.py:51
  734.7 10.6 %fusion.118 = f32[512,1024]{1,0:T(8,128)} fusion(bf16[512,4096]{1,0:T(8,128)(2,1)} %fusion.5, bf16[1024,4096]{1,0:T(8,128)(2,1)} %bitcast.327), kind=kOutput, calls=%fused_computation.359 | convolution fusion | flops 4294967296 | bytes 14680064 | tf_op jit(solution)/shard_map/dot_general | solution.py:65
  745.3 9.5 %convolution_convert_fusion = bf16[1024,4096]{1,0:T(8,128)(2,1)} fusion(bf16[512,4096]{1,0:T(8,128)(2,1)} %fusion.5, bf16[512,1024]{1,0:T(8,128)(2,1)S(1)} %copy-done.137, f32[1024]{0:T(1024)S(1)} %copy-done.194, f32[512]{0:T(512)S(1)} %copy-done.226, f32[512]{0:T(512)S(1)} %copy-done.203), kind=kOutput, calls=%fused_computation.16 | convolution fusion | flops 4301783040 | bytes 13639680 | tf_op jit(solution)/shard_map/dot_general | solution.py:59
  796.7 13.8 %collective-permute-done.89.refs_4_ = bf16[2,2,3,32,2048]{4,3,2,1,0:T(8,128)(2,1)S(1)} collective-permute-done((bf16[2,2,3,32,2048]{4,3,2,1,0:T(8,128)(2,1)S(1)}, bf16[2,2,3,32,2048]{4,3,2,1,0:T(8,128)(2,1)S(1)}, u32[]{:S(2)}, u32[]{:S(2)}) %collective-permute-start.89) | collective-permute-done | bytes 1572896 | tf_op jit(solution)/shard_map/ppermute | solution.py:133
  825.2 8.7 collective-permute-done.96
  833.8 18.0 %collective-permute-done.93.refs_2_ = bf16[2,2,3,32,2048]{4,3,2,1,0:T(8,128)(2,1)S(1)} collective-permute-done((bf16[2,2,3,32,2048]{4,3,2,1,0:T(8,128)(2,1)S(1)}, bf16[2,2,3,32,2048]{4,3,2,1,0:T(8,128)(2,1)S(1)}, u32[]{:S(2)}, u32[]{:S(2)}) %collective-permute-start.93) | collective-permute-done | bytes 1572896 | tf_op jit(solution)/shard_map/ppermute | solution.py:133
  892.8 8.6 collective-permute-done.105
  (1014 shorter events, 594.9 us)
Async XLA Ops:
  66.5 36.9 %collective-permute-start.15 = (bf16[2,2,3,32,2048]{4,3,2,1,0:T(8,128)(2,1)S(1)}, bf16[2,2,3,32,2048]{4,3,2,1,0:T(8,128)(2,1)S(1)}, u32[]{:S(2)}, u32[]{:S(2)}) collective-permute-start(bf16[2,2,3,32,2048]{4,3,2,1,0:T(8,128)(2,1)S(1)} %get-tuple-element.350.refs_2_), channel_id=1, source_target_pairs={{0,4},{4,0},{8,12},{12,8},{16,20},{20,16},{24,28},{28,24},{1,5},{5... | collective-permute-start | bytes 4718600 | tf_op jit(solution)/shard_map/ppermute | solution.py:133
  109.4 36.6 %collective-permute-start.20 = (bf16[2,2,3,32,2048]{4,3,2,1,0:T(8,128)(2,1)S(1)}, bf16[2,2,3,32,2048]{4,3,2,1,0:T(8,128)(2,1)}, u32[]{:S(2)}, u32[]{:S(2)}) collective-permute-start(bf16[2,2,3,32,2048]{4,3,2,1,0:T(8,128)(2,1)S(1)} %get-tuple-element.362.refs_4_.refs_2_), channel_id=1, source_target_pairs={{0,4},{4,0},{8,12},{12,8},{16,20},{20,16},{24,28},{28,24},{1,5},{5... | collective-permute-start | bytes 4718600 | tf_op jit(solution)/shard_map/ppermute | solution.py:133
  201.5 42.5 %collective-permute-start.33 = (bf16[2,128,1024]{2,1,0:T(8,128)(2,1)}, bf16[2,128,1024]{2,1,0:T(8,128)(2,1)}, u32[]{:S(2)}, u32[]{:S(2)}) collective-permute-start(bf16[2,128,1024]{2,1,0:T(8,128)(2,1)} %shard_map.242.refs_0_), channel_id=1, source_target_pairs={{0,16},{4,20},{8,24},{12,28},{16,0},{20,4},{24,8},{28,12},{1,17},{... | collective-permute-start | bytes 1572872 | tf_op jit(solution)/shard_map/ppermute | solution.py:133
  202.8 41.2 %collective-permute-start.30 = (bf16[2,2,3,32,2048]{4,3,2,1,0:T(8,128)(2,1)S(1)}, bf16[2,2,3,32,2048]{4,3,2,1,0:T(8,128)(2,1)S(1)}, u32[]{:S(2)}, u32[]{:S(2)}) collective-permute-start(bf16[2,2,3,32,2048]{4,3,2,1,0:T(8,128)(2,1)S(1)} %get-tuple-element.389.refs_4_.refs_0_.refs_2_), channel_id=1, source_target_pairs={{0,4},{4,0},{8,12},{12,8},{16,20},{20,16},{24,28},{28,24},{1,5},{5... | collective-permute-start | bytes 4718600 | tf_op jit(solution)/shard_map/ppermute | solution.py:133
  204.3 40.9 %collective-permute-start.31 = (bf16[2,2,3,32,2048]{4,3,2,1,0:T(8,128)(2,1)}, bf16[2,2,3,32,2048]{4,3,2,1,0:T(8,128)(2,1)}, u32[]{:S(2)}, u32[]{:S(2)}) collective-permute-start(bf16[2,2,3,32,2048]{4,3,2,1,0:T(8,128)(2,1)} %copy-done.19), channel_id=1, source_target_pairs={{0,2},{1,3},{2,0},{3,1},{4,6},{5,7},{6,4},{7,5},{8,10},{9,11},{10,... | collective-permute-start | bytes 4718600 | tf_op jit(solution)/shard_map/ppermute | solution.py:133
  204.8 39.2 %collective-permute-start.32 = (bf16[2,32,4096]{2,1,0:T(8,128)(2,1)}, bf16[2,32,4096]{2,1,0:T(8,128)(2,1)}, u32[]{:S(2)}, u32[]{:S(2)}) collective-permute-start(bf16[2,32,4096]{2,1,0:T(8,128)(2,1)} %copy-done.92), channel_id=1, source_target_pairs={{0,8},{4,12},{8,0},{12,4},{16,24},{20,28},{24,16},{28,20},{1,9},{5... | collective-permute-start | bytes 1572872 | tf_op jit(solution)/shard_map/ppermute | solution.py:133
  253.2 55.4 %collective-permute-start.35 = (bf16[2,2,3,32,2048]{4,3,2,1,0:T(8,128)(2,1)S(1)}, bf16[2,2,3,32,2048]{4,3,2,1,0:T(8,128)(2,1)S(1)}, u32[]{:S(2)}, u32[]{:S(2)}) collective-permute-start(bf16[2,2,3,32,2048]{4,3,2,1,0:T(8,128)(2,1)S(1)} %get-tuple-element.406.refs_4_.refs_0_.refs_2_), channel_id=1, source_target_pairs={{0,4},{4,0},{8,12},{12,8},{16,20},{20,16},{24,28},{28,24},{1,5},{5... | collective-permute-start | bytes 4718600 | tf_op jit(solution)/shard_map/ppermute | solution.py:133
  254.7 53.9 %collective-permute-start.36 = (bf16[2,2,3,32,2048]{4,3,2,1,0:T(8,128)(2,1)}, bf16[2,2,3,32,2048]{4,3,2,1,0:T(8,128)(2,1)}, u32[]{:S(2)}, u32[]{:S(2)}) collective-permute-start(bf16[2,2,3,32,2048]{4,3,2,1,0:T(8,128)(2,1)} %get-tuple-element.408.refs_2_.refs_0_), channel_id=1, source_target_pairs={{0,2},{1,3},{2,0},{3,1},{4,6},{5,7},{6,4},{7,5},{8,10},{9,11},{10,... | collective-permute-start | bytes 4718600 | tf_op jit(solution)/shard_map/ppermute | solution.py:133
  256.9 51.8 %collective-permute-start.38 = (bf16[2,128,1024]{2,1,0:T(8,128)(2,1)}, bf16[2,128,1024]{2,1,0:T(8,128)(2,1)}, u32[]{:S(2)}, u32[]{:S(2)}) collective-permute-start(bf16[2,128,1024]{2,1,0:T(8,128)(2,1)} %shard_map.247.refs_0_), channel_id=1, source_target_pairs={{0,16},{4,20},{8,24},{12,28},{16,0},{20,4},{24,8},{28,12},{1,17},{... | collective-permute-start | bytes 1572872 | tf_op jit(solution)/shard_map/ppermute | solution.py:133
  262.1 46.6 %collective-permute-start.37 = (bf16[2,2,128,1024]{3,2,1,0:T(8,128)(2,1)S(1)}, bf16[2,2,128,1024]{3,2,1,0:T(8,128)(2,1)S(1)}, u32[]{:S(2)}, u32[]{:S(2)}) collective-permute-start(bf16[2,2,128,1024]{3,2,1,0:T(8,128)(2,1)S(1)} %shard_map.246.refs_0_), channel_id=1, source_target_pairs={{0,8},{4,12},{8,0},{12,4},{16,24},{20,28},{24,16},{28,20},{1,9},{5... | collective-permute-start | bytes 3145736 | tf_op jit(solution)/shard_map/ppermute | solution.py:133
  457.6 37.7 %collective-permute-start.58 = (bf16[2,128,1024]{2,1,0:T(8,128)(2,1)}, bf16[2,128,1024]{2,1,0:T(8,128)(2,1)}, u32[]{:S(2)}, u32[]{:S(2)}) collective-permute-start(bf16[2,128,1024]{2,1,0:T(8,128)(2,1)} %get-tuple-element.685), channel_id=1, source_target_pairs={{0,8},{4,12},{8,0},{12,4},{16,24},{20,28},{24,16},{28,20},{1,9},{5... | collective-permute-start | bytes 1572872 | tf_op jit(solution)/shard_map/ppermute | solution.py:133
  503.2 76.3 %collective-permute-start.66 = (bf16[2,2,2,2,32,4096]{5,4,3,2,1,0:T(8,128)(2,1)}, bf16[2,2,2,2,32,4096]{5,4,3,2,1,0:T(8,128)(2,1)}, u32[]{:S(2)}, u32[]{:S(2)}) collective-permute-start(bf16[2,2,2,2,32,4096]{5,4,3,2,1,0:T(8,128)(2,1)} %get-tuple-element.451), channel_id=1, source_target_pairs={{0,1},{1,0},{2,3},{3,2},{4,5},{5,4},{6,7},{7,6},{8,9},{9,8},{10,11... | collective-permute-start | bytes 12582920 | tf_op jit(solution)/shard_map/ppermute | solution.py:133
  516.6 62.9 %collective-permute-start.67 = (bf16[2,2,2,32,2048]{4,3,2,1,0:T(8,128)(2,1)S(1)}, bf16[2,2,2,32,2048]{4,3,2,1,0:T(8,128)(2,1)}, u32[]{:S(2)}, u32[]{:S(2)}) collective-permute-start(bf16[2,2,2,32,2048]{4,3,2,1,0:T(8,128)(2,1)S(1)} %get-tuple-element.447.refs_2_.refs_1_), channel_id=1, source_target_pairs={{0,4},{4,0},{8,12},{12,8},{16,20},{20,16},{24,28},{28,24},{1,5},{5... | collective-permute-start | bytes 3145736 | tf_op jit(solution)/shard_map/ppermute | solution.py:133
  522.6 56.9 %collective-permute-start.68 = (bf16[2,2,2,32,2048]{4,3,2,1,0:T(8,128)(2,1)}, bf16[2,2,2,32,2048]{4,3,2,1,0:T(8,128)(2,1)}, u32[]{:S(2)}, u32[]{:S(2)}) collective-permute-start(bf16[2,2,2,32,2048]{4,3,2,1,0:T(8,128)(2,1)} %get-tuple-element.453), channel_id=1, source_target_pairs={{0,2},{1,3},{2,0},{3,1},{4,6},{5,7},{6,4},{7,5},{8,10},{9,11},{10,... | collective-permute-start | bytes 3145736 | tf_op jit(solution)/shard_map/ppermute | solution.py:133
  588.2 39.3 %collective-permute-start.72 = (bf16[2,2,3,32,2048]{4,3,2,1,0:T(8,128)(2,1)S(1)}, bf16[2,2,3,32,2048]{4,3,2,1,0:T(8,128)(2,1)S(1)}, u32[]{:S(2)}, u32[]{:S(2)}) collective-permute-start(bf16[2,2,3,32,2048]{4,3,2,1,0:T(8,128)(2,1)S(1)} %get-tuple-element.469.refs_6_.refs_2_), channel_id=1, source_target_pairs={{0,4},{4,0},{8,12},{12,8},{16,20},{20,16},{24,28},{28,24},{1,5},{5... | collective-permute-start | bytes 4718600 | tf_op jit(solution)/shard_map/ppermute | solution.py:133
  595.0 37.1 %collective-permute-start.71 = (bf16[2,2,2,2,32,4096]{5,4,3,2,1,0:T(8,128)(2,1)}, bf16[2,2,2,2,32,4096]{5,4,3,2,1,0:T(8,128)(2,1)}, u32[]{:S(2)}, u32[]{:S(2)}) collective-permute-start(bf16[2,2,2,2,32,4096]{5,4,3,2,1,0:T(8,128)(2,1)} %get-tuple-element.476), channel_id=1, source_target_pairs={{0,1},{1,0},{2,3},{3,2},{4,5},{5,4},{6,7},{7,6},{8,9},{9,8},{10,11... | collective-permute-start | bytes 12582920 | tf_op jit(solution)/shard_map/ppermute | solution.py:133
  595.0 37.1 %collective-permute-start.73 = (bf16[2,2,3,32,2048]{4,3,2,1,0:T(8,128)(2,1)}, bf16[2,2,3,32,2048]{4,3,2,1,0:T(8,128)(2,1)}, u32[]{:S(2)}, u32[]{:S(2)}) collective-permute-start(bf16[2,2,3,32,2048]{4,3,2,1,0:T(8,128)(2,1)} %get-tuple-element.478), channel_id=1, source_target_pairs={{0,2},{1,3},{2,0},{3,1},{4,6},{5,7},{6,4},{7,5},{8,10},{9,11},{10,... | collective-permute-start | bytes 4718600 | tf_op jit(solution)/shard_map/ppermute | solution.py:133
  705.9 50.4 %collective-permute-start.84 = (bf16[2,2,2,32,2048]{4,3,2,1,0:T(8,128)(2,1)S(1)}, bf16[2,2,2,32,2048]{4,3,2,1,0:T(8,128)(2,1)}, u32[]{:S(2)}, u32[]{:S(2)}) collective-permute-start(bf16[2,2,2,32,2048]{4,3,2,1,0:T(8,128)(2,1)S(1)} %get-tuple-element.533.refs_8_.refs_1_), channel_id=1, source_target_pairs={{0,4},{4,0},{8,12},{12,8},{16,20},{20,16},{24,28},{28,24},{1,5},{5... | collective-permute-start | bytes 3145736 | tf_op jit(solution)/shard_map/ppermute | solution.py:133
  711.1 45.2 %collective-permute-start.82 = (bf16[2,2,2,2,32,4096]{5,4,3,2,1,0:T(8,128)(2,1)}, bf16[2,2,2,2,32,4096]{5,4,3,2,1,0:T(8,128)(2,1)S(1)}, u32[]{:S(2)}, u32[]{:S(2)}) collective-permute-start(bf16[2,2,2,2,32,4096]{5,4,3,2,1,0:T(8,128)(2,1)} %get-tuple-element.537), channel_id=1, source_target_pairs={{0,1},{1,0},{2,3},{3,2},{4,5},{5,4},{6,7},{7,6},{8,9},{9,8},{10,11... | collective-permute-start | bytes 12582920 | tf_op jit(solution)/shard_map/ppermute | solution.py:133
  711.1 45.1 %collective-permute-start.83 = (bf16[32,4096]{1,0:T(8,128)(2,1)}, bf16[32,4096]{1,0:T(8,128)(2,1)S(1)}, u32[]{:S(2)}, u32[]{:S(2)}) collective-permute-start(bf16[32,4096]{1,0:T(8,128)(2,1)} %get-tuple-element.539), channel_id=1, source_target_pairs={{0,16},{4,20},{8,24},{12,28},{16,0},{20,4},{24,8},{28,12},{1,17},{... | collective-permute-start | bytes 786440 | tf_op jit(solution)/shard_map/ppermute | solution.py:133
  711.4 44.9 %collective-permute-start.85 = (bf16[2,2,2,32,2048]{4,3,2,1,0:T(8,128)(2,1)}, bf16[2,2,2,32,2048]{4,3,2,1,0:T(8,128)(2,1)S(1)}, u32[]{:S(2)}, u32[]{:S(2)}) collective-permute-start(bf16[2,2,2,32,2048]{4,3,2,1,0:T(8,128)(2,1)} %get-tuple-element.541), channel_id=1, source_target_pairs={{0,2},{1,3},{2,0},{3,1},{4,6},{5,7},{6,4},{7,5},{8,10},{9,11},{10,... | collective-permute-start | bytes 3145736 | tf_op jit(solution)/shard_map/ppermute | solution.py:133
  712.7 43.6 %collective-permute-start.86 = (bf16[2,32,4096]{2,1,0:T(8,128)(2,1)}, bf16[2,32,4096]{2,1,0:T(8,128)(2,1)S(1)}, u32[]{:S(2)}, u32[]{:S(2)}) collective-permute-start(bf16[2,32,4096]{2,1,0:T(8,128)(2,1)} %get-tuple-element.542), channel_id=1, source_target_pairs={{0,8},{4,12},{8,0},{12,4},{16,24},{20,28},{24,16},{28,20},{1,9},{5... | collective-permute-start | bytes 1572872 | tf_op jit(solution)/shard_map/ppermute | solution.py:133
  767.4 45.4 %collective-permute-start.87 = (bf16[2,2,2,2,32,4096]{5,4,3,2,1,0:T(8,128)(2,1)}, bf16[2,2,2,2,32,4096]{5,4,3,2,1,0:T(8,128)(2,1)}, u32[]{:S(2)}, u32[]{:S(2)}) collective-permute-start(bf16[2,2,2,2,32,4096]{5,4,3,2,1,0:T(8,128)(2,1)} %get-tuple-element.560), channel_id=1, source_target_pairs={{0,1},{1,0},{2,3},{3,2},{4,5},{5,4},{6,7},{7,6},{8,9},{9,8},{10,11... | collective-permute-start | bytes 12582920 | tf_op jit(solution)/shard_map/ppermute | solution.py:133
  773.7 36.8 %collective-permute-start.89 = (bf16[2,2,3,32,2048]{4,3,2,1,0:T(8,128)(2,1)S(1)}, bf16[2,2,3,32,2048]{4,3,2,1,0:T(8,128)(2,1)S(1)}, u32[]{:S(2)}, u32[]{:S(2)}) collective-permute-start(bf16[2,2,3,32,2048]{4,3,2,1,0:T(8,128)(2,1)S(1)} %get-tuple-element.554.refs_8_.refs_1_), channel_id=1, source_target_pairs={{0,4},{4,0},{8,12},{12,8},{16,20},{20,16},{24,28},{28,24},{1,5},{5... | collective-permute-start | bytes 4718600 | tf_op jit(solution)/shard_map/ppermute | solution.py:133
  (338 other events, 3117.7 us)

commit v5 on v4

--- a/solution.py
+++ b/solution.py
@@ -25,26 +25,6 @@
     center = values - jnp.mean(values, axis=-1, keepdims=True)
     variance = jnp.mean(center * center, axis=-1, keepdims=True)
     return center * lax.rsqrt(variance + eps) * gain_row
-
-
-def rotate(values, cosine, sine_table):
-    half_width = values.shape[-1] // 2
-    lead_part = values[..., :half_width]
-    tail_part = values[..., half_width:]
-    return jnp.concatenate(
-        [lead_part * cosine - tail_part * sine_table, tail_part * cosine + lead_part * sine_table],
-        axis=-1,
-    )
-
-
-def rotate_back(grads, cosine, sine_table):
-    half_width = grads.shape[-1] // 2
-    lead_part = grads[..., :half_width]
-    tail_part = grads[..., half_width:]
-    return jnp.concatenate(
-        [lead_part * cosine + tail_part * sine_table, tail_part * cosine - lead_part * sine_table],
-        axis=-1,
-    )
 
 
 def lowered(values):
@@ -142,15 +122,67 @@
         return values
 
     def join(self, values, got, at, place):
+        if self.tuned and values.dtype != jnp.int32:
+            shape = values.shape[:place] + (2,) + values.shape[place:]
+
+            def plan(where, sources, targets):
+                for by in range(2):
+                    index = (slice(None),) * place + (flip(where[at], by),)
+                    yield sources[by], targets[0].at[index]
+
+            return local_copies(plan, [values, got], [shape])[0]
         mine = self.mine(at)
         first = jnp.where(mine == 0, values, got)
         second = jnp.where(mine == 0, got, values)
         return jnp.stack([first, second], axis=place)
 
+    def place(self):
+        dp, head = lax.axis_index("dp"), lax.axis_index("head")
+        parts = jnp.array([4, 2, 1, 0, 0]), jnp.array([0, 0, 0, 2, 1])
+        either = jnp.where(parts[0] > 0, dp & parts[0], head & parts[1])
+        return (either > 0).astype(jnp.int32)
+
     def total(self, values):
         for at in range(len(self.bits)):
             values = values + self.swap(values, at)
         return values
+
+
+TAPS = 32
+
+
+def joined_vectors(parts):
+    devices, rows, width = parts.shape
+
+    def kernel(parts_ref, out_ref):
+        pieces = [parts_ref[at].astype(jnp.float32) for at in range(devices)]
+        out_ref[...] = jnp.concatenate(pieces, axis=1)
+
+    return pl.pallas_call(
+        kernel,
+        out_shape=jax.ShapeDtypeStruct((rows, devices * width), jnp.float32),
+        compiler_params=pltpu.CompilerParams(vmem_limit_bytes=16 << 20),
+    )(parts)
+
+
+def parted_vectors(arrays, devices):
+    rows = sum(array.shape[0] for array in arrays)
+    width = D // devices
+
+    def kernel(*refs):
+        start = 0
+        for ref in refs[:-1]:
+            count = ref.shape[0]
+            values = ref[...]
+            for at in range(devices):
+                refs[-1][at, start : start + count, :] = values[:, at * width : (at + 1) * width]
+            start += count
+
+    return pl.pallas_call(
+        kernel,
+        out_shape=jax.ShapeDtypeStruct((devices, rows, width), jnp.float32),
+        compiler_params=pltpu.CompilerParams(vmem_limit_bytes=16 << 20),
+    )(*arrays)
 
 
 class VectorGathering:
@@ -219,50 +251,53 @@
     return lax.dynamic_index_in_dim(values, index, place, keepdims=False)
 
 
+def halves_kernel(at, place, *refs):
+    dp, head = lax.axis_index("dp"), lax.axis_index("head")
+    mine = (dp // 4, dp // 2 % 2, dp % 2, head // 2, head % 2)[at]
+    keep, got, send_ref, keep_ref = refs
+    for out, by in ((send_ref, 1), (keep_ref, 0)):
+        index = (slice(None),) * place + (flip(mine, by),)
+        total = keep[index].astype(jnp.float32) + got[index].astype(jnp.float32)
+        out[...] = total.astype(out.dtype)
+
+
 class Summing:
     def __init__(self, cube, values, order):
         self.cube, self.order = cube, list(order)
         self.held = sorted(order)
-        self.keep, self.got, self.last = values, None, None
-
-    @property
-    def state(self):
-        return [part for part in (self.keep, self.got) if part is not None]
-
-    @state.setter
-    def state(self, parts):
-        self.keep = parts[0]
-        if len(parts) > 1:
-            self.got = parts[1]
-
-    def part(self, at, want_mine):
-        keep, got = self.keep, self.got
-        if self.last is not None:
-            keep = pick_of(keep, self.cube.mine(self.last[0]), self.last[1])
-        if at is not None:
-            mine, place = self.cube.mine(at), self.held.index(at)
-            index = mine if want_mine else 1 - mine
-            keep = pick_of(keep, index, place)
-            got = None if got is None else pick_of(got, index, place)
-        if got is None:
-            return keep
-        return keep.astype(jnp.float32) + got.astype(jnp.float32)
+        self.state = [values]
 
     def step(self):
-        at = self.order.pop(0)
-        kind = self.keep.dtype
+        cube, at = self.cube, self.order.pop(0)
         place = self.held.index(at)
-        send = self.part(at, False).astype(kind)
-        if self.got is None:
-            self.last = (at, place)
+        self.held.remove(at)
+        left = self.state[0].shape[:place] + self.state[0].shape[place + 1 :]
+        if not cube.tuned:
+            values = sum(part.astype(jnp.float32) for part in self.state)
+            values = values.astype(self.state[0].dtype)
+            send = pick_of(values, 1 - cube.mine(at), place)
+            keep = pick_of(values, cube.mine(at), place)
+        elif len(self.state) == 1:
+
+            def plan(where, sources, targets):
+                for by in range(2):
+                    index = (slice(None),) * place + (flip(where[at], 1 - by),)
+                    yield sources[0].at[index], targets[by]
+
+            send, keep = local_copies(plan, self.state, [left, left])
         else:
-            self.keep = self.part(at, True).astype(kind)
-            self.last = None
-        self.got = self.cube.swap(send, at)
-        self.held.remove(at)
+            size = math.prod(left) * self.state[0].dtype.itemsize
+            send, keep = pl.pallas_call(
+                functools.partial(halves_kernel, at, place),
+                out_shape=[jax.ShapeDtypeStruct(left, self.state[0].dtype)] * 2,
+                in_specs=[VMEM] * 2,
+                out_specs=[VMEM] * 2,
+                compiler_params=pltpu.CompilerParams(vmem_limit_bytes=6 * size + (4 << 20)),
+            )(*self.state)
+        self.state = [keep, cube.swap(send, at)]
 
     def result(self):
-        return self.part(None, True)
+        return sum(part.astype(jnp.float32) for part in self.state)
 
 
 class Gather:
@@ -410,6 +445,130 @@
         self.cube = cube
         self.state = {}
         self.results = []
+        self.queue = []
+
+    def sums(self, sent, after):
+        old = self.state
+        half = COLUMNS // 2
+        inputs, in_specs, names, shapes, out_specs, jobs = [], [], [], [], [], []
+        mine = lambda w, at: (w[at] + sent) % 2
+
+        def take(name, block, index):
+            inputs.append(old[name])
+            in_specs.append(pl.BlockSpec(block, index))
+            return len(inputs) - 1
+
+        def make(name, shape, block, index):
+            names.append(name)
+            shapes.append(jax.ShapeDtypeStruct(shape, jnp.bfloat16))
+            out_specs.append(pl.BlockSpec(block, index))
+            return len(names) - 1
+
+        has_n, has_m = "ck" in old, "ak" in old
+        slots = 2 * has_n + has_m
+        corner = (None, None)
+        if sent and slots:
+            sent_shape = (2, 2, slots, ROWS, half)
+            x_out = make("x", sent_shape, corner + sent_shape[2:], lambda a, b, w: (a, b, 0, 0, 0))
+            y_out = make("y", sent_shape, corner + sent_shape[2:], lambda a, b, w: (a, b, 0, 0, 0))
+        if has_n:
+            left_block, right_block = corner + (2, None, ROWS, half), corner + (None, 2, ROWS, half)
+            left_index = lambda a, b, w: (a, b, 0, mine(w, Y), 0, 0)
+            right_index = lambda a, b, w: (a, b, mine(w, X), 0, 0, 1)
+            lefts = [take(name, left_block, left_index) for name in ("ck", "cg")]
+            rights = [take(name, right_block, right_index) for name in ("ck", "cg")]
+            if not sent:
+                kept = (2, 2, 2, ROWS, half)
+                y_out = make("ak", kept, corner + kept[2:], lambda a, b, w: (a, b, 0, 0, 0))
+                x_out = make("bk", kept, corner + kept[2:], lambda a, b, w: (a, b, 0, 0, 0))
+
+            def job_n(s, o, y_out=y_out, x_out=x_out):
+                for k in range(2):
+                    added(o[y_out], k, s[lefts[0]], k, s[lefts[1]], k)
+                    added(o[x_out], k, s[rights[0]], k, s[rights[1]], k)
+
+            jobs.append(job_n)
+        if has_m:
+            block = corner + (None, ROWS, half)
+            x_index = lambda a, b, w: (a, b, mine(w, X), 0, 0)
+            y_index = lambda a, b, w: (a, b, mine(w, Y), 0, 0)
+            lefts_m = take("ak", block, x_index), take("yg", block, x_index)
+            rights_m = take("bk", block, y_index), take("xg", block, y_index)
+            place = slots - 1 if sent else slice(None)
+            if not sent:
+                kept = (2, 2, ROWS, half)
+                a_out = make("a4k", kept, corner + kept[2:], lambda a, b, w: (a, b, 0, 0))
+                b_out = make("b4k", kept, corner + kept[2:], lambda a, b, w: (a, b, 0, 0))
+            else:
+                a_out, b_out = x_out, y_out
+
+            def job_m(s, o):
+                every = slice(None)
+                added(o[a_out], place, s[lefts_m[0]], every, s[lefts_m[1]], every)
+                added(o[b_out], place, s[rights_m[0]], every, s[rights_m[1]], every)
+
+            jobs.append(job_m)
+        if "a4k" in old:
+            last = old["xg"].shape[2] - 1
+            block = (None, None, ROWS, half)
+            index = lambda a, b, w: (a, mine(w, Z0), 0, 0)
+            got_block = (None, None, None, ROWS, half)
+            got_index = lambda a, b, w: (a, mine(w, Z0), last, 0, 0)
+            lefts_z = take("a4k", block, index), take("xg", got_block, got_index)
+            rights_z = take("b4k", block, index), take("yg", got_block, got_index)
+            z_out = make(
+                "z" if sent else "zk",
+                (2, ROWS, COLUMNS),
+                (None, ROWS, COLUMNS),
+                lambda a, b, w: (a, 0, 0),
+            )
+
+            def job_z(s, o):
+                @pl.when(pl.program_id(1) == 0)
+                def _():
+                    every = slice(None)
+                    left = (every, slice(0, half))
+                    right = (every, slice(half, COLUMNS))
+                    added(o[z_out], left, s[lefts_z[0]], every, s[lefts_z[1]], every)
+                    added(o[z_out], right, s[rights_z[0]], every, s[rights_z[1]], every)
+
+            jobs.append(job_z)
+        if "zk" in old:
+            block, index = (None, ROWS, COLUMNS), lambda a, b, w: (mine(w, Z1), 0, 0)
+            pair = take("zk", block, index), take("zg", block, index)
+            f_out = make(
+                "f" if sent else "fk", (ROWS, COLUMNS), (ROWS, COLUMNS), lambda a, b, w: (0, 0)
+            )
+
+            def job_f(s, o):
+                @pl.when((pl.program_id(0) == 0) & (pl.program_id(1) == 0))
+                def _():
+                    every = slice(None)
+                    added(o[f_out], every, s[pair[0]], every, s[pair[1]], every)
+
+            jobs.append(job_f)
+        if not jobs:
+            return {}
+
+        def kernel(where, *refs):
+            sources, targets = refs[: len(inputs)], refs[len(inputs) + len(after) :]
+            for job in jobs:
+                job(sources, targets)
+
+        size = sum(math.prod(shape.shape) for shape in shapes)
+        made = pl.pallas_call(
+            kernel,
+            grid_spec=pltpu.PrefetchScalarGridSpec(
+                num_scalar_prefetch=1,
+                grid=(2, 2),
+                in_specs=in_specs + [ANY] * len(after),
+                out_specs=out_specs,
+            ),
+            out_shape=shapes,
+            cost_estimate=pl.CostEstimate(flops=size, bytes_accessed=6 * size, transcendentals=0),
+            compiler_params=pltpu.CompilerParams(vmem_limit_bytes=9 << 20),
+        )(self.cube.where, *inputs, *after)
+        return dict(zip(names, made))
 
     def stage(self, piece=None):
         cube, old, new = self.cube, self.state, {}
@@ -424,117 +583,19 @@
                     ]
                 )
             return
-        half = COLUMNS // 2
-        inputs, shapes, jobs = [], [], []
-
-        def give(name):
-            inputs.append(old[name])
-            return len(inputs) - 1
-
-        def make(sent, *shape):
-            shapes.append((sent, shape))
-            return len(shapes) - 1
-
-        left, right = slice(0, half), slice(half, COLUMNS)
-        has_n, has_m = "ck" in old, "ak" in old
-        slots = 2 * has_n + has_m
-        if slots:
-            x_out, y_out = (make(1, 2, 2, slots, ROWS, half) for _ in range(2))
-        corners = [(a, b) for a in range(2) for b in range(2)]
-        if has_n:
-            ck, cg = give("ck"), give("cg")
-            a_out, b_out = (make(0, 2, 2, 2, ROWS, half) for _ in range(2))
-
-            def job_n(w, s, o, sent):
-                y, x = flip(w[Y], sent), flip(w[X], sent)
-                for a, b in corners:
-                    for k in range(2):
-                        from_a = (a, b, k, y, slice(None), left)
-                        from_b = (a, b, x, k, slice(None), right)
-                        out_a, out_b = o[y_out if sent else a_out], o[x_out if sent else b_out]
-                        added(out_a, (a, b, k), s[ck], from_a, s[cg], from_a)
-                        added(out_b, (a, b, k), s[ck], from_b, s[cg], from_b)
-
-            jobs.append(job_n)
-        if has_m:
-            ak, bk, xg, yg = (give(name) for name in ("ak", "bk", "xg", "yg"))
-            a4_out, b4_out = (make(0, 2, 2, ROWS, half) for _ in range(2))
-
-            def job_m(w, s, o, sent):
-                y, x = flip(w[Y], sent), flip(w[X], sent)
-                for a, b in corners:
-                    place = (a, b, slots - 1) if sent else (a, b)
-                    added(o[x_out if sent else a4_out], place, s[ak], (a, b, x), s[yg], (a, b, x))
-                    added(o[y_out if sent else b4_out], place, s[bk], (a, b, y), s[xg], (a, b, y))
-
-            jobs.append(job_m)
-        if "a4k" in old:
-            a4k, b4k = give("a4k"), give("b4k")
-            x4g, y4g = (xg, yg) if has_m else (give("xg"), give("yg"))
-            last = old["xg"].shape[2] - 1
-            z_out, zk_out = (make(sent, 2, ROWS, COLUMNS) for sent in (1, 0))
-
-            def job_z(w, s, o, sent):
-                z = flip(w[Z0], sent)
-                out = o[z_out if sent else zk_out]
-                for a in range(2):
-                    added(out, (a, slice(None), left), s[a4k], (a, z), s[x4g], (a, z, last))
-                    added(out, (a, slice(None), right), s[b4k], (a, z), s[y4g], (a, z, last))
-
-            jobs.append(job_z)
-        if "zk" in old:
-            zk, zg = give("zk"), give("zg")
-            f_out, fk_out = (make(sent, ROWS, COLUMNS) for sent in (1, 0))
-
-            def job_f(w, s, o, sent):
-                z = flip(w[Z1], sent)
-                added(o[f_out if sent else fk_out], slice(None), s[zk], z, s[zg], z)
-
-            jobs.append(job_f)
+        sends = self.sums(1, [])
+        for name, at, got in (("x", X, "xg"), ("y", Y, "yg"), ("z", Z0, "zg"), ("f", Z1, "fg")):
+            if name in sends:
+                new[got] = cube.swap(sends[name], at)
+        first = list(sends.values())[:1]
+        new.update(self.sums(0, first))
         if "fk" in old:
             kind, arrays = self.queue.pop(0)
             total = old["fk"].astype(jnp.float32) + old["fg"].astype(jnp.float32)
             self.results.append(split_shard(kind, arrays, total))
-        made = {}
-        for sent in (1, 0) if jobs else ():
-            chosen = [at for at, (side, shape) in enumerate(shapes) if side == sent]
-            after = [made[x_out if slots else z_out if "a4k" in old else f_out]] if made else []
-
-            def kernel(*refs):
-                dp, head = lax.axis_index("dp"), lax.axis_index("head")
-                where = (dp // 4, dp // 2 % 2, dp % 2, head // 2, head % 2)
-                outs = dict(zip(chosen, refs[len(inputs) + len(after) :]))
-                for job in jobs:
-                    job(where, refs[: len(inputs)], outs, sent)
-
-            size = sum(math.prod(shapes[at][1]) for at in chosen)
-            results = pl.pallas_call(
-                kernel,
-                out_shape=[jax.ShapeDtypeStruct(shapes[at][1], jnp.bfloat16) for at in chosen],
-                in_specs=[VMEM] * len(inputs) + [ANY] * len(after),
-                out_specs=[VMEM] * len(chosen),
-                cost_estimate=pl.CostEstimate(
-                    flops=size, bytes_accessed=6 * size, transcendentals=0
-                ),
-                compiler_params=pltpu.CompilerParams(
-                    vmem_limit_bytes=2 * size + 2 * sum(each.size for each in inputs) + (1 << 20)
-                ),
-            )(*inputs, *after)
-            made.update(zip(chosen, results))
-        if jobs:
-            if slots:
-                new["xg"], new["yg"] = cube.swap(made[x_out], X), cube.swap(made[y_out], Y)
-            if has_n:
-                new["ak"], new["bk"] = made[a_out], made[b_out]
-            if has_m:
-                new["a4k"], new["b4k"] = made[a4_out], made[b4_out]
-            if "a4k" in old:
-                new["zk"], new["zg"] = made[zk_out], cube.swap(made[z_out], Z0)
-            if "zk" in old:
-                new["fk"], new["fg"] = made[fk_out], cube.swap(made[f_out], Z1)
         if piece is not None:
             kind, arrays, grads = piece
-            self.queue = getattr(self, "queue", []) + [(kind, arrays)]
+            self.queue.append((kind, arrays))
             bits = [
                 grad.reshape((2, 2, 2, 2, 2) + array.shape) for grad, array in zip(grads, arrays)
             ]
@@ -553,9 +614,7 @@
                             o[sent].at[:, :, :, :, :, pl.ds(COLUMNS - spare, spare)],
                         )
 
-            keep, send = local_copies(
-                plan, bits, [(2, 2, 2, 2, ROWS, COLUMNS)] * 2, [made[x_out]] if slots else []
-            )
+            keep, send = local_copies(plan, bits, [(2, 2, 2, 2, ROWS, COLUMNS)] * 2, first)
             new["ck"], new["cg"] = keep, cube.swap(send, C)
         self.state = new
 
@@ -641,7 +700,8 @@
     plain, squares = lax.fori_loop(0, length // chunk, step, (zero, zero))
     sums_ref[0:1, :] = plain
     sums_ref[1:2, :] = squares
-    sums_ref[2:8, :] = jnp.zeros((6, width), jnp.float32)
+    sums_ref[2:3, :] = jnp.broadcast_to(jnp.sum(valid, axis=0, keepdims=True), (1, width))
+    sums_ref[3:8, :] = jnp.zeros((5, width), jnp.float32)
 
 
 def conv_forward(expanded, valid, taps):
@@ -655,7 +715,7 @@
             pl.BlockSpec((rows, width), lambda i: (0, i)),
             pl.BlockSpec((rows, width), lambda i: (0, i + count)),
             pl.BlockSpec((rows, 1), lambda i: (0, 0)),
-            pl.BlockSpec((32, width), lambda i: (0, i)),
+            pl.BlockSpec((TAPS + 16, width), lambda i: (0, i)),
         ],
         out_specs=[
             pl.BlockSpec((rows, width), lambda i: (0, i)),
@@ -683,7 +743,8 @@
     taps_ref,
     conv_ref,
     grad_ref,
-    vectors_ref,
+    sums_ref,
+    back_sums_ref,
     out_lead_ref,
     out_gate_ref,
     taps_grad_ref,
@@ -692,7 +753,12 @@
     tap_sums,
 ):
     length, width = lead_ref.shape
-    inverse, plain, scaled = vectors_ref[0:1, :], vectors_ref[1:2, :], vectors_ref[2:3, :]
+    count = sums_ref[2:3, :]
+    mean = sums_ref[0:1, :] / count
+    inverse = lax.rsqrt(sums_ref[1:2, :] / count - mean * mean + eps)
+    variance_grad = -0.5 * inverse * inverse * back_sums_ref[1:2, :]
+    plain = (-inverse * back_sums_ref[0:1, :] - 2.0 * mean * variance_grad) / count
+    scaled = 2.0 * variance_grad / count
     pad[0:16, :] = jnp.zeros((16, width), jnp.float32)
     pad[16 : 16 + length, :] = (
         grad_ref[...] * inverse + (plain + scaled * conv_ref[...]) * valid_ref[...]
@@ -724,7 +790,7 @@
     taps_grad_ref[...] = jnp.sum(tap_sums[...], axis=1)
 
 
-def conv_backward(expanded, valid, taps, conv_out, grads, vectors):
+def conv_backward(expanded, valid, taps, conv_out, grads, sums, back_sums):
     rows = expanded.shape[0]
     width = 128
     count = D // width
@@ -736,12 +802,13 @@
             block,
             pl.BlockSpec((rows, width), lambda i: (0, i + count)),
             pl.BlockSpec((rows, 1), lambda i: (0, 0)),
-            pl.BlockSpec((32, width), lambda i: (0, i)),
+            pl.BlockSpec((TAPS + 16, width), lambda i: (0, i)),
             block,
             block,
             pl.BlockSpec((8, width), lambda i: (0, i)),
+            pl.BlockSpec((8, width), lambda i: (0, i)),
         ],
-        out_specs=[block, block, pl.BlockSpec((32, width), lambda i: (0, i))],
+        out_specs=[block, block, pl.BlockSpec((TAPS, width), lambda i: (0, i))],
         out_shape=[
             jax.ShapeDtypeStruct((rows, D), jnp.bfloat16),
             jax.ShapeDtypeStruct((rows, D), jnp.bfloat16),
@@ -756,7 +823,190 @@
             flops=160 * rows * D, bytes_accessed=20 * rows * D, transcendentals=rows * D
         ),
         compiler_params=pltpu.CompilerParams(vmem_limit_bytes=8 << 20),
-    )(expanded, expanded, valid, taps, conv_out, grads, vectors)
+    )(expanded, expanded, valid, taps, conv_out, grads, sums, back_sums)
+
+
+def nt_dot(left, right):
+    return lax.dot_general(left, right, (((1,), (1,)), ((), ())), preferred_element_type=jnp.float32)
+
+
+def act_back_kernel(grad_ref, weight_ref, pre_ref, out_ref):
+    pre = pre_ref[...].astype(jnp.float32)
+    gate = jax.nn.sigmoid(pre)
+    slope = gate * (1.0 + pre * (1.0 - gate))
+    out_ref[...] = (nt_dot(grad_ref[...], weight_ref[...]) * slope).astype(jnp.bfloat16)
+
+
+def act_back(grad_lo, weight, pre):
+    rows, inner = grad_lo.shape
+    total = weight.shape[0]
+    width = min(512, total)
+    return pl.pallas_call(
+        act_back_kernel,
+        grid=(total // width,),
+        in_specs=[
+            pl.BlockSpec((rows, inner), lambda i: (0, 0)),
+            pl.BlockSpec((width, inner), lambda i: (i, 0)),
+            pl.BlockSpec((rows, width), lambda i: (0, i)),
+        ],
+        out_specs=pl.BlockSpec((rows, width), lambda i: (0, i)),
+        out_shape=jax.ShapeDtypeStruct((rows, total), jnp.bfloat16),
+        cost_estimate=pl.CostEstimate(
+            flops=2 * rows * inner * total,
+            bytes_accessed=2 * total * (inner + 2 * rows),
+            transcendentals=rows * total,
+        ),
+        compiler_params=pltpu.CompilerParams(vmem_limit_bytes=10 << 20),
+    )(grad_lo, weight, pre)
+
+
+def norm_back_kernel(
+    row, grad_ref, weight_ref, values_ref, vectors_ref, above_ref, out_ref, gain_out, total
+):
+    step = pl.program_id(0)
+
+    @pl.when(step == 0)
+    def _():
+        total[...] = jnp.zeros(total.shape, jnp.float32)
+
+    total[...] += nt_dot(grad_ref[...], weight_ref[...])
+
+    @pl.when(step == pl.num_programs(0) - 1)
+    def _():
+        rows = 128
+        gain = vectors_ref[TAPS + row : TAPS + row + 1, :]
+
+        def part(at, gain_total):
+            here = pl.ds(pl.multiple_of(at * rows, rows), rows)
+            values, grads = values_ref[here, :], total[here, :]
+            center = values - jnp.mean(values, axis=-1, keepdims=True)
+            scale = lax.rsqrt(jnp.mean(center * center, axis=-1, keepdims=True) + eps)
+            normed = center * scale
+            scaled = grads * gain
+            mean = jnp.mean(scaled, axis=-1, keepdims=True)
+            along = jnp.mean(scaled * normed, axis=-1, keepdims=True)
+            out_ref[here, :] = above_ref[here, :] + (scaled - mean - normed * along) * scale
+            return gain_total + jnp.sum(grads * normed, axis=0, keepdims=True)
+
+        gain_out[...] = lax.fori_loop(
+            0, total.shape[0] // rows, part, jnp.zeros(gain_out.shape, jnp.float32)
+        )
+
+
+def product_norm_back(grad_lo, weight, values, vectors, row, above):
+    rows, inner = grad_lo.shape
+    width = 512
+    whole, vector = VMEM, VMEM
+    return pl.pallas_call(
+        functools.partial(norm_back_kernel, row),
+        grid=(inner // width,),
+        in_specs=[
+            pl.BlockSpec((rows, width), lambda i: (0, i)),
+            pl.BlockSpec((D, width), lambda i: (0, i)),
+            whole,
+            vector,
+            whole,
+        ],
+        out_specs=[whole, vector],
+        out_shape=[
+            jax.ShapeDtypeStruct((rows, D), jnp.float32),
+            jax.ShapeDtypeStruct((1, D), jnp.float32),
+        ],
+        scratch_shapes=[pltpu.VMEM((rows, D), jnp.float32)],
+        cost_estimate=pl.CostEstimate(
+            flops=2 * rows * inner * D,
+            bytes_accessed=2 * inner * (D + rows) + 12 * rows * D,
+            transcendentals=0,
+        ),
+        compiler_params=pltpu.CompilerParams(vmem_limit_bytes=14 << 20),
+    )(grad_lo, weight, values, vectors, above)
+
+
+def turned(values, cosine, sine):
+    half = HD // 2
+    lead, tail = values[:, :half], values[:, half:]
+    return jnp.concatenate([lead * cosine - tail * sine, tail * cosine + lead * sine], axis=1)
+
+
+def attend_kernel(
+    query_ref, key_ref, value_ref, cosine_ref, sine_ref, bias_ref, out_ref, query_out, key_out, value_out, log_out
+):
+    cosine, sine = cosine_ref[...], sine_ref[...]
+    query = turned(query_ref[...], cosine, sine).astype(jnp.bfloat16)
+    key = turned(key_ref[...], cosine, sine).astype(jnp.bfloat16)
+    value = value_ref[...].astype(jnp.bfloat16)
+    query_out[...], key_out[...], value_out[...] = query, key, value
+    scores = jnp.where(bias_ref[...] > 0, nt_dot(query, key) * HD**-0.5, -1e30)
+    top = jnp.max(scores, axis=-1, keepdims=True)
+    weights = jnp.exp(scores - top)
+    total = jnp.sum(weights, axis=-1, keepdims=True)
+    probs = (weights * (1.0 / total)).astype(jnp.bfloat16)
+    out_ref[...] = jnp.dot(probs, value, preferred_element_type=jnp.float32).astype(jnp.bfloat16)
+    log_out[...] = jnp.broadcast_to(top + jnp.log(total), log_out.shape)
+
+
+def attend(mixed, cosine, sine, valid):
+    rows = mixed.shape[0]
+    head = lambda shift: pl.BlockSpec((rows, HD), lambda i: (0, i + shift))
+    fixed = lambda *shape: pl.BlockSpec(shape, lambda i: (0, 0))
+    return pl.pallas_call(
+        attend_kernel,
+        grid=(H,),
+        in_specs=[
+            head(0),
+            head(H),
+            head(2 * H),
+            fixed(rows, HD // 2),
+            fixed(rows, HD // 2),
+            fixed(1, rows),
+        ],
+        out_specs=[head(0)] * 5,
+        out_shape=[jax.ShapeDtypeStruct((rows, D), jnp.bfloat16)] * 4
+        + [jax.ShapeDtypeStruct((rows, D), jnp.float32)],
+        cost_estimate=pl.CostEstimate(
+            flops=4 * rows * rows * D,
+            bytes_accessed=28 * rows * D,
+            transcendentals=rows * rows * H,
+        ),
+        compiler_params=pltpu.CompilerParams(vmem_limit_bytes=12 << 20),
+    )(mixed, mixed, mixed, cosine, sine, valid)
+
+
+def attend_back_kernel(
+    query_ref, key_ref, value_ref, log_ref, grad_ref, cosine_ref, sine_ref, bias_ref, query_out, key_out, value_out
+):
+    query, key, value, grad = query_ref[...], key_ref[...], value_ref[...], grad_ref[...]
+    cosine, sine = cosine_ref[...], -sine_ref[...]
+    scores = jnp.where(bias_ref[...] > 0, nt_dot(query, key) * HD**-0.5, -1e30)
+    probs = jnp.exp(scores - log_ref[:, :1])
+    grad_probs = nt_dot(grad, value)
+    along = jnp.sum(probs * grad_probs, axis=-1, keepdims=True)
+    grad_scores = (probs * (grad_probs - along)).astype(jnp.bfloat16)
+    value_out[...] = matmul_tn(probs.astype(jnp.bfloat16), grad).astype(jnp.bfloat16)
+    query_grad = matmul(grad_scores, key) * HD**-0.5
+    key_grad = matmul_tn(grad_scores, query) * HD**-0.5
+    query_out[...] = turned(query_grad, cosine, sine).astype(jnp.bfloat16)
+    key_out[...] = turned(key_grad, cosine, sine).astype(jnp.bfloat16)
+
+
+def attend_back(query, key, value, logs, grads, cosine, sine, valid):
+    rows = query.shape[0]
+    head = pl.BlockSpec((rows, HD), lambda i: (0, i))
+    fixed = lambda *shape: pl.BlockSpec(shape, lambda i: (0, 0))
+    return pl.pallas_call(
+        attend_back_kernel,
+        grid=(H,),
+        in_specs=[head] * 5
+        + [fixed(rows, HD // 2), fixed(rows, HD // 2), fixed(1, rows)],
+        out_specs=[head] * 3,
+        out_shape=[jax.ShapeDtypeStruct((rows, D), jnp.bfloat16)] * 3,
+        cost_estimate=pl.CostEstimate(
+            flops=10 * rows * rows * D,
+            bytes_accessed=18 * rows * D,
+            transcendentals=rows * rows * H,
+        ),
+        compiler_params=pltpu.CompilerParams(vmem_limit_bytes=12 << 20),
+    )(query, key, value, logs, grads, cosine, sine, valid)
 
 
 def fence(flows, *values):
@@ -788,6 +1038,7 @@
     out_grad,
 ):
     cube = Cube(sizes)
+    cube.where = lax.optimization_barrier(cube.place()) if cube.tuned else None
     devices = sizes["dp"] * sizes["head"]
     ff = ffn_inner.shape[2]
     all_bits = list(range(len(cube.bits)))
@@ -815,9 +1066,7 @@
     valid_rows = valid_mat.reshape(row_total).astype(jnp.float32)
     frequency = 10000.0 ** (-(jnp.arange(HD // 2, dtype=jnp.float32) * 2.0) / HD)
     angles = positions.astype(jnp.float32)[:, None] * frequency[None, :]
-    cosine = jnp.cos(angles)[:, None, :]
-    sine_table = jnp.sin(angles)[:, None, :]
-    score_scale = HD ** (-0.5)
+    cosine, sine_table = jnp.cos(angles), jnp.sin(angles)
 
     slots = UTT_DEV * NSPAN * SPAN
     slot_at = (mask_starts[:, :, None] + jnp.arange(SPAN, dtype=jnp.int32)).reshape(UTT_DEV, -1)
@@ -836,7 +1085,7 @@
 
     loss_scale = jnp.float32(devices * UTT_DEV * NSPAN * SPAN)
     hops = [C, Z1, Z0, X, Y] if cube.tuned else all_bits
-    vector_in = VectorGathering(cube, jnp.concatenate([norm_gains, conv_depth], axis=0), hops)
+    vector_in = VectorGathering(cube, jnp.concatenate([conv_depth, norm_gains, jnp.zeros_like(conv_depth[:10])], axis=0), hops)
     vector_in.step(2)
     group_codes = cube.gather(picked_codes, head_order).reshape(group * slots)
     rows_in.stage(-3)
@@ -857,8 +1106,8 @@
     vector_in.step(len(hops))
     fence([rows_in, vector_in], loss_scale)
     (vectors,) = vector_in.state
-    vectors = jnp.moveaxis(vectors.reshape((devices,) + vectors.shape[-2:]), 0, 1).reshape(-1, D)
-    gain_f, depth_f = vectors[:6].astype(jnp.float32), vectors[6:].astype(jnp.float32)
+    vectors = fence([], joined_vectors(vectors.reshape((devices,) + vectors.shape[-2:])))
+    gain_f = vectors[TAPS : TAPS + 6]
     norm_first = lowered(layer_norm(inputs, gain_f[0]))
     group_live = (group_codes >= 0).astype(jnp.float32)
     local_codes = group_codes - lax.axis_index("head") * vocab_cols
@@ -867,6 +1116,7 @@
     (inner_0,) = rows_in.wholes[0]
     pre_first = matmul(norm_first, inner_0)
     act_first = lowered(jax.nn.silu(pre_first))
+    pre_first = lowered(pre_first)
     pre_first, act_first = fence([rows_in], pre_first, act_first)
 
     rows_in.stage(2)
@@ -879,31 +1129,9 @@
     heads[0].step("far")
     mix_weight, proj_weight = rows_in.wholes[2]
     mixed = matmul(norm_attn, mix_weight)
-    mixed = mixed.reshape(UTT_DEV, SEQ, 3, H, HD)
-    queries = lowered(rotate(mixed[:, :, 0], cosine, sine_table))
-    key_rows = lowered(rotate(mixed[:, :, 1], cosine, sine_table))
-    value_rows = lowered(mixed[:, :, 2])
-
-    def scores_of(query_one, key_one, key_ok):
-        scores = (
-            jnp.einsum("qhd,khd->hqk", query_one, key_one, preferred_element_type=jnp.float32)
-            * score_scale
-        )
-        return jnp.where(key_ok[None, None, :], scores, -1e30)
-
-    def attend_one(query_one, key_one, value_one, key_ok):
-        scores = scores_of(query_one, key_one, key_ok)
-        row_top = jnp.max(scores, axis=-1, keepdims=True)
-        weights = jnp.exp(scores - row_top)
-        totals = jnp.sum(weights, axis=-1, keepdims=True)
-        attn_probs = weights / totals
-        attended = jnp.einsum(
-            "hqk,khd->qhd", lowered(attn_probs), value_one, preferred_element_type=jnp.float32
-        )
-        return (attended, row_top[..., 0] + jnp.log(totals[..., 0]))
-
-    attended, log_totals = attend_one(queries[0], key_rows[0], value_rows[0], valid_mat[0])
-    attended_lo = lowered(attended.reshape(row_total, D))
+    attended_lo, queries, key_rows, value_rows, log_totals = attend(
+        mixed, cosine, sine_table, valid_rows[None, :]
+    )
     after_attention = after_first + matmul(attended_lo, proj_weight)
     norm_conv = lowered(layer_norm(after_attention, gain_f[2]))
     after_attention, norm_conv, attended_lo, queries, key_rows, value_rows, log_totals = fence(
@@ -922,9 +1150,8 @@
     heads[1].step("far")
     expand_weight, conv_weight = rows_in.wholes[3]
     expanded = matmul(norm_conv, expand_weight)
-    conv_out, conv_sums = conv_forward(expanded, valid_rows[:, None], depth_f)
-    valid_total = jnp.broadcast_to(jnp.sum(valid_rows), (1, D))
-    sums = cube.total(jnp.concatenate([conv_sums[:2], valid_total], axis=0))
+    conv_out, conv_sums = conv_forward(expanded, valid_rows[:, None], vectors)
+    sums = cube.total(conv_sums)
     sums, conv_out, after_attention, expanded, norm_conv = fence(
         [rows_in, *heads], sums, conv_out, after_attention, expanded, norm_conv
     )
@@ -943,6 +1170,7 @@
     norm_second = lowered(layer_norm(after_conv, gain_f[4]))
     pre_second = matmul(norm_second, inner_1)
     act_second = lowered(jax.nn.silu(pre_second))
+    pre_second = lowered(pre_second)
     after_conv, norm_second, pre_second, act_second, swish_lo = fence(
         [rows_in, *heads], after_conv, norm_second, pre_second, act_second, swish_lo
     )
@@ -984,11 +1212,10 @@
         weight_grad = lowered(matmul_tn(act_lo, grad_out_lo))
         return grad_out_lo, ("tall", [ffn_outer[0]], [weight_grad])
 
-    def inner_back(grad_out_lo, normed_lo, pre_act, inner_weight, outer_weight):
-        grad_pre = lowered(silu_back(pre_act, matmul_nt(grad_out_lo, outer_weight)))
+    def inner_back(grad_out_lo, normed_lo, pre_act, outer_weight):
+        grad_pre = act_back(grad_out_lo, outer_weight, pre_act)
         weight_grad = lowered(matmul_tn(normed_lo, grad_pre))
-        below = matmul_nt(grad_pre, inner_weight)
-        return below, ("wide", [ffn_inner[0]], [weight_grad])
+        return grad_pre, ("wide", [ffn_inner[0]], [weight_grad])
 
     rows_out = Scatter(cube)
     grad_second, gain_grad_final = norm_back(after_second, gain_f[5], grad_output)
@@ -999,11 +1226,12 @@
 
     head_flow.step()
     rows_out.stage(piece)
-    below_second, piece = inner_back(grad_out_lo, norm_second, pre_second, inner_1, outer_1)
-    below_second, piece[2][0] = fence([head_flow, rows_out], below_second, piece[2][0])
-
-    norm_part, gain_grad_second = norm_back(after_conv, gain_f[4], below_second)
-    grad_conv_res = grad_second + norm_part
+    grad_pre, piece = inner_back(grad_out_lo, norm_second, pre_second, outer_1)
+    grad_conv_res, gain_grad_second = product_norm_back(
+        grad_pre, inner_1, after_conv, vectors, 4, grad_second
+    )
+    grad_conv_res, piece[2][0] = fence([head_flow, rows_out], grad_conv_res, piece[2][0])
+
     conv_res_lo = lowered(grad_conv_res)
     grad_bn = silu_back(normed_bn, matmul_nt(conv_res_lo, conv_weight))
     gain_grad_bn = jnp.sum(grad_bn * normalized, axis=0)
@@ -1015,6 +1243,7 @@
                 jnp.sum(grad_normalized * normalized, axis=0),
                 jnp.broadcast_to(ce_group / group, (D,)),
             ]
+            + [jnp.zeros((D,), jnp.float32)] * 5
         )
     )
     conv_proj_grad = lowered(matmul_tn(swish_lo, conv_res_lo))
@@ -1028,68 +1257,41 @@
 
     head_flow.step()
     rows_out.stage(piece)
-    sum_plain, sum_scaled = back_sums[0], back_sums[1]
     loss = back_sums[2, 0] / loss_scale
-    grad_variance = -0.5 * inverse * inverse * sum_scaled
-    grad_mean = -inverse * sum_plain - 2.0 * channel_mean * grad_variance
-    back_vectors = jnp.stack(
-        [inverse, grad_mean / frame_count, 2.0 * grad_variance / frame_count]
-        + [jnp.zeros_like(inverse)] * 5
-    )
     grad_lead, grad_gate, depth_grad = conv_backward(
-        expanded, valid_rows[:, None], depth_f, conv_out, grad_normalized, back_vectors
+        expanded, valid_rows[:, None], vectors, conv_out, grad_normalized, sums, back_sums
     )
     grad_expanded = jnp.concatenate([grad_lead, grad_gate], axis=1)
     expand_grad = lowered(matmul_tn(norm_conv, grad_expanded))
     grad_expanded, expand_grad = fence([rows_out, head_flow], grad_expanded, expand_grad)
 
     rows_out.stage(("wide", [conv_expand, conv_proj], [expand_grad, conv_proj_grad]))
-    norm_part, gain_grad_conv = norm_back(
-        after_attention, gain_f[2], matmul_nt(grad_expanded, expand_weight)
-    )
-    grad_attn_res = grad_conv_res + norm_part
+    grad_attn_res, gain_grad_conv = product_norm_back(
+        grad_expanded, expand_weight, after_attention, vectors, 2, grad_conv_res
+    )
     attn_res_lo = lowered(grad_attn_res)
     proj_grad = lowered(matmul_tn(attended_lo, attn_res_lo))
-    grad_attended = lowered(matmul_nt(attn_res_lo, proj_weight)).reshape(UTT_DEV, SEQ, H, HD)
-
-    def attend_back(query_one, key_one, value_one, key_ok, log_total, grad_one):
-        attn_probs = jnp.exp(scores_of(query_one, key_one, key_ok) - log_total[:, :, None])
-        grad_value = jnp.einsum(
-            "hqk,qhd->khd", lowered(attn_probs), grad_one, preferred_element_type=jnp.float32
-        )
-        grad_probs = jnp.einsum(
-            "qhd,khd->hqk", grad_one, value_one, preferred_element_type=jnp.float32
-        )
-        grad_scores = lowered(
-            attn_probs * (grad_probs - jnp.sum(attn_probs * grad_probs, axis=-1, keepdims=True))
-        )
-        grad_query = (
-            jnp.einsum("hqk,khd->qhd", grad_scores, key_one, preferred_element_type=jnp.float32)
-            * score_scale
-        )
-        grad_key = (
-            jnp.einsum("hqk,qhd->khd", grad_scores, query_one, preferred_element_type=jnp.float32)
-            * score_scale
-        )
-        return (grad_query, grad_key, grad_value)
-
-    grad_query, grad_key, grad_value = attend_back(
-        queries[0], key_rows[0], value_rows[0], valid_mat[0], log_totals, grad_attended[0]
-    )
+    grad_attended = lowered(matmul_nt(attn_res_lo, proj_weight))
     grad_mixed = jnp.concatenate(
-        [
-            lowered(rotate_back(grad_query, cosine[:, :, :], sine_table)).reshape(row_total, D),
-            lowered(rotate_back(grad_key, cosine, sine_table)).reshape(row_total, D),
-            lowered(grad_value).reshape(row_total, D),
-        ],
+        attend_back(
+            queries,
+            key_rows,
+            value_rows,
+            log_totals,
+            grad_attended,
+            cosine,
+            sine_table,
+            valid_rows[None, :],
+        ),
         axis=1,
     )
     grad_mixed, proj_grad, grad_attn_res = fence([rows_out], grad_mixed, proj_grad, grad_attn_res)
 
     rows_out.stage()
     mix_grad = lowered(matmul_tn(norm_attn, grad_mixed))
-    norm_part, gain_grad_attn = norm_back(after_first, gain_f[1], matmul_nt(grad_mixed, mix_weight))
-    grad_first_res = grad_attn_res + norm_part
+    grad_first_res, gain_grad_attn = product_norm_back(
+        grad_mixed, mix_weight, after_first, vectors, 1, grad_attn_res
+    )
     grad_first_res, mix_grad = fence([rows_out], grad_first_res, mix_grad)
 
     rows_out.stage(("wide", [attn_qkv, attn_proj], [mix_grad, proj_grad]))
@@ -1097,30 +1299,25 @@
     grad_out_lo, piece[2][0] = fence([rows_out], grad_out_lo, piece[2][0])
 
     rows_out.stage(piece)
-    below_first, piece = inner_back(grad_out_lo, norm_first, pre_first, inner_0, outer_0)
-    below_first, piece[2][0] = fence([rows_out], below_first, piece[2][0])
+    grad_pre, piece = inner_back(grad_out_lo, norm_first, pre_first, outer_0)
+    grad_pre, piece[2][0] = fence([rows_out], grad_pre, piece[2][0])
 
     rows_out.stage(piece)
-    norm_part, gain_grad_first = norm_back(inputs, gain_f[0], below_first)
-    input_grad = grad_first_res + norm_part
-    vector_grad = jnp.concatenate(
+    input_grad, gain_grad_first = product_norm_back(
+        grad_pre, inner_0, inputs, vectors, 0, grad_first_res
+    )
+    vector_grad = parted_vectors(
         [
-            jnp.stack(
-                [
-                    gain_grad_first,
-                    gain_grad_attn,
-                    gain_grad_conv,
-                    gain_grad_bn,
-                    gain_grad_second,
-                    gain_grad_final,
-                ],
-                axis=0,
-            ),
             depth_grad,
+            gain_grad_first,
+            gain_grad_attn,
+            gain_grad_conv,
+            gain_grad_bn.reshape(1, D),
+            gain_grad_second,
+            gain_grad_final.reshape(1, D),
         ],
-        axis=0,
-    )
-    vector_grad = jnp.moveaxis(vector_grad.reshape(vector_grad.shape[0], devices, -1), 1, 0)
+        devices,
+    )
     vector_flow = Summing(
         cube, vector_grad.reshape((2,) * len(cube.bits) + vector_grad.shape[1:]), hops
     )
@@ -1154,9 +1351,9 @@
         mix_grad,
         proj_grad,
         expand_grad,
-        vector_grad[6:],
+        vector_grad[:TAPS],
         conv_proj_grad,
-        vector_grad[:6],
+        vector_grad[TAPS:],
         head_flow.result(),
     )
 

time: 914 us -> 815 us (0.89)
  matrix products: 171 us -> 93.5 us
  other arithmetic: 95.8 us -> 21.1 us
  Pallas kernels: 137 us -> 183 us
  waiting for transfers between devices: 284 us -> 327 us
  local copies, waits for them, and re-layouts: 98.2 us -> 56.2 us
    pallas_call x20 -> x39, Pallas kernels: 35.5 us -> 120 us  [the longest x20 44 us: sums(): pl.pallas_call(kernel, grid_spec=pltpu.PrefetchScalarGridSpec(num_scalar_...]
    dot_general x9 -> x3, matrix products: 55.4 us -> 10.7 us  [matmul_nt(): lax.dot_general(operand, weight, (((1,), (1,)), ((), ())), preferred_elem...]
    ppermute x106, waiting for transfers between devices: 284 us -> 327 us  [swap(): lax.ppermute(values, axis, [(i, i ^ bit) for i in range(self.sizes[axis])])]
    pallas_call x31 -> x44, Pallas kernels: 76.3 us -> 36.5 us  [local_copies(): pl.pallas_call(kernel, out_shape=[jax.ShapeDtypeStruct(shape, inputs[0].d...]
    convert_element_type x11 -> x8, other arithmetic: 29.6 us -> 6.18 us  [lowered(): return values.astype(jnp.bfloat16)]
    dot_general x7 -> x0, matrix products: 20.9 us -> none  [the longest x1 7.1 us: attend_back(): jnp.einsum('qhd,khd->hqk', grad_one, value_one, preferred_element_type=jn...]
    reduce_sum x9 -> x2, other arithmetic: 13 us -> 0.92 us  [layer_norm(): center = values - jnp.mean(values, axis=-1, keepdims=True)]
    unnamed x520 -> x304, local copies, waits for them, and re-layouts: 57.5 us -> 47 us
  transfers between devices with their start and end apart: 106 -> 106, of which waited for: 51 -> 55; matrix products, arithmetic and copies ran while one was open for 31% -> 13% of each run, Pallas kernels for 7% -> 16%
where the time goes in v5:
time: 815 us; the launch traced here: 805 us
  waiting for transfers between devices  327 us (40%)
  Pallas kernels  183 us (22%)
  starting transfers between devices  117 us (14%)
  matrix products  93.5 us (11%)
  local copies, waits for them, and re-layouts  56.2 us (7%)
  other arithmetic  21.1 us (3%)
    ppermute x106, waiting for transfers between devices, swap(): lax.ppermute(values, axis, [(i, i ^ bit) for i in range(self.sizes[axis])])  327 us
    ppermute x106, starting transfers between devices, swap(): lax.ppermute(values, axis, [(i, i ^ bit) for i in range(self.sizes[axis])])  117 us
    unnamed x304, local copies, waits for them, and re-layouts  47 us
    dot_general x10, matrix products, matmul_tn(): lax.dot_general(operand, weight, (((0,), (0,)), ((), ())), preferred_elem...  46.7 us
    pallas_call x20, Pallas kernels, sums(): pl.pallas_call(kernel, grid_spec=pltpu.PrefetchScalarGridSpec(num_scalar_...  44 us
    pallas_call x44, Pallas kernels, local_copies(): pl.pallas_call(kernel, out_shape=[jax.ShapeDtypeStruct(shape, inputs[0].d...  36.5 us
    dot_general x10, matrix products, matmul(): return jnp.dot(operand, weight, preferred_element_type=jnp.float32)  36.2 us
    pallas_call x4, Pallas kernels, product_norm_back(): pl.pallas_call(functools.partial(norm_back_kernel, row), grid=(inner // w...  31.7 us
  transfers between devices with their start and end apart: 106, of which 55 were waited for; matrix products, arithmetic and copies ran while one was open for 13% of the time, Pallas kernels for 16%

profile of v5, /device:TPU:0, one launch (start us, length us, event | category | flops | bytes accessed | tf_op | source)
XLA Modules:
  0.0 805.4 jit_solution(630743573035248467)
XLA Ops:
  16.0 8.5 %collective-permute-done.2.refs_1_ = bf16[2,48,32]{2,1,0:T(8,128)(2,1)S(1)} collective-permute-done((bf16[2,48,32]{2,1,0:T(8,128)(2,1)S(1)}, bf16[2,48,32]{2,1,0:T(8,128)(2,1)S(1)}, u32[]{:S(2)}, u32[]{:S(2)}) %collective-permute-start.2) | collective-permute-done | bytes 6176 | tf_op jit(solution)/shard_map/ppermute | solution.py:113
  29.2 17.0 %collective-permute-done.9.refs_1_ = bf16[2,2,48,32]{3,2,1,0:T(8,128)(2,1)S(1)} collective-permute-done((bf16[2,2,48,32]{3,2,1,0:T(8,128)(2,1)S(1)}, bf16[2,2,48,32]{3,2,1,0:T(8,128)(2,1)S(1)}, u32[]{:S(2)}, u32[]{:S(2)}) %collective-permute-start.9) | collective-permute-done | bytes 12320 | tf_op jit(solution)/shard_map/ppermute | solution.py:113
  73.5 31.4 %collective-permute-done.19.refs_1_ = bf16[2,2,2,2,48,32]{5,4,3,2,1,0:T(8,128)(2,1)S(1)} collective-permute-done((bf16[2,2,2,2,48,32]{5,4,3,2,1,0:T(8,128)(2,1)S(1)}, bf16[2,2,2,2,48,32]{5,4,3,2,1,0:T(8,128)(2,1)S(1)}, u32[]{:S(2)}, u32[]{:S(2)}) %collective-permute-start.19) | collective-permute-done | bytes 49184 | tf_op jit(solution)/shard_map/ppermute | solution.py:113
  130.2 16.3 %collective-permute-done.20.refs_3_ = bf16[2,2,3,32,2048]{4,3,2,1,0:T(8,128)(2,1)S(1)} collective-permute-done((bf16[2,2,3,32,2048]{4,3,2,1,0:T(8,128)(2,1)S(1)}, bf16[2,2,3,32,2048]{4,3,2,1,0:T(8,128)(2,1)S(1)}, u32[]{:S(2)}, u32[]{:S(2)}) %collective-permute-start.20) | collective-permute-done | bytes 1572896 | tf_op jit(solution)/shard_map/ppermute | solution.py:113
  170.0 15.9 %collective-permute-done.25.refs_3_ = bf16[2,2,3,32,2048]{4,3,2,1,0:T(8,128)(2,1)S(1)} collective-permute-done((bf16[2,2,3,32,2048]{4,3,2,1,0:T(8,128)(2,1)S(1)}, bf16[2,2,3,32,2048]{4,3,2,1,0:T(8,128)(2,1)S(1)}, u32[]{:S(2)}, u32[]{:S(2)}) %collective-permute-start.25) | collective-permute-done | bytes 1572896 | tf_op jit(solution)/shard_map/ppermute | solution.py:113
  201.9 12.8 %shard_map.269 = (bf16[512,1024]{1,0:T(8,128)(2,1)S(1)}, bf16[512,1024]{1,0:T(8,128)(2,1)S(1)}, bf16[512,1024]{1,0:T(8,128)(2,1)S(1)}, bf16[512,1024]{1,0:T(8,128)(2,1)S(1)}, f32[512,1024]{1,0:T(8,128)S(1)}) custom-call(f32[512,3072]{1,0:T(8,128)S(1)} %fusion.34.query_ref.key_ref.value_ref, f32[512,3072]{1,0:T(8,128)S(1)} %fusion.34.query_ref.key_ref.value_ref, ...), custom_call_target="tpu_custom_call" | custom-call | flops 1073741824 | bytes 14680064 | tf_op jit(solution)/shard_map/pallas_call | solution.py:952
  218.8 9.3 %collective-permute-done.30.refs_1_.refs_3_ = bf16[2,2,3,32,2048]{4,3,2,1,0:T(8,128)(2,1)S(1)} collective-permute-done((bf16[2,2,3,32,2048]{4,3,2,1,0:T(8,128)(2,1)S(1)}, bf16[2,2,3,32,2048]{4,3,2,1,0:T(8,128)(2,1)S(1)}, u32[]{:S(2)}, u32[]{:S(2)}) %collective-permute-start.30) | collective-permute-done | bytes 1572896 | tf_op jit(solution)/shard_map/ppermute | solution.py:113
  241.0 10.9 %shard_map.275 = (f32[512,1024]{1,0:T(8,128)S(1)}, f32[8,1024]{1,0:T(8,128)S(1)}) custom-call(f32[512,2048]{1,0:T(8,128)S(1)} %fusion.35.lead_ref.gate_ref, f32[512,2048]{1,0:T(8,128)S(1)} %fusion.35.lead_ref.gate_ref, f32[512,1]{1,0:T(8,128)S(1)} %fusion.12.valid_ref, f32[48,1024]{1,0:T(8,128)S(1)} %shard_map.259.taps_ref.vectors_ref), custom_call_target="tpu_custom_call" | custom-call | flops 41943040 | bytes 8388608 | tf_op jit(solution)/shard_map/pallas_call | solution.py:711
  253.1 16.5 %collective-permute-done.40 = f32[8,1024]{1,0:T(8,128)S(1)} collective-permute-done((f32[8,1024]{1,0:T(8,128)S(1)}, f32[8,1024]{1,0:T(8,128)S(1)}, u32[]{:S(2)}, u32[]{:S(2)}) %collective-permute-start.40) | collective-permute-done | bytes 32800 | tf_op jit(solution)/shard_map/ppermute | solution.py:113
  300.3 11.5 %collective-permute-done.47.refs_3_ = bf16[2,2,128,1024]{3,2,1,0:T(8,128)(2,1)S(1)} collective-permute-done((bf16[2,2,128,1024]{3,2,1,0:T(8,128)(2,1)S(1)}, bf16[2,2,128,1024]{3,2,1,0:T(8,128)(2,1)S(1)}, u32[]{:S(2)}, u32[]{:S(2)}) %collective-permute-start.47) | collective-permute-done | bytes 1048608 | tf_op jit(solution)/shard_map/ppermute | solution.py:113
  329.5 11.0 %collective-permute-done.50.refs_1_ = bf16[200,1024]{1,0:T(8,128)(2,1)S(1)} collective-permute-done((bf16[200,1024]{1,0:T(8,128)(2,1)S(1)}, bf16[200,1024]{1,0:T(8,128)(2,1)S(1)}, u32[]{:S(2)}, u32[]{:S(2)}) %collective-permute-start.50) | collective-permute-done | bytes 409632 | tf_op jit(solution)/shard_map/ppermute | solution.py:113
  389.9 10.5 %collective-permute-done.54.refs_1_ = bf16[2,2,128,1024]{3,2,1,0:T(8,128)(2,1)S(1)} collective-permute-done((bf16[2,2,128,1024]{3,2,1,0:T(8,128)(2,1)S(1)}, bf16[2,2,128,1024]{3,2,1,0:T(8,128)(2,1)S(1)}, u32[]{:S(2)}, u32[]{:S(2)}) %collective-permute-start.54) | collective-permute-done | bytes 1048608 | tf_op jit(solution)/shard_map/ppermute | solution.py:113
  438.2 8.9 %shard_map.295 = (f32[512,1024]{1,0:T(8,128)S(1)}, f32[1,1024]{1,0:T(1,128)S(1)}) custom-call(bf16[512,4096]{1,0:T(8,128)(2,1)S(1)} %shard_map.294.grad_ref, bf16[1024,4096]{1,0:T(8,128)(2,1)S(1)} %bitcast.137, f32[512,1024]{1,0:T(8,128)S(1)} %get-tuple-element.467.values_ref, f32[48,1024]{1,0:T(8,128)S(1)} %shard_map.259.taps_ref.vectors_ref, ...), custom_call_target="tpu_custom_call" | custom-call | flops 4294967296 | bytes 18874368 | tf_op jit(solution)/shard_map/pallas_call | solution.py:900
  491.5 15.4 %shard_map.301 = (bf16[512,1024]{1,0:T(8,128)(2,1)S(1)}, bf16[512,1024]{1,0:T(8,128)(2,1)S(1)}, f32[32,1024]{1,0:T(8,128)S(1)}) custom-call(f32[512,2048]{1,0:T(8,128)S(1)} %copy-done.4, f32[512,2048]{1,0:T(8,128)S(1)} %copy-done.4, f32[512,1]{1,0:T(8,128)S(1)} %copy-done.34, f32[48,1024]{1,0:T(8,128)S(1)} %shard_map.259.taps_ref.vectors_ref, ...), custom_call_target="tpu_custom_call" | custom-call | flops 83886080 | bytes 10485760 | tf_op jit(solution)/shard_map/pallas_call | solution.py:798
  532.4 13.1 %shard_map.306 = (bf16[512,1024]{1,0:T(8,128)(2,1)S(1)}, bf16[512,1024]{1,0:T(8,128)(2,1)S(1)}, bf16[512,1024]{1,0:T(8,128)(2,1)S(1)}) custom-call(bf16[512,1024]{1,0:T(8,128)(2,1)S(1)} %copy-done.104, bf16[512,1024]{1,0:T(8,128)(2,1)S(1)} %copy-done.106, bf16[512,1024]{1,0:T(8,128)(2,1)S(1)} %copy-done.108, f32[512,1024]{1,0:T(8,128)S(1)} %copy-done.97, ...), custom_call_target="tpu_custom_call" | custom-call | flops 2684354560 | bytes 9437184 | tf_op jit(solution)/shard_map/pallas_call | solution.py:996
  576.0 18.1 %collective-permute-done.74.refs_3_.refs_5_ = bf16[2,2,3,32,2048]{4,3,2,1,0:T(8,128)(2,1)S(1)} collective-permute-done((bf16[2,2,3,32,2048]{4,3,2,1,0:T(8,128)(2,1)}, bf16[2,2,3,32,2048]{4,3,2,1,0:T(8,128)(2,1)S(1)}, u32[]{:S(2)}, u32[]{:S(2)}) %collective-permute-start.74) | collective-permute-done | bytes 1572896 | tf_op jit(solution)/shard_map/ppermute | solution.py:113
  604.1 9.2 %convolution_convert_fusion.1 = bf16[4096,1024]{1,0:T(8,128)(2,1)} fusion(bf16[512,4096]{1,0:T(8,128)(2,1)} %copy-done.140, bf16[512,1024]{1,0:T(8,128)(2,1)S(1)} %multiply_convert_fusion.3.grad_ref), kind=kOutput, calls=%fused_computation.3 | convolution fusion | flops 4299161600 | bytes 13631488 | tf_op jit(solution)/shard_map/dot_general | solution.py:39
  643.5 8.5 %convolution_convert_fusion = bf16[1024,4096]{1,0:T(8,128)(2,1)} fusion(bf16[512,4096]{1,0:T(8,128)(2,1)S(1)} %shard_map.316.grad_ref, bf16[512,1024]{1,0:T(8,128)(2,1)} %param.16, f32[1024]{0:T(1024)S(1)} %bitcast.187, f32[512]{0:T(512)S(1)} %copy-done.136, f32[512]{0:T(512)S(1)} %copy-done.132), kind=kOutput, calls=%fused_computation.2 | convolution fusion | flops 4301783040 | bytes 13639680 | tf_op jit(solution)/shard_map/dot_general | solution.py:39
  675.8 10.2 %shard_map.320 = (f32[512,1024]{1,0:T(8,128)}, f32[1,1024]{1,0:T(1,128)S(1)}) custom-call(bf16[512,4096]{1,0:T(8,128)(2,1)S(1)} %shard_map.316.grad_ref, bf16[1024,4096]{1,0:T(8,128)(2,1)S(1)} %bitcast.129, f32[512,1024]{1,0:T(8,128)S(1)} %convert_element_type.186.values_ref, f32[48,1024]{1,0:T(8,128)S(1)} %shard_map.259.taps_ref.vectors_ref, ...), custom_call_target="tpu_custom_call" | custom-call | flops 4294967296 | bytes 18874368 | tf_op jit(solution)/shard_map/pallas_call | solution.py:900
  694.1 14.9 %collective-permute-done.92.refs_1_ = f32[2,2,2,38,32]{4,3,2,1,0:T(8,128)S(1)} collective-permute-done((f32[2,2,2,38,32]{4,3,2,1,0:T(8,128)S(1)}, f32[2,2,2,38,32]{4,3,2,1,0:T(8,128)S(1)}, u32[]{:S(2)}, u32[]{:S(2)}) %collective-permute-start.92) | collective-permute-done | bytes 38944 | tf_op jit(solution)/shard_map/ppermute | solution.py:113
  720.8 9.3 %collective-permute-done.95.refs_9_ = bf16[2,32,4096]{2,1,0:T(8,128)(2,1)S(1)} collective-permute-done((bf16[2,32,4096]{2,1,0:T(8,128)(2,1)S(1)}, bf16[2,32,4096]{2,1,0:T(8,128)(2,1)S(1)}, u32[]{:S(2)}, u32[]{:S(2)}) %collective-permute-start.95) | collective-permute-done | bytes 524320 | tf_op jit(solution)/shard_map/ppermute | solution.py:113
  730.1 17.1 %collective-permute-done.93.refs_3_.refs_5_ = bf16[2,2,3,32,2048]{4,3,2,1,0:T(8,128)(2,1)S(1)} collective-permute-done((bf16[2,2,3,32,2048]{4,3,2,1,0:T(8,128)(2,1)S(1)}, bf16[2,2,3,32,2048]{4,3,2,1,0:T(8,128)(2,1)S(1)}, u32[]{:S(2)}, u32[]{:S(2)}) %collective-permute-start.93) | collective-permute-done | bytes 1572896 | tf_op jit(solution)/shard_map/ppermute | solution.py:113
  774.9 11.4 %collective-permute-done.102 = bf16[32,4096]{1,0:T(8,128)(2,1)S(1)} collective-permute-done((bf16[32,4096]{1,0:T(8,128)(2,1)S(1)}, bf16[32,4096]{1,0:T(8,128)(2,1)S(1)}, u32[]{:S(2)}, u32[]{:S(2)}) %collective-permute-start.102) | collective-permute-done | bytes 262176 | tf_op jit(solution)/shard_map/ppermute | solution.py:113
  793.0 8.4 %collective-permute-done.105 = bf16[32,4096]{1,0:T(8,128)(2,1)S(1)} collective-permute-done((bf16[32,4096]{1,0:T(8,128)(2,1)S(1)}, bf16[32,4096]{1,0:T(8,128)(2,1)S(1)}, u32[]{:S(2)}, u32[]{:S(2)}) %collective-permute-start.105) | collective-permute-done | bytes 262176 | tf_op jit(solution)/shard_map/ppermute | solution.py:113
  (716 shorter events, 482.2 us)
Async XLA Ops:
  66.6 38.6 %collective-permute-start.15 = (bf16[2,2,3,32,2048]{4,3,2,1,0:T(8,128)(2,1)S(1)}, bf16[2,2,3,32,2048]{4,3,2,1,0:T(8,128)(2,1)S(1)}, u32[]{:S(2)}, u32[]{:S(2)}) collective-permute-start(bf16[2,2,3,32,2048]{4,3,2,1,0:T(8,128)(2,1)S(1)} %get-tuple-element.392.refs_2_), channel_id=1, source_target_pairs={{0,4},{4,0},{8,12},{12,8},{16,20},{20,16},{24,28},{28,24},{1,5},{5... | collective-permute-start | bytes 4718600 | tf_op jit(solution)/shard_map/ppermute | solution.py:113
  67.2 38.0 %collective-permute-start.16 = (bf16[2,2,3,32,2048]{4,3,2,1,0:T(8,128)(2,1)S(1)}, bf16[2,2,3,32,2048]{4,3,2,1,0:T(8,128)(2,1)S(1)}, u32[]{:S(2)}, u32[]{:S(2)}) collective-permute-start(bf16[2,2,3,32,2048]{4,3,2,1,0:T(8,128)(2,1)S(1)} %get-tuple-element.394.refs_4_.refs_0_), channel_id=1, source_target_pairs={{0,2},{1,3},{2,0},{3,1},{4,6},{5,7},{6,4},{7,5},{8,10},{9,11},{10,... | collective-permute-start | bytes 4718600 | tf_op jit(solution)/shard_map/ppermute | solution.py:113
  68.7 36.5 %collective-permute-start.17 = (bf16[2,32,4096]{2,1,0:T(8,128)(2,1)S(1)}, bf16[2,32,4096]{2,1,0:T(8,128)(2,1)S(1)}, u32[]{:S(2)}, u32[]{:S(2)}) collective-permute-start(bf16[2,32,4096]{2,1,0:T(8,128)(2,1)S(1)} %get-tuple-element.396.refs_6_), channel_id=1, source_target_pairs={{0,8},{4,12},{8,0},{12,4},{16,24},{20,28},{24,16},{28,20},{1,9},{5... | collective-permute-start | bytes 1572872 | tf_op jit(solution)/shard_map/ppermute | solution.py:113
  109.9 36.5 %collective-permute-start.20 = (bf16[2,2,3,32,2048]{4,3,2,1,0:T(8,128)(2,1)S(1)}, bf16[2,2,3,32,2048]{4,3,2,1,0:T(8,128)(2,1)S(1)}, u32[]{:S(2)}, u32[]{:S(2)}) collective-permute-start(bf16[2,2,3,32,2048]{4,3,2,1,0:T(8,128)(2,1)S(1)} %get-tuple-element.404.refs_4_.refs_2_), channel_id=1, source_target_pairs={{0,4},{4,0},{8,12},{12,8},{16,20},{20,16},{24,28},{28,24},{1,5},{5... | collective-permute-start | bytes 4718600 | tf_op jit(solution)/shard_map/ppermute | solution.py:113
  111.6 36.3 %collective-permute-start.21 = (bf16[2,2,3,32,2048]{4,3,2,1,0:T(8,128)(2,1)S(1)}, bf16[2,2,3,32,2048]{4,3,2,1,0:T(8,128)(2,1)S(1)}, u32[]{:S(2)}, u32[]{:S(2)}) collective-permute-start(bf16[2,2,3,32,2048]{4,3,2,1,0:T(8,128)(2,1)S(1)} %get-tuple-element.406.refs_4_.refs_0_), channel_id=1, source_target_pairs={{0,2},{1,3},{2,0},{3,1},{4,6},{5,7},{6,4},{7,5},{8,10},{9,11},{10,... | collective-permute-start | bytes 4718600 | tf_op jit(solution)/shard_map/ppermute | solution.py:113
  149.4 36.6 %collective-permute-start.25 = (bf16[2,2,3,32,2048]{4,3,2,1,0:T(8,128)(2,1)S(1)}, bf16[2,2,3,32,2048]{4,3,2,1,0:T(8,128)(2,1)S(1)}, u32[]{:S(2)}, u32[]{:S(2)}) collective-permute-start(bf16[2,2,3,32,2048]{4,3,2,1,0:T(8,128)(2,1)S(1)} %get-tuple-element.416.refs_4_.refs_2_), channel_id=1, source_target_pairs={{0,4},{4,0},{8,12},{12,8},{16,20},{20,16},{24,28},{28,24},{1,5},{5... | collective-permute-start | bytes 4718600 | tf_op jit(solution)/shard_map/ppermute | solution.py:113
  149.9 36.3 %collective-permute-start.26 = (bf16[2,2,3,32,2048]{4,3,2,1,0:T(8,128)(2,1)S(1)}, bf16[2,2,3,32,2048]{4,3,2,1,0:T(8,128)(2,1)S(1)}, u32[]{:S(2)}, u32[]{:S(2)}) collective-permute-start(bf16[2,2,3,32,2048]{4,3,2,1,0:T(8,128)(2,1)S(1)} %get-tuple-element.418.refs_4_.refs_0_), channel_id=1, source_target_pairs={{0,2},{1,3},{2,0},{3,1},{4,6},{5,7},{6,4},{7,5},{8,10},{9,11},{10,... | collective-permute-start | bytes 4718600 | tf_op jit(solution)/shard_map/ppermute | solution.py:113
  191.6 36.5 %collective-permute-start.30 = (bf16[2,2,3,32,2048]{4,3,2,1,0:T(8,128)(2,1)S(1)}, bf16[2,2,3,32,2048]{4,3,2,1,0:T(8,128)(2,1)S(1)}, u32[]{:S(2)}, u32[]{:S(2)}) collective-permute-start(bf16[2,2,3,32,2048]{4,3,2,1,0:T(8,128)(2,1)S(1)} %get-tuple-element.436.refs_4_.refs_0_.refs_2_), channel_id=1, source_target_pairs={{0,4},{4,0},{8,12},{12,8},{16,20},{20,16},{24,28},{28,24},{1,5},{5... | collective-permute-start | bytes 4718600 | tf_op jit(solution)/shard_map/ppermute | solution.py:113
  193.1 36.2 %collective-permute-start.31 = (bf16[2,2,3,32,2048]{4,3,2,1,0:T(8,128)(2,1)S(1)}, bf16[2,2,3,32,2048]{4,3,2,1,0:T(8,128)(2,1)S(1)}, u32[]{:S(2)}, u32[]{:S(2)}) collective-permute-start(bf16[2,2,3,32,2048]{4,3,2,1,0:T(8,128)(2,1)S(1)} %get-tuple-element.438.refs_2_.refs_0_), channel_id=1, source_target_pairs={{0,2},{1,3},{2,0},{3,1},{4,6},{5,7},{6,4},{7,5},{8,10},{9,11},{10,... | collective-permute-start | bytes 4718600 | tf_op jit(solution)/shard_map/ppermute | solution.py:113
  230.2 52.3 %collective-permute-start.35 = (bf16[2,2,3,32,2048]{4,3,2,1,0:T(8,128)(2,1)S(1)}, bf16[2,2,3,32,2048]{4,3,2,1,0:T(8,128)(2,1)S(1)}, u32[]{:S(2)}, u32[]{:S(2)}) collective-permute-start(bf16[2,2,3,32,2048]{4,3,2,1,0:T(8,128)(2,1)S(1)} %get-tuple-element.453.refs_4_.refs_0_.refs_2_), channel_id=1, source_target_pairs={{0,4},{4,0},{8,12},{12,8},{16,20},{20,16},{24,28},{28,24},{1,5},{5... | collective-permute-start | bytes 4718600 | tf_op jit(solution)/shard_map/ppermute | solution.py:113
  230.8 51.7 %collective-permute-start.36 = (bf16[2,2,3,32,2048]{4,3,2,1,0:T(8,128)(2,1)S(1)}, bf16[2,2,3,32,2048]{4,3,2,1,0:T(8,128)(2,1)S(1)}, u32[]{:S(2)}, u32[]{:S(2)}) collective-permute-start(bf16[2,2,3,32,2048]{4,3,2,1,0:T(8,128)(2,1)S(1)} %get-tuple-element.455.refs_2_.refs_0_), channel_id=1, source_target_pairs={{0,2},{1,3},{2,0},{3,1},{4,6},{5,7},{6,4},{7,5},{8,10},{9,11},{10,... | collective-permute-start | bytes 4718600 | tf_op jit(solution)/shard_map/ppermute | solution.py:113
  232.6 49.9 %collective-permute-start.37 = (bf16[2,2,128,1024]{3,2,1,0:T(8,128)(2,1)S(1)}, bf16[2,2,128,1024]{3,2,1,0:T(8,128)(2,1)S(1)}, u32[]{:S(2)}, u32[]{:S(2)}) collective-permute-start(bf16[2,2,128,1024]{3,2,1,0:T(8,128)(2,1)S(1)} %shard_map.271.refs_0_), channel_id=1, source_target_pairs={{0,8},{4,12},{8,0},{12,4},{16,24},{20,28},{24,16},{28,20},{1,9},{5... | collective-permute-start | bytes 3145736 | tf_op jit(solution)/shard_map/ppermute | solution.py:113
  235.4 47.1 %collective-permute-start.38 = (bf16[2,128,1024]{2,1,0:T(8,128)(2,1)S(1)}, bf16[2,128,1024]{2,1,0:T(8,128)(2,1)S(1)}, u32[]{:S(2)}, u32[]{:S(2)}) collective-permute-start(bf16[2,128,1024]{2,1,0:T(8,128)(2,1)S(1)} %shard_map.272.refs_0_), channel_id=1, source_target_pairs={{0,16},{4,20},{8,24},{12,28},{16,0},{20,4},{24,8},{28,12},{1,17},{... | collective-permute-start | bytes 1572872 | tf_op jit(solution)/shard_map/ppermute | solution.py:113
  407.9 39.2 %collective-permute-start.60 = (bf16[2,2,2,2,32,4096]{5,4,3,2,1,0:T(8,128)(2,1)}, bf16[2,2,2,2,32,4096]{5,4,3,2,1,0:T(8,128)(2,1)}, u32[]{:S(2)}, u32[]{:S(2)}) collective-permute-start(bf16[2,2,2,2,32,4096]{5,4,3,2,1,0:T(8,128)(2,1)} %get-tuple-element.495), channel_id=1, source_target_pairs={{0,1},{1,0},{2,3},{3,2},{4,5},{5,4},{6,7},{7,6},{8,9},{9,8},{10,11... | collective-permute-start | bytes 12582920 | tf_op jit(solution)/shard_map/ppermute | solution.py:113
  411.4 35.7 %collective-permute-start.59 = (bf16[2,128,1024]{2,1,0:T(8,128)(2,1)}, bf16[2,128,1024]{2,1,0:T(8,128)(2,1)S(1)}, u32[]{:S(2)}, u32[]{:S(2)}) collective-permute-start(bf16[2,128,1024]{2,1,0:T(8,128)(2,1)} %get-tuple-element.493), channel_id=1, source_target_pairs={{0,16},{4,20},{8,24},{12,28},{16,0},{20,4},{24,8},{28,12},{1,17},{... | collective-permute-start | bytes 1572872 | tf_op jit(solution)/shard_map/ppermute | solution.py:113
  457.5 53.1 %collective-permute-start.66 = (bf16[2,2,2,2,32,4096]{5,4,3,2,1,0:T(8,128)(2,1)}, bf16[2,2,2,2,32,4096]{5,4,3,2,1,0:T(8,128)(2,1)}, u32[]{:S(2)}, u32[]{:S(2)}) collective-permute-start(bf16[2,2,2,2,32,4096]{5,4,3,2,1,0:T(8,128)(2,1)} %get-tuple-element.511), channel_id=1, source_target_pairs={{0,1},{1,0},{2,3},{3,2},{4,5},{5,4},{6,7},{7,6},{8,9},{9,8},{10,11... | collective-permute-start | bytes 12582920 | tf_op jit(solution)/shard_map/ppermute | solution.py:113
  516.9 37.7 %collective-permute-start.71 = (bf16[2,2,2,2,32,4096]{5,4,3,2,1,0:T(8,128)(2,1)S(1)}, bf16[2,2,2,2,32,4096]{5,4,3,2,1,0:T(8,128)(2,1)S(1)}, u32[]{:S(2)}, u32[]{:S(2)}) collective-permute-start(bf16[2,2,2,2,32,4096]{5,4,3,2,1,0:T(8,128)(2,1)S(1)} %get-tuple-element.540), channel_id=1, source_target_pairs={{0,1},{1,0},{2,3},{3,2},{4,5},{5,4},{6,7},{7,6},{8,9},{9,8},{10,11... | collective-permute-start | bytes 12582920 | tf_op jit(solution)/shard_map/ppermute | solution.py:113
  517.0 36.8 %collective-permute-start.72 = (bf16[2,2,3,32,2048]{4,3,2,1,0:T(8,128)(2,1)S(1)}, bf16[2,2,3,32,2048]{4,3,2,1,0:T(8,128)(2,1)S(1)}, u32[]{:S(2)}, u32[]{:S(2)}) collective-permute-start(bf16[2,2,3,32,2048]{4,3,2,1,0:T(8,128)(2,1)S(1)} %get-tuple-element.533.refs_8_.refs_2_), channel_id=1, source_target_pairs={{0,4},{4,0},{8,12},{12,8},{16,20},{20,16},{24,28},{28,24},{1,5},{5... | collective-permute-start | bytes 4718600 | tf_op jit(solution)/shard_map/ppermute | solution.py:113
  518.0 36.7 %collective-permute-start.73 = (bf16[2,2,3,32,2048]{4,3,2,1,0:T(8,128)(2,1)}, bf16[2,2,3,32,2048]{4,3,2,1,0:T(8,128)(2,1)S(1)}, u32[]{:S(2)}, u32[]{:S(2)}) collective-permute-start(bf16[2,2,3,32,2048]{4,3,2,1,0:T(8,128)(2,1)} %get-tuple-element.542), channel_id=1, source_target_pairs={{0,2},{1,3},{2,0},{3,1},{4,6},{5,7},{6,4},{7,5},{8,10},{9,11},{10,... | collective-permute-start | bytes 4718600 | tf_op jit(solution)/shard_map/ppermute | solution.py:113
  558.2 35.9 %collective-permute-start.74 = (bf16[2,2,3,32,2048]{4,3,2,1,0:T(8,128)(2,1)}, bf16[2,2,3,32,2048]{4,3,2,1,0:T(8,128)(2,1)S(1)}, u32[]{:S(2)}, u32[]{:S(2)}) collective-permute-start(bf16[2,2,3,32,2048]{4,3,2,1,0:T(8,128)(2,1)} %get-tuple-element.562.refs_12_), channel_id=1, source_target_pairs={{0,4},{4,0},{8,12},{12,8},{16,20},{20,16},{24,28},{28,24},{1,5},{5... | collective-permute-start | bytes 4718600 | tf_op jit(solution)/shard_map/ppermute | solution.py:113
  671.8 37.6 %collective-permute-start.87 = (bf16[2,2,2,2,32,4096]{5,4,3,2,1,0:T(8,128)(2,1)}, bf16[2,2,2,2,32,4096]{5,4,3,2,1,0:T(8,128)(2,1)S(1)}, u32[]{:S(2)}, u32[]{:S(2)}) collective-permute-start(bf16[2,2,2,2,32,4096]{5,4,3,2,1,0:T(8,128)(2,1)} %get-tuple-element.629), channel_id=1, source_target_pairs={{0,1},{1,0},{2,3},{3,2},{4,5},{5,4},{6,7},{7,6},{8,9},{9,8},{10,11... | collective-permute-start | bytes 12582920 | tf_op jit(solution)/shard_map/ppermute | solution.py:113
  671.9 37.1 %collective-permute-start.89 = (bf16[2,2,3,32,2048]{4,3,2,1,0:T(8,128)(2,1)S(1)}, bf16[2,2,3,32,2048]{4,3,2,1,0:T(8,128)(2,1)S(1)}, u32[]{:S(2)}, u32[]{:S(2)}) collective-permute-start(bf16[2,2,3,32,2048]{4,3,2,1,0:T(8,128)(2,1)S(1)} %get-tuple-element.623.refs_10_.refs_1_), channel_id=1, source_target_pairs={{0,4},{4,0},{8,12},{12,8},{16,20},{20,16},{24,28},{28,24},{1,5},{5... | collective-permute-start | bytes 4718600 | tf_op jit(solution)/shard_map/ppermute | solution.py:113
  672.8 36.7 %collective-permute-start.90 = (bf16[2,2,3,32,2048]{4,3,2,1,0:T(8,128)(2,1)}, bf16[2,2,3,32,2048]{4,3,2,1,0:T(8,128)(2,1)S(1)}, u32[]{:S(2)}, u32[]{:S(2)}) collective-permute-start(bf16[2,2,3,32,2048]{4,3,2,1,0:T(8,128)(2,1)} %get-tuple-element.633), channel_id=1, source_target_pairs={{0,2},{1,3},{2,0},{3,1},{4,6},{5,7},{6,4},{7,5},{8,10},{9,11},{10,... | collective-permute-start | bytes 4718600 | tf_op jit(solution)/shard_map/ppermute | solution.py:113
  711.5 35.8 %collective-permute-start.93 = (bf16[2,2,3,32,2048]{4,3,2,1,0:T(8,128)(2,1)S(1)}, bf16[2,2,3,32,2048]{4,3,2,1,0:T(8,128)(2,1)S(1)}, u32[]{:S(2)}, u32[]{:S(2)}) collective-permute-start(bf16[2,2,3,32,2048]{4,3,2,1,0:T(8,128)(2,1)S(1)} %get-tuple-element.654.refs_12_), channel_id=1, source_target_pairs={{0,4},{4,0},{8,12},{12,8},{16,20},{20,16},{24,28},{28,24},{1,5},{5... | collective-permute-start | bytes 4718600 | tf_op jit(solution)/shard_map/ppermute | solution.py:113
  (234 other events, 2607.0 us)

commit v6 on v5

--- a/solution.py
+++ b/solution.py
@@ -57,6 +57,7 @@
 
 
 AXES = ("dp", "head")
+BRIEF = pl.CostEstimate(flops=0, bytes_accessed=0, transcendentals=0)
 ANY = pl.BlockSpec(memory_space=pl.ANY)
 VMEM = pl.BlockSpec(memory_space=pltpu.VMEM)
 Z1, Z0, X, Y, C = range(5)
@@ -83,7 +84,7 @@
         in_specs=[ANY] * (count + len(after)),
         out_specs=[VMEM] * len(outputs),
         scratch_shapes=[pltpu.SemaphoreType.DMA((16,))],
-        cost_estimate=pl.CostEstimate(flops=0, bytes_accessed=2 * size, transcendentals=0),
+        cost_estimate=BRIEF,
         compiler_params=pltpu.CompilerParams(vmem_limit_bytes=size + (1 << 20)),
     )(*inputs, *after)
     return list(results)
@@ -143,7 +144,7 @@
         return (either > 0).astype(jnp.int32)
 
     def total(self, values):
-        for at in range(len(self.bits)):
+        for at in (C, Z0, Z1, X, Y) if self.tuned else range(len(self.bits)):
             values = values + self.swap(values, at)
         return values
 
@@ -446,6 +447,7 @@
         self.state = {}
         self.results = []
         self.queue = []
+        self.first = []
 
     def sums(self, sent, after):
         old = self.state
@@ -565,25 +567,18 @@
                 out_specs=out_specs,
             ),
             out_shape=shapes,
-            cost_estimate=pl.CostEstimate(flops=size, bytes_accessed=6 * size, transcendentals=0),
+            cost_estimate=BRIEF,
             compiler_params=pltpu.CompilerParams(vmem_limit_bytes=9 << 20),
         )(self.cube.where, *inputs, *after)
         return dict(zip(names, made))
 
-    def stage(self, piece=None):
+    def stage(self, value=None):
         cube, old, new = self.cube, self.state, {}
         if not cube.tuned:
-            if piece is not None:
-                self.results.append(
-                    [
-                        lax.psum_scatter(grad, AXES, scatter_dimension=0, tiled=True).astype(
-                            jnp.float32
-                        )
-                        for grad in piece[2]
-                    ]
-                )
-            return
+            return value
         sends = self.sums(1, [])
+        if value is not None:
+            sends, value = lax.optimization_barrier((sends, value))
         for name, at, got in (("x", X, "xg"), ("y", Y, "yg"), ("z", Z0, "zg"), ("f", Z1, "fg")):
             if name in sends:
                 new[got] = cube.swap(sends[name], at)
@@ -593,30 +588,21 @@
             kind, arrays = self.queue.pop(0)
             total = old["fk"].astype(jnp.float32) + old["fg"].astype(jnp.float32)
             self.results.append(split_shard(kind, arrays, total))
-        if piece is not None:
-            kind, arrays, grads = piece
-            self.queue.append((kind, arrays))
-            bits = [
-                grad.reshape((2, 2, 2, 2, 2) + array.shape) for grad, array in zip(grads, arrays)
-            ]
-
-            def plan(w, s, o):
-                for sent in range(2):
-                    for at, rows, columns in tiles_of(kind, arrays):
-                        yield (
-                            s[at].at[:, :, :, :, flip(w[C], sent), rows],
-                            o[sent].at[:, :, :, :, :, columns],
-                        )
-                    spare = COLUMNS - sum(array.size for array in arrays) // ROWS
-                    if spare:
-                        yield (
-                            s[0].at[:, :, :, :, flip(w[C], sent), :, pl.ds(0, spare)],
-                            o[sent].at[:, :, :, :, :, pl.ds(COLUMNS - spare, spare)],
-                        )
-
-            keep, send = local_copies(plan, bits, [(2, 2, 2, 2, ROWS, COLUMNS)] * 2, first)
-            new["ck"], new["cg"] = keep, cube.swap(send, C)
-        self.state = new
+        self.first, self.state = first, new
+        return value
+
+    def push(self, kind, arrays, grads):
+        if not self.cube.tuned:
+            self.results.append(
+                [
+                    lax.psum_scatter(grad, AXES, scatter_dimension=0, tiled=True).astype(jnp.float32)
+                    for grad in grads
+                ]
+            )
+            return
+        self.queue.append((kind, arrays))
+        keep, send = grads
+        self.state["ck"], self.state["cg"] = keep, self.cube.swap(send, C)
 
 
 def split_shard(kind, arrays, total):
@@ -729,9 +715,7 @@
             pltpu.VMEM((rows + 40, width), jnp.float32),
             pltpu.VMEM((8, rows + 32, width), jnp.float32),
         ],
-        cost_estimate=pl.CostEstimate(
-            flops=80 * rows * D, bytes_accessed=16 * rows * D, transcendentals=rows * D
-        ),
+        cost_estimate=BRIEF,
         compiler_params=pltpu.CompilerParams(vmem_limit_bytes=8 << 20),
     )(expanded, expanded, valid, taps)
 
@@ -745,8 +729,7 @@
     grad_ref,
     sums_ref,
     back_sums_ref,
-    out_lead_ref,
-    out_gate_ref,
+    out_ref,
     taps_grad_ref,
     pad,
     shift,
@@ -782,8 +765,8 @@
             total += part * taps[j]
             tap_sums[j] += jnp.sum((part * gated).reshape(chunk // 8, 8, width), axis=0)
         grad = total * valid
-        out_lead_ref[here, :] = (grad * gate).astype(jnp.bfloat16)
-        out_gate_ref[here, :] = (grad * lead * gate * (1.0 - gate)).astype(jnp.bfloat16)
+        out_ref[0, here, :] = (grad * gate).astype(jnp.bfloat16)
+        out_ref[1, here, :] = (grad * lead * gate * (1.0 - gate)).astype(jnp.bfloat16)
         return carry
 
     lax.fori_loop(0, length // chunk, step, 0)
@@ -808,10 +791,12 @@
             pl.BlockSpec((8, width), lambda i: (0, i)),
             pl.BlockSpec((8, width), lambda i: (0, i)),
         ],
-        out_specs=[block, block, pl.BlockSpec((TAPS, width), lambda i: (0, i))],
+        out_specs=[
+            pl.BlockSpec((2, rows, width), lambda i: (0, 0, i)),
+            pl.BlockSpec((TAPS, width), lambda i: (0, i)),
+        ],
         out_shape=[
-            jax.ShapeDtypeStruct((rows, D), jnp.bfloat16),
-            jax.ShapeDtypeStruct((rows, D), jnp.bfloat16),
+            jax.ShapeDtypeStruct((2, rows, D), jnp.bfloat16),
             jax.ShapeDtypeStruct((32, D), jnp.float32),
         ],
         scratch_shapes=[
@@ -819,9 +804,7 @@
             pltpu.VMEM((8, rows + 32, width), jnp.float32),
             pltpu.VMEM((32, 8, width), jnp.float32),
         ],
-        cost_estimate=pl.CostEstimate(
-            flops=160 * rows * D, bytes_accessed=20 * rows * D, transcendentals=rows * D
-        ),
+        cost_estimate=BRIEF,
         compiler_params=pltpu.CompilerParams(vmem_limit_bytes=8 << 20),
     )(expanded, expanded, valid, taps, conv_out, grads, sums, back_sums)
 
@@ -840,7 +823,8 @@
 def act_back(grad_lo, weight, pre):
     rows, inner = grad_lo.shape
     total = weight.shape[0]
-    width = min(512, total)
+    width = 512
+    each = D // width
     return pl.pallas_call(
         act_back_kernel,
         grid=(total // width,),
@@ -849,15 +833,111 @@
             pl.BlockSpec((width, inner), lambda i: (i, 0)),
             pl.BlockSpec((rows, width), lambda i: (0, i)),
         ],
-        out_specs=pl.BlockSpec((rows, width), lambda i: (0, i)),
-        out_shape=jax.ShapeDtypeStruct((rows, total), jnp.bfloat16),
-        cost_estimate=pl.CostEstimate(
-            flops=2 * rows * inner * total,
-            bytes_accessed=2 * total * (inner + 2 * rows),
-            transcendentals=rows * total,
-        ),
+        out_specs=pl.BlockSpec((None, rows, width), lambda i: (i // each, 0, i % each)),
+        out_shape=jax.ShapeDtypeStruct((total // D, rows, D), jnp.bfloat16),
+        cost_estimate=BRIEF,
         compiler_params=pltpu.CompilerParams(vmem_limit_bytes=10 << 20),
     )(grad_lo, weight, pre)
+
+
+def weight_grads_kernel(counts, *refs):
+    lefts, rights = refs[: len(counts)], refs[len(counts) : 2 * len(counts)]
+    keep_ref, send_ref = refs[-2:]
+    core = lax.axis_index("head") % 2
+    step, start = pl.program_id(0), 0
+    for left, right, count in zip(lefts, rights, counts):
+
+        @pl.when((step >= start) & (step < start + count))
+        def _(left=left, right=right):
+            total = matmul_tn(left[...], right[...]).astype(jnp.bfloat16)
+            for at in range(16):
+                first, second = (
+                    total[(2 * at + by) * ROWS : (2 * at + by + 1) * ROWS, :] for by in range(2)
+                )
+                place = (at // 8, at // 4 % 2, at // 2 % 2, at % 2)
+
+                @pl.when(core == 0)
+                def _():
+                    keep_ref[place], send_ref[place] = first, second
+
+                @pl.when(core == 1)
+                def _():
+                    keep_ref[place], send_ref[place] = second, first
+
+        start += count
+
+    @pl.when(step >= start)
+    def _():
+        keep_ref[...] = jnp.zeros(keep_ref.shape, jnp.bfloat16)
+        send_ref[...] = jnp.zeros(send_ref.shape, jnp.bfloat16)
+
+
+def tall_grads_kernel(left_ref, right_ref, keep_ref, send_ref):
+    core = lax.axis_index("head") % 2
+    total = matmul_tn(left_ref[...], right_ref[...]).astype(jnp.bfloat16)
+    for at in range(4):
+        for group in range(4):
+            first, second = (
+                total[((2 * at + by) * 4 + group) * ROWS : ((2 * at + by) * 4 + group + 1) * ROWS, :]
+                for by in range(2)
+            )
+            place = (at // 2, at % 2, slice(None), slice(group * D, (group + 1) * D))
+
+            @pl.when(core == 0)
+            def _():
+                keep_ref[place], send_ref[place] = first, second
+
+            @pl.when(core == 1)
+            def _():
+                keep_ref[place], send_ref[place] = second, first
+
+
+def weight_grads(cube, kind, pairs):
+    if not cube.tuned:
+        return [
+            jnp.concatenate([lowered(matmul_tn(left, each)) for each in rights], axis=1)
+            for left, rights in pairs
+        ]
+    shape = (2, 2, 2, 2, ROWS, COLUMNS)
+    rows = pairs[0][0].shape[0]
+    common = dict(
+        out_shape=[jax.ShapeDtypeStruct(shape, jnp.bfloat16)] * 2,
+        cost_estimate=BRIEF,
+        compiler_params=pltpu.CompilerParams(vmem_limit_bytes=22 << 20),
+    )
+    if kind == "tall":
+        ((left, right),) = pairs
+        return pl.pallas_call(
+            tall_grads_kernel,
+            grid=(4,),
+            in_specs=[
+                pl.BlockSpec((rows, D), lambda i: (0, i)),
+                pl.BlockSpec((None, rows, D), lambda i: (0, 0, 0)),
+            ],
+            out_specs=[
+                pl.BlockSpec((None, None, 2, 2, ROWS, COLUMNS), lambda i: (i // 2, i % 2, 0, 0, 0, 0))
+            ]
+            * 2,
+            **common,
+        )(left, right)
+    counts, right_specs, start = [], [], 0
+    for _, right in pairs:
+        count = right.shape[0]
+        right_specs.append(
+            pl.BlockSpec(
+                (None, rows, D),
+                lambda i, start=start, count=count: (jnp.clip(i - start, 0, count - 1), 0, 0),
+            )
+        )
+        counts.append(count)
+        start += count
+    return pl.pallas_call(
+        functools.partial(weight_grads_kernel, counts),
+        grid=(COLUMNS // D,),
+        in_specs=[pl.BlockSpec((rows, D), lambda i: (0, 0))] * len(pairs) + right_specs,
+        out_specs=[pl.BlockSpec(shape[:5] + (D,), lambda i: (0, 0, 0, 0, 0, i))] * 2,
+        **common,
+    )(*[left for left, _ in pairs], *[right for _, right in pairs])
 
 
 def norm_back_kernel(
@@ -894,14 +974,16 @@
 
 
 def product_norm_back(grad_lo, weight, values, vectors, row, above):
-    rows, inner = grad_lo.shape
+    _, rows, _ = grad_lo.shape
+    inner = weight.shape[1]
     width = 512
+    each = D // width
     whole, vector = VMEM, VMEM
     return pl.pallas_call(
         functools.partial(norm_back_kernel, row),
         grid=(inner // width,),
         in_specs=[
-            pl.BlockSpec((rows, width), lambda i: (0, i)),
+            pl.BlockSpec((None, rows, width), lambda i: (i // each, 0, i % each)),
             pl.BlockSpec((D, width), lambda i: (0, i)),
             whole,
             vector,
@@ -913,11 +995,7 @@
             jax.ShapeDtypeStruct((1, D), jnp.float32),
         ],
         scratch_shapes=[pltpu.VMEM((rows, D), jnp.float32)],
-        cost_estimate=pl.CostEstimate(
-            flops=2 * rows * inner * D,
-            bytes_accessed=2 * inner * (D + rows) + 12 * rows * D,
-            transcendentals=0,
-        ),
+        cost_estimate=BRIEF,
         compiler_params=pltpu.CompilerParams(vmem_limit_bytes=14 << 20),
     )(grad_lo, weight, values, vectors, above)
 
@@ -963,17 +1041,13 @@
         out_specs=[head(0)] * 5,
         out_shape=[jax.ShapeDtypeStruct((rows, D), jnp.bfloat16)] * 4
         + [jax.ShapeDtypeStruct((rows, D), jnp.float32)],
-        cost_estimate=pl.CostEstimate(
-            flops=4 * rows * rows * D,
-            bytes_accessed=28 * rows * D,
-            transcendentals=rows * rows * H,
-        ),
+        cost_estimate=BRIEF,
         compiler_params=pltpu.CompilerParams(vmem_limit_bytes=12 << 20),
     )(mixed, mixed, mixed, cosine, sine, valid)
 
 
 def attend_back_kernel(
-    query_ref, key_ref, value_ref, log_ref, grad_ref, cosine_ref, sine_ref, bias_ref, query_out, key_out, value_out
+    query_ref, key_ref, value_ref, log_ref, grad_ref, cosine_ref, sine_ref, bias_ref, out_ref
 ):
     query, key, value, grad = query_ref[...], key_ref[...], value_ref[...], grad_ref[...]
     cosine, sine = cosine_ref[...], -sine_ref[...]
@@ -982,11 +1056,11 @@
     grad_probs = nt_dot(grad, value)
     along = jnp.sum(probs * grad_probs, axis=-1, keepdims=True)
     grad_scores = (probs * (grad_probs - along)).astype(jnp.bfloat16)
-    value_out[...] = matmul_tn(probs.astype(jnp.bfloat16), grad).astype(jnp.bfloat16)
+    out_ref[2] = matmul_tn(probs.astype(jnp.bfloat16), grad).astype(jnp.bfloat16)
     query_grad = matmul(grad_scores, key) * HD**-0.5
     key_grad = matmul_tn(grad_scores, query) * HD**-0.5
-    query_out[...] = turned(query_grad, cosine, sine).astype(jnp.bfloat16)
-    key_out[...] = turned(key_grad, cosine, sine).astype(jnp.bfloat16)
+    out_ref[0] = turned(query_grad, cosine, sine).astype(jnp.bfloat16)
+    out_ref[1] = turned(key_grad, cosine, sine).astype(jnp.bfloat16)
 
 
 def attend_back(query, key, value, logs, grads, cosine, sine, valid):
@@ -998,13 +1072,9 @@
         grid=(H,),
         in_specs=[head] * 5
         + [fixed(rows, HD // 2), fixed(rows, HD // 2), fixed(1, rows)],
-        out_specs=[head] * 3,
-        out_shape=[jax.ShapeDtypeStruct((rows, D), jnp.bfloat16)] * 3,
-        cost_estimate=pl.CostEstimate(
-            flops=10 * rows * rows * D,
-            bytes_accessed=18 * rows * D,
-            transcendentals=rows * rows * H,
-        ),
+        out_specs=pl.BlockSpec((3, rows, HD), lambda i: (0, 0, i)),
+        out_shape=jax.ShapeDtypeStruct((3, rows, D), jnp.bfloat16),
+        cost_estimate=BRIEF,
         compiler_params=pltpu.CompilerParams(vmem_limit_bytes=12 << 20),
     )(query, key, value, logs, grads, cosine, sine, valid)
 
@@ -1104,7 +1174,8 @@
 
     rows_in.stage(0)
     vector_in.step(len(hops))
-    fence([rows_in, vector_in], loss_scale)
+    heads[0].step("far")
+    fence([rows_in, vector_in, heads[0]], loss_scale)
     (vectors,) = vector_in.state
     vectors = fence([], joined_vectors(vectors.reshape((devices,) + vectors.shape[-2:])))
     gain_f = vectors[TAPS : TAPS + 6]
@@ -1126,7 +1197,7 @@
     after_first, norm_attn = fence([rows_in], after_first, norm_attn)
 
     rows_in.stage(3)
-    heads[0].step("far")
+    heads[0].step("near")
     mix_weight, proj_weight = rows_in.wholes[2]
     mixed = matmul(norm_attn, mix_weight)
     attended_lo, queries, key_rows, value_rows, log_totals = attend(
@@ -1146,7 +1217,6 @@
     )
 
     rows_in.stage(4)
-    heads[0].step("near")
     heads[1].step("far")
     expand_weight, conv_weight = rows_in.wholes[3]
     expanded = matmul(norm_conv, expand_weight)
@@ -1207,30 +1277,21 @@
     row_grads = lowered(row_sum.result())
     grad_output = out_grad.astype(jnp.float32) + matmul_tn(pick_lo, row_grads)
 
-    def outer_back(grad_in, act_lo):
-        grad_out_lo = lowered(0.5 * grad_in)
-        weight_grad = lowered(matmul_tn(act_lo, grad_out_lo))
-        return grad_out_lo, ("tall", [ffn_outer[0]], [weight_grad])
-
-    def inner_back(grad_out_lo, normed_lo, pre_act, outer_weight):
-        grad_pre = act_back(grad_out_lo, outer_weight, pre_act)
-        weight_grad = lowered(matmul_tn(normed_lo, grad_pre))
-        return grad_pre, ("wide", [ffn_inner[0]], [weight_grad])
-
     rows_out = Scatter(cube)
     grad_second, gain_grad_final = norm_back(after_second, gain_f[5], grad_output)
-    grad_out_lo, piece = outer_back(grad_second, act_second)
-    grad_second, grad_out_lo, piece[2][0] = fence(
-        [head_flow], grad_second, grad_out_lo, piece[2][0]
-    )
+    grad_out_lo = lowered(0.5 * grad_second)
+    piece = weight_grads(cube, "tall", [(act_second, grad_out_lo[None])])
+    grad_second, grad_out_lo, piece = fence([head_flow], grad_second, grad_out_lo, piece)
 
     head_flow.step()
-    rows_out.stage(piece)
-    grad_pre, piece = inner_back(grad_out_lo, norm_second, pre_second, outer_1)
+    rows_out.stage()
+    rows_out.push("tall", [ffn_outer[1]], piece)
+    grad_pre = act_back(grad_out_lo, outer_1, pre_second)
+    piece = weight_grads(cube, "wide", [(norm_second, grad_pre)])
     grad_conv_res, gain_grad_second = product_norm_back(
         grad_pre, inner_1, after_conv, vectors, 4, grad_second
     )
-    grad_conv_res, piece[2][0] = fence([head_flow, rows_out], grad_conv_res, piece[2][0])
+    grad_conv_res, piece = fence([head_flow, rows_out], grad_conv_res, piece)
 
     conv_res_lo = lowered(grad_conv_res)
     grad_bn = silu_back(normed_bn, matmul_nt(conv_res_lo, conv_weight))
@@ -1246,63 +1307,62 @@
             + [jnp.zeros((D,), jnp.float32)] * 5
         )
     )
-    conv_proj_grad = lowered(matmul_tn(swish_lo, conv_res_lo))
-    back_sums, grad_normalized, grad_conv_res, conv_proj_grad = fence(
-        [],
-        back_sums,
-        grad_normalized,
-        grad_conv_res,
-        conv_proj_grad,
+    back_sums, grad_normalized, grad_conv_res, conv_res_lo, piece = fence(
+        [], back_sums, grad_normalized, grad_conv_res, conv_res_lo, piece
     )
 
     head_flow.step()
-    rows_out.stage(piece)
+    rows_out.stage()
+    rows_out.push("wide", [ffn_inner[1]], piece)
     loss = back_sums[2, 0] / loss_scale
-    grad_lead, grad_gate, depth_grad = conv_backward(
+    grad_expanded, depth_grad = conv_backward(
         expanded, valid_rows[:, None], vectors, conv_out, grad_normalized, sums, back_sums
     )
-    grad_expanded = jnp.concatenate([grad_lead, grad_gate], axis=1)
-    expand_grad = lowered(matmul_tn(norm_conv, grad_expanded))
-    grad_expanded, expand_grad = fence([rows_out, head_flow], grad_expanded, expand_grad)
-
-    rows_out.stage(("wide", [conv_expand, conv_proj], [expand_grad, conv_proj_grad]))
+    piece = weight_grads(cube, "wide", [(norm_conv, grad_expanded), (swish_lo, conv_res_lo[None])])
+    grad_expanded, piece = fence([rows_out, head_flow], grad_expanded, piece)
+
+    rows_out.stage()
+    rows_out.push("wide", [conv_expand, conv_proj], piece)
     grad_attn_res, gain_grad_conv = product_norm_back(
         grad_expanded, expand_weight, after_attention, vectors, 2, grad_conv_res
     )
     attn_res_lo = lowered(grad_attn_res)
-    proj_grad = lowered(matmul_tn(attended_lo, attn_res_lo))
     grad_attended = lowered(matmul_nt(attn_res_lo, proj_weight))
-    grad_mixed = jnp.concatenate(
-        attend_back(
-            queries,
-            key_rows,
-            value_rows,
-            log_totals,
-            grad_attended,
-            cosine,
-            sine_table,
-            valid_rows[None, :],
-        ),
-        axis=1,
-    )
-    grad_mixed, proj_grad, grad_attn_res = fence([rows_out], grad_mixed, proj_grad, grad_attn_res)
+    grad_mixed = attend_back(
+        queries,
+        key_rows,
+        value_rows,
+        log_totals,
+        grad_attended,
+        cosine,
+        sine_table,
+        valid_rows[None, :],
+    )
+    grad_mixed, attn_res_lo, grad_attn_res = fence(
+        [rows_out], grad_mixed, attn_res_lo, grad_attn_res
+    )
 
     rows_out.stage()
-    mix_grad = lowered(matmul_tn(norm_attn, grad_mixed))
+    piece = weight_grads(cube, "wide", [(norm_attn, grad_mixed), (attended_lo, attn_res_lo[None])])
     grad_first_res, gain_grad_attn = product_norm_back(
         grad_mixed, mix_weight, after_first, vectors, 1, grad_attn_res
     )
-    grad_first_res, mix_grad = fence([rows_out], grad_first_res, mix_grad)
-
-    rows_out.stage(("wide", [attn_qkv, attn_proj], [mix_grad, proj_grad]))
-    grad_out_lo, piece = outer_back(grad_first_res, act_first)
-    grad_out_lo, piece[2][0] = fence([rows_out], grad_out_lo, piece[2][0])
-
-    rows_out.stage(piece)
-    grad_pre, piece = inner_back(grad_out_lo, norm_first, pre_first, outer_0)
-    grad_pre, piece[2][0] = fence([rows_out], grad_pre, piece[2][0])
-
-    rows_out.stage(piece)
+    grad_out_lo = lowered(0.5 * grad_first_res)
+    grad_first_res, grad_out_lo, piece = fence([rows_out], grad_first_res, grad_out_lo, piece)
+
+    rows_out.stage()
+    rows_out.push("wide", [attn_qkv, attn_proj], piece)
+    piece = weight_grads(cube, "tall", [(act_first, grad_out_lo[None])])
+    grad_out_lo, piece = fence([rows_out], grad_out_lo, piece)
+
+    rows_out.stage()
+    rows_out.push("tall", [ffn_outer[0]], piece)
+    grad_pre = act_back(grad_out_lo, outer_0, pre_first)
+    piece = weight_grads(cube, "wide", [(norm_first, grad_pre)])
+    grad_pre, piece = fence([rows_out], grad_pre, piece)
+
+    rows_out.stage()
+    rows_out.push("wide", [ffn_inner[0]], piece)
     input_grad, gain_grad_first = product_norm_back(
         grad_pre, inner_0, inputs, vectors, 0, grad_first_res
     )

time: 815 us -> 790 us (0.969)
  matrix products: 93.5 us -> 50.2 us
  Pallas kernels: 183 us -> 211 us
  starting transfers between devices: 117 us -> 108 us
  waiting for transfers between devices: 327 us -> 336 us
    pallas_call x0 -> x6, Pallas kernels: none -> 40.9 us  [the longest x4 26.5 us: weight_grads(): pl.pallas_call(functools.partial(weight_grads_kernel, counts), grid=(COLU...]
    dot_general x10 -> x2, matrix products: 46.7 us -> 5.99 us  [matmul_tn(): lax.dot_general(operand, weight, (((0,), (0,)), ((), ())), preferred_elem...]
    pallas_call x44 -> x38, Pallas kernels: 36.5 us -> 25.4 us  [local_copies(): pl.pallas_call(kernel, out_shape=[jax.ShapeDtypeStruct(shape, inputs[0].d...]
    ppermute x106, starting transfers between devices: 117 us -> 108 us  [swap(): lax.ppermute(values, axis, [(i, i ^ bit) for i in range(self.sizes[axis])])]
    ppermute x106, waiting for transfers between devices: 327 us -> 336 us  [swap(): lax.ppermute(values, axis, [(i, i ^ bit) for i in range(self.sizes[axis])])]
    unnamed x304 -> x247, local copies, waits for them, and re-layouts: 47 us -> 39.4 us
  transfers between devices with their start and end apart: 106 -> 106, of which waited for: 55 -> 62; matrix products, arithmetic and copies ran while one was open for 13% -> 7% of each run, Pallas kernels for 16% -> 24%
where the time goes in v6:
time: 790 us; the launch traced here: 780 us
  waiting for transfers between devices  336 us (43%)
  Pallas kernels  211 us (27%)
  starting transfers between devices  108 us (14%)
  matrix products  50.2 us (6%)
  local copies, waits for them, and re-layouts  48.4 us (6%)
  other arithmetic  19.7 us (2%)
    ppermute x106, waiting for transfers between devices, swap(): lax.ppermute(values, axis, [(i, i ^ bit) for i in range(self.sizes[axis])])  336 us
    ppermute x106, starting transfers between devices, swap(): lax.ppermute(values, axis, [(i, i ^ bit) for i in range(self.sizes[axis])])  108 us
    pallas_call x20, Pallas kernels, sums(): pl.pallas_call(kernel, grid_spec=pltpu.PrefetchScalarGridSpec(num_scalar_...  40 us
    unnamed x247, local copies, waits for them, and re-layouts  39.4 us
    dot_general x10, matrix products, matmul(): return jnp.dot(operand, weight, preferred_element_type=jnp.float32)  35.8 us
    pallas_call x4, Pallas kernels, product_norm_back(): pl.pallas_call(functools.partial(norm_back_kernel, row), grid=(inner // w...  32.1 us
    pallas_call x4, Pallas kernels, weight_grads(): pl.pallas_call(functools.partial(weight_grads_kernel, counts), grid=(COLU...  26.5 us
    pallas_call x38, Pallas kernels, local_copies(): pl.pallas_call(kernel, out_shape=[jax.ShapeDtypeStruct(shape, inputs[0].d...  25.4 us
  transfers between devices with their start and end apart: 106, of which 62 were waited for; matrix products, arithmetic and copies ran while one was open for 7% of the time, Pallas kernels for 24%

profile of v6, /device:TPU:0, one launch (start us, length us, event | category | flops | bytes accessed | tf_op | source)
XLA Modules:
  0.0 780.0 jit_solution(8597787923083646761)
XLA Ops:
  16.0 8.5 %collective-permute-done.2.refs_1_ = bf16[2,48,32]{2,1,0:T(8,128)(2,1)S(1)} collective-permute-done((bf16[2,48,32]{2,1,0:T(8,128)(2,1)S(1)}, bf16[2,48,32]{2,1,0:T(8,128)(2,1)S(1)}, u32[]{:S(2)}, u32[]{:S(2)}) %collective-permute-start.2) | collective-permute-done | bytes 6176 | tf_op jit(solution)/shard_map/ppermute | solution.py:114
  29.2 17.0 %collective-permute-done.9.refs_1_ = bf16[2,2,48,32]{3,2,1,0:T(8,128)(2,1)S(1)} collective-permute-done((bf16[2,2,48,32]{3,2,1,0:T(8,128)(2,1)S(1)}, bf16[2,2,48,32]{3,2,1,0:T(8,128)(2,1)S(1)}, u32[]{:S(2)}, u32[]{:S(2)}) %collective-permute-start.9) | collective-permute-done | bytes 12320 | tf_op jit(solution)/shard_map/ppermute | solution.py:114
  52.9 8.3 %collective-permute-done.14.refs_1_ = bf16[2,2,2,48,32]{4,3,2,1,0:T(8,128)(2,1)S(1)} collective-permute-done((bf16[2,2,2,48,32]{4,3,2,1,0:T(8,128)(2,1)S(1)}, bf16[2,2,2,48,32]{4,3,2,1,0:T(8,128)(2,1)S(1)}, u32[]{:S(2)}, u32[]{:S(2)}) %collective-permute-start.14) | collective-permute-done | bytes 24608 | tf_op jit(solution)/shard_map/ppermute | solution.py:114
  73.7 31.3 %collective-permute-done.19.refs_1_ = bf16[2,2,2,2,48,32]{5,4,3,2,1,0:T(8,128)(2,1)S(1)} collective-permute-done((bf16[2,2,2,2,48,32]{5,4,3,2,1,0:T(8,128)(2,1)S(1)}, bf16[2,2,2,2,48,32]{5,4,3,2,1,0:T(8,128)(2,1)S(1)}, u32[]{:S(2)}, u32[]{:S(2)}) %collective-permute-start.19) | collective-permute-done | bytes 49184 | tf_op jit(solution)/shard_map/ppermute | solution.py:114
  108.0 8.6 %collective-permute-done.18.refs_1_ = bf16[32,4096]{1,0:T(8,128)(2,1)S(1)} collective-permute-done((bf16[32,4096]{1,0:T(8,128)(2,1)S(1)}, bf16[32,4096]{1,0:T(8,128)(2,1)S(1)}, u32[]{:S(2)}, u32[]{:S(2)}) %collective-permute-start.18) | collective-permute-done | bytes 262176 | tf_op jit(solution)/shard_map/ppermute | solution.py:114
  142.1 13.1 %collective-permute-done.21.refs_3_ = bf16[2,2,3,32,2048]{4,3,2,1,0:T(8,128)(2,1)S(1)} collective-permute-done((bf16[2,2,3,32,2048]{4,3,2,1,0:T(8,128)(2,1)S(1)}, bf16[2,2,3,32,2048]{4,3,2,1,0:T(8,128)(2,1)S(1)}, u32[]{:S(2)}, u32[]{:S(2)}) %collective-permute-start.21) | collective-permute-done | bytes 1572896 | tf_op jit(solution)/shard_map/ppermute | solution.py:114
  178.5 18.3 %collective-permute-done.26.refs_3_ = bf16[2,2,3,32,2048]{4,3,2,1,0:T(8,128)(2,1)S(1)} collective-permute-done((bf16[2,2,3,32,2048]{4,3,2,1,0:T(8,128)(2,1)S(1)}, bf16[2,2,3,32,2048]{4,3,2,1,0:T(8,128)(2,1)S(1)}, u32[]{:S(2)}, u32[]{:S(2)}) %collective-permute-start.26) | collective-permute-done | bytes 1572896 | tf_op jit(solution)/shard_map/ppermute | solution.py:114
  210.5 12.7 %shard_map.270 = (bf16[512,1024]{1,0:T(8,128)(2,1)S(1)}, bf16[512,1024]{1,0:T(8,128)(2,1)S(1)}, bf16[512,1024]{1,0:T(8,128)(2,1)S(1)}, bf16[512,1024]{1,0:T(8,128)(2,1)S(1)}, f32[512,1024]{1,0:T(8,128)S(1)}) custom-call(f32[512,3072]{1,0:T(8,128)S(1)} %fusion.26.query_ref.key_ref.value_ref, f32[512,3072]{1,0:T(8,128)S(1)} %fusion.26.query_ref.key_ref.value_ref, ...), custom_call_target="tpu_custom_call" | custom-call | tf_op jit(solution)/shard_map/pallas_call | solution.py:1030
  226.5 10.2 %collective-permute-done.33.refs_5_ = bf16[2,32,4096]{2,1,0:T(8,128)(2,1)S(1)} collective-permute-done((bf16[2,32,4096]{2,1,0:T(8,128)(2,1)S(1)}, bf16[2,32,4096]{2,1,0:T(8,128)(2,1)S(1)}, u32[]{:S(2)}, u32[]{:S(2)}) %collective-permute-start.33) | collective-permute-done | bytes 524320 | tf_op jit(solution)/shard_map/ppermute | solution.py:114
  251.1 10.9 %shard_map.275 = (f32[512,1024]{1,0:T(8,128)S(1)}, f32[8,1024]{1,0:T(8,128)S(1)}) custom-call(f32[512,2048]{1,0:T(8,128)S(1)} %fusion.27.lead_ref.gate_ref, f32[512,2048]{1,0:T(8,128)S(1)} %fusion.27.lead_ref.gate_ref, f32[512,1]{1,0:T(8,128)S(1)} %fusion.5.valid_ref, f32[48,1024]{1,0:T(8,128)S(1)} %shard_map.260.taps_ref.vectors_ref), custom_call_target="tpu_custom_call" | custom-call | tf_op jit(solution)/shard_map/pallas_call | solution.py:697
  299.0 13.1 %collective-permute-done.47.refs_3_ = bf16[2,2,128,1024]{3,2,1,0:T(8,128)(2,1)} collective-permute-done((bf16[2,2,128,1024]{3,2,1,0:T(8,128)(2,1)S(1)}, bf16[2,2,128,1024]{3,2,1,0:T(8,128)(2,1)}, u32[]{:S(2)}, u32[]{:S(2)}) %collective-permute-start.47) | collective-permute-done | bytes 1048608 | tf_op jit(solution)/shard_map/ppermute | solution.py:114
  330.2 11.0 %collective-permute-done.50.refs_1_ = bf16[200,1024]{1,0:T(8,128)(2,1)S(1)} collective-permute-done((bf16[200,1024]{1,0:T(8,128)(2,1)S(1)}, bf16[200,1024]{1,0:T(8,128)(2,1)S(1)}, u32[]{:S(2)}, u32[]{:S(2)}) %collective-permute-start.50) | collective-permute-done | bytes 409632 | tf_op jit(solution)/shard_map/ppermute | solution.py:114
  438.7 9.0 %shard_map.295 = (f32[512,1024]{1,0:T(8,128)S(1)}, f32[1,1024]{1,0:T(1,128)S(1)}) custom-call(bf16[4,512,1024]{2,1,0:T(8,128)(2,1)S(1)} %shard_map.294.grad_ref.refs_1_, bf16[1024,4096]{1,0:T(8,128)(2,1)S(1)} %bitcast.121, f32[512,1024]{1,0:T(8,128)S(1)} %copy-done.15, f32[48,1024]{1,0:T(8,128)S(1)} %shard_map.260.taps_ref.vectors_ref, ...), custom_call_target="tpu_custom_call" | custom-call | tf_op jit(solution)/shard_map/pallas_call | solution.py:982
  487.5 15.3 %shard_map.301 = (bf16[2,512,1024]{2,1,0:T(8,128)(2,1)S(1)}, f32[32,1024]{1,0:T(8,128)S(1)}) custom-call(f32[512,2048]{1,0:T(8,128)S(1)} %copy-done.3, f32[512,2048]{1,0:T(8,128)S(1)} %copy-done.3, f32[512,1]{1,0:T(8,128)S(1)} %copy-done.56, f32[48,1024]{1,0:T(8,128)S(1)} %shard_map.260.taps_ref.vectors_ref, f32[512,1024]{1,0:T(8,128)S(1)} %copy-done.18, ...), custom_call_target="tpu_custom_call" | custom-call | tf_op jit(solution)/shard_map/pallas_call | solution.py:781
  527.6 12.8 %shard_map.306.grad_ref.refs_2_ = bf16[3,512,1024]{2,1,0:T(8,128)(2,1)S(1)} custom-call(bf16[512,1024]{1,0:T(8,128)(2,1)S(1)} %copy-done.75, bf16[512,1024]{1,0:T(8,128)(2,1)S(1)} %copy-done.77, bf16[512,1024]{1,0:T(8,128)(2,1)S(1)} %copy-done.79, f32[512,1024]{1,0:T(8,128)S(1)} %copy-done.69, bf16[512,1024]{1,0:T(8,128)(2,1)S(1)} %convolution_convert_fusion.2.grad_ref, ...), custom_call_target="tpu_custom_call" | custom-call | tf_op jit(solution)/shard_map/pallas_call | solution.py:1070
  540.4 8.5 %collective-permute-done.72.refs_7_.refs_9_ = bf16[2,2,3,32,2048]{4,3,2,1,0:T(8,128)(2,1)S(1)} collective-permute-done((bf16[2,2,3,32,2048]{4,3,2,1,0:T(8,128)(2,1)S(1)}, bf16[2,2,3,32,2048]{4,3,2,1,0:T(8,128)(2,1)S(1)}, u32[]{:S(2)}, u32[]{:S(2)}) %collective-permute-start.72) | collective-permute-done | bytes 1572896 | tf_op jit(solution)/shard_map/ppermute | solution.py:114
  571.4 16.1 %collective-permute-done.74.refs_3_.refs_5_ = bf16[2,2,3,32,2048]{4,3,2,1,0:T(8,128)(2,1)S(1)} collective-permute-done((bf16[2,2,3,32,2048]{4,3,2,1,0:T(8,128)(2,1)S(1)}, bf16[2,2,3,32,2048]{4,3,2,1,0:T(8,128)(2,1)S(1)}, u32[]{:S(2)}, u32[]{:S(2)}) %collective-permute-start.74) | collective-permute-done | bytes 1572896 | tf_op jit(solution)/shard_map/ppermute | solution.py:114
  651.8 10.3 %shard_map.320 = (f32[512,1024]{1,0:T(8,128)}, f32[1,1024]{1,0:T(1,128)S(1)}) custom-call(bf16[4,512,1024]{2,1,0:T(8,128)(2,1)S(1)} %shard_map.316.refs_1_.grad_ref, bf16[1024,4096]{1,0:T(8,128)(2,1)S(1)} %bitcast.115, f32[512,1024]{1,0:T(8,128)S(1)} %convert_element_type.162.values_ref, f32[48,1024]{1,0:T(8,128)S(1)} %shard_map.260.taps_ref.vectors_ref, ...), custom_call_target="tpu_custom_call" | custom-call | tf_op jit(solution)/shard_map/pallas_call | solution.py:982
  669.6 15.6 %collective-permute-done.92.refs_1_ = f32[2,2,2,38,32]{4,3,2,1,0:T(8,128)S(1)} collective-permute-done((f32[2,2,2,38,32]{4,3,2,1,0:T(8,128)S(1)}, f32[2,2,2,38,32]{4,3,2,1,0:T(8,128)S(1)}, u32[]{:S(2)}, u32[]{:S(2)}) %collective-permute-start.92) | collective-permute-done | bytes 38944 | tf_op jit(solution)/shard_map/ppermute | solution.py:114
  695.5 9.7 %collective-permute-done.95.refs_9_ = bf16[2,32,4096]{2,1,0:T(8,128)(2,1)S(1)} collective-permute-done((bf16[2,32,4096]{2,1,0:T(8,128)(2,1)S(1)}, bf16[2,32,4096]{2,1,0:T(8,128)(2,1)S(1)}, u32[]{:S(2)}, u32[]{:S(2)}) %collective-permute-start.95) | collective-permute-done | bytes 524320 | tf_op jit(solution)/shard_map/ppermute | solution.py:114
  705.2 18.1 %collective-permute-done.93.refs_3_.refs_5_ = bf16[2,2,3,32,2048]{4,3,2,1,0:T(8,128)(2,1)S(1)} collective-permute-done((bf16[2,2,3,32,2048]{4,3,2,1,0:T(8,128)(2,1)S(1)}, bf16[2,2,3,32,2048]{4,3,2,1,0:T(8,128)(2,1)S(1)}, u32[]{:S(2)}, u32[]{:S(2)}) %collective-permute-start.93) | collective-permute-done | bytes 1572896 | tf_op jit(solution)/shard_map/ppermute | solution.py:114
  734.0 9.2 %collective-permute-done.97 = bf16[32,4096]{1,0:T(8,128)(2,1)S(1)} collective-permute-done((bf16[32,4096]{1,0:T(8,128)(2,1)S(1)}, bf16[32,4096]{1,0:T(8,128)(2,1)S(1)}, u32[]{:S(2)}, u32[]{:S(2)}) %collective-permute-start.97) | collective-permute-done | bytes 262176 | tf_op jit(solution)/shard_map/ppermute | solution.py:114
  751.0 9.5 %collective-permute-done.102 = bf16[32,4096]{1,0:T(8,128)(2,1)S(1)} collective-permute-done((bf16[32,4096]{1,0:T(8,128)(2,1)S(1)}, bf16[32,4096]{1,0:T(8,128)(2,1)S(1)}, u32[]{:S(2)}, u32[]{:S(2)}) %collective-permute-start.102) | collective-permute-done | bytes 262176 | tf_op jit(solution)/shard_map/ppermute | solution.py:114
  766.6 9.5 %collective-permute-done.105 = bf16[32,4096]{1,0:T(8,128)(2,1)S(1)} collective-permute-done((bf16[32,4096]{1,0:T(8,128)(2,1)S(1)}, bf16[32,4096]{1,0:T(8,128)(2,1)S(1)}, u32[]{:S(2)}, u32[]{:S(2)}) %collective-permute-start.105) | collective-permute-done | bytes 262176 | tf_op jit(solution)/shard_map/ppermute | solution.py:114
  (651 shorter events, 466.7 us)
Async XLA Ops:
  66.6 50.0 %collective-permute-start.15 = (bf16[2,2,3,32,2048]{4,3,2,1,0:T(8,128)(2,1)S(1)}, bf16[2,2,3,32,2048]{4,3,2,1,0:T(8,128)(2,1)S(1)}, u32[]{:S(2)}, u32[]{:S(2)}) collective-permute-start(bf16[2,2,3,32,2048]{4,3,2,1,0:T(8,128)(2,1)S(1)} %get-tuple-element.401.refs_2_), channel_id=1, source_target_pairs={{0,4},{4,0},{8,12},{12,8},{16,20},{20,16},{24,28},{28,24},{1,5},{5... | collective-permute-start | bytes 4718600 | tf_op jit(solution)/shard_map/ppermute | solution.py:114
  67.2 49.4 %collective-permute-start.16 = (bf16[2,2,3,32,2048]{4,3,2,1,0:T(8,128)(2,1)S(1)}, bf16[2,2,3,32,2048]{4,3,2,1,0:T(8,128)(2,1)S(1)}, u32[]{:S(2)}, u32[]{:S(2)}) collective-permute-start(bf16[2,2,3,32,2048]{4,3,2,1,0:T(8,128)(2,1)S(1)} %get-tuple-element.403.refs_4_.refs_0_), channel_id=1, source_target_pairs={{0,2},{1,3},{2,0},{3,1},{4,6},{5,7},{6,4},{7,5},{8,10},{9,11},{10,... | collective-permute-start | bytes 4718600 | tf_op jit(solution)/shard_map/ppermute | solution.py:114
  68.9 47.7 %collective-permute-start.20 = (bf16[2,128,1024]{2,1,0:T(8,128)(2,1)S(1)}, bf16[2,128,1024]{2,1,0:T(8,128)(2,1)S(1)}, u32[]{:S(2)}, u32[]{:S(2)}) collective-permute-start(bf16[2,128,1024]{2,1,0:T(8,128)(2,1)S(1)} %shard_map.258.refs_0_), channel_id=1, source_target_pairs={{0,16},{4,20},{8,24},{12,28},{16,0},{20,4},{24,8},{28,12},{1,17},{... | collective-permute-start | bytes 1572872 | tf_op jit(solution)/shard_map/ppermute | solution.py:114
  72.0 44.6 %collective-permute-start.17 = (bf16[2,32,4096]{2,1,0:T(8,128)(2,1)S(1)}, bf16[2,32,4096]{2,1,0:T(8,128)(2,1)S(1)}, u32[]{:S(2)}, u32[]{:S(2)}) collective-permute-start(bf16[2,32,4096]{2,1,0:T(8,128)(2,1)S(1)} %get-tuple-element.405.refs_6_), channel_id=1, source_target_pairs={{0,8},{4,12},{8,0},{12,4},{16,24},{20,28},{24,16},{28,20},{1,9},{5... | collective-permute-start | bytes 1572872 | tf_op jit(solution)/shard_map/ppermute | solution.py:114
  119.0 36.2 %collective-permute-start.21 = (bf16[2,2,3,32,2048]{4,3,2,1,0:T(8,128)(2,1)S(1)}, bf16[2,2,3,32,2048]{4,3,2,1,0:T(8,128)(2,1)S(1)}, u32[]{:S(2)}, u32[]{:S(2)}) collective-permute-start(bf16[2,2,3,32,2048]{4,3,2,1,0:T(8,128)(2,1)S(1)} %get-tuple-element.413.refs_4_.refs_2_), channel_id=1, source_target_pairs={{0,4},{4,0},{8,12},{12,8},{16,20},{20,16},{24,28},{28,24},{1,5},{5... | collective-permute-start | bytes 4718600 | tf_op jit(solution)/shard_map/ppermute | solution.py:114
  120.7 35.9 %collective-permute-start.22 = (bf16[2,2,3,32,2048]{4,3,2,1,0:T(8,128)(2,1)S(1)}, bf16[2,2,3,32,2048]{4,3,2,1,0:T(8,128)(2,1)S(1)}, u32[]{:S(2)}, u32[]{:S(2)}) collective-permute-start(bf16[2,2,3,32,2048]{4,3,2,1,0:T(8,128)(2,1)S(1)} %get-tuple-element.415.refs_4_.refs_0_), channel_id=1, source_target_pairs={{0,2},{1,3},{2,0},{3,1},{4,6},{5,7},{6,4},{7,5},{8,10},{9,11},{10,... | collective-permute-start | bytes 4718600 | tf_op jit(solution)/shard_map/ppermute | solution.py:114
  160.3 36.5 %collective-permute-start.26 = (bf16[2,2,3,32,2048]{4,3,2,1,0:T(8,128)(2,1)S(1)}, bf16[2,2,3,32,2048]{4,3,2,1,0:T(8,128)(2,1)S(1)}, u32[]{:S(2)}, u32[]{:S(2)}) collective-permute-start(bf16[2,2,3,32,2048]{4,3,2,1,0:T(8,128)(2,1)S(1)} %get-tuple-element.425.refs_4_.refs_2_), channel_id=1, source_target_pairs={{0,4},{4,0},{8,12},{12,8},{16,20},{20,16},{24,28},{28,24},{1,5},{5... | collective-permute-start | bytes 4718600 | tf_op jit(solution)/shard_map/ppermute | solution.py:114
  160.9 36.2 %collective-permute-start.27 = (bf16[2,2,3,32,2048]{4,3,2,1,0:T(8,128)(2,1)S(1)}, bf16[2,2,3,32,2048]{4,3,2,1,0:T(8,128)(2,1)S(1)}, u32[]{:S(2)}, u32[]{:S(2)}) collective-permute-start(bf16[2,2,3,32,2048]{4,3,2,1,0:T(8,128)(2,1)S(1)} %get-tuple-element.427.refs_4_.refs_0_), channel_id=1, source_target_pairs={{0,2},{1,3},{2,0},{3,1},{4,6},{5,7},{6,4},{7,5},{8,10},{9,11},{10,... | collective-permute-start | bytes 4718600 | tf_op jit(solution)/shard_map/ppermute | solution.py:114
  201.4 36.5 %collective-permute-start.31 = (bf16[2,2,3,32,2048]{4,3,2,1,0:T(8,128)(2,1)S(1)}, bf16[2,2,3,32,2048]{4,3,2,1,0:T(8,128)(2,1)S(1)}, u32[]{:S(2)}, u32[]{:S(2)}) collective-permute-start(bf16[2,2,3,32,2048]{4,3,2,1,0:T(8,128)(2,1)S(1)} %get-tuple-element.445.refs_4_.refs_0_.refs_2_), channel_id=1, source_target_pairs={{0,4},{4,0},{8,12},{12,8},{16,20},{20,16},{24,28},{28,24},{1,5},{5... | collective-permute-start | bytes 4718600 | tf_op jit(solution)/shard_map/ppermute | solution.py:114
  202.9 36.2 %collective-permute-start.32 = (bf16[2,2,3,32,2048]{4,3,2,1,0:T(8,128)(2,1)S(1)}, bf16[2,2,3,32,2048]{4,3,2,1,0:T(8,128)(2,1)S(1)}, u32[]{:S(2)}, u32[]{:S(2)}) collective-permute-start(bf16[2,2,3,32,2048]{4,3,2,1,0:T(8,128)(2,1)S(1)} %get-tuple-element.447.refs_2_.refs_0_), channel_id=1, source_target_pairs={{0,2},{1,3},{2,0},{3,1},{4,6},{5,7},{6,4},{7,5},{8,10},{9,11},{10,... | collective-permute-start | bytes 4718600 | tf_op jit(solution)/shard_map/ppermute | solution.py:114
  240.1 41.7 %collective-permute-start.36 = (bf16[2,2,3,32,2048]{4,3,2,1,0:T(8,128)(2,1)S(1)}, bf16[2,2,3,32,2048]{4,3,2,1,0:T(8,128)(2,1)S(1)}, u32[]{:S(2)}, u32[]{:S(2)}) collective-permute-start(bf16[2,2,3,32,2048]{4,3,2,1,0:T(8,128)(2,1)S(1)} %get-tuple-element.462.refs_4_.refs_0_.refs_2_), channel_id=1, source_target_pairs={{0,4},{4,0},{8,12},{12,8},{16,20},{20,16},{24,28},{28,24},{1,5},{5... | collective-permute-start | bytes 4718600 | tf_op jit(solution)/shard_map/ppermute | solution.py:114
  240.7 41.1 %collective-permute-start.37 = (bf16[2,2,3,32,2048]{4,3,2,1,0:T(8,128)(2,1)S(1)}, bf16[2,2,3,32,2048]{4,3,2,1,0:T(8,128)(2,1)S(1)}, u32[]{:S(2)}, u32[]{:S(2)}) collective-permute-start(bf16[2,2,3,32,2048]{4,3,2,1,0:T(8,128)(2,1)S(1)} %get-tuple-element.464.refs_2_.refs_0_), channel_id=1, source_target_pairs={{0,2},{1,3},{2,0},{3,1},{4,6},{5,7},{6,4},{7,5},{8,10},{9,11},{10,... | collective-permute-start | bytes 4718600 | tf_op jit(solution)/shard_map/ppermute | solution.py:114
  242.5 39.3 %collective-permute-start.38 = (bf16[2,128,1024]{2,1,0:T(8,128)(2,1)S(1)}, bf16[2,128,1024]{2,1,0:T(8,128)(2,1)S(1)}, u32[]{:S(2)}, u32[]{:S(2)}) collective-permute-start(bf16[2,128,1024]{2,1,0:T(8,128)(2,1)S(1)} %shard_map.272.refs_0_), channel_id=1, source_target_pairs={{0,16},{4,20},{8,24},{12,28},{16,0},{20,4},{24,8},{28,12},{1,17},{... | collective-permute-start | bytes 1572872 | tf_op jit(solution)/shard_map/ppermute | solution.py:114
  402.7 45.0 %collective-permute-start.60 = (bf16[2,2,2,2,32,4096]{5,4,3,2,1,0:T(8,128)(2,1)}, bf16[2,2,2,2,32,4096]{5,4,3,2,1,0:T(8,128)(2,1)}, u32[]{:S(2)}, u32[]{:S(2)}) collective-permute-start(bf16[2,2,2,2,32,4096]{5,4,3,2,1,0:T(8,128)(2,1)} %get-tuple-element.505), channel_id=1, source_target_pairs={{0,1},{1,0},{2,3},{3,2},{4,5},{5,4},{6,7},{7,6},{8,9},{9,8},{10,11... | collective-permute-start | bytes 12582920 | tf_op jit(solution)/shard_map/ppermute | solution.py:114
  404.4 43.3 %collective-permute-start.59 = (bf16[2,128,1024]{2,1,0:T(8,128)(2,1)}, bf16[2,128,1024]{2,1,0:T(8,128)(2,1)}, u32[]{:S(2)}, u32[]{:S(2)}) collective-permute-start(bf16[2,128,1024]{2,1,0:T(8,128)(2,1)} %get-tuple-element.504), channel_id=1, source_target_pairs={{0,16},{4,20},{8,24},{12,28},{16,0},{20,4},{24,8},{28,12},{1,17},{... | collective-permute-start | bytes 1572872 | tf_op jit(solution)/shard_map/ppermute | solution.py:114
  408.5 39.2 %collective-permute-start.58 = (bf16[2,128,1024]{2,1,0:T(8,128)(2,1)}, bf16[2,128,1024]{2,1,0:T(8,128)(2,1)}, u32[]{:S(2)}, u32[]{:S(2)}) collective-permute-start(bf16[2,128,1024]{2,1,0:T(8,128)(2,1)} %get-tuple-element.500), channel_id=1, source_target_pairs={{0,8},{4,12},{8,0},{12,4},{16,24},{20,28},{24,16},{28,20},{1,9},{5... | collective-permute-start | bytes 1572872 | tf_op jit(solution)/shard_map/ppermute | solution.py:114
  471.6 36.9 %collective-permute-start.66 = (bf16[2,2,2,2,32,4096]{5,4,3,2,1,0:T(8,128)(2,1)}, bf16[2,2,2,2,32,4096]{5,4,3,2,1,0:T(8,128)(2,1)}, u32[]{:S(2)}, u32[]{:S(2)}) collective-permute-start(bf16[2,2,2,2,32,4096]{5,4,3,2,1,0:T(8,128)(2,1)} %copy-done.98), channel_id=1, source_target_pairs={{0,1},{1,0},{2,3},{3,2},{4,5},{5,4},{6,7},{7,6},{8,9},{9,8},{10,11... | collective-permute-start | bytes 12582920 | tf_op jit(solution)/shard_map/ppermute | solution.py:114
  508.6 41.2 %collective-permute-start.71 = (bf16[2,2,2,2,32,4096]{5,4,3,2,1,0:T(8,128)(2,1)S(1)}, bf16[2,2,2,2,32,4096]{5,4,3,2,1,0:T(8,128)(2,1)S(1)}, u32[]{:S(2)}, u32[]{:S(2)}) collective-permute-start(bf16[2,2,2,2,32,4096]{5,4,3,2,1,0:T(8,128)(2,1)S(1)} %get-tuple-element.553), channel_id=1, source_target_pairs={{0,1},{1,0},{2,3},{3,2},{4,5},{5,4},{6,7},{7,6},{8,9},{9,8},{10,11... | collective-permute-start | bytes 12582920 | tf_op jit(solution)/shard_map/ppermute | solution.py:114
  512.1 36.8 %collective-permute-start.72 = (bf16[2,2,3,32,2048]{4,3,2,1,0:T(8,128)(2,1)S(1)}, bf16[2,2,3,32,2048]{4,3,2,1,0:T(8,128)(2,1)S(1)}, u32[]{:S(2)}, u32[]{:S(2)}) collective-permute-start(bf16[2,2,3,32,2048]{4,3,2,1,0:T(8,128)(2,1)S(1)} %get-tuple-element.548.refs_8_), channel_id=1, source_target_pairs={{0,4},{4,0},{8,12},{12,8},{16,20},{20,16},{24,28},{28,24},{1,5},{5... | collective-permute-start | bytes 4718600 | tf_op jit(solution)/shard_map/ppermute | solution.py:114
  513.2 36.5 %collective-permute-start.73 = (bf16[2,2,3,32,2048]{4,3,2,1,0:T(8,128)(2,1)S(1)}, bf16[2,2,3,32,2048]{4,3,2,1,0:T(8,128)(2,1)S(1)}, u32[]{:S(2)}, u32[]{:S(2)}) collective-permute-start(bf16[2,2,3,32,2048]{4,3,2,1,0:T(8,128)(2,1)S(1)} %get-tuple-element.555), channel_id=1, source_target_pairs={{0,2},{1,3},{2,0},{3,1},{4,6},{5,7},{6,4},{7,5},{8,10},{9,11},{10,... | collective-permute-start | bytes 4718600 | tf_op jit(solution)/shard_map/ppermute | solution.py:114
  641.3 44.2 %collective-permute-start.87 = (bf16[2,2,2,2,32,4096]{5,4,3,2,1,0:T(8,128)(2,1)S(1)}, bf16[2,2,2,2,32,4096]{5,4,3,2,1,0:T(8,128)(2,1)S(1)}, u32[]{:S(2)}, u32[]{:S(2)}) collective-permute-start(bf16[2,2,2,2,32,4096]{5,4,3,2,1,0:T(8,128)(2,1)S(1)} %get-tuple-element.642), channel_id=1, source_target_pairs={{0,1},{1,0},{2,3},{3,2},{4,5},{5,4},{6,7},{7,6},{8,9},{9,8},{10,11... | collective-permute-start | bytes 12582920 | tf_op jit(solution)/shard_map/ppermute | solution.py:114
  648.5 36.8 %collective-permute-start.89 = (bf16[2,2,3,32,2048]{4,3,2,1,0:T(8,128)(2,1)}, bf16[2,2,3,32,2048]{4,3,2,1,0:T(8,128)(2,1)S(1)}, u32[]{:S(2)}, u32[]{:S(2)}) collective-permute-start(bf16[2,2,3,32,2048]{4,3,2,1,0:T(8,128)(2,1)} %get-tuple-element.637.refs_10_), channel_id=1, source_target_pairs={{0,4},{4,0},{8,12},{12,8},{16,20},{20,16},{24,28},{28,24},{1,5},{5... | collective-permute-start | bytes 4718600 | tf_op jit(solution)/shard_map/ppermute | solution.py:114
  649.3 36.2 %collective-permute-start.90 = (bf16[2,2,3,32,2048]{4,3,2,1,0:T(8,128)(2,1)S(1)}, bf16[2,2,3,32,2048]{4,3,2,1,0:T(8,128)(2,1)S(1)}, u32[]{:S(2)}, u32[]{:S(2)}) collective-permute-start(bf16[2,2,3,32,2048]{4,3,2,1,0:T(8,128)(2,1)S(1)} %get-tuple-element.646), channel_id=1, source_target_pairs={{0,2},{1,3},{2,0},{3,1},{4,6},{5,7},{6,4},{7,5},{8,10},{9,11},{10,... | collective-permute-start | bytes 4718600 | tf_op jit(solution)/shard_map/ppermute | solution.py:114
  687.5 35.9 %collective-permute-start.93 = (bf16[2,2,3,32,2048]{4,3,2,1,0:T(8,128)(2,1)S(1)}, bf16[2,2,3,32,2048]{4,3,2,1,0:T(8,128)(2,1)S(1)}, u32[]{:S(2)}, u32[]{:S(2)}) collective-permute-start(bf16[2,2,3,32,2048]{4,3,2,1,0:T(8,128)(2,1)S(1)} %get-tuple-element.668.refs_12_), channel_id=1, source_target_pairs={{0,4},{4,0},{8,12},{12,8},{16,20},{20,16},{24,28},{28,24},{1,5},{5... | collective-permute-start | bytes 4718600 | tf_op jit(solution)/shard_map/ppermute | solution.py:114
  (206 other events, 2376.6 us)

commit v7 on v6

--- a/solution.py
+++ b/solution.py
@@ -1284,7 +1284,6 @@
     grad_second, grad_out_lo, piece = fence([head_flow], grad_second, grad_out_lo, piece)
 
     head_flow.step()
-    rows_out.stage()
     rows_out.push("tall", [ffn_outer[1]], piece)
     grad_pre = act_back(grad_out_lo, outer_1, pre_second)
     piece = weight_grads(cube, "wide", [(norm_second, grad_pre)])
@@ -1338,31 +1337,22 @@
         sine_table,
         valid_rows[None, :],
     )
-    grad_mixed, attn_res_lo, grad_attn_res = fence(
-        [rows_out], grad_mixed, attn_res_lo, grad_attn_res
-    )
+    piece = weight_grads(cube, "wide", [(norm_attn, grad_mixed), (attended_lo, attn_res_lo[None])])
+    grad_mixed, grad_attn_res, piece = fence([rows_out], grad_mixed, grad_attn_res, piece)
 
     rows_out.stage()
-    piece = weight_grads(cube, "wide", [(norm_attn, grad_mixed), (attended_lo, attn_res_lo[None])])
+    rows_out.push("wide", [attn_qkv, attn_proj], piece)
     grad_first_res, gain_grad_attn = product_norm_back(
         grad_mixed, mix_weight, after_first, vectors, 1, grad_attn_res
     )
     grad_out_lo = lowered(0.5 * grad_first_res)
-    grad_first_res, grad_out_lo, piece = fence([rows_out], grad_first_res, grad_out_lo, piece)
-
-    rows_out.stage()
-    rows_out.push("wide", [attn_qkv, attn_proj], piece)
     piece = weight_grads(cube, "tall", [(act_first, grad_out_lo[None])])
-    grad_out_lo, piece = fence([rows_out], grad_out_lo, piece)
+    grad_pre = act_back(grad_out_lo, outer_0, pre_first)
+    grad_first_res, grad_pre, piece = fence([rows_out], grad_first_res, grad_pre, piece)
 
     rows_out.stage()
     rows_out.push("tall", [ffn_outer[0]], piece)
-    grad_pre = act_back(grad_out_lo, outer_0, pre_first)
     piece = weight_grads(cube, "wide", [(norm_first, grad_pre)])
-    grad_pre, piece = fence([rows_out], grad_pre, piece)
-
-    rows_out.stage()
-    rows_out.push("wide", [ffn_inner[0]], piece)
     input_grad, gain_grad_first = product_norm_back(
         grad_pre, inner_0, inputs, vectors, 0, grad_first_res
     )
@@ -1382,8 +1372,12 @@
         cube, vector_grad.reshape((2,) * len(cube.bits) + vector_grad.shape[1:]), hops
     )
     vector_flow.step()
+    input_grad, piece = fence([rows_out, vector_flow], input_grad, piece)
+
+    rows_out.stage()
+    rows_out.push("wide", [ffn_inner[0]], piece)
     vector_flow.step()
-    input_grad = fence([rows_out, vector_flow], input_grad)
+    fence([rows_out, vector_flow], loss)
 
     for _ in range(4):
         rows_out.stage()

time: 790 us -> 786 us (level)
  waiting for transfers between devices: 336 us -> 325 us
    ppermute x106 -> x104, waiting for transfers between devices: 336 us -> 325 us  [swap(): lax.ppermute(values, axis, [(i, i ^ bit) for i in range(self.sizes[axis])])]
    unnamed x247 -> x295, local copies, waits for them, and re-layouts: 39.4 us -> 43.9 us
    ppermute x106 -> x104, starting transfers between devices: 108 us -> 105 us  [swap(): lax.ppermute(values, axis, [(i, i ^ bit) for i in range(self.sizes[axis])])]
    pallas_call x20 -> x18, Pallas kernels: 40 us -> 40.4 us  [sums(): pl.pallas_call(kernel, grid_spec=pltpu.PrefetchScalarGridSpec(num_scalar_...]
  transfers between devices with their start and end apart: 106 -> 104, of which waited for: 62 -> 66; matrix products, arithmetic and copies ran while one was open for 7% -> 7% of each run, Pallas kernels for 24% -> 25%
where the time goes in v7:
time: 786 us; the launch traced here: 775 us
  waiting for transfers between devices  325 us (41%)
  Pallas kernels  214 us (27%)
  starting transfers between devices  105 us (13%)
  local copies, waits for them, and re-layouts  54.1 us (7%)
  matrix products  51.4 us (7%)
  other arithmetic  20 us (3%)
    ppermute x104, waiting for transfers between devices, swap(): lax.ppermute(values, axis, [(i, i ^ bit) for i in range(self.sizes[axis])])  325 us
    ppermute x104, starting transfers between devices, swap(): lax.ppermute(values, axis, [(i, i ^ bit) for i in range(self.sizes[axis])])  105 us
    unnamed x295, local copies, waits for them, and re-layouts  43.9 us
    pallas_call x18, Pallas kernels, sums(): pl.pallas_call(kernel, grid_spec=pltpu.PrefetchScalarGridSpec(num_scalar_...  40.4 us
    dot_general x10, matrix products, matmul(): return jnp.dot(operand, weight, preferred_element_type=jnp.float32)  35.8 us
    pallas_call x4, Pallas kernels, product_norm_back(): pl.pallas_call(functools.partial(norm_back_kernel, row), grid=(inner // w...  31.9 us
    pallas_call x4, Pallas kernels, weight_grads(): pl.pallas_call(functools.partial(weight_grads_kernel, counts), grid=(COLU...  28.5 us
    pallas_call x38, Pallas kernels, local_copies(): pl.pallas_call(kernel, out_shape=[jax.ShapeDtypeStruct(shape, inputs[0].d...  24.9 us
  transfers between devices with their start and end apart: 104, of which 66 were waited for; matrix products, arithmetic and copies ran while one was open for 7% of the time, Pallas kernels for 25%

profile of v7, /device:TPU:0, one launch (start us, length us, event | category | flops | bytes accessed | tf_op | source)
XLA Modules:
  0.0 775.4 jit_solution(4235825756814430954)
XLA Ops:
  16.7 7.9 %collective-permute-done.2.refs_1_ = bf16[2,48,32]{2,1,0:T(8,128)(2,1)S(1)} collective-permute-done((bf16[2,48,32]{2,1,0:T(8,128)(2,1)S(1)}, bf16[2,48,32]{2,1,0:T(8,128)(2,1)S(1)}, u32[]{:S(2)}, u32[]{:S(2)}) %collective-permute-start.2) | collective-permute-done | bytes 6176 | tf_op jit(solution)/shard_map/ppermute | solution.py:114
  29.3 17.0 %collective-permute-done.9.refs_1_ = bf16[2,2,48,32]{3,2,1,0:T(8,128)(2,1)S(1)} collective-permute-done((bf16[2,2,48,32]{3,2,1,0:T(8,128)(2,1)S(1)}, bf16[2,2,48,32]{3,2,1,0:T(8,128)(2,1)S(1)}, u32[]{:S(2)}, u32[]{:S(2)}) %collective-permute-start.9) | collective-permute-done | bytes 12320 | tf_op jit(solution)/shard_map/ppermute | solution.py:114
  53.0 8.3 %collective-permute-done.14.refs_1_ = bf16[2,2,2,48,32]{4,3,2,1,0:T(8,128)(2,1)S(1)} collective-permute-done((bf16[2,2,2,48,32]{4,3,2,1,0:T(8,128)(2,1)S(1)}, bf16[2,2,2,48,32]{4,3,2,1,0:T(8,128)(2,1)S(1)}, u32[]{:S(2)}, u32[]{:S(2)}) %collective-permute-start.14) | collective-permute-done | bytes 24608 | tf_op jit(solution)/shard_map/ppermute | solution.py:114
  73.8 31.3 %collective-permute-done.19.refs_1_ = bf16[2,2,2,2,48,32]{5,4,3,2,1,0:T(8,128)(2,1)S(1)} collective-permute-done((bf16[2,2,2,2,48,32]{5,4,3,2,1,0:T(8,128)(2,1)S(1)}, bf16[2,2,2,2,48,32]{5,4,3,2,1,0:T(8,128)(2,1)S(1)}, u32[]{:S(2)}, u32[]{:S(2)}) %collective-permute-start.19) | collective-permute-done | bytes 49184 | tf_op jit(solution)/shard_map/ppermute | solution.py:114
  108.1 8.6 %collective-permute-done.18.refs_1_ = bf16[32,4096]{1,0:T(8,128)(2,1)S(1)} collective-permute-done((bf16[32,4096]{1,0:T(8,128)(2,1)S(1)}, bf16[32,4096]{1,0:T(8,128)(2,1)S(1)}, u32[]{:S(2)}, u32[]{:S(2)}) %collective-permute-start.18) | collective-permute-done | bytes 262176 | tf_op jit(solution)/shard_map/ppermute | solution.py:114
  134.3 8.0 %collective-permute-done.23.refs_7_ = bf16[2,32,4096]{2,1,0:T(8,128)(2,1)S(1)} collective-permute-done((bf16[2,32,4096]{2,1,0:T(8,128)(2,1)S(1)}, bf16[2,32,4096]{2,1,0:T(8,128)(2,1)S(1)}, u32[]{:S(2)}, u32[]{:S(2)}) %collective-permute-start.23) | collective-permute-done | bytes 524320 | tf_op jit(solution)/shard_map/ppermute | solution.py:114
  142.3 13.1 %collective-permute-done.21.refs_3_ = bf16[2,2,3,32,2048]{4,3,2,1,0:T(8,128)(2,1)S(1)} collective-permute-done((bf16[2,2,3,32,2048]{4,3,2,1,0:T(8,128)(2,1)S(1)}, bf16[2,2,3,32,2048]{4,3,2,1,0:T(8,128)(2,1)S(1)}, u32[]{:S(2)}, u32[]{:S(2)}) %collective-permute-start.21) | collective-permute-done | bytes 1572896 | tf_op jit(solution)/shard_map/ppermute | solution.py:114
  178.9 18.3 %collective-permute-done.26.refs_3_ = bf16[2,2,3,32,2048]{4,3,2,1,0:T(8,128)(2,1)S(1)} collective-permute-done((bf16[2,2,3,32,2048]{4,3,2,1,0:T(8,128)(2,1)S(1)}, bf16[2,2,3,32,2048]{4,3,2,1,0:T(8,128)(2,1)S(1)}, u32[]{:S(2)}, u32[]{:S(2)}) %collective-permute-start.26) | collective-permute-done | bytes 1572896 | tf_op jit(solution)/shard_map/ppermute | solution.py:114
  210.9 12.8 %shard_map.270 = (bf16[512,1024]{1,0:T(8,128)(2,1)S(1)}, bf16[512,1024]{1,0:T(8,128)(2,1)S(1)}, bf16[512,1024]{1,0:T(8,128)(2,1)S(1)}, bf16[512,1024]{1,0:T(8,128)(2,1)S(1)}, f32[512,1024]{1,0:T(8,128)S(1)}) custom-call(f32[512,3072]{1,0:T(8,128)S(1)} %fusion.27.query_ref.key_ref.value_ref, f32[512,3072]{1,0:T(8,128)S(1)} %fusion.27.query_ref.key_ref.value_ref, ...), custom_call_target="tpu_custom_call" | custom-call | tf_op jit(solution)/shard_map/pallas_call | solution.py:1030
  227.0 10.1 %collective-permute-done.33.refs_5_ = bf16[2,32,4096]{2,1,0:T(8,128)(2,1)S(1)} collective-permute-done((bf16[2,32,4096]{2,1,0:T(8,128)(2,1)S(1)}, bf16[2,32,4096]{2,1,0:T(8,128)(2,1)S(1)}, u32[]{:S(2)}, u32[]{:S(2)}) %collective-permute-start.33) | collective-permute-done | bytes 524320 | tf_op jit(solution)/shard_map/ppermute | solution.py:114
  251.7 10.9 %shard_map.275 = (f32[512,1024]{1,0:T(8,128)S(1)}, f32[8,1024]{1,0:T(8,128)S(1)}) custom-call(f32[512,2048]{1,0:T(8,128)S(1)} %fusion.28.lead_ref.gate_ref, f32[512,2048]{1,0:T(8,128)S(1)} %fusion.28.lead_ref.gate_ref, f32[512,1]{1,0:T(8,128)S(1)} %fusion.6.valid_ref, f32[48,1024]{1,0:T(8,128)S(1)} %shard_map.260.taps_ref.vectors_ref), custom_call_target="tpu_custom_call" | custom-call | tf_op jit(solution)/shard_map/pallas_call | solution.py:697
  299.4 13.1 %collective-permute-done.47.refs_3_ = bf16[2,2,128,1024]{3,2,1,0:T(8,128)(2,1)} collective-permute-done((bf16[2,2,128,1024]{3,2,1,0:T(8,128)(2,1)S(1)}, bf16[2,2,128,1024]{3,2,1,0:T(8,128)(2,1)}, u32[]{:S(2)}, u32[]{:S(2)}) %collective-permute-start.47) | collective-permute-done | bytes 1048608 | tf_op jit(solution)/shard_map/ppermute | solution.py:114
  331.0 11.0 %collective-permute-done.50.refs_1_ = bf16[200,1024]{1,0:T(8,128)(2,1)S(1)} collective-permute-done((bf16[200,1024]{1,0:T(8,128)(2,1)S(1)}, bf16[200,1024]{1,0:T(8,128)(2,1)S(1)}, u32[]{:S(2)}, u32[]{:S(2)}) %collective-permute-start.50) | collective-permute-done | bytes 409632 | tf_op jit(solution)/shard_map/ppermute | solution.py:114
  417.7 7.9 %shard_map.294.grad_ref.refs_1_ = bf16[4,512,1024]{2,1,0:T(8,128)(2,1)S(1)} custom-call(bf16[512,1024]{1,0:T(8,128)(2,1)S(1)} %copy-done.21, bf16[4096,1024]{1,0:T(8,128)(2,1)S(1)} %bitcast.120, bf16[512,4096]{1,0:T(8,128)(2,1)S(1)} %copy-done.30), custom_call_target="tpu_custom_call" | custom-call | tf_op jit(solution)/shard_map/pallas_call | solution.py:828
  440.0 8.9 %shard_map.295 = (f32[512,1024]{1,0:T(8,128)S(1)}, f32[1,1024]{1,0:T(1,128)S(1)}) custom-call(bf16[4,512,1024]{2,1,0:T(8,128)(2,1)S(1)} %shard_map.294.grad_ref.refs_1_, bf16[1024,4096]{1,0:T(8,128)(2,1)S(1)} %bitcast.118, f32[512,1024]{1,0:T(8,128)S(1)} %copy-done.19, f32[48,1024]{1,0:T(8,128)S(1)} %shard_map.260.taps_ref.vectors_ref, ...), custom_call_target="tpu_custom_call" | custom-call | tf_op jit(solution)/shard_map/pallas_call | solution.py:982
  489.5 15.3 %shard_map.301 = (bf16[2,512,1024]{2,1,0:T(8,128)(2,1)S(1)}, f32[32,1024]{1,0:T(8,128)S(1)}) custom-call(f32[512,2048]{1,0:T(8,128)S(1)} %copy-done.3, f32[512,2048]{1,0:T(8,128)S(1)} %copy-done.3, f32[512,1]{1,0:T(8,128)S(1)} %fusion.6.valid_ref, f32[48,1024]{1,0:T(8,128)S(1)} %shard_map.260.taps_ref.vectors_ref, f32[512,1024]{1,0:T(8,128)S(1)} %copy-done.24, ...), custom_call_target="tpu_custom_call" | custom-call | tf_op jit(solution)/shard_map/pallas_call | solution.py:781
  530.0 12.7 %shard_map.306.refs_2_.grad_ref = bf16[3,512,1024]{2,1,0:T(8,128)(2,1)S(1)} custom-call(bf16[512,1024]{1,0:T(8,128)(2,1)S(1)} %copy-done.85, bf16[512,1024]{1,0:T(8,128)(2,1)S(1)} %copy-done.87, bf16[512,1024]{1,0:T(8,128)(2,1)S(1)} %copy-done.89, f32[512,1024]{1,0:T(8,128)S(1)} %copy-done.81, bf16[512,1024]{1,0:T(8,128)(2,1)S(1)} %convolution_convert_fusion.2.grad_ref, ...), custom_call_target="tpu_custom_call" | custom-call | tf_op jit(solution)/shard_map/pallas_call | solution.py:1070
  584.5 7.9 %shard_map.311.grad_ref.refs_1_ = bf16[4,512,1024]{2,1,0:T(8,128)(2,1)S(1)} custom-call(bf16[512,1024]{1,0:T(8,128)(2,1)S(1)} %multiply_convert_fusion.3.grad_ref, bf16[4096,1024]{1,0:T(8,128)(2,1)S(1)} %bitcast.116, bf16[512,4096]{1,0:T(8,128)(2,1)S(1)} %copy-done.29), custom_call_target="tpu_custom_call" | custom-call | tf_op jit(solution)/shard_map/pallas_call | solution.py:828
  604.8 10.3 %shard_map.315 = (f32[512,1024]{1,0:T(8,128)}, f32[1,1024]{1,0:T(1,128)S(1)}) custom-call(bf16[4,512,1024]{2,1,0:T(8,128)(2,1)S(1)} %shard_map.311.grad_ref.refs_1_, bf16[1024,4096]{1,0:T(8,128)(2,1)S(1)} %bitcast.114, f32[512,1024]{1,0:T(8,128)S(1)} %convert_element_type.162.values_ref, f32[48,1024]{1,0:T(8,128)S(1)} %shard_map.260.taps_ref.vectors_ref, ...), custom_call_target="tpu_custom_call" | custom-call | tf_op jit(solution)/shard_map/pallas_call | solution.py:982
  656.1 11.4 %collective-permute-done.85 = bf16[32,4096]{1,0:T(8,128)(2,1)S(1)} collective-permute-done((bf16[32,4096]{1,0:T(8,128)(2,1)S(1)}, bf16[32,4096]{1,0:T(8,128)(2,1)S(1)}, u32[]{:S(2)}, u32[]{:S(2)}) %collective-permute-start.85) | collective-permute-done | bytes 262176 | tf_op jit(solution)/shard_map/ppermute | solution.py:114
  701.8 13.4 %collective-permute-done.91.refs_3_.refs_5_ = bf16[2,2,3,32,2048]{4,3,2,1,0:T(8,128)(2,1)S(1)} collective-permute-done((bf16[2,2,3,32,2048]{4,3,2,1,0:T(8,128)(2,1)S(1)}, bf16[2,2,3,32,2048]{4,3,2,1,0:T(8,128)(2,1)S(1)}, u32[]{:S(2)}, u32[]{:S(2)}) %collective-permute-start.91) | collective-permute-done | bytes 1572896 | tf_op jit(solution)/shard_map/ppermute | solution.py:114
  725.5 9.9 %collective-permute-done.95 = bf16[32,4096]{1,0:T(8,128)(2,1)S(1)} collective-permute-done((bf16[32,4096]{1,0:T(8,128)(2,1)S(1)}, bf16[32,4096]{1,0:T(8,128)(2,1)S(1)}, u32[]{:S(2)}, u32[]{:S(2)}) %collective-permute-start.95) | collective-permute-done | bytes 262176 | tf_op jit(solution)/shard_map/ppermute | solution.py:114
  744.5 10.3 %collective-permute-done.100 = bf16[32,4096]{1,0:T(8,128)(2,1)S(1)} collective-permute-done((bf16[32,4096]{1,0:T(8,128)(2,1)S(1)}, bf16[32,4096]{1,0:T(8,128)(2,1)S(1)}, u32[]{:S(2)}, u32[]{:S(2)}) %collective-permute-start.100) | collective-permute-done | bytes 262176 | tf_op jit(solution)/shard_map/ppermute | solution.py:114
  761.0 10.5 %collective-permute-done.103 = bf16[32,4096]{1,0:T(8,128)(2,1)S(1)} collective-permute-done((bf16[32,4096]{1,0:T(8,128)(2,1)S(1)}, bf16[32,4096]{1,0:T(8,128)(2,1)S(1)}, u32[]{:S(2)}, u32[]{:S(2)}) %collective-permute-start.103) | collective-permute-done | bytes 262176 | tf_op jit(solution)/shard_map/ppermute | solution.py:114
  (691 shorter events, 479.4 us)
Async XLA Ops:
  66.7 50.0 %collective-permute-start.15 = (bf16[2,2,3,32,2048]{4,3,2,1,0:T(8,128)(2,1)S(1)}, bf16[2,2,3,32,2048]{4,3,2,1,0:T(8,128)(2,1)S(1)}, u32[]{:S(2)}, u32[]{:S(2)}) collective-permute-start(bf16[2,2,3,32,2048]{4,3,2,1,0:T(8,128)(2,1)S(1)} %get-tuple-element.396.refs_2_), channel_id=1, source_target_pairs={{0,4},{4,0},{8,12},{12,8},{16,20},{20,16},{24,28},{28,24},{1,5},{5... | collective-permute-start | bytes 4718600 | tf_op jit(solution)/shard_map/ppermute | solution.py:114
  67.3 49.4 %collective-permute-start.16 = (bf16[2,2,3,32,2048]{4,3,2,1,0:T(8,128)(2,1)S(1)}, bf16[2,2,3,32,2048]{4,3,2,1,0:T(8,128)(2,1)S(1)}, u32[]{:S(2)}, u32[]{:S(2)}) collective-permute-start(bf16[2,2,3,32,2048]{4,3,2,1,0:T(8,128)(2,1)S(1)} %get-tuple-element.398.refs_4_.refs_0_), channel_id=1, source_target_pairs={{0,2},{1,3},{2,0},{3,1},{4,6},{5,7},{6,4},{7,5},{8,10},{9,11},{10,... | collective-permute-start | bytes 4718600 | tf_op jit(solution)/shard_map/ppermute | solution.py:114
  69.0 47.7 %collective-permute-start.20 = (bf16[2,128,1024]{2,1,0:T(8,128)(2,1)S(1)}, bf16[2,128,1024]{2,1,0:T(8,128)(2,1)S(1)}, u32[]{:S(2)}, u32[]{:S(2)}) collective-permute-start(bf16[2,128,1024]{2,1,0:T(8,128)(2,1)S(1)} %shard_map.258.refs_0_), channel_id=1, source_target_pairs={{0,16},{4,20},{8,24},{12,28},{16,0},{20,4},{24,8},{28,12},{1,17},{... | collective-permute-start | bytes 1572872 | tf_op jit(solution)/shard_map/ppermute | solution.py:114
  72.1 44.6 %collective-permute-start.17 = (bf16[2,32,4096]{2,1,0:T(8,128)(2,1)S(1)}, bf16[2,32,4096]{2,1,0:T(8,128)(2,1)S(1)}, u32[]{:S(2)}, u32[]{:S(2)}) collective-permute-start(bf16[2,32,4096]{2,1,0:T(8,128)(2,1)S(1)} %get-tuple-element.400.refs_6_), channel_id=1, source_target_pairs={{0,8},{4,12},{8,0},{12,4},{16,24},{20,28},{24,16},{28,20},{1,9},{5... | collective-permute-start | bytes 1572872 | tf_op jit(solution)/shard_map/ppermute | solution.py:114
  160.7 36.5 %collective-permute-start.26 = (bf16[2,2,3,32,2048]{4,3,2,1,0:T(8,128)(2,1)S(1)}, bf16[2,2,3,32,2048]{4,3,2,1,0:T(8,128)(2,1)S(1)}, u32[]{:S(2)}, u32[]{:S(2)}) collective-permute-start(bf16[2,2,3,32,2048]{4,3,2,1,0:T(8,128)(2,1)S(1)} %get-tuple-element.420.refs_4_.refs_2_), channel_id=1, source_target_pairs={{0,4},{4,0},{8,12},{12,8},{16,20},{20,16},{24,28},{28,24},{1,5},{5... | collective-permute-start | bytes 4718600 | tf_op jit(solution)/shard_map/ppermute | solution.py:114
  240.6 41.7 %collective-permute-start.36 = (bf16[2,2,3,32,2048]{4,3,2,1,0:T(8,128)(2,1)S(1)}, bf16[2,2,3,32,2048]{4,3,2,1,0:T(8,128)(2,1)S(1)}, u32[]{:S(2)}, u32[]{:S(2)}) collective-permute-start(bf16[2,2,3,32,2048]{4,3,2,1,0:T(8,128)(2,1)S(1)} %get-tuple-element.457.refs_4_.refs_0_.refs_2_), channel_id=1, source_target_pairs={{0,4},{4,0},{8,12},{12,8},{16,20},{20,16},{24,28},{28,24},{1,5},{5... | collective-permute-start | bytes 4718600 | tf_op jit(solution)/shard_map/ppermute | solution.py:114
  241.2 41.1 %collective-permute-start.37 = (bf16[2,2,3,32,2048]{4,3,2,1,0:T(8,128)(2,1)S(1)}, bf16[2,2,3,32,2048]{4,3,2,1,0:T(8,128)(2,1)S(1)}, u32[]{:S(2)}, u32[]{:S(2)}) collective-permute-start(bf16[2,2,3,32,2048]{4,3,2,1,0:T(8,128)(2,1)S(1)} %get-tuple-element.459.refs_2_.refs_0_), channel_id=1, source_target_pairs={{0,2},{1,3},{2,0},{3,1},{4,6},{5,7},{6,4},{7,5},{8,10},{9,11},{10,... | collective-permute-start | bytes 4718600 | tf_op jit(solution)/shard_map/ppermute | solution.py:114
  243.0 39.3 %collective-permute-start.38 = (bf16[2,128,1024]{2,1,0:T(8,128)(2,1)S(1)}, bf16[2,128,1024]{2,1,0:T(8,128)(2,1)S(1)}, u32[]{:S(2)}, u32[]{:S(2)}) collective-permute-start(bf16[2,128,1024]{2,1,0:T(8,128)(2,1)S(1)} %shard_map.272.refs_0_), channel_id=1, source_target_pairs={{0,16},{4,20},{8,24},{12,28},{16,0},{20,4},{24,8},{28,12},{1,17},{... | collective-permute-start | bytes 1572872 | tf_op jit(solution)/shard_map/ppermute | solution.py:114
  403.5 45.5 %collective-permute-start.60 = (bf16[2,2,2,2,32,4096]{5,4,3,2,1,0:T(8,128)(2,1)}, bf16[2,2,2,2,32,4096]{5,4,3,2,1,0:T(8,128)(2,1)}, u32[]{:S(2)}, u32[]{:S(2)}) collective-permute-start(bf16[2,2,2,2,32,4096]{5,4,3,2,1,0:T(8,128)(2,1)} %get-tuple-element.500), channel_id=1, source_target_pairs={{0,1},{1,0},{2,3},{3,2},{4,5},{5,4},{6,7},{7,6},{8,9},{9,8},{10,11... | collective-permute-start | bytes 12582920 | tf_op jit(solution)/shard_map/ppermute | solution.py:114
  404.5 44.5 %collective-permute-start.59 = (bf16[2,128,1024]{2,1,0:T(8,128)(2,1)}, bf16[2,128,1024]{2,1,0:T(8,128)(2,1)}, u32[]{:S(2)}, u32[]{:S(2)}) collective-permute-start(bf16[2,128,1024]{2,1,0:T(8,128)(2,1)} %get-tuple-element.499), channel_id=1, source_target_pairs={{0,16},{4,20},{8,24},{12,28},{16,0},{20,4},{24,8},{28,12},{1,17},{... | collective-permute-start | bytes 1572872 | tf_op jit(solution)/shard_map/ppermute | solution.py:114
  408.6 40.4 %collective-permute-start.58 = (bf16[2,128,1024]{2,1,0:T(8,128)(2,1)}, bf16[2,128,1024]{2,1,0:T(8,128)(2,1)}, u32[]{:S(2)}, u32[]{:S(2)}) collective-permute-start(bf16[2,128,1024]{2,1,0:T(8,128)(2,1)} %get-tuple-element.495), channel_id=1, source_target_pairs={{0,8},{4,12},{8,0},{12,4},{16,24},{20,28},{24,16},{28,20},{1,9},{5... | collective-permute-start | bytes 1572872 | tf_op jit(solution)/shard_map/ppermute | solution.py:114
  473.6 37.9 %collective-permute-start.66 = (bf16[2,2,2,2,32,4096]{5,4,3,2,1,0:T(8,128)(2,1)}, bf16[2,2,2,2,32,4096]{5,4,3,2,1,0:T(8,128)(2,1)}, u32[]{:S(2)}, u32[]{:S(2)}) collective-permute-start(bf16[2,2,2,2,32,4096]{5,4,3,2,1,0:T(8,128)(2,1)} %copy-done.112), channel_id=1, source_target_pairs={{0,1},{1,0},{2,3},{3,2},{4,5},{5,4},{6,7},{7,6},{8,9},{9,8},{10,11... | collective-permute-start | bytes 12582920 | tf_op jit(solution)/shard_map/ppermute | solution.py:114
  511.5 42.4 %collective-permute-start.71 = (bf16[2,2,2,2,32,4096]{5,4,3,2,1,0:T(8,128)(2,1)}, bf16[2,2,2,2,32,4096]{5,4,3,2,1,0:T(8,128)(2,1)S(1)}, u32[]{:S(2)}, u32[]{:S(2)}) collective-permute-start(bf16[2,2,2,2,32,4096]{5,4,3,2,1,0:T(8,128)(2,1)} %get-tuple-element.548), channel_id=1, source_target_pairs={{0,1},{1,0},{2,3},{3,2},{4,5},{5,4},{6,7},{7,6},{8,9},{9,8},{10,11... | collective-permute-start | bytes 12582920 | tf_op jit(solution)/shard_map/ppermute | solution.py:114
  516.0 36.8 %collective-permute-start.72 = (bf16[2,2,3,32,2048]{4,3,2,1,0:T(8,128)(2,1)S(1)}, bf16[2,2,3,32,2048]{4,3,2,1,0:T(8,128)(2,1)S(1)}, u32[]{:S(2)}, u32[]{:S(2)}) collective-permute-start(bf16[2,2,3,32,2048]{4,3,2,1,0:T(8,128)(2,1)S(1)} %get-tuple-element.543.refs_8_), channel_id=1, source_target_pairs={{0,4},{4,0},{8,12},{12,8},{16,20},{20,16},{24,28},{28,24},{1,5},{5... | collective-permute-start | bytes 4718600 | tf_op jit(solution)/shard_map/ppermute | solution.py:114
  517.2 36.7 %collective-permute-start.73 = (bf16[2,2,3,32,2048]{4,3,2,1,0:T(8,128)(2,1)}, bf16[2,2,3,32,2048]{4,3,2,1,0:T(8,128)(2,1)S(1)}, u32[]{:S(2)}, u32[]{:S(2)}) collective-permute-start(bf16[2,2,3,32,2048]{4,3,2,1,0:T(8,128)(2,1)} %get-tuple-element.550), channel_id=1, source_target_pairs={{0,2},{1,3},{2,0},{3,1},{4,6},{5,7},{6,4},{7,5},{8,10},{9,11},{10,... | collective-permute-start | bytes 4718600 | tf_op jit(solution)/shard_map/ppermute | solution.py:114
  553.9 41.3 %collective-permute-start.74 = (bf16[2,2,2,2,32,4096]{5,4,3,2,1,0:T(8,128)(2,1)}, bf16[2,2,2,2,32,4096]{5,4,3,2,1,0:T(8,128)(2,1)S(1)}, u32[]{:S(2)}, u32[]{:S(2)}) collective-permute-start(bf16[2,2,2,2,32,4096]{5,4,3,2,1,0:T(8,128)(2,1)} %get-tuple-element.574), channel_id=1, source_target_pairs={{0,1},{1,0},{2,3},{3,2},{4,5},{5,4},{6,7},{7,6},{8,9},{9,8},{10,11... | collective-permute-start | bytes 12582920 | tf_op jit(solution)/shard_map/ppermute | solution.py:114
  557.5 37.0 %collective-permute-start.75 = (bf16[2,2,3,32,2048]{4,3,2,1,0:T(8,128)(2,1)}, bf16[2,2,3,32,2048]{4,3,2,1,0:T(8,128)(2,1)S(1)}, u32[]{:S(2)}, u32[]{:S(2)}) collective-permute-start(bf16[2,2,3,32,2048]{4,3,2,1,0:T(8,128)(2,1)} %get-tuple-element.569.refs_12_), channel_id=1, source_target_pairs={{0,4},{4,0},{8,12},{12,8},{16,20},{20,16},{24,28},{28,24},{1,5},{5... | collective-permute-start | bytes 4718600 | tf_op jit(solution)/shard_map/ppermute | solution.py:114
  558.4 36.7 %collective-permute-start.76 = (bf16[2,2,3,32,2048]{4,3,2,1,0:T(8,128)(2,1)}, bf16[2,2,3,32,2048]{4,3,2,1,0:T(8,128)(2,1)S(1)}, u32[]{:S(2)}, u32[]{:S(2)}) collective-permute-start(bf16[2,2,3,32,2048]{4,3,2,1,0:T(8,128)(2,1)} %get-tuple-element.576), channel_id=1, source_target_pairs={{0,2},{1,3},{2,0},{3,1},{4,6},{5,7},{6,4},{7,5},{8,10},{9,11},{10,... | collective-permute-start | bytes 4718600 | tf_op jit(solution)/shard_map/ppermute | solution.py:114
  595.1 41.5 %collective-permute-start.78 = (bf16[2,2,2,2,32,4096]{5,4,3,2,1,0:T(8,128)(2,1)}, bf16[2,2,2,2,32,4096]{5,4,3,2,1,0:T(8,128)(2,1)S(1)}, u32[]{:S(2)}, u32[]{:S(2)}) collective-permute-start(bf16[2,2,2,2,32,4096]{5,4,3,2,1,0:T(8,128)(2,1)} %get-tuple-element.600), channel_id=1, source_target_pairs={{0,1},{1,0},{2,3},{3,2},{4,5},{5,4},{6,7},{7,6},{8,9},{9,8},{10,11... | collective-permute-start | bytes 12582920 | tf_op jit(solution)/shard_map/ppermute | solution.py:114
  598.8 37.0 %collective-permute-start.80 = (bf16[2,2,3,32,2048]{4,3,2,1,0:T(8,128)(2,1)}, bf16[2,2,3,32,2048]{4,3,2,1,0:T(8,128)(2,1)S(1)}, u32[]{:S(2)}, u32[]{:S(2)}) collective-permute-start(bf16[2,2,3,32,2048]{4,3,2,1,0:T(8,128)(2,1)} %get-tuple-element.595.refs_14_), channel_id=1, source_target_pairs={{0,4},{4,0},{8,12},{12,8},{16,20},{20,16},{24,28},{28,24},{1,5},{5... | collective-permute-start | bytes 4718600 | tf_op jit(solution)/shard_map/ppermute | solution.py:114
  599.9 36.7 %collective-permute-start.81 = (bf16[2,2,3,32,2048]{4,3,2,1,0:T(8,128)(2,1)}, bf16[2,2,3,32,2048]{4,3,2,1,0:T(8,128)(2,1)S(1)}, u32[]{:S(2)}, u32[]{:S(2)}) collective-permute-start(bf16[2,2,3,32,2048]{4,3,2,1,0:T(8,128)(2,1)} %get-tuple-element.604), channel_id=1, source_target_pairs={{0,2},{1,3},{2,0},{3,1},{4,6},{5,7},{6,4},{7,5},{8,10},{9,11},{10,... | collective-permute-start | bytes 4718600 | tf_op jit(solution)/shard_map/ppermute | solution.py:114
  636.6 40.7 %collective-permute-start.84 = (bf16[2,2,2,2,32,4096]{5,4,3,2,1,0:T(8,128)(2,1)}, bf16[2,2,2,2,32,4096]{5,4,3,2,1,0:T(8,128)(2,1)S(1)}, u32[]{:S(2)}, u32[]{:S(2)}) collective-permute-start(bf16[2,2,2,2,32,4096]{5,4,3,2,1,0:T(8,128)(2,1)} %copy-done.113), channel_id=1, source_target_pairs={{0,1},{1,0},{2,3},{3,2},{4,5},{5,4},{6,7},{7,6},{8,9},{9,8},{10,11... | collective-permute-start | bytes 12582920 | tf_op jit(solution)/shard_map/ppermute | solution.py:114
  639.8 36.9 %collective-permute-start.86 = (bf16[2,2,3,32,2048]{4,3,2,1,0:T(8,128)(2,1)S(1)}, bf16[2,2,3,32,2048]{4,3,2,1,0:T(8,128)(2,1)S(1)}, u32[]{:S(2)}, u32[]{:S(2)}) collective-permute-start(bf16[2,2,3,32,2048]{4,3,2,1,0:T(8,128)(2,1)S(1)} %get-tuple-element.630.refs_14_), channel_id=1, source_target_pairs={{0,4},{4,0},{8,12},{12,8},{16,20},{20,16},{24,28},{28,24},{1,5},{5... | collective-permute-start | bytes 4718600 | tf_op jit(solution)/shard_map/ppermute | solution.py:114
  640.8 36.5 %collective-permute-start.87 = (bf16[2,2,3,32,2048]{4,3,2,1,0:T(8,128)(2,1)S(1)}, bf16[2,2,3,32,2048]{4,3,2,1,0:T(8,128)(2,1)S(1)}, u32[]{:S(2)}, u32[]{:S(2)}) collective-permute-start(bf16[2,2,3,32,2048]{4,3,2,1,0:T(8,128)(2,1)S(1)} %get-tuple-element.639), channel_id=1, source_target_pairs={{0,2},{1,3},{2,0},{3,1},{4,6},{5,7},{6,4},{7,5},{8,10},{9,11},{10,... | collective-permute-start | bytes 4718600 | tf_op jit(solution)/shard_map/ppermute | solution.py:114
  (228 other events, 2878.5 us)

commit v8 on v7

--- a/solution.py
+++ b/solution.py
@@ -309,6 +309,27 @@
         if cube.tuned:
             self.shards = [uniform_shard(kind, arrays) for kind, arrays in pieces]
         self.state = {}
+
+    def start(self):
+        cube = self.cube
+        if not cube.tuned:
+            return
+        own = self.shards[0]
+        far = cube.swap(own, Z1)
+        near, both = cube.swap(own, Z0), cube.swap(far, Z0)
+
+        def plan(w, s, o):
+            for at in range(2):
+                for by in range(2):
+                    yield s[2 * at + by], o[at].at[flip(w[Z1], by)]
+
+        pairs = local_copies(plan, [own, far, near, both], [(2, ROWS, COLUMNS)] * 2)
+        self.state = {
+            "z0s": pairs[0],
+            "z0g": pairs[1],
+            "z1s": self.shards[1],
+            "z1g": cube.swap(self.shards[1], Z1),
+        }
 
     def stage(self, t):
         cube, old, new = self.cube, self.state, {}
@@ -1154,18 +1175,20 @@
     vocab_cols = head_proj.shape[1]
 
     loss_scale = jnp.float32(devices * UTT_DEV * NSPAN * SPAN)
-    hops = [C, Z1, Z0, X, Y] if cube.tuned else all_bits
+    hops = [C, Y, X, Z1, Z0] if cube.tuned else all_bits
     vector_in = VectorGathering(cube, jnp.concatenate([conv_depth, norm_gains, jnp.zeros_like(conv_depth[:10])], axis=0), hops)
-    vector_in.step(2)
+    vector_in.step(3)
     group_codes = cube.gather(picked_codes, head_order).reshape(group * slots)
-    rows_in.stage(-3)
-    heads[0].step("x")
-    heads[1].step("x")
+    rows_in.start()
+    if cube.tuned:
+        head_got = cube.swap(head_proj, X)
+        for at, flow in enumerate(heads):
+            columns = slice(at * head_half, (at + 1) * head_half)
+            flow.state = [head_proj[:, columns], head_got[:, columns]]
+    else:
+        heads[0].step("x")
+        heads[1].step("x")
     group_codes = fence([rows_in, vector_in, *heads], group_codes)
-
-    rows_in.stage(-2)
-    vector_in.step()
-    fence([rows_in, vector_in], loss_scale)
 
     rows_in.stage(-1)
     vector_in.step()
@@ -1369,7 +1392,9 @@
         devices,
     )
     vector_flow = Summing(
-        cube, vector_grad.reshape((2,) * len(cube.bits) + vector_grad.shape[1:]), hops
+        cube,
+        vector_grad.reshape((2,) * len(cube.bits) + vector_grad.shape[1:]),
+        [C, Z1, Z0, X, Y] if cube.tuned else all_bits,
     )
     vector_flow.step()
     input_grad, piece = fence([rows_out, vector_flow], input_grad, piece)

time: 786 us -> 763 us (0.971)
  waiting for transfers between devices: 325 us -> 292 us
    ppermute x104, waiting for transfers between devices: 325 us -> 292 us  [swap(): lax.ppermute(values, axis, [(i, i ^ bit) for i in range(self.sizes[axis])])]
    unnamed x295 -> x291, local copies, waits for them, and re-layouts: 43.9 us -> 43.6 us
  transfers between devices with their start and end apart: 104 -> 104, of which waited for: 66 -> 66; matrix products, arithmetic and copies ran while one was open for 7% -> 8% of each run, Pallas kernels for 25% -> 26%
where the time goes in v8:
time: 763 us; the launch traced here: 753 us
  waiting for transfers between devices  292 us (38%)
  Pallas kernels  214 us (28%)
  starting transfers between devices  112 us (15%)
  local copies, waits for them, and re-layouts  55.6 us (7%)
  matrix products  51.4 us (7%)
  other arithmetic  20 us (3%)
    ppermute x104, waiting for transfers between devices, swap(): lax.ppermute(values, axis, [(i, i ^ bit) for i in range(self.sizes[axis])])  292 us
    ppermute x104, starting transfers between devices, swap(): lax.ppermute(values, axis, [(i, i ^ bit) for i in range(self.sizes[axis])])  112 us
    unnamed x291, local copies, waits for them, and re-layouts  43.6 us
    pallas_call x18, Pallas kernels, sums(): pl.pallas_call(kernel, grid_spec=pltpu.PrefetchScalarGridSpec(num_scalar_...  40.5 us
    dot_general x10, matrix products, matmul(): return jnp.dot(operand, weight, preferred_element_type=jnp.float32)  35.8 us
    pallas_call x4, Pallas kernels, product_norm_back(): pl.pallas_call(functools.partial(norm_back_kernel, row), grid=(inner // w...  31.9 us
    pallas_call x4, Pallas kernels, weight_grads(): pl.pallas_call(functools.partial(weight_grads_kernel, counts), grid=(COLU...  28.5 us
    pallas_call x38, Pallas kernels, local_copies(): pl.pallas_call(kernel, out_shape=[jax.ShapeDtypeStruct(shape, inputs[0].d...  25.4 us
  transfers between devices with their start and end apart: 104, of which 66 were waited for; matrix products, arithmetic and copies ran while one was open for 8% of the time, Pallas kernels for 26%

profile of v8, /device:TPU:0, one launch (start us, length us, event | category | flops | bytes accessed | tf_op | source)
XLA Modules:
  0.0 752.5 jit_solution(3962560445300490979)
XLA Ops:
  41.5 11.6 %collective-permute-done.14.refs_1_ = bf16[2,2,2,48,32]{4,3,2,1,0:T(8,128)(2,1)S(1)} collective-permute-done((bf16[2,2,2,48,32]{4,3,2,1,0:T(8,128)(2,1)S(1)}, bf16[2,2,2,48,32]{4,3,2,1,0:T(8,128)(2,1)S(1)}, u32[]{:S(2)}, u32[]{:S(2)}) %collective-permute-start.14) | collective-permute-done | bytes 24608 | tf_op jit(solution)/shard_map/ppermute | solution.py:114
  62.8 14.1 %collective-permute-done.19.refs_1_ = bf16[2,2,2,2,48,32]{5,4,3,2,1,0:T(8,128)(2,1)S(1)} collective-permute-done((bf16[2,2,2,2,48,32]{5,4,3,2,1,0:T(8,128)(2,1)S(1)}, bf16[2,2,2,2,48,32]{5,4,3,2,1,0:T(8,128)(2,1)S(1)}, u32[]{:S(2)}, u32[]{:S(2)}) %collective-permute-start.19) | collective-permute-done | bytes 49184 | tf_op jit(solution)/shard_map/ppermute | solution.py:114
  81.9 9.2 %collective-permute-done.18.refs_1_ = bf16[32,4096]{1,0:T(8,128)(2,1)S(1)} collective-permute-done((bf16[32,4096]{1,0:T(8,128)(2,1)S(1)}, bf16[32,4096]{1,0:T(8,128)(2,1)S(1)}, u32[]{:S(2)}, u32[]{:S(2)}) %collective-permute-start.18) | collective-permute-done | bytes 262176 | tf_op jit(solution)/shard_map/ppermute | solution.py:114
  117.7 15.3 %collective-permute-done.21.refs_3_ = bf16[2,2,3,32,2048]{4,3,2,1,0:T(8,128)(2,1)S(1)} collective-permute-done((bf16[2,2,3,32,2048]{4,3,2,1,0:T(8,128)(2,1)S(1)}, bf16[2,2,3,32,2048]{4,3,2,1,0:T(8,128)(2,1)S(1)}, u32[]{:S(2)}, u32[]{:S(2)}) %collective-permute-start.21) | collective-permute-done | bytes 1572896 | tf_op jit(solution)/shard_map/ppermute | solution.py:114
  156.7 16.0 %collective-permute-done.26.refs_3_ = bf16[2,2,3,32,2048]{4,3,2,1,0:T(8,128)(2,1)S(1)} collective-permute-done((bf16[2,2,3,32,2048]{4,3,2,1,0:T(8,128)(2,1)S(1)}, bf16[2,2,3,32,2048]{4,3,2,1,0:T(8,128)(2,1)S(1)}, u32[]{:S(2)}, u32[]{:S(2)}) %collective-permute-start.26) | collective-permute-done | bytes 1572896 | tf_op jit(solution)/shard_map/ppermute | solution.py:114
  186.8 12.8 %shard_map.270 = (bf16[512,1024]{1,0:T(8,128)(2,1)S(1)}, bf16[512,1024]{1,0:T(8,128)(2,1)S(1)}, bf16[512,1024]{1,0:T(8,128)(2,1)S(1)}, bf16[512,1024]{1,0:T(8,128)(2,1)S(1)}, f32[512,1024]{1,0:T(8,128)S(1)}) custom-call(f32[512,3072]{1,0:T(8,128)S(1)} %fusion.28.query_ref.key_ref.value_ref, f32[512,3072]{1,0:T(8,128)S(1)} %fusion.28.query_ref.key_ref.value_ref, ...), custom_call_target="tpu_custom_call" | custom-call | tf_op jit(solution)/shard_map/pallas_call | solution.py:1051
  202.9 10.7 %collective-permute-done.33.refs_5_ = bf16[2,32,4096]{2,1,0:T(8,128)(2,1)S(1)} collective-permute-done((bf16[2,32,4096]{2,1,0:T(8,128)(2,1)S(1)}, bf16[2,32,4096]{2,1,0:T(8,128)(2,1)S(1)}, u32[]{:S(2)}, u32[]{:S(2)}) %collective-permute-start.33) | collective-permute-done | bytes 524320 | tf_op jit(solution)/shard_map/ppermute | solution.py:114
  228.5 10.9 %shard_map.275 = (f32[512,1024]{1,0:T(8,128)S(1)}, f32[8,1024]{1,0:T(8,128)S(1)}) custom-call(f32[512,2048]{1,0:T(8,128)S(1)} %fusion.29.lead_ref.gate_ref, f32[512,2048]{1,0:T(8,128)S(1)} %fusion.29.lead_ref.gate_ref, f32[512,1]{1,0:T(8,128)S(1)} %fusion.6.valid_ref, f32[48,1024]{1,0:T(8,128)S(1)} %shard_map.260.taps_ref.vectors_ref), custom_call_target="tpu_custom_call" | custom-call | tf_op jit(solution)/shard_map/pallas_call | solution.py:718
  276.0 13.3 %collective-permute-done.47.refs_3_ = bf16[2,2,128,1024]{3,2,1,0:T(8,128)(2,1)} collective-permute-done((bf16[2,2,128,1024]{3,2,1,0:T(8,128)(2,1)S(1)}, bf16[2,2,128,1024]{3,2,1,0:T(8,128)(2,1)}, u32[]{:S(2)}, u32[]{:S(2)}) %collective-permute-start.47) | collective-permute-done | bytes 1048608 | tf_op jit(solution)/shard_map/ppermute | solution.py:114
  307.6 11.2 %collective-permute-done.50.refs_1_ = bf16[200,1024]{1,0:T(8,128)(2,1)S(1)} collective-permute-done((bf16[200,1024]{1,0:T(8,128)(2,1)S(1)}, bf16[200,1024]{1,0:T(8,128)(2,1)S(1)}, u32[]{:S(2)}, u32[]{:S(2)}) %collective-permute-start.50) | collective-permute-done | bytes 409632 | tf_op jit(solution)/shard_map/ppermute | solution.py:114
  364.4 7.6 %shard_map.291 = (bf16[2,2,2,2,32,4096]{5,4,3,2,1,0:T(8,128)(2,1)S(1)}, bf16[2,2,2,2,32,4096]{5,4,3,2,1,0:T(8,128)(2,1)}) custom-call(bf16[512,4096]{1,0:T(8,128)(2,1)S(1)} %copy-done.44, bf16[1,512,1024]{2,1,0:T(8,128)(2,1)S(1)} %bitcast.121), custom_call_target="tpu_custom_call" | custom-call | tf_op jit(solution)/shard_map/pallas_call | solution.py:931
  394.7 7.9 %shard_map.294.grad_ref.refs_1_ = bf16[4,512,1024]{2,1,0:T(8,128)(2,1)S(1)} custom-call(bf16[512,1024]{1,0:T(8,128)(2,1)S(1)} %copy-done.21, bf16[4096,1024]{1,0:T(8,128)(2,1)S(1)} %bitcast.120, bf16[512,4096]{1,0:T(8,128)(2,1)S(1)} %copy-done.30), custom_call_target="tpu_custom_call" | custom-call | tf_op jit(solution)/shard_map/pallas_call | solution.py:849
  416.9 9.0 %shard_map.295 = (f32[512,1024]{1,0:T(8,128)S(1)}, f32[1,1024]{1,0:T(1,128)S(1)}) custom-call(bf16[4,512,1024]{2,1,0:T(8,128)(2,1)S(1)} %shard_map.294.grad_ref.refs_1_, bf16[1024,4096]{1,0:T(8,128)(2,1)S(1)} %bitcast.118, f32[512,1024]{1,0:T(8,128)S(1)} %copy-done.19, f32[48,1024]{1,0:T(8,128)S(1)} %shard_map.260.taps_ref.vectors_ref, ...), custom_call_target="tpu_custom_call" | custom-call | tf_op jit(solution)/shard_map/pallas_call | solution.py:1003
  466.3 15.3 %shard_map.301 = (bf16[2,512,1024]{2,1,0:T(8,128)(2,1)S(1)}, f32[32,1024]{1,0:T(8,128)S(1)}) custom-call(f32[512,2048]{1,0:T(8,128)S(1)} %copy-done.3, f32[512,2048]{1,0:T(8,128)S(1)} %copy-done.3, f32[512,1]{1,0:T(8,128)S(1)} %fusion.6.valid_ref, f32[48,1024]{1,0:T(8,128)S(1)} %shard_map.260.taps_ref.vectors_ref, f32[512,1024]{1,0:T(8,128)S(1)} %copy-done.24, ...), custom_call_target="tpu_custom_call" | custom-call | tf_op jit(solution)/shard_map/pallas_call | solution.py:802
  506.8 12.7 %shard_map.306.refs_2_.grad_ref = bf16[3,512,1024]{2,1,0:T(8,128)(2,1)S(1)} custom-call(bf16[512,1024]{1,0:T(8,128)(2,1)S(1)} %copy-done.85, bf16[512,1024]{1,0:T(8,128)(2,1)S(1)} %copy-done.87, bf16[512,1024]{1,0:T(8,128)(2,1)S(1)} %copy-done.89, f32[512,1024]{1,0:T(8,128)S(1)} %copy-done.81, bf16[512,1024]{1,0:T(8,128)(2,1)S(1)} %convolution_convert_fusion.2.grad_ref, ...), custom_call_target="tpu_custom_call" | custom-call | tf_op jit(solution)/shard_map/pallas_call | solution.py:1091
  521.0 7.9 %shard_map.307 = (bf16[2,2,2,2,32,4096]{5,4,3,2,1,0:T(8,128)(2,1)S(1)}, bf16[2,2,2,2,32,4096]{5,4,3,2,1,0:T(8,128)(2,1)}) custom-call(bf16[512,1024]{1,0:T(8,128)(2,1)S(1)} %copy-done.50, bf16[512,1024]{1,0:T(8,128)(2,1)S(1)} %copy-done.83, bf16[3,512,1024]{2,1,0:T(8,128)(2,1)S(1)} %shard_map.306.refs_2_.grad_ref, ...), custom_call_target="tpu_custom_call" | custom-call | tf_op jit(solution)/shard_map/pallas_call | solution.py:955
  549.7 7.7 %shard_map.312 = (bf16[2,2,2,2,32,4096]{5,4,3,2,1,0:T(8,128)(2,1)S(1)}, bf16[2,2,2,2,32,4096]{5,4,3,2,1,0:T(8,128)(2,1)}) custom-call(bf16[512,4096]{1,0:T(8,128)(2,1)S(1)} %copy-done.42, bf16[1,512,1024]{2,1,0:T(8,128)(2,1)S(1)} %fusion.56.right_ref), custom_call_target="tpu_custom_call" | custom-call | tf_op jit(solution)/shard_map/pallas_call | solution.py:931
  561.0 7.9 %shard_map.311.grad_ref.refs_1_ = bf16[4,512,1024]{2,1,0:T(8,128)(2,1)S(1)} custom-call(bf16[512,1024]{1,0:T(8,128)(2,1)S(1)} %multiply_convert_fusion.3.grad_ref, bf16[4096,1024]{1,0:T(8,128)(2,1)S(1)} %bitcast.116, bf16[512,4096]{1,0:T(8,128)(2,1)S(1)} %copy-done.29), custom_call_target="tpu_custom_call" | custom-call | tf_op jit(solution)/shard_map/pallas_call | solution.py:849
  581.5 10.3 %shard_map.315 = (f32[512,1024]{1,0:T(8,128)}, f32[1,1024]{1,0:T(1,128)S(1)}) custom-call(bf16[4,512,1024]{2,1,0:T(8,128)(2,1)S(1)} %shard_map.311.grad_ref.refs_1_, bf16[1024,4096]{1,0:T(8,128)(2,1)S(1)} %bitcast.114, f32[512,1024]{1,0:T(8,128)S(1)} %convert_element_type.162.values_ref, f32[48,1024]{1,0:T(8,128)S(1)} %shard_map.260.taps_ref.vectors_ref, ...), custom_call_target="tpu_custom_call" | custom-call | tf_op jit(solution)/shard_map/pallas_call | solution.py:1003
  632.9 11.4 %collective-permute-done.85 = bf16[32,4096]{1,0:T(8,128)(2,1)S(1)} collective-permute-done((bf16[32,4096]{1,0:T(8,128)(2,1)S(1)}, bf16[32,4096]{1,0:T(8,128)(2,1)S(1)}, u32[]{:S(2)}, u32[]{:S(2)}) %collective-permute-start.85) | collective-permute-done | bytes 262176 | tf_op jit(solution)/shard_map/ppermute | solution.py:114
  678.7 13.3 %collective-permute-done.91.refs_3_.refs_5_ = bf16[2,2,3,32,2048]{4,3,2,1,0:T(8,128)(2,1)S(1)} collective-permute-done((bf16[2,2,3,32,2048]{4,3,2,1,0:T(8,128)(2,1)S(1)}, bf16[2,2,3,32,2048]{4,3,2,1,0:T(8,128)(2,1)S(1)}, u32[]{:S(2)}, u32[]{:S(2)}) %collective-permute-start.91) | collective-permute-done | bytes 1572896 | tf_op jit(solution)/shard_map/ppermute | solution.py:114
  702.3 9.5 %collective-permute-done.95 = bf16[32,4096]{1,0:T(8,128)(2,1)S(1)} collective-permute-done((bf16[32,4096]{1,0:T(8,128)(2,1)S(1)}, bf16[32,4096]{1,0:T(8,128)(2,1)S(1)}, u32[]{:S(2)}, u32[]{:S(2)}) %collective-permute-start.95) | collective-permute-done | bytes 262176 | tf_op jit(solution)/shard_map/ppermute | solution.py:114
  721.5 10.0 %collective-permute-done.100 = bf16[32,4096]{1,0:T(8,128)(2,1)S(1)} collective-permute-done((bf16[32,4096]{1,0:T(8,128)(2,1)S(1)}, bf16[32,4096]{1,0:T(8,128)(2,1)S(1)}, u32[]{:S(2)}, u32[]{:S(2)}) %collective-permute-start.100) | collective-permute-done | bytes 262176 | tf_op jit(solution)/shard_map/ppermute | solution.py:114
  737.7 10.9 %collective-permute-done.103 = bf16[32,4096]{1,0:T(8,128)(2,1)S(1)} collective-permute-done((bf16[32,4096]{1,0:T(8,128)(2,1)S(1)}, bf16[32,4096]{1,0:T(8,128)(2,1)S(1)}, u32[]{:S(2)}, u32[]{:S(2)}) %collective-permute-start.103) | collective-permute-done | bytes 262176 | tf_op jit(solution)/shard_map/ppermute | solution.py:114
  (688 shorter events, 478.9 us)
Async XLA Ops:
  54.2 37.6 %collective-permute-start.15 = (bf16[2,2,3,32,2048]{4,3,2,1,0:T(8,128)(2,1)S(1)}, bf16[2,2,3,32,2048]{4,3,2,1,0:T(8,128)(2,1)S(1)}, u32[]{:S(2)}, u32[]{:S(2)}) collective-permute-start(bf16[2,2,3,32,2048]{4,3,2,1,0:T(8,128)(2,1)S(1)} %get-tuple-element.394.refs_2_), channel_id=1, source_target_pairs={{0,4},{4,0},{8,12},{12,8},{16,20},{20,16},{24,28},{28,24},{1,5},{5... | collective-permute-start | bytes 4718600 | tf_op jit(solution)/shard_map/ppermute | solution.py:114
  96.5 36.5 %collective-permute-start.21 = (bf16[2,2,3,32,2048]{4,3,2,1,0:T(8,128)(2,1)S(1)}, bf16[2,2,3,32,2048]{4,3,2,1,0:T(8,128)(2,1)S(1)}, u32[]{:S(2)}, u32[]{:S(2)}) collective-permute-start(bf16[2,2,3,32,2048]{4,3,2,1,0:T(8,128)(2,1)S(1)} %get-tuple-element.406.refs_4_.refs_2_), channel_id=1, source_target_pairs={{0,4},{4,0},{8,12},{12,8},{16,20},{20,16},{24,28},{28,24},{1,5},{5... | collective-permute-start | bytes 4718600 | tf_op jit(solution)/shard_map/ppermute | solution.py:114
  98.3 36.3 %collective-permute-start.22 = (bf16[2,2,3,32,2048]{4,3,2,1,0:T(8,128)(2,1)S(1)}, bf16[2,2,3,32,2048]{4,3,2,1,0:T(8,128)(2,1)S(1)}, u32[]{:S(2)}, u32[]{:S(2)}) collective-permute-start(bf16[2,2,3,32,2048]{4,3,2,1,0:T(8,128)(2,1)S(1)} %get-tuple-element.408.refs_4_.refs_0_), channel_id=1, source_target_pairs={{0,2},{1,3},{2,0},{3,1},{4,6},{5,7},{6,4},{7,5},{8,10},{9,11},{10,... | collective-permute-start | bytes 4718600 | tf_op jit(solution)/shard_map/ppermute | solution.py:114
  136.3 36.5 %collective-permute-start.26 = (bf16[2,2,3,32,2048]{4,3,2,1,0:T(8,128)(2,1)S(1)}, bf16[2,2,3,32,2048]{4,3,2,1,0:T(8,128)(2,1)S(1)}, u32[]{:S(2)}, u32[]{:S(2)}) collective-permute-start(bf16[2,2,3,32,2048]{4,3,2,1,0:T(8,128)(2,1)S(1)} %get-tuple-element.418.refs_4_.refs_2_), channel_id=1, source_target_pairs={{0,4},{4,0},{8,12},{12,8},{16,20},{20,16},{24,28},{28,24},{1,5},{5... | collective-permute-start | bytes 4718600 | tf_op jit(solution)/shard_map/ppermute | solution.py:114
  178.5 36.5 %collective-permute-start.31 = (bf16[2,2,3,32,2048]{4,3,2,1,0:T(8,128)(2,1)S(1)}, bf16[2,2,3,32,2048]{4,3,2,1,0:T(8,128)(2,1)S(1)}, u32[]{:S(2)}, u32[]{:S(2)}) collective-permute-start(bf16[2,2,3,32,2048]{4,3,2,1,0:T(8,128)(2,1)S(1)} %get-tuple-element.438.refs_4_.refs_0_.refs_2_), channel_id=1, source_target_pairs={{0,4},{4,0},{8,12},{12,8},{16,20},{20,16},{24,28},{28,24},{1,5},{5... | collective-permute-start | bytes 4718600 | tf_op jit(solution)/shard_map/ppermute | solution.py:114
  217.4 41.5 %collective-permute-start.36 = (bf16[2,2,3,32,2048]{4,3,2,1,0:T(8,128)(2,1)S(1)}, bf16[2,2,3,32,2048]{4,3,2,1,0:T(8,128)(2,1)S(1)}, u32[]{:S(2)}, u32[]{:S(2)}) collective-permute-start(bf16[2,2,3,32,2048]{4,3,2,1,0:T(8,128)(2,1)S(1)} %get-tuple-element.455.refs_4_.refs_0_.refs_2_), channel_id=1, source_target_pairs={{0,4},{4,0},{8,12},{12,8},{16,20},{20,16},{24,28},{28,24},{1,5},{5... | collective-permute-start | bytes 4718600 | tf_op jit(solution)/shard_map/ppermute | solution.py:114
  218.0 41.0 %collective-permute-start.37 = (bf16[2,2,3,32,2048]{4,3,2,1,0:T(8,128)(2,1)S(1)}, bf16[2,2,3,32,2048]{4,3,2,1,0:T(8,128)(2,1)S(1)}, u32[]{:S(2)}, u32[]{:S(2)}) collective-permute-start(bf16[2,2,3,32,2048]{4,3,2,1,0:T(8,128)(2,1)S(1)} %get-tuple-element.457.refs_2_.refs_0_), channel_id=1, source_target_pairs={{0,2},{1,3},{2,0},{3,1},{4,6},{5,7},{6,4},{7,5},{8,10},{9,11},{10,... | collective-permute-start | bytes 4718600 | tf_op jit(solution)/shard_map/ppermute | solution.py:114
  219.8 39.1 %collective-permute-start.38 = (bf16[2,128,1024]{2,1,0:T(8,128)(2,1)S(1)}, bf16[2,128,1024]{2,1,0:T(8,128)(2,1)S(1)}, u32[]{:S(2)}, u32[]{:S(2)}) collective-permute-start(bf16[2,128,1024]{2,1,0:T(8,128)(2,1)S(1)} %shard_map.272.refs_0_), channel_id=1, source_target_pairs={{0,16},{4,20},{8,24},{12,28},{16,0},{20,4},{24,8},{28,12},{1,17},{... | collective-permute-start | bytes 1572872 | tf_op jit(solution)/shard_map/ppermute | solution.py:114
  380.3 45.7 %collective-permute-start.60 = (bf16[2,2,2,2,32,4096]{5,4,3,2,1,0:T(8,128)(2,1)}, bf16[2,2,2,2,32,4096]{5,4,3,2,1,0:T(8,128)(2,1)}, u32[]{:S(2)}, u32[]{:S(2)}) collective-permute-start(bf16[2,2,2,2,32,4096]{5,4,3,2,1,0:T(8,128)(2,1)} %get-tuple-element.498), channel_id=1, source_target_pairs={{0,1},{1,0},{2,3},{3,2},{4,5},{5,4},{6,7},{7,6},{8,9},{9,8},{10,11... | collective-permute-start | bytes 12582920 | tf_op jit(solution)/shard_map/ppermute | solution.py:114
  381.2 44.7 %collective-permute-start.59 = (bf16[2,128,1024]{2,1,0:T(8,128)(2,1)}, bf16[2,128,1024]{2,1,0:T(8,128)(2,1)}, u32[]{:S(2)}, u32[]{:S(2)}) collective-permute-start(bf16[2,128,1024]{2,1,0:T(8,128)(2,1)} %get-tuple-element.497), channel_id=1, source_target_pairs={{0,16},{4,20},{8,24},{12,28},{16,0},{20,4},{24,8},{28,12},{1,17},{... | collective-permute-start | bytes 1572872 | tf_op jit(solution)/shard_map/ppermute | solution.py:114
  385.5 40.4 %collective-permute-start.58 = (bf16[2,128,1024]{2,1,0:T(8,128)(2,1)}, bf16[2,128,1024]{2,1,0:T(8,128)(2,1)}, u32[]{:S(2)}, u32[]{:S(2)}) collective-permute-start(bf16[2,128,1024]{2,1,0:T(8,128)(2,1)} %get-tuple-element.493), channel_id=1, source_target_pairs={{0,8},{4,12},{8,0},{12,4},{16,24},{20,28},{24,16},{28,20},{1,9},{5... | collective-permute-start | bytes 1572872 | tf_op jit(solution)/shard_map/ppermute | solution.py:114
  450.6 37.7 %collective-permute-start.66 = (bf16[2,2,2,2,32,4096]{5,4,3,2,1,0:T(8,128)(2,1)}, bf16[2,2,2,2,32,4096]{5,4,3,2,1,0:T(8,128)(2,1)}, u32[]{:S(2)}, u32[]{:S(2)}) collective-permute-start(bf16[2,2,2,2,32,4096]{5,4,3,2,1,0:T(8,128)(2,1)} %copy-done.110), channel_id=1, source_target_pairs={{0,1},{1,0},{2,3},{3,2},{4,5},{5,4},{6,7},{7,6},{8,9},{9,8},{10,11... | collective-permute-start | bytes 12582920 | tf_op jit(solution)/shard_map/ppermute | solution.py:114
  488.2 42.5 %collective-permute-start.71 = (bf16[2,2,2,2,32,4096]{5,4,3,2,1,0:T(8,128)(2,1)}, bf16[2,2,2,2,32,4096]{5,4,3,2,1,0:T(8,128)(2,1)S(1)}, u32[]{:S(2)}, u32[]{:S(2)}) collective-permute-start(bf16[2,2,2,2,32,4096]{5,4,3,2,1,0:T(8,128)(2,1)} %get-tuple-element.546), channel_id=1, source_target_pairs={{0,1},{1,0},{2,3},{3,2},{4,5},{5,4},{6,7},{7,6},{8,9},{9,8},{10,11... | collective-permute-start | bytes 12582920 | tf_op jit(solution)/shard_map/ppermute | solution.py:114
  492.8 36.8 %collective-permute-start.72 = (bf16[2,2,3,32,2048]{4,3,2,1,0:T(8,128)(2,1)S(1)}, bf16[2,2,3,32,2048]{4,3,2,1,0:T(8,128)(2,1)S(1)}, u32[]{:S(2)}, u32[]{:S(2)}) collective-permute-start(bf16[2,2,3,32,2048]{4,3,2,1,0:T(8,128)(2,1)S(1)} %get-tuple-element.541.refs_8_), channel_id=1, source_target_pairs={{0,4},{4,0},{8,12},{12,8},{16,20},{20,16},{24,28},{28,24},{1,5},{5... | collective-permute-start | bytes 4718600 | tf_op jit(solution)/shard_map/ppermute | solution.py:114
  494.0 36.7 %collective-permute-start.73 = (bf16[2,2,3,32,2048]{4,3,2,1,0:T(8,128)(2,1)}, bf16[2,2,3,32,2048]{4,3,2,1,0:T(8,128)(2,1)S(1)}, u32[]{:S(2)}, u32[]{:S(2)}) collective-permute-start(bf16[2,2,3,32,2048]{4,3,2,1,0:T(8,128)(2,1)} %get-tuple-element.548), channel_id=1, source_target_pairs={{0,2},{1,3},{2,0},{3,1},{4,6},{5,7},{6,4},{7,5},{8,10},{9,11},{10,... | collective-permute-start | bytes 4718600 | tf_op jit(solution)/shard_map/ppermute | solution.py:114
  530.7 41.2 %collective-permute-start.74 = (bf16[2,2,2,2,32,4096]{5,4,3,2,1,0:T(8,128)(2,1)}, bf16[2,2,2,2,32,4096]{5,4,3,2,1,0:T(8,128)(2,1)S(1)}, u32[]{:S(2)}, u32[]{:S(2)}) collective-permute-start(bf16[2,2,2,2,32,4096]{5,4,3,2,1,0:T(8,128)(2,1)} %get-tuple-element.572), channel_id=1, source_target_pairs={{0,1},{1,0},{2,3},{3,2},{4,5},{5,4},{6,7},{7,6},{8,9},{9,8},{10,11... | collective-permute-start | bytes 12582920 | tf_op jit(solution)/shard_map/ppermute | solution.py:114
  534.3 37.0 %collective-permute-start.75 = (bf16[2,2,3,32,2048]{4,3,2,1,0:T(8,128)(2,1)}, bf16[2,2,3,32,2048]{4,3,2,1,0:T(8,128)(2,1)S(1)}, u32[]{:S(2)}, u32[]{:S(2)}) collective-permute-start(bf16[2,2,3,32,2048]{4,3,2,1,0:T(8,128)(2,1)} %get-tuple-element.567.refs_12_), channel_id=1, source_target_pairs={{0,4},{4,0},{8,12},{12,8},{16,20},{20,16},{24,28},{28,24},{1,5},{5... | collective-permute-start | bytes 4718600 | tf_op jit(solution)/shard_map/ppermute | solution.py:114
  535.2 36.7 %collective-permute-start.76 = (bf16[2,2,3,32,2048]{4,3,2,1,0:T(8,128)(2,1)}, bf16[2,2,3,32,2048]{4,3,2,1,0:T(8,128)(2,1)S(1)}, u32[]{:S(2)}, u32[]{:S(2)}) collective-permute-start(bf16[2,2,3,32,2048]{4,3,2,1,0:T(8,128)(2,1)} %get-tuple-element.574), channel_id=1, source_target_pairs={{0,2},{1,3},{2,0},{3,1},{4,6},{5,7},{6,4},{7,5},{8,10},{9,11},{10,... | collective-permute-start | bytes 4718600 | tf_op jit(solution)/shard_map/ppermute | solution.py:114
  571.9 41.5 %collective-permute-start.78 = (bf16[2,2,2,2,32,4096]{5,4,3,2,1,0:T(8,128)(2,1)}, bf16[2,2,2,2,32,4096]{5,4,3,2,1,0:T(8,128)(2,1)S(1)}, u32[]{:S(2)}, u32[]{:S(2)}) collective-permute-start(bf16[2,2,2,2,32,4096]{5,4,3,2,1,0:T(8,128)(2,1)} %get-tuple-element.598), channel_id=1, source_target_pairs={{0,1},{1,0},{2,3},{3,2},{4,5},{5,4},{6,7},{7,6},{8,9},{9,8},{10,11... | collective-permute-start | bytes 12582920 | tf_op jit(solution)/shard_map/ppermute | solution.py:114
  575.6 37.0 %collective-permute-start.80 = (bf16[2,2,3,32,2048]{4,3,2,1,0:T(8,128)(2,1)}, bf16[2,2,3,32,2048]{4,3,2,1,0:T(8,128)(2,1)S(1)}, u32[]{:S(2)}, u32[]{:S(2)}) collective-permute-start(bf16[2,2,3,32,2048]{4,3,2,1,0:T(8,128)(2,1)} %get-tuple-element.593.refs_14_), channel_id=1, source_target_pairs={{0,4},{4,0},{8,12},{12,8},{16,20},{20,16},{24,28},{28,24},{1,5},{5... | collective-permute-start | bytes 4718600 | tf_op jit(solution)/shard_map/ppermute | solution.py:114
  576.7 36.7 %collective-permute-start.81 = (bf16[2,2,3,32,2048]{4,3,2,1,0:T(8,128)(2,1)}, bf16[2,2,3,32,2048]{4,3,2,1,0:T(8,128)(2,1)S(1)}, u32[]{:S(2)}, u32[]{:S(2)}) collective-permute-start(bf16[2,2,3,32,2048]{4,3,2,1,0:T(8,128)(2,1)} %get-tuple-element.602), channel_id=1, source_target_pairs={{0,2},{1,3},{2,0},{3,1},{4,6},{5,7},{6,4},{7,5},{8,10},{9,11},{10,... | collective-permute-start | bytes 4718600 | tf_op jit(solution)/shard_map/ppermute | solution.py:114
  613.4 40.6 %collective-permute-start.84 = (bf16[2,2,2,2,32,4096]{5,4,3,2,1,0:T(8,128)(2,1)}, bf16[2,2,2,2,32,4096]{5,4,3,2,1,0:T(8,128)(2,1)S(1)}, u32[]{:S(2)}, u32[]{:S(2)}) collective-permute-start(bf16[2,2,2,2,32,4096]{5,4,3,2,1,0:T(8,128)(2,1)} %copy-done.111), channel_id=1, source_target_pairs={{0,1},{1,0},{2,3},{3,2},{4,5},{5,4},{6,7},{7,6},{8,9},{9,8},{10,11... | collective-permute-start | bytes 12582920 | tf_op jit(solution)/shard_map/ppermute | solution.py:114
  616.6 36.9 %collective-permute-start.86 = (bf16[2,2,3,32,2048]{4,3,2,1,0:T(8,128)(2,1)S(1)}, bf16[2,2,3,32,2048]{4,3,2,1,0:T(8,128)(2,1)S(1)}, u32[]{:S(2)}, u32[]{:S(2)}) collective-permute-start(bf16[2,2,3,32,2048]{4,3,2,1,0:T(8,128)(2,1)S(1)} %get-tuple-element.628.refs_14_), channel_id=1, source_target_pairs={{0,4},{4,0},{8,12},{12,8},{16,20},{20,16},{24,28},{28,24},{1,5},{5... | collective-permute-start | bytes 4718600 | tf_op jit(solution)/shard_map/ppermute | solution.py:114
  617.6 36.5 %collective-permute-start.87 = (bf16[2,2,3,32,2048]{4,3,2,1,0:T(8,128)(2,1)S(1)}, bf16[2,2,3,32,2048]{4,3,2,1,0:T(8,128)(2,1)S(1)}, u32[]{:S(2)}, u32[]{:S(2)}) collective-permute-start(bf16[2,2,3,32,2048]{4,3,2,1,0:T(8,128)(2,1)S(1)} %get-tuple-element.637), channel_id=1, source_target_pairs={{0,2},{1,3},{2,0},{3,1},{4,6},{5,7},{6,4},{7,5},{8,10},{9,11},{10,... | collective-permute-start | bytes 4718600 | tf_op jit(solution)/shard_map/ppermute | solution.py:114
  (226 other events, 2624.0 us)

commit v9 on v8

--- a/solution.py
+++ b/solution.py
@@ -1298,15 +1298,20 @@
     for _ in head_order:
         row_sum.step()
     row_grads = lowered(row_sum.result())
+    if cube.tuned:
+        keeps, row_grads = lax.optimization_barrier(
+            ([part.state[0] for part in head_flow.parts], row_grads)
+        )
+        for part, keep in zip(head_flow.parts, keeps):
+            part.state[0] = keep
     grad_output = out_grad.astype(jnp.float32) + matmul_tn(pick_lo, row_grads)
 
     rows_out = Scatter(cube)
     grad_second, gain_grad_final = norm_back(after_second, gain_f[5], grad_output)
     grad_out_lo = lowered(0.5 * grad_second)
     piece = weight_grads(cube, "tall", [(act_second, grad_out_lo[None])])
-    grad_second, grad_out_lo, piece = fence([head_flow], grad_second, grad_out_lo, piece)
-
-    head_flow.step()
+    grad_second, grad_out_lo, piece = fence([], grad_second, grad_out_lo, piece)
+
     rows_out.push("tall", [ffn_outer[1]], piece)
     grad_pre = act_back(grad_out_lo, outer_1, pre_second)
     piece = weight_grads(cube, "wide", [(norm_second, grad_pre)])
@@ -1343,6 +1348,7 @@
     piece = weight_grads(cube, "wide", [(norm_conv, grad_expanded), (swish_lo, conv_res_lo[None])])
     grad_expanded, piece = fence([rows_out, head_flow], grad_expanded, piece)
 
+    head_flow.step()
     rows_out.stage()
     rows_out.push("wide", [conv_expand, conv_proj], piece)
     grad_attn_res, gain_grad_conv = product_norm_back(
@@ -1361,7 +1367,9 @@
         valid_rows[None, :],
     )
     piece = weight_grads(cube, "wide", [(norm_attn, grad_mixed), (attended_lo, attn_res_lo[None])])
-    grad_mixed, grad_attn_res, piece = fence([rows_out], grad_mixed, grad_attn_res, piece)
+    grad_mixed, grad_attn_res, piece = fence(
+        [rows_out, head_flow], grad_mixed, grad_attn_res, piece
+    )
 
     rows_out.stage()
     rows_out.push("wide", [attn_qkv, attn_proj], piece)

time: 763 us -> 756 us (level)
  waiting for transfers between devices: 292 us -> 284 us
    ppermute x104, waiting for transfers between devices: 292 us -> 284 us  [swap(): lax.ppermute(values, axis, [(i, i ^ bit) for i in range(self.sizes[axis])])]
  transfers between devices with their start and end apart: 104 -> 104, of which waited for: 66 -> 62; matrix products, arithmetic and copies ran while one was open for 8% -> 7% of each run, Pallas kernels for 26% -> 25%
where the time goes in v9:
time: 756 us; the launch traced here: 746 us
  waiting for transfers between devices  284 us (38%)
  Pallas kernels  215 us (28%)
  starting transfers between devices  110 us (15%)
  local copies, waits for them, and re-layouts  56.6 us (7%)
  matrix products  51.4 us (7%)
  other arithmetic  21.1 us (3%)
    ppermute x104, waiting for transfers between devices, swap(): lax.ppermute(values, axis, [(i, i ^ bit) for i in range(self.sizes[axis])])  284 us
    ppermute x104, starting transfers between devices, swap(): lax.ppermute(values, axis, [(i, i ^ bit) for i in range(self.sizes[axis])])  110 us
    unnamed x291, local copies, waits for them, and re-layouts  44.5 us
    pallas_call x18, Pallas kernels, sums(): pl.pallas_call(kernel, grid_spec=pltpu.PrefetchScalarGridSpec(num_scalar_...  39.5 us
    dot_general x10, matrix products, matmul(): return jnp.dot(operand, weight, preferred_element_type=jnp.float32)  35.8 us
    pallas_call x4, Pallas kernels, product_norm_back(): pl.pallas_call(functools.partial(norm_back_kernel, row), grid=(inner // w...  31.8 us
    pallas_call x4, Pallas kernels, weight_grads(): pl.pallas_call(functools.partial(weight_grads_kernel, counts), grid=(COLU...  29.3 us
    pallas_call x38, Pallas kernels, local_copies(): pl.pallas_call(kernel, out_shape=[jax.ShapeDtypeStruct(shape, inputs[0].d...  27.4 us
  transfers between devices with their start and end apart: 104, of which 62 were waited for; matrix products, arithmetic and copies ran while one was open for 7% of the time, Pallas kernels for 25%

profile of v9, /device:TPU:0, one launch (start us, length us, event | category | flops | bytes accessed | tf_op | source)
XLA Modules:
  0.0 745.5 jit_solution(8894005374849078366)
XLA Ops:
  41.5 11.6 %collective-permute-done.14.refs_1_ = bf16[2,2,2,48,32]{4,3,2,1,0:T(8,128)(2,1)S(1)} collective-permute-done((bf16[2,2,2,48,32]{4,3,2,1,0:T(8,128)(2,1)S(1)}, bf16[2,2,2,48,32]{4,3,2,1,0:T(8,128)(2,1)S(1)}, u32[]{:S(2)}, u32[]{:S(2)}) %collective-permute-start.14) | collective-permute-done | bytes 24608 | tf_op jit(solution)/shard_map/ppermute | solution.py:114
  62.8 14.1 %collective-permute-done.19.refs_1_ = bf16[2,2,2,2,48,32]{5,4,3,2,1,0:T(8,128)(2,1)S(1)} collective-permute-done((bf16[2,2,2,2,48,32]{5,4,3,2,1,0:T(8,128)(2,1)S(1)}, bf16[2,2,2,2,48,32]{5,4,3,2,1,0:T(8,128)(2,1)S(1)}, u32[]{:S(2)}, u32[]{:S(2)}) %collective-permute-start.19) | collective-permute-done | bytes 49184 | tf_op jit(solution)/shard_map/ppermute | solution.py:114
  81.9 9.2 %collective-permute-done.18.refs_1_ = bf16[32,4096]{1,0:T(8,128)(2,1)S(1)} collective-permute-done((bf16[32,4096]{1,0:T(8,128)(2,1)S(1)}, bf16[32,4096]{1,0:T(8,128)(2,1)S(1)}, u32[]{:S(2)}, u32[]{:S(2)}) %collective-permute-start.18) | collective-permute-done | bytes 262176 | tf_op jit(solution)/shard_map/ppermute | solution.py:114
  117.7 15.3 %collective-permute-done.21.refs_3_ = bf16[2,2,3,32,2048]{4,3,2,1,0:T(8,128)(2,1)S(1)} collective-permute-done((bf16[2,2,3,32,2048]{4,3,2,1,0:T(8,128)(2,1)S(1)}, bf16[2,2,3,32,2048]{4,3,2,1,0:T(8,128)(2,1)S(1)}, u32[]{:S(2)}, u32[]{:S(2)}) %collective-permute-start.21) | collective-permute-done | bytes 1572896 | tf_op jit(solution)/shard_map/ppermute | solution.py:114
  156.7 16.0 %collective-permute-done.26.refs_3_ = bf16[2,2,3,32,2048]{4,3,2,1,0:T(8,128)(2,1)S(1)} collective-permute-done((bf16[2,2,3,32,2048]{4,3,2,1,0:T(8,128)(2,1)S(1)}, bf16[2,2,3,32,2048]{4,3,2,1,0:T(8,128)(2,1)S(1)}, u32[]{:S(2)}, u32[]{:S(2)}) %collective-permute-start.26) | collective-permute-done | bytes 1572896 | tf_op jit(solution)/shard_map/ppermute | solution.py:114
  186.8 12.8 %shard_map.270 = (bf16[512,1024]{1,0:T(8,128)(2,1)S(1)}, bf16[512,1024]{1,0:T(8,128)(2,1)S(1)}, bf16[512,1024]{1,0:T(8,128)(2,1)S(1)}, bf16[512,1024]{1,0:T(8,128)(2,1)S(1)}, f32[512,1024]{1,0:T(8,128)S(1)}) custom-call(f32[512,3072]{1,0:T(8,128)S(1)} %fusion.28.query_ref.key_ref.value_ref, f32[512,3072]{1,0:T(8,128)S(1)} %fusion.28.query_ref.key_ref.value_ref, ...), custom_call_target="tpu_custom_call" | custom-call | tf_op jit(solution)/shard_map/pallas_call | solution.py:1051
  202.9 10.7 %collective-permute-done.33.refs_5_ = bf16[2,32,4096]{2,1,0:T(8,128)(2,1)S(1)} collective-permute-done((bf16[2,32,4096]{2,1,0:T(8,128)(2,1)S(1)}, bf16[2,32,4096]{2,1,0:T(8,128)(2,1)S(1)}, u32[]{:S(2)}, u32[]{:S(2)}) %collective-permute-start.33) | collective-permute-done | bytes 524320 | tf_op jit(solution)/shard_map/ppermute | solution.py:114
  228.5 10.9 %shard_map.275 = (f32[512,1024]{1,0:T(8,128)S(1)}, f32[8,1024]{1,0:T(8,128)S(1)}) custom-call(f32[512,2048]{1,0:T(8,128)S(1)} %fusion.29.lead_ref.gate_ref, f32[512,2048]{1,0:T(8,128)S(1)} %fusion.29.lead_ref.gate_ref, f32[512,1]{1,0:T(8,128)S(1)} %fusion.6.valid_ref, f32[48,1024]{1,0:T(8,128)S(1)} %shard_map.260.taps_ref.vectors_ref), custom_call_target="tpu_custom_call" | custom-call | tf_op jit(solution)/shard_map/pallas_call | solution.py:718
  276.1 13.2 %collective-permute-done.47.refs_3_ = bf16[2,2,128,1024]{3,2,1,0:T(8,128)(2,1)} collective-permute-done((bf16[2,2,128,1024]{3,2,1,0:T(8,128)(2,1)S(1)}, bf16[2,2,128,1024]{3,2,1,0:T(8,128)(2,1)}, u32[]{:S(2)}, u32[]{:S(2)}) %collective-permute-start.47) | collective-permute-done | bytes 1048608 | tf_op jit(solution)/shard_map/ppermute | solution.py:114
  307.6 11.2 %collective-permute-done.50.refs_1_ = bf16[200,1024]{1,0:T(8,128)(2,1)S(1)} collective-permute-done((bf16[200,1024]{1,0:T(8,128)(2,1)S(1)}, bf16[200,1024]{1,0:T(8,128)(2,1)S(1)}, u32[]{:S(2)}, u32[]{:S(2)}) %collective-permute-start.50) | collective-permute-done | bytes 409632 | tf_op jit(solution)/shard_map/ppermute | solution.py:114
  383.6 7.9 %shard_map.292.grad_ref.refs_1_ = bf16[4,512,1024]{2,1,0:T(8,128)(2,1)S(1)} custom-call(bf16[512,1024]{1,0:T(8,128)(2,1)S(1)} %copy-done.22, bf16[4096,1024]{1,0:T(8,128)(2,1)S(1)} %bitcast.121, bf16[512,4096]{1,0:T(8,128)(2,1)S(1)} %copy-done.31), custom_call_target="tpu_custom_call" | custom-call | tf_op jit(solution)/shard_map/pallas_call | solution.py:849
  405.9 8.9 %shard_map.293 = (f32[512,1024]{1,0:T(8,128)S(1)}, f32[1,1024]{1,0:T(1,128)S(1)}) custom-call(bf16[4,512,1024]{2,1,0:T(8,128)(2,1)S(1)} %shard_map.292.grad_ref.refs_1_, bf16[1024,4096]{1,0:T(8,128)(2,1)S(1)} %bitcast.119, f32[512,1024]{1,0:T(8,128)S(1)} %copy-done.20, f32[48,1024]{1,0:T(8,128)S(1)} %shard_map.260.taps_ref.vectors_ref, ...), custom_call_target="tpu_custom_call" | custom-call | tf_op jit(solution)/shard_map/pallas_call | solution.py:1003
  457.7 15.3 %shard_map.299 = (bf16[2,512,1024]{2,1,0:T(8,128)(2,1)S(1)}, f32[32,1024]{1,0:T(8,128)S(1)}) custom-call(f32[512,2048]{1,0:T(8,128)S(1)} %copy-done.4, f32[512,2048]{1,0:T(8,128)S(1)} %copy-done.4, f32[512,1]{1,0:T(8,128)S(1)} %fusion.6.valid_ref, f32[48,1024]{1,0:T(8,128)S(1)} %shard_map.260.taps_ref.vectors_ref, f32[512,1024]{1,0:T(8,128)S(1)} %copy-done.25, ...), custom_call_target="tpu_custom_call" | custom-call | tf_op jit(solution)/shard_map/pallas_call | solution.py:802
  500.1 12.7 %shard_map.306.refs_2_.grad_ref = bf16[3,512,1024]{2,1,0:T(8,128)(2,1)S(1)} custom-call(bf16[512,1024]{1,0:T(8,128)(2,1)S(1)} %copy-done.87, bf16[512,1024]{1,0:T(8,128)(2,1)S(1)} %copy-done.89, bf16[512,1024]{1,0:T(8,128)(2,1)S(1)} %copy-done.91, f32[512,1024]{1,0:T(8,128)S(1)} %copy-done.79, bf16[512,1024]{1,0:T(8,128)(2,1)S(1)} %convolution_convert_fusion.2.grad_ref, ...), custom_call_target="tpu_custom_call" | custom-call | tf_op jit(solution)/shard_map/pallas_call | solution.py:1091
  514.4 7.9 %shard_map.307 = (bf16[2,2,2,2,32,4096]{5,4,3,2,1,0:T(8,128)(2,1)S(1)}, bf16[2,2,2,2,32,4096]{5,4,3,2,1,0:T(8,128)(2,1)}) custom-call(bf16[512,1024]{1,0:T(8,128)(2,1)S(1)} %copy-done.51, bf16[512,1024]{1,0:T(8,128)(2,1)S(1)} %copy-done.85, bf16[3,512,1024]{2,1,0:T(8,128)(2,1)S(1)} %shard_map.306.refs_2_.grad_ref, ...), custom_call_target="tpu_custom_call" | custom-call | tf_op jit(solution)/shard_map/pallas_call | solution.py:955
  557.1 7.9 %shard_map.311.grad_ref.refs_1_ = bf16[4,512,1024]{2,1,0:T(8,128)(2,1)S(1)} custom-call(bf16[512,1024]{1,0:T(8,128)(2,1)S(1)} %multiply_convert_fusion.3.grad_ref, bf16[4096,1024]{1,0:T(8,128)(2,1)S(1)} %bitcast.117, bf16[512,4096]{1,0:T(8,128)(2,1)S(1)} %copy-done.30), custom_call_target="tpu_custom_call" | custom-call | tf_op jit(solution)/shard_map/pallas_call | solution.py:849
  577.6 10.3 %shard_map.315 = (f32[512,1024]{1,0:T(8,128)}, f32[1,1024]{1,0:T(1,128)S(1)}) custom-call(bf16[4,512,1024]{2,1,0:T(8,128)(2,1)S(1)} %shard_map.311.grad_ref.refs_1_, bf16[1024,4096]{1,0:T(8,128)(2,1)S(1)} %bitcast.115, f32[512,1024]{1,0:T(8,128)S(1)} %convert_element_type.162.values_ref, f32[48,1024]{1,0:T(8,128)S(1)} %shard_map.260.taps_ref.vectors_ref, ...), custom_call_target="tpu_custom_call" | custom-call | tf_op jit(solution)/shard_map/pallas_call | solution.py:1003
  591.3 8.0 %shard_map.318 = (bf16[2,2,2,2,32,4096]{5,4,3,2,1,0:T(8,128)(2,1)S(1)}, bf16[2,2,2,2,32,4096]{5,4,3,2,1,0:T(8,128)(2,1)}) custom-call(bf16[512,1024]{1,0:T(8,128)(2,1)S(1)} %copy-done.47, bf16[4,512,1024]{2,1,0:T(8,128)(2,1)S(1)} %shard_map.311.grad_ref.refs_1_), custom_call_target="tpu_custom_call" | custom-call | tf_op jit(solution)/shard_map/pallas_call | solution.py:955
  627.8 9.8 %collective-permute-done.85 = bf16[32,4096]{1,0:T(8,128)(2,1)S(1)} collective-permute-done((bf16[32,4096]{1,0:T(8,128)(2,1)S(1)}, bf16[32,4096]{1,0:T(8,128)(2,1)S(1)}, u32[]{:S(2)}, u32[]{:S(2)}) %collective-permute-start.85) | collective-permute-done | bytes 262176 | tf_op jit(solution)/shard_map/ppermute | solution.py:114
  637.6 10.0 %collective-permute-done.86.refs_7_.refs_9_ = bf16[2,2,3,32,2048]{4,3,2,1,0:T(8,128)(2,1)S(1)} collective-permute-done((bf16[2,2,3,32,2048]{4,3,2,1,0:T(8,128)(2,1)S(1)}, bf16[2,2,3,32,2048]{4,3,2,1,0:T(8,128)(2,1)S(1)}, u32[]{:S(2)}, u32[]{:S(2)}) %collective-permute-start.86) | collective-permute-done | bytes 1572896 | tf_op jit(solution)/shard_map/ppermute | solution.py:114
  673.0 13.5 %collective-permute-done.91.refs_3_.refs_5_ = bf16[2,2,3,32,2048]{4,3,2,1,0:T(8,128)(2,1)S(1)} collective-permute-done((bf16[2,2,3,32,2048]{4,3,2,1,0:T(8,128)(2,1)S(1)}, bf16[2,2,3,32,2048]{4,3,2,1,0:T(8,128)(2,1)S(1)}, u32[]{:S(2)}, u32[]{:S(2)}) %collective-permute-start.91) | collective-permute-done | bytes 1572896 | tf_op jit(solution)/shard_map/ppermute | solution.py:114
  695.9 10.6 %collective-permute-done.95 = bf16[32,4096]{1,0:T(8,128)(2,1)S(1)} collective-permute-done((bf16[32,4096]{1,0:T(8,128)(2,1)S(1)}, bf16[32,4096]{1,0:T(8,128)(2,1)S(1)}, u32[]{:S(2)}, u32[]{:S(2)}) %collective-permute-start.95) | collective-permute-done | bytes 262176 | tf_op jit(solution)/shard_map/ppermute | solution.py:114
  714.8 10.2 %collective-permute-done.100 = bf16[32,4096]{1,0:T(8,128)(2,1)S(1)} collective-permute-done((bf16[32,4096]{1,0:T(8,128)(2,1)S(1)}, bf16[32,4096]{1,0:T(8,128)(2,1)S(1)}, u32[]{:S(2)}, u32[]{:S(2)}) %collective-permute-start.100) | collective-permute-done | bytes 262176 | tf_op jit(solution)/shard_map/ppermute | solution.py:114
  731.2 10.4 %collective-permute-done.103 = bf16[32,4096]{1,0:T(8,128)(2,1)S(1)} collective-permute-done((bf16[32,4096]{1,0:T(8,128)(2,1)S(1)}, bf16[32,4096]{1,0:T(8,128)(2,1)S(1)}, u32[]{:S(2)}, u32[]{:S(2)}) %collective-permute-start.103) | collective-permute-done | bytes 262176 | tf_op jit(solution)/shard_map/ppermute | solution.py:114
  (689 shorter events, 470.0 us)
Async XLA Ops:
  54.2 37.6 %collective-permute-start.15 = (bf16[2,2,3,32,2048]{4,3,2,1,0:T(8,128)(2,1)S(1)}, bf16[2,2,3,32,2048]{4,3,2,1,0:T(8,128)(2,1)S(1)}, u32[]{:S(2)}, u32[]{:S(2)}) collective-permute-start(bf16[2,2,3,32,2048]{4,3,2,1,0:T(8,128)(2,1)S(1)} %get-tuple-element.397.refs_2_), channel_id=1, source_target_pairs={{0,4},{4,0},{8,12},{12,8},{16,20},{20,16},{24,28},{28,24},{1,5},{5... | collective-permute-start | bytes 4718600 | tf_op jit(solution)/shard_map/ppermute | solution.py:114
  96.5 36.5 %collective-permute-start.21 = (bf16[2,2,3,32,2048]{4,3,2,1,0:T(8,128)(2,1)S(1)}, bf16[2,2,3,32,2048]{4,3,2,1,0:T(8,128)(2,1)S(1)}, u32[]{:S(2)}, u32[]{:S(2)}) collective-permute-start(bf16[2,2,3,32,2048]{4,3,2,1,0:T(8,128)(2,1)S(1)} %get-tuple-element.409.refs_4_.refs_2_), channel_id=1, source_target_pairs={{0,4},{4,0},{8,12},{12,8},{16,20},{20,16},{24,28},{28,24},{1,5},{5... | collective-permute-start | bytes 4718600 | tf_op jit(solution)/shard_map/ppermute | solution.py:114
  136.3 36.5 %collective-permute-start.26 = (bf16[2,2,3,32,2048]{4,3,2,1,0:T(8,128)(2,1)S(1)}, bf16[2,2,3,32,2048]{4,3,2,1,0:T(8,128)(2,1)S(1)}, u32[]{:S(2)}, u32[]{:S(2)}) collective-permute-start(bf16[2,2,3,32,2048]{4,3,2,1,0:T(8,128)(2,1)S(1)} %get-tuple-element.421.refs_4_.refs_2_), channel_id=1, source_target_pairs={{0,4},{4,0},{8,12},{12,8},{16,20},{20,16},{24,28},{28,24},{1,5},{5... | collective-permute-start | bytes 4718600 | tf_op jit(solution)/shard_map/ppermute | solution.py:114
  178.5 36.5 %collective-permute-start.31 = (bf16[2,2,3,32,2048]{4,3,2,1,0:T(8,128)(2,1)S(1)}, bf16[2,2,3,32,2048]{4,3,2,1,0:T(8,128)(2,1)S(1)}, u32[]{:S(2)}, u32[]{:S(2)}) collective-permute-start(bf16[2,2,3,32,2048]{4,3,2,1,0:T(8,128)(2,1)S(1)} %get-tuple-element.441.refs_4_.refs_0_.refs_2_), channel_id=1, source_target_pairs={{0,4},{4,0},{8,12},{12,8},{16,20},{20,16},{24,28},{28,24},{1,5},{5... | collective-permute-start | bytes 4718600 | tf_op jit(solution)/shard_map/ppermute | solution.py:114
  217.4 41.5 %collective-permute-start.36 = (bf16[2,2,3,32,2048]{4,3,2,1,0:T(8,128)(2,1)S(1)}, bf16[2,2,3,32,2048]{4,3,2,1,0:T(8,128)(2,1)S(1)}, u32[]{:S(2)}, u32[]{:S(2)}) collective-permute-start(bf16[2,2,3,32,2048]{4,3,2,1,0:T(8,128)(2,1)S(1)} %get-tuple-element.458.refs_4_.refs_0_.refs_2_), channel_id=1, source_target_pairs={{0,4},{4,0},{8,12},{12,8},{16,20},{20,16},{24,28},{28,24},{1,5},{5... | collective-permute-start | bytes 4718600 | tf_op jit(solution)/shard_map/ppermute | solution.py:114
  218.0 41.0 %collective-permute-start.37 = (bf16[2,2,3,32,2048]{4,3,2,1,0:T(8,128)(2,1)S(1)}, bf16[2,2,3,32,2048]{4,3,2,1,0:T(8,128)(2,1)S(1)}, u32[]{:S(2)}, u32[]{:S(2)}) collective-permute-start(bf16[2,2,3,32,2048]{4,3,2,1,0:T(8,128)(2,1)S(1)} %get-tuple-element.460.refs_2_.refs_0_), channel_id=1, source_target_pairs={{0,2},{1,3},{2,0},{3,1},{4,6},{5,7},{6,4},{7,5},{8,10},{9,11},{10,... | collective-permute-start | bytes 4718600 | tf_op jit(solution)/shard_map/ppermute | solution.py:114
  219.8 39.1 %collective-permute-start.38 = (bf16[2,128,1024]{2,1,0:T(8,128)(2,1)S(1)}, bf16[2,128,1024]{2,1,0:T(8,128)(2,1)S(1)}, u32[]{:S(2)}, u32[]{:S(2)}) collective-permute-start(bf16[2,128,1024]{2,1,0:T(8,128)(2,1)S(1)} %shard_map.272.refs_0_), channel_id=1, source_target_pairs={{0,16},{4,20},{8,24},{12,28},{16,0},{20,4},{24,8},{28,12},{1,17},{... | collective-permute-start | bytes 1572872 | tf_op jit(solution)/shard_map/ppermute | solution.py:114
  374.1 40.8 %collective-permute-start.58 = (bf16[2,2,2,2,32,4096]{5,4,3,2,1,0:T(8,128)(2,1)}, bf16[2,2,2,2,32,4096]{5,4,3,2,1,0:T(8,128)(2,1)}, u32[]{:S(2)}, u32[]{:S(2)}) collective-permute-start(bf16[2,2,2,2,32,4096]{5,4,3,2,1,0:T(8,128)(2,1)} %get-tuple-element.496), channel_id=1, source_target_pairs={{0,1},{1,0},{2,3},{3,2},{4,5},{5,4},{6,7},{7,6},{8,9},{9,8},{10,11... | collective-permute-start | bytes 12582920 | tf_op jit(solution)/shard_map/ppermute | solution.py:114
  374.1 40.8 %collective-permute-start.56 = (bf16[2,2,128,1024]{3,2,1,0:T(8,128)(2,1)}, bf16[2,2,128,1024]{3,2,1,0:T(8,128)(2,1)}, u32[]{:S(2)}, u32[]{:S(2)}) collective-permute-start(bf16[2,2,128,1024]{3,2,1,0:T(8,128)(2,1)} %get-tuple-element.490), channel_id=1, source_target_pairs={{0,4},{4,0},{8,12},{12,8},{16,20},{20,16},{24,28},{28,24},{1,5},{5... | collective-permute-start | bytes 3145736 | tf_op jit(solution)/shard_map/ppermute | solution.py:114
  374.5 40.4 %collective-permute-start.57 = (bf16[2,2,128,1024]{3,2,1,0:T(8,128)(2,1)}, bf16[2,2,128,1024]{3,2,1,0:T(8,128)(2,1)}, u32[]{:S(2)}, u32[]{:S(2)}) collective-permute-start(bf16[2,2,128,1024]{3,2,1,0:T(8,128)(2,1)} %get-tuple-element.492), channel_id=1, source_target_pairs={{0,8},{4,12},{8,0},{12,4},{16,24},{20,28},{24,16},{28,20},{1,9},{5... | collective-permute-start | bytes 3145736 | tf_op jit(solution)/shard_map/ppermute | solution.py:114
  439.5 40.1 %collective-permute-start.64 = (bf16[2,2,2,2,32,4096]{5,4,3,2,1,0:T(8,128)(2,1)}, bf16[2,2,2,2,32,4096]{5,4,3,2,1,0:T(8,128)(2,1)}, u32[]{:S(2)}, u32[]{:S(2)}) collective-permute-start(bf16[2,2,2,2,32,4096]{5,4,3,2,1,0:T(8,128)(2,1)} %copy-done.117), channel_id=1, source_target_pairs={{0,1},{1,0},{2,3},{3,2},{4,5},{5,4},{6,7},{7,6},{8,9},{9,8},{10,11... | collective-permute-start | bytes 12582920 | tf_op jit(solution)/shard_map/ppermute | solution.py:114
  479.6 46.2 %collective-permute-start.69 = (bf16[2,2,2,2,32,4096]{5,4,3,2,1,0:T(8,128)(2,1)}, bf16[2,2,2,2,32,4096]{5,4,3,2,1,0:T(8,128)(2,1)S(1)}, u32[]{:S(2)}, u32[]{:S(2)}) collective-permute-start(bf16[2,2,2,2,32,4096]{5,4,3,2,1,0:T(8,128)(2,1)} %get-tuple-element.544), channel_id=1, source_target_pairs={{0,1},{1,0},{2,3},{3,2},{4,5},{5,4},{6,7},{7,6},{8,9},{9,8},{10,11... | collective-permute-start | bytes 12582920 | tf_op jit(solution)/shard_map/ppermute | solution.py:114
  483.2 42.6 %collective-permute-start.70 = (bf16[2,2,3,32,2048]{4,3,2,1,0:T(8,128)(2,1)S(1)}, bf16[2,2,3,32,2048]{4,3,2,1,0:T(8,128)(2,1)S(1)}, u32[]{:S(2)}, u32[]{:S(2)}) collective-permute-start(bf16[2,2,3,32,2048]{4,3,2,1,0:T(8,128)(2,1)S(1)} %get-tuple-element.539.refs_8_), channel_id=1, source_target_pairs={{0,4},{4,0},{8,12},{12,8},{16,20},{20,16},{24,28},{28,24},{1,5},{5... | collective-permute-start | bytes 4718600 | tf_op jit(solution)/shard_map/ppermute | solution.py:114
  484.6 41.2 %collective-permute-start.71 = (bf16[2,2,3,32,2048]{4,3,2,1,0:T(8,128)(2,1)S(1)}, bf16[2,2,3,32,2048]{4,3,2,1,0:T(8,128)(2,1)S(1)}, u32[]{:S(2)}, u32[]{:S(2)}) collective-permute-start(bf16[2,2,3,32,2048]{4,3,2,1,0:T(8,128)(2,1)S(1)} %get-tuple-element.546), channel_id=1, source_target_pairs={{0,2},{1,3},{2,0},{3,1},{4,6},{5,7},{6,4},{7,5},{8,10},{9,11},{10,... | collective-permute-start | bytes 4718600 | tf_op jit(solution)/shard_map/ppermute | solution.py:114
  489.2 36.5 %collective-permute-start.73 = (bf16[128,1024]{1,0:T(8,128)(2,1)S(1)}, bf16[128,1024]{1,0:T(8,128)(2,1)}, u32[]{:S(2)}, u32[]{:S(2)}) collective-permute-start(bf16[128,1024]{1,0:T(8,128)(2,1)S(1)} %get-tuple-element.554), channel_id=1, source_target_pairs={{0,4},{4,0},{8,12},{12,8},{16,20},{20,16},{24,28},{28,24},{1,5},{5... | collective-permute-start | bytes 786440 | tf_op jit(solution)/shard_map/ppermute | solution.py:114
  525.8 41.7 %collective-permute-start.74 = (bf16[2,2,2,2,32,4096]{5,4,3,2,1,0:T(8,128)(2,1)}, bf16[2,2,2,2,32,4096]{5,4,3,2,1,0:T(8,128)(2,1)S(1)}, u32[]{:S(2)}, u32[]{:S(2)}) collective-permute-start(bf16[2,2,2,2,32,4096]{5,4,3,2,1,0:T(8,128)(2,1)} %get-tuple-element.578), channel_id=1, source_target_pairs={{0,1},{1,0},{2,3},{3,2},{4,5},{5,4},{6,7},{7,6},{8,9},{9,8},{10,11... | collective-permute-start | bytes 12582920 | tf_op jit(solution)/shard_map/ppermute | solution.py:114
  529.5 37.0 %collective-permute-start.75 = (bf16[2,2,3,32,2048]{4,3,2,1,0:T(8,128)(2,1)}, bf16[2,2,3,32,2048]{4,3,2,1,0:T(8,128)(2,1)S(1)}, u32[]{:S(2)}, u32[]{:S(2)}) collective-permute-start(bf16[2,2,3,32,2048]{4,3,2,1,0:T(8,128)(2,1)} %get-tuple-element.573.refs_12_), channel_id=1, source_target_pairs={{0,4},{4,0},{8,12},{12,8},{16,20},{20,16},{24,28},{28,24},{1,5},{5... | collective-permute-start | bytes 4718600 | tf_op jit(solution)/shard_map/ppermute | solution.py:114
  530.8 36.7 %collective-permute-start.76 = (bf16[2,2,3,32,2048]{4,3,2,1,0:T(8,128)(2,1)}, bf16[2,2,3,32,2048]{4,3,2,1,0:T(8,128)(2,1)S(1)}, u32[]{:S(2)}, u32[]{:S(2)}) collective-permute-start(bf16[2,2,3,32,2048]{4,3,2,1,0:T(8,128)(2,1)} %get-tuple-element.580), channel_id=1, source_target_pairs={{0,2},{1,3},{2,0},{3,1},{4,6},{5,7},{6,4},{7,5},{8,10},{9,11},{10,... | collective-permute-start | bytes 4718600 | tf_op jit(solution)/shard_map/ppermute | solution.py:114
  567.5 41.1 %collective-permute-start.78 = (bf16[2,2,2,2,32,4096]{5,4,3,2,1,0:T(8,128)(2,1)}, bf16[2,2,2,2,32,4096]{5,4,3,2,1,0:T(8,128)(2,1)S(1)}, u32[]{:S(2)}, u32[]{:S(2)}) collective-permute-start(bf16[2,2,2,2,32,4096]{5,4,3,2,1,0:T(8,128)(2,1)} %get-tuple-element.604), channel_id=1, source_target_pairs={{0,1},{1,0},{2,3},{3,2},{4,5},{5,4},{6,7},{7,6},{8,9},{9,8},{10,11... | collective-permute-start | bytes 12582920 | tf_op jit(solution)/shard_map/ppermute | solution.py:114
  571.2 37.0 %collective-permute-start.80 = (bf16[2,2,3,32,2048]{4,3,2,1,0:T(8,128)(2,1)}, bf16[2,2,3,32,2048]{4,3,2,1,0:T(8,128)(2,1)S(1)}, u32[]{:S(2)}, u32[]{:S(2)}) collective-permute-start(bf16[2,2,3,32,2048]{4,3,2,1,0:T(8,128)(2,1)} %get-tuple-element.599.refs_14_), channel_id=1, source_target_pairs={{0,4},{4,0},{8,12},{12,8},{16,20},{20,16},{24,28},{28,24},{1,5},{5... | collective-permute-start | bytes 4718600 | tf_op jit(solution)/shard_map/ppermute | solution.py:114
  571.9 36.7 %collective-permute-start.81 = (bf16[2,2,3,32,2048]{4,3,2,1,0:T(8,128)(2,1)}, bf16[2,2,3,32,2048]{4,3,2,1,0:T(8,128)(2,1)S(1)}, u32[]{:S(2)}, u32[]{:S(2)}) collective-permute-start(bf16[2,2,3,32,2048]{4,3,2,1,0:T(8,128)(2,1)} %get-tuple-element.608), channel_id=1, source_target_pairs={{0,2},{1,3},{2,0},{3,1},{4,6},{5,7},{6,4},{7,5},{8,10},{9,11},{10,... | collective-permute-start | bytes 4718600 | tf_op jit(solution)/shard_map/ppermute | solution.py:114
  608.6 40.0 %collective-permute-start.84 = (bf16[2,2,2,2,32,4096]{5,4,3,2,1,0:T(8,128)(2,1)}, bf16[2,2,2,2,32,4096]{5,4,3,2,1,0:T(8,128)(2,1)S(1)}, u32[]{:S(2)}, u32[]{:S(2)}) collective-permute-start(bf16[2,2,2,2,32,4096]{5,4,3,2,1,0:T(8,128)(2,1)} %get-tuple-element.639), channel_id=1, source_target_pairs={{0,1},{1,0},{2,3},{3,2},{4,5},{5,4},{6,7},{7,6},{8,9},{9,8},{10,11... | collective-permute-start | bytes 12582920 | tf_op jit(solution)/shard_map/ppermute | solution.py:114
  610.8 36.9 %collective-permute-start.86 = (bf16[2,2,3,32,2048]{4,3,2,1,0:T(8,128)(2,1)S(1)}, bf16[2,2,3,32,2048]{4,3,2,1,0:T(8,128)(2,1)S(1)}, u32[]{:S(2)}, u32[]{:S(2)}) collective-permute-start(bf16[2,2,3,32,2048]{4,3,2,1,0:T(8,128)(2,1)S(1)} %get-tuple-element.634.refs_14_), channel_id=1, source_target_pairs={{0,4},{4,0},{8,12},{12,8},{16,20},{20,16},{24,28},{28,24},{1,5},{5... | collective-permute-start | bytes 4718600 | tf_op jit(solution)/shard_map/ppermute | solution.py:114
  612.1 36.5 %collective-permute-start.87 = (bf16[2,2,3,32,2048]{4,3,2,1,0:T(8,128)(2,1)S(1)}, bf16[2,2,3,32,2048]{4,3,2,1,0:T(8,128)(2,1)S(1)}, u32[]{:S(2)}, u32[]{:S(2)}) collective-permute-start(bf16[2,2,3,32,2048]{4,3,2,1,0:T(8,128)(2,1)S(1)} %get-tuple-element.643), channel_id=1, source_target_pairs={{0,2},{1,3},{2,0},{3,1},{4,6},{5,7},{6,4},{7,5},{8,10},{9,11},{10,... | collective-permute-start | bytes 4718600 | tf_op jit(solution)/shard_map/ppermute | solution.py:114
  (226 other events, 2658.5 us)
